TPU v7x, 32 devices: a whole 2x2x4 slice. The times are simulated.
32 devices in a mesh: groups: 2 (over y), field: 4 (over x, core), wave: 4 (over z).
Axes of the slice: x: 2, y: 2, z: 4, core: 2. Of those that a mesh axis runs over, the one named last changes fastest.
Arguments:
- mode_basis: bfloat16 [22, 512, 512], P(None, 'wave'), may hold values from -6 to 6
- coef_table: bfloat16 [4096, 22], replicated, may hold values from -1.5 to 1.5
- table_index: int32 [64], P(('groups', 'field')), parts along dimension 0, may hold values from 0 to 4095
- wave_lengths: float32 [8], P('wave'), may hold values from 0.32 to 1.05
- sed_table: float32 [1024, 8], replicated, may hold values from 0.05 to 1
- template_ids: int32 [64, 8], P(('groups', 'field')), parts along dimension 0, may hold values from 0 to 1023
Outputs:
- mixed: bfloat16 [64, 8, 256, 256], P(('groups', 'field'), None, 'wave'), parts along dimension 0
There are 2 independent parts, one for each index of `groups`. A program takes and returns all parts, laid end to end along the dimension named above; an argument that names none is the same for every part. Nothing has to cross between parts.
All inputs are finite; a program needn't handle non-finite values.
Results may differ from a plain program's by a relative error of at most 0.0065.
Values may be sent and summed in bfloat16 or wider, within the bound.
No kernel may reach another device: no remote copies, remote signals or barrier semaphores. Data moves between devices by JAX's collectives and lax.ppermute only.
A program may use at most 128 MiB of HBM per device.

v0:
```python
import math

import jax
import jax.numpy as jnp
from jax import lax
from jax.sharding import PartitionSpec as P

PUP = 512
PIX = 256


TWO_PI = 2.0 * math.pi
SAMPLING = 0.25
EPSILON = 1e-06


def transform_table(wave_lengths, pixels, pupil_side):
    pixel_offset = jnp.arange(pixels, dtype=jnp.int32) - pixels // 2
    pupil_offset = 2 * jnp.arange(pupil_side, dtype=jnp.int32) - pupil_side + 1
    products = (pixel_offset[:, None] * pupil_offset[None, :]).astype(jnp.float32)
    factor = TWO_PI * SAMPLING / (2.0 * pupil_side) / wave_lengths
    angles = products[None, :, :] * factor[:, None, None]
    cosine = jnp.cos(angles)
    sine_part = jnp.sin(angles)
    upper_half = jnp.concatenate([cosine, sine_part], axis=2)
    lower_half = jnp.concatenate([-sine_part, cosine], axis=2)
    return jnp.concatenate([upper_half, lower_half], axis=1).astype(jnp.bfloat16)


def aperture_rows(row_start, row_count, pupil_side):
    row_pos = 2 * (row_start + jnp.arange(row_count, dtype=jnp.int32)) - pupil_side + 1
    col_pos = 2 * jnp.arange(pupil_side, dtype=jnp.int32) - pupil_side + 1
    radius_sq = row_pos[:, None] * row_pos[:, None] + col_pos[None, :] * col_pos[None, :]
    inner_edge = 61 * pupil_side // 100
    inside = (radius_sq <= pupil_side * pupil_side) & (radius_sq >= inner_edge * inner_edge)
    return inside.astype(jnp.float32)


def pupil_section(path_rows, wave_lengths, kernel_table, row_start):
    row_count = path_rows.shape[1]
    pupil_side = path_rows.shape[2]
    opening = aperture_rows(row_start, row_count, pupil_side)
    phase_map = path_rows[:, None, :, :] * (TWO_PI / wave_lengths)[None, :, None, None]
    field_real = opening * jnp.cos(phase_map)
    field_imag = opening * jnp.sin(phase_map)
    pupil_field = jnp.concatenate([field_real, field_imag], axis=3).astype(jnp.bfloat16)
    first_pass = jnp.einsum(
        "flxy,luy->flxu", pupil_field, kernel_table, preferred_element_type=jnp.float32
    )
    return first_pass.astype(jnp.bfloat16)


def finish_section(first_pass, kernel_table):
    pixels = first_pass.shape[3] // 2
    stacked = jnp.concatenate([first_pass[..., :pixels], first_pass[..., pixels:]], axis=2)
    image_field = jnp.einsum(
        "lux,flxv->fluv", kernel_table, stacked, preferred_element_type=jnp.float32
    )
    intensity = (
        image_field[:, :, :pixels] * image_field[:, :, :pixels]
        + image_field[:, :, pixels:] * image_field[:, :, pixels:]
    )
    mean_level = jnp.mean(intensity, axis=(2, 3), keepdims=True)
    return (intensity / (mean_level + EPSILON)).astype(jnp.bfloat16)


def local(mode_basis, coef_table, table_index, wave_lengths, sed_table, template_ids):
    kernel_table = transform_table(wave_lengths, PIX, PUP)
    table_rows = coef_table.shape[0]
    selector = (table_index[:, None] == jnp.arange(table_rows, dtype=jnp.int32)[None, :]).astype(
        jnp.bfloat16
    )
    coeffs = jnp.dot(selector, coef_table, preferred_element_type=jnp.float32).astype(jnp.bfloat16)
    mode_count = mode_basis.shape[0]
    positions = coeffs.shape[0]
    whole_basis = lax.all_gather(mode_basis, "wave", axis=1, tiled=True)
    path_diff = jnp.dot(
        coeffs, whole_basis.reshape(mode_count, -1), preferred_element_type=jnp.float32
    )
    path_diff = path_diff.reshape(positions, PUP, PUP)
    first_pass = pupil_section(path_diff, wave_lengths, kernel_table, 0)
    spectra = finish_section(first_pass, kernel_table)
    pixel_slabs = lax.all_to_all(spectra, "wave", split_axis=2, concat_axis=1, tiled=True)
    sed_rows = sed_table.shape[0]
    one_hot = (
        template_ids[:, :, None] == jnp.arange(sed_rows, dtype=jnp.int32)[None, None, :]
    ).astype(jnp.float32)
    raw_weights = jnp.einsum("fjn,nl->fjl", one_hot, sed_table, precision=lax.Precision.HIGHEST)
    weights = (raw_weights / jnp.sum(raw_weights, axis=2, keepdims=True)).astype(jnp.bfloat16)
    mixed = jnp.einsum("fjl,flrp->fjrp", weights, pixel_slabs, preferred_element_type=jnp.float32)
    return mixed.astype(jnp.bfloat16)


def solution(mesh):
    return jax.shard_map(
        local,
        mesh=mesh,
        in_specs=(
            P(None, "wave", None),
            P(),
            P(("groups", "field")),
            P("wave"),
            P(),
            P(("groups", "field"), None),
        ),
        out_specs=P(("groups", "field"), None, "wave", None),
        check_vma=False,
    )
```

profile of v0, /device:TPU:0, one launch (start us, length us, event | category | flops | bytes accessed | tf_op | source)
XLA Modules:
  0.0 431.0 jit_solution(3552195632405545953)
XLA Ops:
  6.5 0.0 copy-start
  6.5 0.0 all-gather.2.cloned.1.call-start
  6.5 0.7 all-gather.2.cloned.1.call-update
  7.3 0.7 broadcast_divide_fusion.1
  8.0 0.1 multiply_convert_fusion
  8.1 0.2 fusion.30
  8.3 4.1 fusion.22
  12.4 0.0 copy-start.3
  12.4 200.3 %all-gather.2.cloned.1.call-done = bf16[22,512,512]{2,1,0:T(8,128)(2,1)} async-done(((bf16[22,128,512]{2,1,0:T(8,128)(2,1)}), bf16[22,512,512]{2,1,0:T(8,128)(2,1)}) %all-gather.2.cloned.1.call-update) | async-done | bytes 11534352 | tf_op jit(solution)/shard_map/all_gather | solution.py:76
  212.7 10.0 %slice_bitcast_fusion = bf16[512,512,22]{1,0,2:T(8,128)(2,1)} fusion(bf16[22,512,512]{2,1,0:T(8,128)(2,1)} %all-gather.2.cloned.1.call-done), kind=kLoop, calls=%fused_computation.13 | loop fusion | bytes 23068672 | tf_op jit(solution)/shard_map/reshape.39
  222.7 0.0 copy-done
  222.7 0.0 copy-done.3
  222.7 24.2 %fusion.9 = f32[8,512,512]{2,0,1:T(8,128)} fusion(bf16[512,512,22]{1,0,2:T(8,128)(2,1)} %slice_bitcast_fusion, bf16[4096,22]{0,1:T(8,128)(2,1)S(1)} %copy-done, s32[8]{0:T(128)S(1)} %copy-done.3), kind=kOutput, calls=%fused_computation.11 | convolution fusion | flops 93749424 | bytes 20103200 | tf_op jit(solution)/shard_map/dot_general | solution.py:77
  247.0 8.2 %copy.20 = f32[8,512,512]{2,1,0:T(8,128)S(1)} copy(f32[8,512,512]{2,0,1:T(8,128)} %fusion.9) | data formatting | bytes 16777216 | tf_op jit(solution)/shard_map/dot_general | solution.py:77
  255.2 64.3 %fusion.2 = (bf16[8,2,512,512]{3,2,0,1:T(8,128)(2,1)}, bf16[8,2,512,512]{3,2,0,1:T(8,128)(2,1)}) fusion(f32[2]{0:T(128)S(1)} %get-tuple-element.13, f32[8,512,512]{2,1,0:T(8,128)S(1)} %copy.20, f32[512,512]{1,0:T(8,128)S(1)} %fusion.30), kind=kLoop, calls=%fused_computation.4 | loop fusion | flops 20971520 | bytes 26214408 | tf_op jit(solution)/shard_map/convert
  319.5 14.6 %convert_bitcast_fusion = bf16[8,2,512,512]{3,2,0,1:T(8,128)(2,1)} fusion(bf16[8,2,512,512]{3,2,0,1:T(8,128)(2,1)} %get-tuple-element.6, bf16[8,2,512,512]{3,2,0,1:T(8,128)(2,1)} %get-tuple-element.5, bf16[2,256,512]{2,1,0:T(8,128)(2,1)S(1)} %get-tuple-element.11, bf16[2,256,512]{2,1,0:T(8,128)(2,1)S(1)} %get-tuple-element.10, ...), kind=kOutput, calls=%fused_computation.18 | convolution fusion | flops 8636071936 | bytes 26738688 | tf_op jit(solution)/shard_map/flxy,luy->flxu/dot_general | solution.py:47
  334.1 5.8 %fusion.41 = (bf16[8,2,512,256]{3,2,0,1:T(8,128)(2,1)}, bf16[8,2,512,256]{3,2,0,1:T(8,128)(2,1)}) fusion(bf16[8,2,512,512]{3,2,0,1:T(8,128)(2,1)} %convert_bitcast_fusion), kind=kLoop, calls=%fused_computation.58 | loop fusion | bytes 16777216 | tf_op jit(solution)/shard_map/slice | solution.py:55
  339.9 11.0 %fusion.18 = f32[8,2,512,256]{2,3,0,1:T(8,128)} fusion(bf16[8,2,512,256]{3,2,0,1:T(8,128)(2,1)} %get-tuple-element.8, bf16[8,2,512,256]{3,2,0,1:T(8,128)(2,1)} %get-tuple-element.7, bf16[2,256,512]{2,1,0:T(8,128)(2,1)S(1)} %get-tuple-element.11, bf16[2,256,512]{2,1,0:T(8,128)(2,1)S(1)} %get-tuple-element.10, bf16[2,256,512]{2,1,0:T(8,128)(2,1)S(1)} %get-tuple-element.9), kind=kOutput, calls=%fused_computation.23 | convolution fusion | flops 4320133120 | bytes 18350080 | tf_op jit(solution)/shard_map/lux,flxv->fluv/dot_general | solution.py:56
  351.0 0.0 copy-start.2
  351.0 4.3 fusion.31
  355.3 1.6 copy-done.2
  356.8 0.8 divide_convert_fusion
  357.6 0.0 copy-start.4
  357.6 0.0 copy-start.5
  357.6 3.1 copy.22
  360.7 3.6 all-to-all-start
  364.3 0.0 copy-done.4
  364.3 0.0 copy-done.5
  364.3 1.0 fusion.32
  365.4 47.6 %all-to-all-done = bf16[8,2,256,256]{3,0,1,2:T(8,128)(2,1)S(1)} async-done(((bf16[8,2,256,256]{3,0,1,2:T(8,128)(2,1)}), bf16[8,2,256,256]{3,0,1,2:T(8,128)(2,1)S(1)}, u32[]{:S(2)}, u32[]{:S(2)}) %all-to-all-start) | async-done | bytes 2097184 | tf_op jit(solution)/shard_map/all_to_all | solution.py:83
  413.0 2.9 copy.24
  415.9 0.0 copy-start.1
  415.9 2.8 all_to_all.16
  418.7 2.0 convolution_convert_fusion
  420.7 3.5 copy.26
  424.2 0.0 copy-done.1
  (4 shorter events, 0.0 us)
Async XLA Ops:
  6.5 216.2 %copy-start = (bf16[4096,22]{0,1:T(8,128)(2,1)S(1)}, bf16[4096,22]{0,1:T(8,128)(2,1)}, u32[]{:S(2)}) copy-start(bf16[4096,22]{0,1:T(8,128)(2,1)} %param.7) | copy-start | bytes 540676
  6.5 206.2 %all-gather.2.cloned.1.call-start = ((), (), s32[]{:S(2)}) async-start(), calls=%async_computation.1 | async-start | bytes 14417920 | tf_op jit(solution)/shard_map/all_gather | solution.py:76
  12.4 210.3 %copy-start.3 = (s32[8]{0:T(128)S(1)}, s32[8]{0:T(128)}, u32[]{:S(2)}) copy-start(s32[8]{0:T(128)} %param.8) | copy-start | bytes 100
  351.0 5.8 %copy-start.2 = (f32[8,2,512,256]{2,3,0,1:T(8,128)S(1)}, f32[8,2,512,256]{2,3,0,1:T(8,128)}, u32[]{:S(2)}) copy-start(f32[8,2,512,256]{2,3,0,1:T(8,128)} %fusion.18) | copy-start | bytes 25165828
  357.6 6.7 %copy-start.4 = (f32[1024,8]{0,1:T(8,128)S(1)}, f32[1024,8]{0,1:T(8,128)}, u32[]{:S(2)}) copy-start(f32[1024,8]{0,1:T(8,128)} %param.10) | copy-start | bytes 98308
  357.6 6.7 %copy-start.5 = (s32[8,8]{1,0:T(8,128)S(1)}, s32[8,8]{1,0:T(8,128)}, u32[]{:S(2)}) copy-start(s32[8,8]{1,0:T(8,128)} %param.11) | copy-start | bytes 772
  360.7 52.3 %all-to-all-start = ((bf16[8,2,256,256]{3,0,1,2:T(8,128)(2,1)}), bf16[8,2,256,256]{3,0,1,2:T(8,128)(2,1)S(1)}, u32[]{:S(2)}, u32[]{:S(2)}) async-start(bf16[8,2,256,256]{3,0,1,2:T(8,128)(2,1)} %copy.22), calls=%async_computation | async-start | bytes 4194304 | tf_op jit(solution)/shard_map/all_to_all | solution.py:83
  415.9 8.3 %copy-start.1 = (bf16[4096,22]{0,1:T(8,128)(2,1)S(1)}, bf16[4096,22]{0,1:T(8,128)(2,1)}, u32[]{:S(2)}) copy-start(bf16[4096,22]{0,1:T(8,128)(2,1)} %param.7) | copy-start | bytes 540676
Sparse Core Ops, SparseCore 0:
  8.9 203.7 all-gather.1
where the time goes:
time: 431 us
  waiting for transfers between devices  249 us (58%)
  other arithmetic  74.5 us (17%)
  matrix products  52.9 us (12%)
  local copies, waits for them, and re-layouts  37.8 us (9%)
  between operations  13.5 us (3%)
    all_gather x1, waiting for transfers between devices, local(): whole_basis = lax.all_gather(mode_basis, 'wave', axis=1, tiled=True)  200 us
    another operation x2, other arithmetic  68.4 us
    all_to_all x1, waiting for transfers between devices, local(): lax.all_to_all(spectra, 'wave', split_axis=2, concat_axis=1, tiled=True)  47.6 us
    dot_general x1, matrix products, local(): jnp.dot(coeffs, whole_basis.reshape(mode_count, -1), preferred_element_ty...  24.2 us
    dot_general x1, matrix products, pupil_section(): jnp.einsum('flxy,luy->flxu', pupil_field, kernel_table, preferred_element...  14.6 us
    dot_general x1, matrix products, finish_section(): jnp.einsum('lux,flxv->fluv', kernel_table, stacked, preferred_element_typ...  11 us
    another operation x1, local copies, waits for them, and re-layouts  9.99 us
  transfers between devices with their start and end apart: 2, of which 2 were waited for; matrix products, arithmetic and copies ran while one was open for 1% of the time, Pallas kernels for 0%

commit v1 on v0

v1 whole, which is shorter than its diff:
```python
import functools
import math

import jax
import jax.numpy as jnp
import numpy as np
from jax import lax
from jax.experimental import pallas as pl
from jax.experimental.pallas import tpu as pltpu
from jax.sharding import PartitionSpec as P

PUP = 512
PIX = 256
TWO_PI = 2.0 * math.pi
SAMPLING = 0.25
EPSILON = 1e-06
INNER = 61 * PUP // 100
BAND = 128
BANDS = PUP // BAND
ROWS = 16
LANES = 128
UNITS = BAND // ROWS
SHARES = 8

SIN_POLY = (4.4428679, -7.30744341, 3.59478797, -0.78437376)
COS_POLY = (1.4142135, -6.97885099, 5.73946117, -1.88356298, 0.31069817)


def band_rows(band):
    low, high = PUP // 2 - 64 * (band + 1), PUP // 2 + 64 * band
    return [low + ROWS * i for i in range(4)] + [high + ROWS * i for i in range(4)]


def band_columns(band):
    low, high = PUP // 2 - 64 * (band + 1), PUP // 2 + 64 * band
    sides = (high, low) if band % 2 == 0 else (low, high)
    return np.concatenate([side + np.arange(64) for side in sides])


def unit_open(row, band):
    a = 2 * (row + np.arange(ROWS)) - PUP + 1
    b = 2 * band_columns(band) - PUP + 1
    radius = a[:, None] ** 2 + b[None, :] ** 2
    return bool(np.any((radius <= PUP * PUP) & (radius >= INNER * INNER)))


CHUNKS = [
    (band, rows)
    for band in range(BANDS)
    for rows in range(BANDS)
    if any(unit_open(row, band) for row in band_rows(rows))
]


@functools.lru_cache(None)
def layout(waves, modes):
    per = PUP // waves
    lists = []
    for wave in range(waves):
        lists.append(
            [
                (band, row)
                for band in range(BANDS)
                for row in range(wave * per, (wave + 1) * per, ROWS)
                if unit_open(row, band)
            ]
        )
    count = max(len(one) for one in lists)
    half = -(-count * modes // (2 * SHARES))
    slabs = 2 * SHARES * half
    pack = np.zeros((waves, count, 3), np.int32)
    for wave, one in enumerate(lists):
        for i, (band, row) in enumerate(one):
            columns = band_columns(band)
            pack[wave, i] = (columns[0] // LANES * LANES, columns[64] // LANES * LANES, row - wave * per)
    place = np.zeros((len(CHUNKS) * UNITS, 4), np.int32)
    for c, (band, rows) in enumerate(CHUNKS):
        columns = band_columns(band)
        for j, row in enumerate(band_rows(rows)):
            wave = row // per
            slab = 0
            if (band, row) in lists[wave]:
                slab = wave * slabs + lists[wave].index((band, row)) * modes
            place[c * UNITS + j] = (slab, row, columns[0], columns[64] - 64)
    return count, half, slabs, pack, place


def pack_kernel(count, modes, table, basis, out):
    left = lax.broadcasted_iota(jnp.int32, (ROWS, LANES), 1) < 64

    def unit(i, carry):
        first = pl.multiple_of(table[i, 0], LANES)
        second = pl.multiple_of(table[i, 1], LANES)
        row = pl.multiple_of(table[i, 2], ROWS)
        for k in range(modes):
            one = basis[k, pl.ds(row, ROWS), pl.ds(first, LANES)].astype(jnp.float32)
            two = basis[k, pl.ds(row, ROWS), pl.ds(second, LANES)].astype(jnp.float32)
            out[i * modes + k] = jnp.where(left, one, two).astype(out.dtype)
        return carry

    lax.fori_loop(0, count, unit, 0)
    for n in range(count * modes, out.shape[0]):
        out[n] = jnp.zeros((ROWS, LANES), out.dtype)


def pack_rows(basis, table, slabs):
    modes = basis.shape[0]
    return pl.pallas_call(
        functools.partial(pack_kernel, table.shape[0], modes),
        out_shape=jax.ShapeDtypeStruct((slabs, ROWS, LANES), basis.dtype),
        in_specs=[pl.BlockSpec(memory_space=pltpu.SMEM), pl.BlockSpec(memory_space=pltpu.VMEM)],
        out_specs=pl.BlockSpec(memory_space=pltpu.VMEM),
        compiler_params=pltpu.CompilerParams(vmem_limit_bytes=24 * 2**20),
    )(table, basis)


def gather_rows(own, half, waves):
    groups, fields = lax.axis_size("groups"), lax.axis_size("field")
    share = (lax.axis_index("groups") % 2) * 4 + lax.axis_index("field") % 4

    def swap(x, mask):
        pairs = [
            (g * fields + f, (g ^ (mask >> 2)) * fields + (f ^ (mask & 3)))
            for g in range(groups)
            for f in range(fields)
        ]
        return lax.ppermute(x, ("groups", "field"), pairs)

    got = {}
    for h in range(2):
        piece = lax.dynamic_slice_in_dim(own, (2 * share + h) * half, half, axis=0)
        parts = [
            lax.ppermute(piece, "wave", [(i, (i + s) % waves) for i in range(waves)])
            for s in range(1, waves)
        ]
        got[0, h] = jnp.stack(parts)
    first, second = 2, 4
    for h in range(2):
        one, two = (first, second) if h == 0 else (second, first)
        got[one, h] = swap(got[0, h], one)
        got[two, h] = swap(got[0, h], two)
        got[one | two, h] = swap(got[one, h], two)
    for h in range(2):
        for mask in (0, 2, 4, 6):
            got[mask | 1, h] = swap(got[mask, h], 1)
    return got


def field_kernel(sizes, place_ref, where_ref, inverse_ref, *refs):
    positions, rows, modes, waves, half, slabs, keys = sizes
    parts = refs[: 1 + len(keys)]
    spread_ref, row_ref, column_ref, image_ref, sum_ref = refs[1 + len(keys) : 6 + len(keys)]
    basis, path, opening, pupil, total, first, sems = refs[6 + len(keys) :]
    wave = where_ref[0]
    share = where_ref[1]

    @pl.when(pl.program_id(0) == 0)
    def _():
        copies = [
            pltpu.make_async_copy(parts[0], basis.at[pl.ds(wave * slabs, slabs)], sems.at[0])
        ]
        n = 1
        for key, part in zip(keys, parts[1:]):
            mask, h = key
            for s in range(1, waves):
                source = lax.rem(wave + (waves - s), waves)
                start = source * slabs + (share ^ mask) * (2 * half) + h * half
                copies.append(
                    pltpu.make_async_copy(part.at[s - 1], basis.at[pl.ds(start, half)], sems.at[n])
                )
                n += 1
        for copy in copies:
            copy.start()
        for copy in copies:
            copy.wait()

        lane = lax.broadcasted_iota(jnp.int32, (ROWS, LANES), 1)
        line = lax.broadcasted_iota(jnp.int32, (ROWS, LANES), 0)

        def unit(u, carry):
            slab, row = place_ref[u, 0], place_ref[u, 1]
            a = 2 * (line + row) - (PUP - 1)
            b = 2 * (lane + jnp.where(lane < 64, place_ref[u, 2], place_ref[u, 3])) - (PUP - 1)
            radius = a * a + b * b
            inside = (radius <= PUP * PUP) & (radius >= INNER * INNER)
            values = basis[pl.ds(slab, modes)].reshape(modes * ROWS, LANES)
            found = jnp.dot(spread_ref[...], values, preferred_element_type=jnp.float32)
            opening[u] = jnp.where(inside, 1.0, 0.0)
            for f in range(positions):
                path[u, f * ROWS : (f + 1) * ROWS] = jnp.where(
                    inside, found[f * ROWS : (f + 1) * ROWS], 0.0
                )
            return carry

        lax.fori_loop(0, len(CHUNKS) * UNITS, unit, 0)

    inverse = inverse_ref[pl.program_id(0)]
    magic = jnp.float32(12582912.0)
    total[...] = jnp.zeros_like(total)

    def chunk(c, carry):
        band, rows_band = place_ref[c * UNITS, 4], place_ref[c * UNITS, 5]
        for j in range(UNITS):
            u = c * UNITS + j
            inside = opening[u]
            for f in range(positions):
                turns = path[u, f * ROWS : (f + 1) * ROWS] * inverse
                r = turns - ((turns + magic) - magic)
                z = r * r
                s = SIN_POLY[-1]
                for value in SIN_POLY[-2::-1]:
                    s = s * z + value
                s = s * r
                k = COS_POLY[-1]
                for value in COS_POLY[-2::-1]:
                    k = k * z + value
                columns = slice(f * LANES, (f + 1) * LANES)
                pupil[2 * ROWS * j : 2 * ROWS * j + ROWS, columns] = (inside - s * s).astype(
                    jnp.bfloat16
                )
                pupil[2 * ROWS * j + ROWS : 2 * ROWS * (j + 1), columns] = (s * k).astype(
                    jnp.bfloat16
                )
        total[band] += jnp.dot(
            row_ref[0, rows_band], pupil[...], preferred_element_type=jnp.float32
        )
        return carry

    lax.fori_loop(0, len(CHUNKS), chunk, 0)

    for band in range(BANDS):
        for f in range(positions):
            for part in range(2):
                first[
                    f * rows : (f + 1) * rows,
                    part * PUP + band * LANES : part * PUP + (band + 1) * LANES,
                ] = total[
                    band, part * rows : (part + 1) * rows, f * LANES : (f + 1) * LANES
                ].astype(jnp.bfloat16)
    for f in range(positions):
        both = jnp.dot(
            first[f * rows : (f + 1) * rows], column_ref[0], preferred_element_type=jnp.float32
        )
        real, imag = both[:, :PIX], both[:, PIX:]
        intensity = real * real + imag * imag
        image_ref[0, f * rows : (f + 1) * rows] = intensity.astype(jnp.bfloat16)
        sum_ref[0, f : f + 1] = jnp.sum(intensity, axis=0, keepdims=True)


def fields(own, got, spread, place, inverse, row_table, column_table, positions, rows, sizes):
    modes, waves, half, slabs = sizes
    keys = sorted(got)
    lengths = row_table.shape[0]
    units = place.shape[0]
    where = jnp.stack(
        [
            lax.axis_index("wave"),
            (lax.axis_index("groups") % 2) * 4 + lax.axis_index("field") % 4,
        ]
    ).astype(jnp.int32)
    place = jnp.concatenate(
        [place, np.repeat(np.array(CHUNKS, np.int32), UNITS, axis=0)], axis=1
    )
    smem = pl.BlockSpec(memory_space=pltpu.SMEM)
    hbm = pl.BlockSpec(memory_space=pl.ANY)
    return pl.pallas_call(
        functools.partial(
            field_kernel, (positions, rows, modes, waves, half, slabs, tuple(keys))
        ),
        grid=(lengths,),
        out_shape=(
            jax.ShapeDtypeStruct((lengths, positions * rows, PIX), jnp.bfloat16),
            jax.ShapeDtypeStruct((lengths, positions, PIX), jnp.float32),
        ),
        in_specs=[smem, smem, smem, hbm]
        + [hbm] * len(keys)
        + [
            pl.BlockSpec(spread.shape, lambda l: (0, 0)),
            pl.BlockSpec((1,) + row_table.shape[1:], lambda l: (l, 0, 0, 0)),
            pl.BlockSpec((1,) + column_table.shape[1:], lambda l: (l, 0, 0)),
        ],
        out_specs=(
            pl.BlockSpec((1, positions * rows, PIX), lambda l: (l, 0, 0)),
            pl.BlockSpec((1, positions, PIX), lambda l: (l, 0, 0)),
        ),
        scratch_shapes=[
            pltpu.VMEM((waves * slabs, ROWS, LANES), jnp.bfloat16),
            pltpu.VMEM((units, positions * ROWS, LANES), jnp.float32),
            pltpu.VMEM((units, ROWS, LANES), jnp.float32),
            pltpu.VMEM((2 * BAND, positions * LANES), jnp.bfloat16),
            pltpu.VMEM((BANDS, 2 * rows, positions * LANES), jnp.float32),
            pltpu.VMEM((positions * rows, 2 * PUP), jnp.bfloat16),
            pltpu.SemaphoreType.DMA((1 + len(keys) * (waves - 1),)),
        ],
        compiler_params=pltpu.CompilerParams(vmem_limit_bytes=56 * 2**20),
    )(place, where, inverse, own, *[got[key] for key in keys], spread, row_table, column_table)


def mix_kernel(weight_ref, image_ref, out_ref):
    f = pl.program_id(0)
    templates = out_ref.shape[1]
    lengths = image_ref.shape[0]
    for start in range(0, image_ref.shape[1], ROWS):
        rows = slice(start, start + ROWS)
        sums = [None] * templates
        for l in range(lengths):
            values = image_ref[l, rows].astype(jnp.float32)
            for j in range(templates):
                term = weight_ref[f, j * lengths + l] * values
                sums[j] = term if l == 0 else sums[j] + term
        for j in range(templates):
            out_ref[0, j, rows] = sums[j].astype(jnp.bfloat16)


def mix(weights, images, rows):
    positions, templates, lengths = weights.shape
    return pl.pallas_call(
        mix_kernel,
        grid=(positions,),
        out_shape=jax.ShapeDtypeStruct((positions, templates, rows, PIX), jnp.bfloat16),
        in_specs=[
            pl.BlockSpec(memory_space=pltpu.SMEM),
            pl.BlockSpec((lengths, rows, PIX), lambda f: (0, f, 0)),
        ],
        out_specs=pl.BlockSpec((1, templates, rows, PIX), lambda f: (f, 0, 0, 0)),
    )(weights.reshape(positions, templates * lengths), images)


def tables(wave_lengths, rows):
    factor = (TWO_PI * SAMPLING / (2.0 * PUP)) / wave_lengths
    y = 2 * np.concatenate([band_columns(band) for band in range(BANDS)]) - PUP + 1
    v = np.arange(PIX) - PIX // 2
    angles = (y[:, None] * v[None, :]).astype(np.float32)[None] * factor[:, None, None]
    cosine, sine = jnp.cos(angles), jnp.sin(angles)
    column_table = jnp.concatenate(
        [
            jnp.concatenate([cosine, -sine], axis=2),
            jnp.concatenate([sine, cosine], axis=2),
        ],
        axis=1,
    ).astype(jnp.bfloat16)
    u = lax.axis_index("wave") * rows + jnp.arange(rows, dtype=jnp.int32) - PIX // 2
    x = np.array(
        [[row + i for row in band_rows(band) for i in range(ROWS)] for band in range(BANDS)]
    )
    x = np.repeat(x.reshape(BANDS, UNITS, 1, ROWS), 2, axis=2).reshape(BANDS, 1, 2 * BAND)
    imag = ((np.arange(2 * BAND) // ROWS) % 2 == 1)[None, None, None, :]
    products = (u[None, :, None] * (2 * x - PUP + 1).astype(np.int32)).astype(jnp.float32)
    angles = products[None] * factor[:, None, None, None]
    cosine, sine = jnp.cos(angles), jnp.sin(angles)
    row_table = jnp.concatenate(
        [jnp.where(imag, sine, cosine), jnp.where(imag, cosine, -sine)], axis=2
    ).astype(jnp.bfloat16)
    return row_table, column_table


def local(mode_basis, coef_table, table_index, wave_lengths, sed_table, template_ids):
    waves = lax.axis_size("wave")
    modes = mode_basis.shape[0]
    positions = table_index.shape[0]
    rows = PIX // waves
    count, half, slabs, pack, place = layout(waves, modes)

    table = jnp.asarray(pack)[lax.axis_index("wave")]
    own = pack_rows(mode_basis, table, slabs)
    got = gather_rows(own, half, waves)

    every = lax.all_gather(wave_lengths, "wave", axis=0, tiled=True)
    row_table, column_table = tables(every, rows)

    selector = (
        table_index[:, None] == jnp.arange(coef_table.shape[0], dtype=jnp.int32)[None, :]
    ).astype(jnp.bfloat16)
    coeffs = jnp.dot(selector, coef_table, preferred_element_type=jnp.float32)
    spread = (
        (coeffs[:, None, :, None] * np.eye(ROWS, dtype=np.float32)[None, :, None, :])
        .reshape(positions * ROWS, modes * ROWS)
        .astype(jnp.bfloat16)
    )

    images, sums = fields(
        own,
        got,
        spread,
        place,
        1.0 / every,
        row_table,
        column_table,
        positions,
        rows,
        (modes, waves, half, slabs),
    )
    level = lax.psum(jnp.sum(sums, axis=2), "wave") / (PIX * PIX)

    one_hot = (
        template_ids[:, :, None]
        == jnp.arange(sed_table.shape[0], dtype=jnp.int32)[None, None, :]
    ).astype(jnp.float32)
    raw_weights = jnp.einsum("fjn,nl->fjl", one_hot, sed_table, precision=lax.Precision.HIGHEST)
    weights = (raw_weights / jnp.sum(raw_weights, axis=2, keepdims=True)).astype(jnp.bfloat16)
    weights = weights.astype(jnp.float32) / (level.T[:, None, :] + EPSILON)
    return mix(weights, images, rows)


def solution(mesh):
    return jax.shard_map(
        local,
        mesh=mesh,
        in_specs=(
            P(None, "wave", None),
            P(),
            P(("groups", "field")),
            P("wave"),
            P(),
            P(("groups", "field"), None),
        ),
        out_specs=P(("groups", "field"), None, "wave", None),
        check_vma=False,
    )
```

time: 431 us -> 223 us (0.52)
  waiting for transfers between devices: 249 us -> 15.7 us
  Pallas kernels: 0 us -> 116 us
  matrix products: 52.9 us -> 1.27 us
  other arithmetic: 74.5 us -> 33.8 us
  local copies, waits for them, and re-layouts: 37.8 us -> 7.57 us
  blocking collectives: 0 us -> 24.7 us
  starting transfers between devices: 3.61 us -> 22.9 us
  between operations: 13.5 us -> 0.85 us
    all_gather x1 -> x0, waiting for transfers between devices: 200 us -> none  [local(): whole_basis = lax.all_gather(mode_basis, 'wave', axis=1, tiled=True)]
    pallas_call x0 -> x3, Pallas kernels: none -> 116 us  [the longest x1 108 us: fields(): pl.pallas_call(functools.partial(field_kernel, (positions, rows, modes, w...]
    dot_general x4 -> x1, matrix products: 51.9 us -> 0.23 us  [local(): coeffs = jnp.dot(selector, coef_table, preferred_element_type=jnp.float32)]
    all_to_all x1 -> x0, waiting for transfers between devices: 47.6 us -> none  [local(): lax.all_to_all(spectra, 'wave', split_axis=2, concat_axis=1, tiled=True)]
    another operation x2 -> x5, other arithmetic: 68.4 us -> 26.3 us
    ppermute x0 -> x20, starting transfers between devices: none -> 22.9 us  [the longest x6 14.3 us: gather_rows(): lax.ppermute(piece, 'wave', [(i, (i + s) % waves) for i in range(waves)])]
    unnamed x0 -> x1, blocking collectives: none -> 15.7 us
    ppermute x0 -> x20, waiting for transfers between devices: none -> 15.7 us  [the longest x14 15.7 us: swap(): return lax.ppermute(x, ('groups', 'field'), pairs)]
  transfers between devices with their start and end apart: 2 -> 20, of which waited for: 2 -> 3; matrix products, arithmetic and copies ran while one was open for 1% -> 16% of each run, Pallas kernels for 0% -> 0%
where the time goes in v1:
time: 223 us
  Pallas kernels  116 us (52%)
  other arithmetic  33.8 us (15%)
  blocking collectives  24.7 us (11%)
  starting transfers between devices  22.9 us (10%)
  waiting for transfers between devices  15.7 us (7%)
  local copies, waits for them, and re-layouts  7.57 us (3%)
    pallas_call x1, Pallas kernels, fields(): pl.pallas_call(functools.partial(field_kernel, (positions, rows, modes, w...  108 us
    another operation x2, other arithmetic  23.7 us
    unnamed x1, blocking collectives  15.7 us
    ppermute x14, waiting for transfers between devices, swap(): return lax.ppermute(x, ('groups', 'field'), pairs)  15.7 us
    ppermute x6, starting transfers between devices, gather_rows(): lax.ppermute(piece, 'wave', [(i, (i + s) % waves) for i in range(waves)])  14.3 us
    psum x1, blocking collectives, local(): level = lax.psum(jnp.sum(sums, axis=2), 'wave') / (PIX * PIX)  8.92 us
    ppermute x14, starting transfers between devices, swap(): return lax.ppermute(x, ('groups', 'field'), pairs)  8.64 us
    pallas_call x1, Pallas kernels, mix(): pl.pallas_call(mix_kernel, grid=(positions,), out_shape=jax.ShapeDtypeStr...  6.78 us
  transfers between devices with their start and end apart: 20, of which 3 were waited for; matrix products, arithmetic and copies ran while one was open for 16% of the time, Pallas kernels for 0%

profile of v1, /device:TPU:0, one launch (start us, length us, event | category | flops | bytes accessed | tf_op | source)
XLA Modules:
  0.0 223.0 jit_solution(12256311089531688687)
XLA Ops:
  0.0 0.7 dynamic-slice_bitcast_fusion
  0.7 0.1 copy.20.table
  0.8 1.8 copy-done.2
  2.6 1.6 shard_map.127.refs_0_
  4.3 0.8 constant_dynamic-slice_fusion
  5.1 5.0 %collective-permute-start.5 = (bf16[35,16,128]{2,1,0:T(8,128)(2,1)S(1)}, bf16[35,16,128]{2,1,0:T(8,128)(2,1)S(1)}, u32[]{:S(2)}, u32[]{:S(2)}) collective-permute-start(bf16[35,16,128]{2,1,0:T(8,128)(2,1)S(1)} %get-tuple-element.9), channel_id=1, source_target_pairs={{0,3},{1,0},{2,1},{3,2},{4,7},{5,4},{6,5},{7,6},{8,11},{9,8},{10,9... | collective-permute-start | bytes 430088 | tf_op jit(solution)/shard_map/ppermute | solution.py:133
  10.2 0.0 collective-permute-start.3
  10.2 1.0 collective-permute-start.4
  11.2 3.4 %collective-permute-start = (bf16[35,16,128]{2,1,0:T(8,128)(2,1)}, bf16[35,16,128]{2,1,0:T(8,128)(2,1)}, u32[]{:S(2)}, u32[]{:S(2)}) collective-permute-start(bf16[35,16,128]{2,1,0:T(8,128)(2,1)} %get-tuple-element.10), channel_id=1, source_target_pairs={{0,1},{1,2},{2,3},{3,0},{4,5},{5,6},{6,7},{7,4},{8,9},{9,10},{10,1... | collective-permute-start | bytes 430088 | tf_op jit(solution)/shard_map/ppermute | solution.py:133
  14.6 0.6 dynamic-slice
  15.8 0.2 dynamic-update-slice
  16.0 0.0 collective-permute-start.1
  16.0 15.7 %all-reduce = f32[8]{0:T(128)S(1)} all-reduce(f32[8]{0:T(128)S(1)} %dynamic-update-slice), channel_id=1, replica_groups=mesh['groups'=2,'field'=4,'wave'=4] {'wave'}, use_global_device_ids=true, to_apply=%add | all-reduce | flops 8 | bytes 64
  31.8 0.5 broadcast_divide_fusion
  32.3 15.7 %fusion.3 = (bf16[8,512,256]{2,1,0:T(8,128)(2,1)S(1)}, bf16[8,512,256]{2,1,0:T(8,128)(2,1)S(1)}, bf16[8,512,256]{2,1,0:T(8,128)(2,1)S(1)}) fusion(f32[8]{0:T(128)S(1)} %get-tuple-element.16, f32[512,256]{1,0:T(8,128)S(1)} %copy-done.5), kind=kLoop, calls=%fused_computation.6 | loop fusion | flops 5242880 | bytes 6815776 | tf_op jit(solution)/shard_map/convert.5
  48.0 0.0 copy-start.17
  48.0 0.0 copy-start.11
  48.0 3.7 %maximum_maximum_fusion.refs_19_ = bf16[8,1024,512]{2,1,0:T(8,128)(2,1)} fusion(bf16[8,512,256]{2,1,0:T(8,128)(2,1)S(1)} %get-tuple-element.13, bf16[8,512,256]{2,1,0:T(8,128)(2,1)S(1)} %get-tuple-element.12, bf16[8,512,256]{2,1,0:T(8,128)(2,1)S(1)} %get-tuple-element.11), kind=kLoop, calls=%fused_computation.1 | loop fusion | flops 33554432 | bytes 14680064 | tf_op jit(solution)/shard_map/concatenate | solution.py:335
  51.8 0.0 collective-permute-done.5
  51.8 4.8 %collective-permute-start.2 = (bf16[35,16,128]{2,1,0:T(8,128)(2,1)}, bf16[35,16,128]{2,1,0:T(8,128)(2,1)S(1)}, u32[]{:S(2)}, u32[]{:S(2)}) collective-permute-start(bf16[35,16,128]{2,1,0:T(8,128)(2,1)} %get-tuple-element.10), channel_id=1, source_target_pairs={{0,3},{1,0},{2,1},{3,2},{4,7},{5,4},{6,5},{7,6},{8,11},{9,8},{10,9... | collective-permute-start | bytes 430088 | tf_op jit(solution)/shard_map/ppermute | solution.py:133
  56.6 0.0 collective-permute-done.3
  56.6 0.0 collective-permute-done.4
  56.6 1.0 pad_maximum_fusion.2.refs_2_
  57.6 1.6 collective-permute-start.13
  59.2 1.5 collective-permute-start.9
  60.7 0.0 collective-permute-done.2
  60.7 1.0 pad_maximum_fusion.1.refs_1_
  61.7 0.6 collective-permute-start.8
  62.3 0.2 fusion.16
  62.6 0.2 multiply_convert_fusion
  62.8 1.4 collective-permute-start.12
  64.2 4.6 %collective-permute-done.13.refs_10_ = bf16[3,35,16,128]{3,2,1,0:T(8,128)(2,1)} collective-permute-done((bf16[3,35,16,128]{3,2,1,0:T(8,128)(2,1)S(1)}, bf16[3,35,16,128]{3,2,1,0:T(8,128)(2,1)}, u32[]{:S(2)}, u32[]{:S(2)}) %collective-permute-start.13) | collective-permute-done | bytes 430112 | tf_op jit(solution)/shard_map/ppermute | solution.py:127
  68.8 0.0 collective-permute-start.6
  68.8 3.2 %collective-permute-done.9.refs_6_ = bf16[3,35,16,128]{3,2,1,0:T(8,128)(2,1)S(1)} collective-permute-done((bf16[3,35,16,128]{3,2,1,0:T(8,128)(2,1)S(1)}, bf16[3,35,16,128]{3,2,1,0:T(8,128)(2,1)S(1)}, u32[]{:S(2)}, u32[]{:S(2)}) %collective-permute-start.9) | collective-permute-done | bytes 430112 | tf_op jit(solution)/shard_map/ppermute | solution.py:127
  72.0 1.5 collective-permute-start.17
  73.5 0.0 collective-permute-done.7.refs_4_
  73.5 0.0 collective-permute-start.11
  73.5 7.8 %collective-permute-done.8.refs_5_ = bf16[3,35,16,128]{3,2,1,0:T(8,128)(2,1)} collective-permute-done((bf16[3,35,16,128]{3,2,1,0:T(8,128)(2,1)S(1)}, bf16[3,35,16,128]{3,2,1,0:T(8,128)(2,1)}, u32[]{:S(2)}, u32[]{:S(2)}) %collective-permute-start.8) | collective-permute-done | bytes 430112 | tf_op jit(solution)/shard_map/ppermute | solution.py:127
  81.4 0.4 collective-permute-start.16
  81.8 0.1 multiply_convert_fusion.1
  81.9 8.0 %fusion.9 = (bf16[8,4,64,256]{3,2,1,0:T(8,128)(2,1)S(1)}, bf16[8,4,64,256]{3,2,1,0:T(8,128)(2,1)S(1)}) fusion(f32[8]{0:T(128)S(1)} %get-tuple-element.16, f32[4,64,256]{2,1,0:T(8,128)S(1)} %multiply_convert_fusion.1, pred[256]{0:T(512)(128)(4,1)S(1)} %copy-done.13), kind=kLoop, calls=%fused_computation.14 | loop fusion | flops 3145728 | bytes 2359584 | tf_op jit(solution)/shard_map/convert.6
  89.8 0.1 collective-permute-start.15
  89.9 0.0 collective-permute-done.6.refs_3_
  90.0 0.5 collective-permute-start.10
  90.5 0.1 collective-permute-start.14
  90.6 0.2 copy-done.8
  90.7 0.5 collective-permute-start.19
  91.2 0.3 copy-done.9
  91.5 0.5 collective-permute-start.18
  92.0 0.6 pad_add_fusion.where_ref
  92.6 0.5 convert_element_type.25
  93.1 0.8 copy.22.refs_17_
  93.8 1.5 pad_maximum_fusion.refs_18_
  95.3 1.0 fusion.14
  96.3 0.0 copy-start.10
  96.4 0.7 copy-done.10
  97.1 107.8 %shard_map.128 = (bf16[8,512,256]{2,1,0:T(8,128)(2,1)}, f32[8,8,256]{2,1,0:T(8,128)}) custom-call(s32[96,6]{1,0:T(8,128)} %constant.86.place_ref, s32[2]{0:T(128)} %pad_add_fusion.where_ref, f32[8]{0:T(128)} %get-tuple-element.17.inverse_ref, bf16[560,16,128]{2,1,0:T(8,128)(2,1)} %copy-done.1, bf16[3,35,16,128]{3,2,1,0:T(8,128)(2,1)} %copy-done.4, ...), custom_call_target="tpu_custom_call" | custom-call | tf_op jit(solution)/shard_map/pallas_call | solution.py:266
  204.9 0.9 reduce_sum.19
  205.9 8.9 %psum.7 = f32[8,8]{1,0:T(8,128)S(1)} all-reduce(f32[8,8]{1,0:T(8,128)S(1)} %reduce_sum.19), channel_id=1, replica_groups=mesh['groups'=2,'field'=4,'wave'=4] {'wave'}, use_global_device_ids=true, to_apply=%region_2.3 | all-reduce | flops 64 | bytes 512 | tf_op jit(solution)/shard_map/psum | solution.py:393
  214.8 0.1 copy.23
  214.9 0.6 fusion.13
  215.5 0.1 copy.24
  215.6 0.7 reshape.23.weight_ref
  216.2 6.8 %shard_map.129 = bf16[8,8,64,256]{3,2,1,0:T(8,128)(2,1)} custom-call(f32[8,64]{1,0:T(8,128)} %reshape.23.weight_ref, bf16[8,512,256]{2,1,0:T(8,128)(2,1)} %get-tuple-element.8.image_ref), custom_call_target="tpu_custom_call" | custom-call | tf_op jit(solution)/shard_map/pallas_call | solution.py:317
  (46 shorter events, 0.1 us)
Async XLA Ops:
  0.0 62.3 %copy-start = (bf16[4096,22]{0,1:T(8,128)(2,1)S(1)}, bf16[4096,22]{0,1:T(8,128)(2,1)}, u32[]{:S(2)}) copy-start(bf16[4096,22]{0,1:T(8,128)(2,1)} %param.14) | copy-start | bytes 540676
  0.8 1.8 copy-start.2
  2.6 11.9 %copy-start.18 = (u32[32]{0:T(128)S(1)}, u32[32]{0:T(128)}, u32[]{:S(2)}) copy-start(u32[32]{0:T(128)} %constant.93) | copy-start | bytes 388
  2.6 13.1 %copy-start.16 = (f32[2]{0:T(128)S(1)}, f32[2]{0:T(128)}, u32[]{:S(2)}) copy-start(f32[2]{0:T(128)} %param.16) | copy-start | bytes 28
  2.6 29.6 %copy-start.5 = (f32[512,256]{1,0:T(8,128)S(1)}, f32[512,256]{1,0:T(8,128)}, u32[]{:S(2)}) copy-start(f32[512,256]{1,0:T(8,128)} %constant.90) | copy-start | bytes 1572868
  4.3 43.7 %copy-start.1 = (bf16[560,16,128]{2,1,0:T(8,128)(2,1)}, bf16[560,16,128]{2,1,0:T(8,128)(2,1)S(1)}, u32[]{:S(2)}) copy-start(bf16[560,16,128]{2,1,0:T(8,128)(2,1)S(1)} %shard_map.127.refs_0_) | copy-start | bytes 6881284
  5.1 46.6 %collective-permute-start.5 = (bf16[35,16,128]{2,1,0:T(8,128)(2,1)S(1)}, bf16[35,16,128]{2,1,0:T(8,128)(2,1)S(1)}, u32[]{:S(2)}, u32[]{:S(2)}) collective-permute-start(bf16[35,16,128]{2,1,0:T(8,128)(2,1)S(1)} %get-tuple-element.9), channel_id=1, source_target_pairs={{0,3},{1,0},{2,1},{3,2},{4,7},{5,4},{6,5},{7,6},{8,11},{9,8},{10,9... | collective-permute-start | bytes 430088 | tf_op jit(solution)/shard_map/ppermute | solution.py:133
  10.2 46.4 %collective-permute-start.3 = (bf16[35,16,128]{2,1,0:T(8,128)(2,1)S(1)}, bf16[35,16,128]{2,1,0:T(8,128)(2,1)S(1)}, u32[]{:S(2)}, u32[]{:S(2)}) collective-permute-start(bf16[35,16,128]{2,1,0:T(8,128)(2,1)S(1)} %get-tuple-element.9), channel_id=1, source_target_pairs={{0,1},{1,2},{2,3},{3,0},{4,5},{5,6},{6,7},{7,4},{8,9},{9,10},{10,1... | collective-permute-start | bytes 430088 | tf_op jit(solution)/shard_map/ppermute | solution.py:133
  10.2 46.4 %collective-permute-start.4 = (bf16[35,16,128]{2,1,0:T(8,128)(2,1)S(1)}, bf16[35,16,128]{2,1,0:T(8,128)(2,1)}, u32[]{:S(2)}, u32[]{:S(2)}) collective-permute-start(bf16[35,16,128]{2,1,0:T(8,128)(2,1)S(1)} %get-tuple-element.9), channel_id=1, source_target_pairs={{0,2},{1,3},{2,0},{3,1},{4,6},{5,7},{6,4},{7,5},{8,10},{9,11},{10,... | collective-permute-start | bytes 430088 | tf_op jit(solution)/shard_map/ppermute | solution.py:133
  11.2 49.5 %collective-permute-start = (bf16[35,16,128]{2,1,0:T(8,128)(2,1)}, bf16[35,16,128]{2,1,0:T(8,128)(2,1)}, u32[]{:S(2)}, u32[]{:S(2)}) collective-permute-start(bf16[35,16,128]{2,1,0:T(8,128)(2,1)} %get-tuple-element.10), channel_id=1, source_target_pairs={{0,1},{1,2},{2,3},{3,0},{4,5},{5,6},{6,7},{7,4},{8,9},{9,10},{10,1... | collective-permute-start | bytes 430088 | tf_op jit(solution)/shard_map/ppermute | solution.py:133
  16.0 44.7 %collective-permute-start.1 = (bf16[35,16,128]{2,1,0:T(8,128)(2,1)}, bf16[35,16,128]{2,1,0:T(8,128)(2,1)}, u32[]{:S(2)}, u32[]{:S(2)}) collective-permute-start(bf16[35,16,128]{2,1,0:T(8,128)(2,1)} %get-tuple-element.10), channel_id=1, source_target_pairs={{0,2},{1,3},{2,0},{3,1},{4,6},{5,7},{6,4},{7,5},{8,10},{9,11},{10,... | collective-permute-start | bytes 430088 | tf_op jit(solution)/shard_map/ppermute | solution.py:133
  48.0 14.3 %copy-start.17 = (s32[8]{0:T(128)S(1)}, s32[8]{0:T(128)}, u32[]{:S(2)}) copy-start(s32[8]{0:T(128)} %param.15) | copy-start | bytes 100
  48.0 14.5 %copy-start.11 = (f32[16,16]{0,1:T(8,128)S(1)}, f32[16,16]{0,1:T(8,128)}, u32[]{:S(2)}) copy-start(f32[16,16]{0,1:T(8,128)} %constant.87) | copy-start | bytes 3076
  51.8 30.0 %copy-start.12 = (s32[4,256]{1,0:T(4,128)S(1)}, s32[4,256]{1,0:T(4,128)}, u32[]{:S(2)}) copy-start(s32[4,256]{1,0:T(4,128)} %constant.89) | copy-start | bytes 12292
  51.8 30.1 %copy-start.13 = (pred[256]{0:T(512)(128)(4,1)S(1)}, pred[256]{0:T(512)(128)(4,1)}, u32[]{:S(2)}) copy-start(pred[256]{0:T(512)(128)(4,1)} %constant.88) | copy-start | bytes 772
  51.8 8.9 %collective-permute-start.2 = (bf16[35,16,128]{2,1,0:T(8,128)(2,1)}, bf16[35,16,128]{2,1,0:T(8,128)(2,1)S(1)}, u32[]{:S(2)}, u32[]{:S(2)}) collective-permute-start(bf16[35,16,128]{2,1,0:T(8,128)(2,1)} %get-tuple-element.10), channel_id=1, source_target_pairs={{0,3},{1,0},{2,1},{3,2},{4,7},{5,4},{6,5},{7,6},{8,11},{9,8},{10,9... | collective-permute-start | bytes 430088 | tf_op jit(solution)/shard_map/ppermute | solution.py:133
  57.6 32.2 %copy-start.3 = (bf16[3,35,16,128]{3,2,1,0:T(8,128)(2,1)}, bf16[3,35,16,128]{3,2,1,0:T(8,128)(2,1)S(1)}, u32[]{:S(2)}) copy-start(bf16[3,35,16,128]{3,2,1,0:T(8,128)(2,1)S(1)} %pad_maximum_fusion.2.refs_2_) | copy-start | bytes 1290244
  57.6 11.2 %collective-permute-start.13 = (bf16[3,35,16,128]{3,2,1,0:T(8,128)(2,1)S(1)}, bf16[3,35,16,128]{3,2,1,0:T(8,128)(2,1)}, u32[]{:S(2)}, u32[]{:S(2)}) collective-permute-start(bf16[3,35,16,128]{3,2,1,0:T(8,128)(2,1)S(1)} %pad_maximum_fusion.2.refs_2_), channel_id=1, source_target_pairs={{0,16},{4,20},{8,24},{12,28},{16,0},{20,4},{24,8},{28,12},{1,17},{... | collective-permute-start | bytes 1290248 | tf_op jit(solution)/shard_map/ppermute | solution.py:127
  59.2 12.8 %collective-permute-start.9 = (bf16[3,35,16,128]{3,2,1,0:T(8,128)(2,1)S(1)}, bf16[3,35,16,128]{3,2,1,0:T(8,128)(2,1)S(1)}, u32[]{:S(2)}, u32[]{:S(2)}) collective-permute-start(bf16[3,35,16,128]{3,2,1,0:T(8,128)(2,1)S(1)} %pad_maximum_fusion.2.refs_2_), channel_id=1, source_target_pairs={{0,8},{4,12},{8,0},{12,4},{16,24},{20,28},{24,16},{28,20},{1,9},{5... | collective-permute-start | bytes 1290248 | tf_op jit(solution)/shard_map/ppermute | solution.py:127
  60.7 12.8 %collective-permute-start.7 = (bf16[3,35,16,128]{3,2,1,0:T(8,128)(2,1)S(1)}, bf16[3,35,16,128]{3,2,1,0:T(8,128)(2,1)S(1)}, u32[]{:S(2)}, u32[]{:S(2)}) collective-permute-start(bf16[3,35,16,128]{3,2,1,0:T(8,128)(2,1)S(1)} %pad_maximum_fusion.2.refs_2_), channel_id=1, source_target_pairs={{0,4},{4,0},{8,12},{12,8},{16,20},{20,16},{24,28},{28,24},{1,5},{5... | collective-permute-start | bytes 1290248 | tf_op jit(solution)/shard_map/ppermute | solution.py:127
  61.7 28.1 %copy-start.4 = (bf16[3,35,16,128]{3,2,1,0:T(8,128)(2,1)}, bf16[3,35,16,128]{3,2,1,0:T(8,128)(2,1)S(1)}, u32[]{:S(2)}) copy-start(bf16[3,35,16,128]{3,2,1,0:T(8,128)(2,1)S(1)} %pad_maximum_fusion.1.refs_1_) | copy-start | bytes 1290244
  61.7 19.6 %collective-permute-start.8 = (bf16[3,35,16,128]{3,2,1,0:T(8,128)(2,1)S(1)}, bf16[3,35,16,128]{3,2,1,0:T(8,128)(2,1)}, u32[]{:S(2)}, u32[]{:S(2)}) collective-permute-start(bf16[3,35,16,128]{3,2,1,0:T(8,128)(2,1)S(1)} %pad_maximum_fusion.1.refs_1_), channel_id=1, source_target_pairs={{0,8},{4,12},{8,0},{12,4},{16,24},{20,28},{24,16},{28,20},{1,9},{5... | collective-permute-start | bytes 1290248 | tf_op jit(solution)/shard_map/ppermute | solution.py:127
  62.8 27.0 %collective-permute-start.12 = (bf16[3,35,16,128]{3,2,1,0:T(8,128)(2,1)S(1)}, bf16[3,35,16,128]{3,2,1,0:T(8,128)(2,1)}, u32[]{:S(2)}, u32[]{:S(2)}) collective-permute-start(bf16[3,35,16,128]{3,2,1,0:T(8,128)(2,1)S(1)} %pad_maximum_fusion.1.refs_1_), channel_id=1, source_target_pairs={{0,16},{4,20},{8,24},{12,28},{16,0},{20,4},{24,8},{28,12},{1,17},{... | collective-permute-start | bytes 1290248 | tf_op jit(solution)/shard_map/ppermute | solution.py:127
  68.8 21.1 %collective-permute-start.6 = (bf16[3,35,16,128]{3,2,1,0:T(8,128)(2,1)S(1)}, bf16[3,35,16,128]{3,2,1,0:T(8,128)(2,1)S(1)}, u32[]{:S(2)}, u32[]{:S(2)}) collective-permute-start(bf16[3,35,16,128]{3,2,1,0:T(8,128)(2,1)S(1)} %pad_maximum_fusion.1.refs_1_), channel_id=1, source_target_pairs={{0,4},{4,0},{8,12},{12,8},{16,20},{20,16},{24,28},{28,24},{1,5},{5... | collective-permute-start | bytes 1290248 | tf_op jit(solution)/shard_map/ppermute | solution.py:127
  72.0 17.9 %copy-start.6 = (bf16[3,35,16,128]{3,2,1,0:T(8,128)(2,1)}, bf16[3,35,16,128]{3,2,1,0:T(8,128)(2,1)S(1)}, u32[]{:S(2)}) copy-start(bf16[3,35,16,128]{3,2,1,0:T(8,128)(2,1)S(1)} %collective-permute-done.9.refs_6_) | copy-start | bytes 1290244
  72.0 18.5 %collective-permute-start.17 = (bf16[3,35,16,128]{3,2,1,0:T(8,128)(2,1)}, bf16[3,35,16,128]{3,2,1,0:T(8,128)(2,1)}, u32[]{:S(2)}, u32[]{:S(2)}) collective-permute-start(bf16[3,35,16,128]{3,2,1,0:T(8,128)(2,1)} %collective-permute-done.13.refs_10_), channel_id=1, source_target_pairs={{0,8},{4,12},{8,0},{12,4},{16,24},{20,28},{24,16},{28,20},{1,9},{5... | collective-permute-start | bytes 1290248 | tf_op jit(solution)/shard_map/ppermute | solution.py:127
  73.5 8.2 %copy-start.7 = (bf16[3,35,16,128]{3,2,1,0:T(8,128)(2,1)}, bf16[3,35,16,128]{3,2,1,0:T(8,128)(2,1)S(1)}, u32[]{:S(2)}) copy-start(bf16[3,35,16,128]{3,2,1,0:T(8,128)(2,1)S(1)} %collective-permute-done.7.refs_4_) | copy-start | bytes 1290244
  73.5 17.1 %collective-permute-start.11 = (bf16[3,35,16,128]{3,2,1,0:T(8,128)(2,1)S(1)}, bf16[3,35,16,128]{3,2,1,0:T(8,128)(2,1)S(1)}, u32[]{:S(2)}, u32[]{:S(2)}) collective-permute-start(bf16[3,35,16,128]{3,2,1,0:T(8,128)(2,1)S(1)} %collective-permute-done.9.refs_6_), channel_id=1, source_target_pairs={{0,4},{4,0},{8,12},{12,8},{16,20},{20,16},{24,28},{28,24},{1,5},{5... | collective-permute-start | bytes 1290248 | tf_op jit(solution)/shard_map/ppermute | solution.py:127
  81.4 10.2 %collective-permute-start.16 = (bf16[3,35,16,128]{3,2,1,0:T(8,128)(2,1)}, bf16[3,35,16,128]{3,2,1,0:T(8,128)(2,1)}, u32[]{:S(2)}, u32[]{:S(2)}) collective-permute-start(bf16[3,35,16,128]{3,2,1,0:T(8,128)(2,1)} %collective-permute-done.8.refs_5_), channel_id=1, source_target_pairs={{0,16},{4,20},{8,24},{12,28},{16,0},{20,4},{24,8},{28,12},{1,17},{... | collective-permute-start | bytes 1290248 | tf_op jit(solution)/shard_map/ppermute | solution.py:127
  89.8 6.5 %collective-permute-start.15 = (bf16[3,35,16,128]{3,2,1,0:T(8,128)(2,1)}, bf16[3,35,16,128]{3,2,1,0:T(8,128)(2,1)S(1)}, u32[]{:S(2)}, u32[]{:S(2)}) collective-permute-start(bf16[3,35,16,128]{3,2,1,0:T(8,128)(2,1)} %collective-permute-done.13.refs_10_), channel_id=1, source_target_pairs={{0,4},{4,0},{8,12},{12,8},{16,20},{20,16},{24,28},{28,24},{1,5},{5... | collective-permute-start | bytes 1290248 | tf_op jit(solution)/shard_map/ppermute | solution.py:127
  89.9 0.8 copy-start.8
  90.0 6.4 %collective-permute-start.10 = (bf16[3,35,16,128]{3,2,1,0:T(8,128)(2,1)}, bf16[3,35,16,128]{3,2,1,0:T(8,128)(2,1)}, u32[]{:S(2)}, u32[]{:S(2)}) collective-permute-start(bf16[3,35,16,128]{3,2,1,0:T(8,128)(2,1)} %collective-permute-done.8.refs_5_), channel_id=1, source_target_pairs={{0,4},{4,0},{8,12},{12,8},{16,20},{20,16},{24,28},{28,24},{1,5},{5... | collective-permute-start | bytes 1290248 | tf_op jit(solution)/shard_map/ppermute | solution.py:127
  90.5 5.9 %collective-permute-start.14 = (bf16[3,35,16,128]{3,2,1,0:T(8,128)(2,1)}, bf16[3,35,16,128]{3,2,1,0:T(8,128)(2,1)}, u32[]{:S(2)}, u32[]{:S(2)}) collective-permute-start(bf16[3,35,16,128]{3,2,1,0:T(8,128)(2,1)} %collective-permute-done.12.refs_9_), channel_id=1, source_target_pairs={{0,4},{4,0},{8,12},{12,8},{16,20},{20,16},{24,28},{28,24},{1,5},{5... | collective-permute-start | bytes 1290248 | tf_op jit(solution)/shard_map/ppermute | solution.py:127
  90.7 0.8 copy-start.9
  90.7 5.6 %collective-permute-start.19 = (bf16[3,35,16,128]{3,2,1,0:T(8,128)(2,1)}, bf16[3,35,16,128]{3,2,1,0:T(8,128)(2,1)}, u32[]{:S(2)}, u32[]{:S(2)}) collective-permute-start(bf16[3,35,16,128]{3,2,1,0:T(8,128)(2,1)} %collective-permute-done.17.refs_14_), channel_id=1, source_target_pairs={{0,4},{4,0},{8,12},{12,8},{16,20},{20,16},{24,28},{28,24},{1,5},{5... | collective-permute-start | bytes 1290248 | tf_op jit(solution)/shard_map/ppermute | solution.py:127
  91.5 4.9 %collective-permute-start.18 = (bf16[3,35,16,128]{3,2,1,0:T(8,128)(2,1)}, bf16[3,35,16,128]{3,2,1,0:T(8,128)(2,1)}, u32[]{:S(2)}, u32[]{:S(2)}) collective-permute-start(bf16[3,35,16,128]{3,2,1,0:T(8,128)(2,1)} %collective-permute-done.16.refs_13_), channel_id=1, source_target_pairs={{0,4},{4,0},{8,12},{12,8},{16,20},{20,16},{24,28},{28,24},{1,5},{5... | collective-permute-start | bytes 1290248 | tf_op jit(solution)/shard_map/ppermute | solution.py:127
  93.8 1.5 copy-start.14
  93.8 1.5 copy-start.15
  96.3 0.8 copy-start.10

commit v2 on v1

--- a/solution.py
+++ b/solution.py
@@ -24,6 +24,19 @@
 
 SIN_POLY = (4.4428679, -7.30744341, 3.59478797, -0.78437376)
 COS_POLY = (1.4142135, -6.97885099, 5.73946117, -1.88356298, 0.31069817)
+
+
+def half_turn(turns):
+    magic = jnp.float32(12582912.0)
+    r = turns - ((turns + magic) - magic)
+    z = r * r
+    s = jnp.float32(SIN_POLY[-1])
+    for value in SIN_POLY[-2::-1]:
+        s = s * z + value
+    k = jnp.float32(COS_POLY[-1])
+    for value in COS_POLY[-2::-1]:
+        k = k * z + value
+    return s * r, k
 
 
 def band_rows(band):
@@ -150,7 +163,7 @@
     positions, rows, modes, waves, half, slabs, keys = sizes
     parts = refs[: 1 + len(keys)]
     spread_ref, row_ref, column_ref, image_ref, sum_ref = refs[1 + len(keys) : 6 + len(keys)]
-    basis, path, opening, pupil, total, first, sems = refs[6 + len(keys) :]
+    basis, path, opening, even, odd, total, first, sems = refs[6 + len(keys) :]
     wave = where_ref[0]
     share = where_ref[1]
 
@@ -177,43 +190,42 @@
         lane = lax.broadcasted_iota(jnp.int32, (ROWS, LANES), 1)
         line = lax.broadcasted_iota(jnp.int32, (ROWS, LANES), 0)
 
-        def unit(u, carry):
-            slab, row = place_ref[u, 0], place_ref[u, 1]
-            a = 2 * (line + row) - (PUP - 1)
-            b = 2 * (lane + jnp.where(lane < 64, place_ref[u, 2], place_ref[u, 3])) - (PUP - 1)
-            radius = a * a + b * b
-            inside = (radius <= PUP * PUP) & (radius >= INNER * INNER)
-            values = basis[pl.ds(slab, modes)].reshape(modes * ROWS, LANES)
+        def chunk(c, carry):
+            values = jnp.concatenate(
+                [
+                    basis[pl.ds(place_ref[c * UNITS + j, 0], modes)].reshape(modes * ROWS, LANES)
+                    for j in range(UNITS)
+                ],
+                axis=1,
+            )
             found = jnp.dot(spread_ref[...], values, preferred_element_type=jnp.float32)
-            opening[u] = jnp.where(inside, 1.0, 0.0)
-            for f in range(positions):
-                path[u, f * ROWS : (f + 1) * ROWS] = jnp.where(
-                    inside, found[f * ROWS : (f + 1) * ROWS], 0.0
-                )
+            for j in range(UNITS):
+                u = c * UNITS + j
+                a = 2 * (line + place_ref[u, 1]) - (PUP - 1)
+                b = 2 * (lane + jnp.where(lane < 64, place_ref[u, 2], place_ref[u, 3])) - (PUP - 1)
+                radius = a * a + b * b
+                inside = (radius <= PUP * PUP) & (radius >= INNER * INNER)
+                opening[u] = jnp.where(inside, 1.0, 0.0)
+                for f in range(positions):
+                    path[u, f * ROWS : (f + 1) * ROWS] = jnp.where(
+                        inside, found[f * ROWS : (f + 1) * ROWS, j * LANES : (j + 1) * LANES], 0.0
+                    )
             return carry
 
-        lax.fori_loop(0, len(CHUNKS) * UNITS, unit, 0)
+        lax.fori_loop(0, len(CHUNKS), chunk, 0)
 
     inverse = inverse_ref[pl.program_id(0)]
-    magic = jnp.float32(12582912.0)
     total[...] = jnp.zeros_like(total)
-
-    def chunk(c, carry):
-        band, rows_band = place_ref[c * UNITS, 4], place_ref[c * UNITS, 5]
+    odd[...] = jnp.zeros_like(odd)
+
+    def form(c, pupil, before, held):
+        band, rows_band = place_ref[before * UNITS, 4], place_ref[before * UNITS, 5]
         for j in range(UNITS):
             u = c * UNITS + j
             inside = opening[u]
             for f in range(positions):
                 turns = path[u, f * ROWS : (f + 1) * ROWS] * inverse
-                r = turns - ((turns + magic) - magic)
-                z = r * r
-                s = SIN_POLY[-1]
-                for value in SIN_POLY[-2::-1]:
-                    s = s * z + value
-                s = s * r
-                k = COS_POLY[-1]
-                for value in COS_POLY[-2::-1]:
-                    k = k * z + value
+                s, k = half_turn(turns)
                 columns = slice(f * LANES, (f + 1) * LANES)
                 pupil[2 * ROWS * j : 2 * ROWS * j + ROWS, columns] = (inside - s * s).astype(
                     jnp.bfloat16
@@ -221,12 +233,21 @@
                 pupil[2 * ROWS * j + ROWS : 2 * ROWS * (j + 1), columns] = (s * k).astype(
                     jnp.bfloat16
                 )
-        total[band] += jnp.dot(
-            row_ref[0, rows_band], pupil[...], preferred_element_type=jnp.float32
-        )
+            width = positions * LANES // UNITS
+            if j % 2 == 1:
+                columns = slice((j - 1) * width, (j + 1) * width)
+                total[band, :, columns] += jnp.dot(
+                    row_ref[0, rows_band], held[:, columns], preferred_element_type=jnp.float32
+                )
+
+    def pair(i, carry):
+        form(2 * i, even, jnp.maximum(2 * i - 1, 0), odd)
+        form(2 * i + 1, odd, 2 * i, even)
         return carry
 
-    lax.fori_loop(0, len(CHUNKS), chunk, 0)
+    lax.fori_loop(0, len(CHUNKS) // 2, pair, 0)
+    band, rows_band = CHUNKS[-1]
+    total[band] += jnp.dot(row_ref[0, rows_band], odd[...], preferred_element_type=jnp.float32)
 
     for band in range(BANDS):
         for f in range(positions):
@@ -237,14 +258,11 @@
                 ] = total[
                     band, part * rows : (part + 1) * rows, f * LANES : (f + 1) * LANES
                 ].astype(jnp.bfloat16)
-    for f in range(positions):
-        both = jnp.dot(
-            first[f * rows : (f + 1) * rows], column_ref[0], preferred_element_type=jnp.float32
-        )
-        real, imag = both[:, :PIX], both[:, PIX:]
-        intensity = real * real + imag * imag
-        image_ref[0, f * rows : (f + 1) * rows] = intensity.astype(jnp.bfloat16)
-        sum_ref[0, f : f + 1] = jnp.sum(intensity, axis=0, keepdims=True)
+    real = jnp.dot(first[...], column_ref[0, :, :PIX], preferred_element_type=jnp.float32)
+    imag = jnp.dot(first[...], column_ref[0, :, PIX:], preferred_element_type=jnp.float32)
+    intensity = real * real + imag * imag
+    image_ref[0] = intensity.astype(jnp.bfloat16)
+    sum_ref[0] = jnp.sum(intensity.reshape(positions, rows, PIX), axis=1)
 
 
 def fields(own, got, spread, place, inverse, row_table, column_table, positions, rows, sizes):
@@ -287,6 +305,7 @@
             pltpu.VMEM((waves * slabs, ROWS, LANES), jnp.bfloat16),
             pltpu.VMEM((units, positions * ROWS, LANES), jnp.float32),
             pltpu.VMEM((units, ROWS, LANES), jnp.float32),
+            pltpu.VMEM((2 * BAND, positions * LANES), jnp.bfloat16),
             pltpu.VMEM((2 * BAND, positions * LANES), jnp.bfloat16),
             pltpu.VMEM((BANDS, 2 * rows, positions * LANES), jnp.float32),
             pltpu.VMEM((positions * rows, 2 * PUP), jnp.bfloat16),
@@ -326,32 +345,83 @@
     )(weights.reshape(positions, templates * lengths), images)
 
 
+def table_kernel(scale_ref, y_ref, v_ref, u_ref, x_ref, row_ref, column_ref):
+    scale = scale_ref[pl.program_id(0)]
+    for start in range(0, PUP, ROWS):
+        s, k = half_turn((y_ref[start : start + ROWS] * v_ref[...]) * scale)
+        cosine, sine = 1.0 - s * s, s * k
+        lower = slice(start, start + ROWS)
+        upper = slice(PUP + start, PUP + start + ROWS)
+        column_ref[0, lower, :PIX] = cosine.astype(jnp.bfloat16)
+        column_ref[0, lower, PIX:] = (-sine).astype(jnp.bfloat16)
+        column_ref[0, upper, :PIX] = sine.astype(jnp.bfloat16)
+        column_ref[0, upper, PIX:] = cosine.astype(jnp.bfloat16)
+    rows = u_ref.shape[0]
+    imag = (lax.broadcasted_iota(jnp.int32, (ROWS, 2 * BAND), 1) // ROWS) % 2 == 1
+    for band in range(BANDS):
+        for start in range(0, rows, ROWS):
+            s, k = half_turn((u_ref[start : start + ROWS] * x_ref[band]) * scale)
+            cosine, sine = 1.0 - s * s, s * k
+            row_ref[0, band, start : start + ROWS] = jnp.where(imag, sine, cosine).astype(
+                jnp.bfloat16
+            )
+            row_ref[0, band, rows + start : rows + start + ROWS] = jnp.where(
+                imag, cosine, -sine
+            ).astype(jnp.bfloat16)
+
+
 def tables(wave_lengths, rows):
-    factor = (TWO_PI * SAMPLING / (2.0 * PUP)) / wave_lengths
+    lengths = wave_lengths.shape[0]
+    scale = (SAMPLING / (2.0 * PUP)) / wave_lengths
     y = 2 * np.concatenate([band_columns(band) for band in range(BANDS)]) - PUP + 1
     v = np.arange(PIX) - PIX // 2
-    angles = (y[:, None] * v[None, :]).astype(np.float32)[None] * factor[:, None, None]
-    cosine, sine = jnp.cos(angles), jnp.sin(angles)
-    column_table = jnp.concatenate(
-        [
-            jnp.concatenate([cosine, -sine], axis=2),
-            jnp.concatenate([sine, cosine], axis=2),
-        ],
-        axis=1,
-    ).astype(jnp.bfloat16)
     u = lax.axis_index("wave") * rows + jnp.arange(rows, dtype=jnp.int32) - PIX // 2
     x = np.array(
         [[row + i for row in band_rows(band) for i in range(ROWS)] for band in range(BANDS)]
     )
     x = np.repeat(x.reshape(BANDS, UNITS, 1, ROWS), 2, axis=2).reshape(BANDS, 1, 2 * BAND)
-    imag = ((np.arange(2 * BAND) // ROWS) % 2 == 1)[None, None, None, :]
-    products = (u[None, :, None] * (2 * x - PUP + 1).astype(np.int32)).astype(jnp.float32)
-    angles = products[None] * factor[:, None, None, None]
-    cosine, sine = jnp.cos(angles), jnp.sin(angles)
-    row_table = jnp.concatenate(
-        [jnp.where(imag, sine, cosine), jnp.where(imag, cosine, -sine)], axis=2
-    ).astype(jnp.bfloat16)
-    return row_table, column_table
+    whole = lambda *shape: pl.BlockSpec(shape, lambda l: (0,) * len(shape))
+    return pl.pallas_call(
+        table_kernel,
+        grid=(lengths,),
+        out_shape=(
+            jax.ShapeDtypeStruct((lengths, BANDS, 2 * rows, 2 * BAND), jnp.bfloat16),
+            jax.ShapeDtypeStruct((lengths, 2 * PUP, 2 * PIX), jnp.bfloat16),
+        ),
+        in_specs=[
+            pl.BlockSpec(memory_space=pltpu.SMEM),
+            whole(PUP, 1),
+            whole(1, PIX),
+            whole(rows, 1),
+            whole(BANDS, 1, 2 * BAND),
+        ],
+        out_specs=(
+            pl.BlockSpec((1, BANDS, 2 * rows, 2 * BAND), lambda l: (l, 0, 0, 0)),
+            pl.BlockSpec((1, 2 * PUP, 2 * PIX), lambda l: (l, 0, 0)),
+        ),
+        cost_estimate=pl.CostEstimate(
+            flops=lengths * 30 * PUP * PIX, bytes_accessed=lengths * 4 * PUP * PIX * 2, transcendentals=0
+        ),
+        compiler_params=pltpu.CompilerParams(vmem_limit_bytes=24 * 2**20),
+    )(
+        scale,
+        jnp.asarray(y[:, None].astype(np.float32)),
+        jnp.asarray(v[None, :].astype(np.float32)),
+        u.astype(jnp.float32)[:, None],
+        jnp.asarray((2 * x - PUP + 1).astype(np.float32)),
+    )
+
+
+def every_length(wave_lengths, waves):
+    mine = lax.axis_index("wave")
+    count = wave_lengths.shape[0]
+    out = jnp.zeros((waves * count,), wave_lengths.dtype)
+    for s in range(waves):
+        part = wave_lengths
+        if s > 0:
+            part = lax.ppermute(part, "wave", [(i, (i + s) % waves) for i in range(waves)])
+        out = lax.dynamic_update_slice(out, part, (((mine - s) % waves) * count,))
+    return out
 
 
 def local(mode_basis, coef_table, table_index, wave_lengths, sed_table, template_ids):
@@ -361,11 +431,11 @@
     rows = PIX // waves
     count, half, slabs, pack, place = layout(waves, modes)
 
+    every = every_length(wave_lengths, waves)
     table = jnp.asarray(pack)[lax.axis_index("wave")]
     own = pack_rows(mode_basis, table, slabs)
     got = gather_rows(own, half, waves)
 
-    every = lax.all_gather(wave_lengths, "wave", axis=0, tiled=True)
     row_table, column_table = tables(every, rows)
 
     selector = (

time: 223 us -> 180 us (0.81)
  other arithmetic: 33.8 us -> 3.71 us
  Pallas kernels: 116 us -> 93 us
  waiting for transfers between devices: 15.7 us -> 29.9 us
  blocking collectives: 24.7 us -> 12.1 us
  local copies, waits for them, and re-layouts: 7.57 us -> 12.9 us
  starting transfers between devices: 22.9 us -> 26.9 us
    pallas_call x1, Pallas kernels: 108 us -> 77.8 us  [fields(): pl.pallas_call(functools.partial(field_kernel, (positions, rows, modes, w...]
    another operation x2 -> x0, other arithmetic: 23.7 us -> none
    unnamed x1 -> x0, blocking collectives: 15.7 us -> none
    ppermute x6, waiting for transfers between devices: 0.02 us -> 11.8 us  [gather_rows(): lax.ppermute(piece, 'wave', [(i, (i + s) % waves) for i in range(waves)])]
    ppermute x0 -> x3, waiting for transfers between devices: none -> 7.9 us  [every_length(): lax.ppermute(part, 'wave', [(i, (i + s) % waves) for i in range(waves)])]
    pallas_call x0 -> x1, Pallas kernels: none -> 6.77 us  [tables(): pl.pallas_call(table_kernel, grid=(lengths,), out_shape=(jax.ShapeDtypeSt...]
    ppermute x0 -> x3, starting transfers between devices: none -> 5.96 us  [every_length(): lax.ppermute(part, 'wave', [(i, (i + s) % waves) for i in range(waves)])]
    ppermute x14, waiting for transfers between devices: 15.7 us -> 10.2 us  [swap(): return lax.ppermute(x, ('groups', 'field'), pairs)]
  transfers between devices with their start and end apart: 20 -> 23, of which waited for: 3 -> 10; matrix products, arithmetic and copies ran while one was open for 16% -> 4% of each run, Pallas kernels for 0% -> 4%
where the time goes in v2:
time: 180 us
  Pallas kernels  93 us (52%)
  waiting for transfers between devices  29.9 us (17%)
  starting transfers between devices  26.9 us (15%)
  local copies, waits for them, and re-layouts  12.9 us (7%)
  blocking collectives  12.1 us (7%)
  other arithmetic  3.71 us (2%)
    pallas_call x1, Pallas kernels, fields(): pl.pallas_call(functools.partial(field_kernel, (positions, rows, modes, w...  77.8 us
    psum x1, blocking collectives, local(): level = lax.psum(jnp.sum(sums, axis=2), 'wave') / (PIX * PIX)  12.1 us
    ppermute x6, waiting for transfers between devices, gather_rows(): lax.ppermute(piece, 'wave', [(i, (i + s) % waves) for i in range(waves)])  11.8 us
    ppermute x6, starting transfers between devices, gather_rows(): lax.ppermute(piece, 'wave', [(i, (i + s) % waves) for i in range(waves)])  10.6 us
    ppermute x14, starting transfers between devices, swap(): return lax.ppermute(x, ('groups', 'field'), pairs)  10.4 us
    ppermute x14, waiting for transfers between devices, swap(): return lax.ppermute(x, ('groups', 'field'), pairs)  10.2 us
    ppermute x3, waiting for transfers between devices, every_length(): lax.ppermute(part, 'wave', [(i, (i + s) % waves) for i in range(waves)])  7.9 us
    unnamed x38, local copies, waits for them, and re-layouts  7.72 us
  transfers between devices with their start and end apart: 23, of which 10 were waited for; matrix products, arithmetic and copies ran while one was open for 4% of the time, Pallas kernels for 4%

profile of v2, /device:TPU:0, one launch (start us, length us, event | category | flops | bytes accessed | tf_op | source)
XLA Modules:
  0.0 180.1 jit_solution(2394694794892488887)
XLA Ops:
  0.0 0.7 dynamic-slice_bitcast_fusion
  0.7 0.1 copy.25.table
  0.8 1.8 %copy-done.3 = bf16[22,128,512]{2,1,0:T(8,128)(2,1)S(1)} copy-done((bf16[22,128,512]{2,1,0:T(8,128)(2,1)S(1)}, bf16[22,128,512]{2,1,0:T(8,128)(2,1)}, u32[]{:S(2)}) %copy-start.3) | copy-done | bytes 2883608
  2.6 1.6 shard_map.127.refs_0_
  4.3 0.0 copy-start.14
  4.4 0.0 copy-start.5
  4.4 0.0 copy-start.6
  4.4 0.0 copy-start.7
  4.5 3.1 %collective-permute-start.6 = (bf16[35,16,128]{2,1,0:T(8,128)(2,1)S(1)}, bf16[35,16,128]{2,1,0:T(8,128)(2,1)S(1)}, u32[]{:S(2)}, u32[]{:S(2)}) collective-permute-start(bf16[35,16,128]{2,1,0:T(8,128)(2,1)S(1)} %get-tuple-element.13), channel_id=1, source_target_pairs={{0,1},{1,2},{2,3},{3,0},{4,5},{5,6},{6,7},{7,4},{8,9},{9,10},{10,1... | collective-permute-start | bytes 430088 | tf_op jit(solution)/shard_map/ppermute | solution.py:146
  7.5 2.6 %collective-permute-start.7 = (bf16[35,16,128]{2,1,0:T(8,128)(2,1)S(1)}, bf16[35,16,128]{2,1,0:T(8,128)(2,1)S(1)}, u32[]{:S(2)}, u32[]{:S(2)}) collective-permute-start(bf16[35,16,128]{2,1,0:T(8,128)(2,1)S(1)} %get-tuple-element.13), channel_id=1, source_target_pairs={{0,2},{1,3},{2,0},{3,1},{4,6},{5,7},{6,4},{7,5},{8,10},{9,11},{10,... | collective-permute-start | bytes 430088 | tf_op jit(solution)/shard_map/ppermute | solution.py:146
  10.1 1.3 collective-permute-start.8
  11.5 0.7 collective-permute-start.3
  12.1 0.3 collective-permute-start.4
  12.5 1.8 collective-permute-done.6
  14.2 2.5 %collective-permute-start.5 = (bf16[35,16,128]{2,1,0:T(8,128)(2,1)S(1)}, bf16[35,16,128]{2,1,0:T(8,128)(2,1)S(1)}, u32[]{:S(2)}, u32[]{:S(2)}) collective-permute-start(bf16[35,16,128]{2,1,0:T(8,128)(2,1)S(1)} %get-tuple-element.14), channel_id=1, source_target_pairs={{0,3},{1,0},{2,1},{3,2},{4,7},{5,4},{6,5},{7,6},{8,11},{9,8},{10,9... | collective-permute-start | bytes 430088 | tf_op jit(solution)/shard_map/ppermute | solution.py:146
  16.8 3.7 %collective-permute-done.7 = bf16[35,16,128]{2,1,0:T(8,128)(2,1)S(1)} collective-permute-done((bf16[35,16,128]{2,1,0:T(8,128)(2,1)S(1)}, bf16[35,16,128]{2,1,0:T(8,128)(2,1)S(1)}, u32[]{:S(2)}, u32[]{:S(2)}) %collective-permute-start.7) | collective-permute-done | bytes 143392 | tf_op jit(solution)/shard_map/ppermute | solution.py:146
  20.4 2.3 %collective-permute-done.8 = bf16[35,16,128]{2,1,0:T(8,128)(2,1)S(1)} collective-permute-done((bf16[35,16,128]{2,1,0:T(8,128)(2,1)S(1)}, bf16[35,16,128]{2,1,0:T(8,128)(2,1)S(1)}, u32[]{:S(2)}, u32[]{:S(2)}) %collective-permute-start.8) | collective-permute-done | bytes 143392 | tf_op jit(solution)/shard_map/ppermute | solution.py:146
  22.8 3.6 %collective-permute-start.16 = (bf16[3,35,16,128]{3,2,1,0:T(8,128)(2,1)S(1)}, bf16[3,35,16,128]{3,2,1,0:T(8,128)(2,1)}, u32[]{:S(2)}, u32[]{:S(2)}) collective-permute-start(bf16[3,35,16,128]{3,2,1,0:T(8,128)(2,1)S(1)} %pad_maximum_fusion.1.refs_2_), channel_id=1, source_target_pairs={{0,16},{4,20},{8,24},{12,28},{16,0},{20,4},{24,8},{28,12},{1,17},{... | collective-permute-start | bytes 1290248 | tf_op jit(solution)/shard_map/ppermute | solution.py:140
  26.4 1.5 collective-permute-start.12
  27.9 4.0 %collective-permute-done.4 = bf16[35,16,128]{2,1,0:T(8,128)(2,1)S(1)} collective-permute-done((bf16[35,16,128]{2,1,0:T(8,128)(2,1)S(1)}, bf16[35,16,128]{2,1,0:T(8,128)(2,1)S(1)}, u32[]{:S(2)}, u32[]{:S(2)}) %collective-permute-start.4) | collective-permute-done | bytes 143392 | tf_op jit(solution)/shard_map/ppermute | solution.py:146
  31.9 0.8 pad_maximum_fusion.refs_1_
  32.7 1.5 collective-permute-start.11
  34.2 3.5 %collective-permute-start = (f32[2]{0:T(128)S(1)}, f32[2]{0:T(128)S(1)}, u32[]{:S(2)}, u32[]{:S(2)}) collective-permute-start(f32[2]{0:T(128)S(1)} %copy-done.18), channel_id=1, source_target_pairs={{0,1},{1,2},{2,3},{3,0},{4,5},{5,6},{6,7},{7,4},{8,9},{9,10},{10,1... | collective-permute-start | bytes 32 | tf_op jit(solution)/shard_map/ppermute | solution.py:422
  37.8 0.2 fusion.7
  38.0 2.3 %collective-permute-done = f32[2]{0:T(128)S(1)} collective-permute-done((f32[2]{0:T(128)S(1)}, f32[2]{0:T(128)S(1)}, u32[]{:S(2)}, u32[]{:S(2)}) %collective-permute-start) | collective-permute-done | bytes 40 | tf_op jit(solution)/shard_map/ppermute | solution.py:422
  40.3 0.4 collective-permute-start.1
  40.7 4.0 %collective-permute-done.1 = f32[2]{0:T(128)S(1)} collective-permute-done((f32[2]{0:T(128)S(1)}, f32[2]{0:T(128)S(1)}, u32[]{:S(2)}, u32[]{:S(2)}) %collective-permute-start.1) | collective-permute-done | bytes 40 | tf_op jit(solution)/shard_map/ppermute | solution.py:422
  44.8 2.0 %collective-permute-start.2 = (f32[2]{0:T(128)S(1)}, f32[2]{0:T(128)S(1)}, u32[]{:S(2)}, u32[]{:S(2)}) collective-permute-start(f32[2]{0:T(128)S(1)} %copy-done.18), channel_id=1, source_target_pairs={{0,3},{1,0},{2,1},{3,2},{4,7},{5,4},{6,5},{7,6},{8,11},{9,8},{10,9... | collective-permute-start | bytes 32 | tf_op jit(solution)/shard_map/ppermute | solution.py:422
  46.8 1.5 collective-permute-done.2
  48.3 1.5 collective-permute-start.15
  49.8 0.6 collective-permute-start.20
  50.4 0.2 collective-permute-start.14
  50.6 0.5 collective-permute-start.19
  51.1 0.2 multiply_convert_fusion
  51.3 1.1 convert_element_type.26
  52.4 1.6 copy.28.refs_17_
  54.0 0.2 dynamic_update_slice.12
  54.2 0.6 pad_add_fusion.where_ref
  54.8 5.1 %collective-permute-done.15.refs_9_ = bf16[3,35,16,128]{3,2,1,0:T(8,128)(2,1)} collective-permute-done((bf16[3,35,16,128]{3,2,1,0:T(8,128)(2,1)}, bf16[3,35,16,128]{3,2,1,0:T(8,128)(2,1)}, u32[]{:S(2)}, u32[]{:S(2)}) %collective-permute-start.15) | collective-permute-done | bytes 430112 | tf_op jit(solution)/shard_map/ppermute | solution.py:140
  59.9 0.5 collective-permute-start.13
  60.4 2.0 %collective-permute-done.20.refs_14_ = bf16[3,35,16,128]{3,2,1,0:T(8,128)(2,1)} collective-permute-done((bf16[3,35,16,128]{3,2,1,0:T(8,128)(2,1)}, bf16[3,35,16,128]{3,2,1,0:T(8,128)(2,1)}, u32[]{:S(2)}, u32[]{:S(2)}) %collective-permute-start.20) | collective-permute-done | bytes 430112 | tf_op jit(solution)/shard_map/ppermute | solution.py:140
  62.5 0.5 collective-permute-start.22
  63.0 3.1 %collective-permute-done.19.refs_13_ = bf16[3,35,16,128]{3,2,1,0:T(8,128)(2,1)} collective-permute-done((bf16[3,35,16,128]{3,2,1,0:T(8,128)(2,1)}, bf16[3,35,16,128]{3,2,1,0:T(8,128)(2,1)}, u32[]{:S(2)}, u32[]{:S(2)}) %collective-permute-start.19) | collective-permute-done | bytes 430112 | tf_op jit(solution)/shard_map/ppermute | solution.py:140
  66.1 1.0 fusion.5
  67.1 0.2 dynamic_update_slice.13
  67.3 0.2 dynamic_update_slice.14
  67.5 0.2 dynamic_update_slice.15
  67.7 0.5 broadcast_divide_fusion
  68.2 6.8 %shard_map.128 = (bf16[8,4,128,256]{3,2,1,0:T(8,128)(2,1)S(1)}, bf16[8,1024,512]{2,1,0:T(8,128)(2,1)S(1)}) custom-call(f32[8]{0:T(128)S(1)} %get-tuple-element.15.scale_ref, f32[512,1]{1,0:T(8,128)S(1)} %copy-done.5, f32[1,256]{1,0:T(1,128)S(1)} %copy-done.7, f32[64,1]{1,0:T(8,128)S(1)} %add_convert_fusion.u_ref, f32[4,1,256]{2,1,0:T(1,128)S(1)} %copy-done.6), custom_call_target="tpu_custom_call" | custom-call | flops 31457280 | bytes 8388608 | tf_op jit(solution)/shard_map/pallas_call | solution.py:384
  75.0 3.3 %copy-done.2 = bf16[8,1024,512]{2,1,0:T(8,128)(2,1)} copy-done((bf16[8,1024,512]{2,1,0:T(8,128)(2,1)}, bf16[8,1024,512]{2,1,0:T(8,128)(2,1)S(1)}, u32[]{:S(2)}) %copy-start.2) | copy-done | bytes 8388632
  78.3 1.3 copy-done.4
  79.7 0.7 copy-done.9
  80.4 0.2 copy-done.10
  80.5 0.2 copy-done.11
  80.7 0.1 copy-done.12
  80.8 0.1 copy-done.13
  80.9 77.8 %shard_map.129 = (bf16[8,512,256]{2,1,0:T(8,128)(2,1)}, f32[8,8,256]{2,1,0:T(8,128)}) custom-call(s32[96,6]{1,0:T(8,128)} %constant.112.place_ref, s32[2]{0:T(128)} %pad_add_fusion.where_ref, f32[8]{0:T(128)} %get-tuple-element.16.inverse_ref, bf16[560,16,128]{2,1,0:T(8,128)(2,1)} %copy-done.1, bf16[3,35,16,128]{3,2,1,0:T(8,128)(2,1)} %pad_maximum_fusion.refs_1_, ...), custom_call_target="tpu_custom_call" | custom-call | tf_op jit(solution)/shard_map/pallas_call | solution.py:284
  158.8 0.9 reduce_sum.19
  159.7 12.1 %psum.7 = f32[8,8]{1,0:T(8,128)S(1)} all-reduce(f32[8,8]{1,0:T(8,128)S(1)} %reduce_sum.19), channel_id=1, replica_groups=mesh['groups'=2,'field'=4,'wave'=4] {'wave'}, use_global_device_ids=true, to_apply=%region_2.3 | all-reduce | flops 64 | bytes 512 | tf_op jit(solution)/shard_map/psum | solution.py:463
  171.8 0.1 copy.29
  171.9 0.6 fusion.4
  172.5 0.1 copy.30
  172.6 0.7 reshape.27.weight_ref
  173.3 6.8 %shard_map.130 = bf16[8,8,64,256]{3,2,1,0:T(8,128)(2,1)} custom-call(f32[8,64]{1,0:T(8,128)} %reshape.27.weight_ref, bf16[8,512,256]{2,1,0:T(8,128)(2,1)} %get-tuple-element.12.image_ref), custom_call_target="tpu_custom_call" | custom-call | tf_op jit(solution)/shard_map/pallas_call | solution.py:336
  (49 shorter events, 0.2 us)
Async XLA Ops:
  0.0 37.7 %copy-start = (bf16[4096,22]{0,1:T(8,128)(2,1)S(1)}, bf16[4096,22]{0,1:T(8,128)(2,1)}, u32[]{:S(2)}) copy-start(bf16[4096,22]{0,1:T(8,128)(2,1)} %param.14) | copy-start | bytes 540676
  0.8 1.8 %copy-start.3 = (bf16[22,128,512]{2,1,0:T(8,128)(2,1)S(1)}, bf16[22,128,512]{2,1,0:T(8,128)(2,1)}, u32[]{:S(2)}) copy-start(bf16[22,128,512]{2,1,0:T(8,128)(2,1)} %basis.1) | copy-start | bytes 8650756
  4.3 48.1 %copy-start.1 = (bf16[560,16,128]{2,1,0:T(8,128)(2,1)}, bf16[560,16,128]{2,1,0:T(8,128)(2,1)S(1)}, u32[]{:S(2)}) copy-start(bf16[560,16,128]{2,1,0:T(8,128)(2,1)S(1)} %shard_map.127.refs_0_) | copy-start | bytes 6881284
  4.3 29.9 %copy-start.18 = (f32[2]{0:T(128)S(1)}, f32[2]{0:T(128)}, u32[]{:S(2)}) copy-start(f32[2]{0:T(128)} %param.16) | copy-start | bytes 28
  4.3 33.4 %copy-start.17 = (s32[8]{0:T(128)S(1)}, s32[8]{0:T(128)}, u32[]{:S(2)}) copy-start(s32[8]{0:T(128)} %param.15) | copy-start | bytes 100
  4.3 46.8 %copy-start.14 = (f32[16,16]{0,1:T(8,128)S(1)}, f32[16,16]{0,1:T(8,128)}, u32[]{:S(2)}) copy-start(f32[16,16]{0,1:T(8,128)} %constant.113) | copy-start | bytes 3076
  4.4 61.7 %copy-start.15 = (f32[1024,8]{0,1:T(8,128)S(1)}, f32[1024,8]{0,1:T(8,128)}, u32[]{:S(2)}) copy-start(f32[1024,8]{0,1:T(8,128)} %param.17) | copy-start | bytes 98308
  4.4 61.7 %copy-start.16 = (s32[8,8]{1,0:T(8,128)S(1)}, s32[8,8]{1,0:T(8,128)}, u32[]{:S(2)}) copy-start(s32[8,8]{1,0:T(8,128)} %param.18) | copy-start | bytes 772
  4.4 63.8 %copy-start.5 = (f32[512,1]{1,0:T(8,128)S(1)}, f32[512,1]{1,0:T(8,128)}, u32[]{:S(2)}) copy-start(f32[512,1]{1,0:T(8,128)} %constant.105.clone.y_ref) | copy-start | bytes 6148
  4.4 63.8 %copy-start.6 = (f32[4,1,256]{2,1,0:T(1,128)S(1)}, f32[4,1,256]{2,1,0:T(1,128)}, u32[]{:S(2)}) copy-start(f32[4,1,256]{2,1,0:T(1,128)} %constant.107.clone.x_ref) | copy-start | bytes 12292
  4.4 63.8 %copy-start.7 = (f32[1,256]{1,0:T(1,128)S(1)}, f32[1,256]{1,0:T(1,128)}, u32[]{:S(2)}) copy-start(f32[1,256]{1,0:T(1,128)} %constant.106.clone.v_ref) | copy-start | bytes 3076
  4.5 9.8 %collective-permute-start.6 = (bf16[35,16,128]{2,1,0:T(8,128)(2,1)S(1)}, bf16[35,16,128]{2,1,0:T(8,128)(2,1)S(1)}, u32[]{:S(2)}, u32[]{:S(2)}) collective-permute-start(bf16[35,16,128]{2,1,0:T(8,128)(2,1)S(1)} %get-tuple-element.13), channel_id=1, source_target_pairs={{0,1},{1,2},{2,3},{3,0},{4,5},{5,6},{6,7},{7,4},{8,9},{9,10},{10,1... | collective-permute-start | bytes 430088 | tf_op jit(solution)/shard_map/ppermute | solution.py:146
  7.5 12.9 %collective-permute-start.7 = (bf16[35,16,128]{2,1,0:T(8,128)(2,1)S(1)}, bf16[35,16,128]{2,1,0:T(8,128)(2,1)S(1)}, u32[]{:S(2)}, u32[]{:S(2)}) collective-permute-start(bf16[35,16,128]{2,1,0:T(8,128)(2,1)S(1)} %get-tuple-element.13), channel_id=1, source_target_pairs={{0,2},{1,3},{2,0},{3,1},{4,6},{5,7},{6,4},{7,5},{8,10},{9,11},{10,... | collective-permute-start | bytes 430088 | tf_op jit(solution)/shard_map/ppermute | solution.py:146
  10.1 12.7 %collective-permute-start.8 = (bf16[35,16,128]{2,1,0:T(8,128)(2,1)S(1)}, bf16[35,16,128]{2,1,0:T(8,128)(2,1)S(1)}, u32[]{:S(2)}, u32[]{:S(2)}) collective-permute-start(bf16[35,16,128]{2,1,0:T(8,128)(2,1)S(1)} %get-tuple-element.13), channel_id=1, source_target_pairs={{0,3},{1,0},{2,1},{3,2},{4,7},{5,4},{6,5},{7,6},{8,11},{9,8},{10,9... | collective-permute-start | bytes 430088 | tf_op jit(solution)/shard_map/ppermute | solution.py:146
  11.5 16.4 %collective-permute-start.3 = (bf16[35,16,128]{2,1,0:T(8,128)(2,1)S(1)}, bf16[35,16,128]{2,1,0:T(8,128)(2,1)S(1)}, u32[]{:S(2)}, u32[]{:S(2)}) collective-permute-start(bf16[35,16,128]{2,1,0:T(8,128)(2,1)S(1)} %get-tuple-element.14), channel_id=1, source_target_pairs={{0,1},{1,2},{2,3},{3,0},{4,5},{5,6},{6,7},{7,4},{8,9},{9,10},{10,1... | collective-permute-start | bytes 430088 | tf_op jit(solution)/shard_map/ppermute | solution.py:146
  12.1 19.7 %collective-permute-start.4 = (bf16[35,16,128]{2,1,0:T(8,128)(2,1)S(1)}, bf16[35,16,128]{2,1,0:T(8,128)(2,1)S(1)}, u32[]{:S(2)}, u32[]{:S(2)}) collective-permute-start(bf16[35,16,128]{2,1,0:T(8,128)(2,1)S(1)} %get-tuple-element.14), channel_id=1, source_target_pairs={{0,2},{1,3},{2,0},{3,1},{4,6},{5,7},{6,4},{7,5},{8,10},{9,11},{10,... | collective-permute-start | bytes 430088 | tf_op jit(solution)/shard_map/ppermute | solution.py:146
  14.2 17.6 %collective-permute-start.5 = (bf16[35,16,128]{2,1,0:T(8,128)(2,1)S(1)}, bf16[35,16,128]{2,1,0:T(8,128)(2,1)S(1)}, u32[]{:S(2)}, u32[]{:S(2)}) collective-permute-start(bf16[35,16,128]{2,1,0:T(8,128)(2,1)S(1)} %get-tuple-element.14), channel_id=1, source_target_pairs={{0,3},{1,0},{2,1},{3,2},{4,7},{5,4},{6,5},{7,6},{8,11},{9,8},{10,9... | collective-permute-start | bytes 430088 | tf_op jit(solution)/shard_map/ppermute | solution.py:146
  22.8 27.8 %copy-start.8 = (bf16[3,35,16,128]{3,2,1,0:T(8,128)(2,1)}, bf16[3,35,16,128]{3,2,1,0:T(8,128)(2,1)S(1)}, u32[]{:S(2)}) copy-start(bf16[3,35,16,128]{3,2,1,0:T(8,128)(2,1)S(1)} %pad_maximum_fusion.1.refs_2_) | copy-start | bytes 1290244
  22.8 27.0 %collective-permute-start.16 = (bf16[3,35,16,128]{3,2,1,0:T(8,128)(2,1)S(1)}, bf16[3,35,16,128]{3,2,1,0:T(8,128)(2,1)}, u32[]{:S(2)}, u32[]{:S(2)}) collective-permute-start(bf16[3,35,16,128]{3,2,1,0:T(8,128)(2,1)S(1)} %pad_maximum_fusion.1.refs_2_), channel_id=1, source_target_pairs={{0,16},{4,20},{8,24},{12,28},{16,0},{20,4},{24,8},{28,12},{1,17},{... | collective-permute-start | bytes 1290248 | tf_op jit(solution)/shard_map/ppermute | solution.py:140
  26.4 23.4 %collective-permute-start.12 = (bf16[3,35,16,128]{3,2,1,0:T(8,128)(2,1)S(1)}, bf16[3,35,16,128]{3,2,1,0:T(8,128)(2,1)}, u32[]{:S(2)}, u32[]{:S(2)}) collective-permute-start(bf16[3,35,16,128]{3,2,1,0:T(8,128)(2,1)S(1)} %pad_maximum_fusion.1.refs_2_), channel_id=1, source_target_pairs={{0,8},{4,12},{8,0},{12,4},{16,24},{20,28},{24,16},{28,20},{1,9},{5... | collective-permute-start | bytes 1290248 | tf_op jit(solution)/shard_map/ppermute | solution.py:140
  27.9 22.5 %collective-permute-start.10 = (bf16[3,35,16,128]{3,2,1,0:T(8,128)(2,1)S(1)}, bf16[3,35,16,128]{3,2,1,0:T(8,128)(2,1)}, u32[]{:S(2)}, u32[]{:S(2)}) collective-permute-start(bf16[3,35,16,128]{3,2,1,0:T(8,128)(2,1)S(1)} %pad_maximum_fusion.1.refs_2_), channel_id=1, source_target_pairs={{0,4},{4,0},{8,12},{12,8},{16,20},{20,16},{24,28},{28,24},{1,5},{5... | collective-permute-start | bytes 1290248 | tf_op jit(solution)/shard_map/ppermute | solution.py:140
  32.7 17.9 %collective-permute-start.11 = (bf16[3,35,16,128]{3,2,1,0:T(8,128)(2,1)}, bf16[3,35,16,128]{3,2,1,0:T(8,128)(2,1)}, u32[]{:S(2)}, u32[]{:S(2)}) collective-permute-start(bf16[3,35,16,128]{3,2,1,0:T(8,128)(2,1)} %pad_maximum_fusion.refs_1_), channel_id=1, source_target_pairs={{0,8},{4,12},{8,0},{12,4},{16,24},{20,28},{24,16},{28,20},{1,9},{5... | collective-permute-start | bytes 1290248 | tf_op jit(solution)/shard_map/ppermute | solution.py:140
  34.2 6.1 %collective-permute-start = (f32[2]{0:T(128)S(1)}, f32[2]{0:T(128)S(1)}, u32[]{:S(2)}, u32[]{:S(2)}) collective-permute-start(f32[2]{0:T(128)S(1)} %copy-done.18), channel_id=1, source_target_pairs={{0,1},{1,2},{2,3},{3,0},{4,5},{5,6},{6,7},{7,4},{8,9},{9,10},{10,1... | collective-permute-start | bytes 32 | tf_op jit(solution)/shard_map/ppermute | solution.py:422
  40.3 4.4 %collective-permute-start.1 = (f32[2]{0:T(128)S(1)}, f32[2]{0:T(128)S(1)}, u32[]{:S(2)}, u32[]{:S(2)}) collective-permute-start(f32[2]{0:T(128)S(1)} %copy-done.18), channel_id=1, source_target_pairs={{0,2},{1,3},{2,0},{3,1},{4,6},{5,7},{6,4},{7,5},{8,10},{9,11},{10,... | collective-permute-start | bytes 32 | tf_op jit(solution)/shard_map/ppermute | solution.py:422
  44.8 3.5 %collective-permute-start.2 = (f32[2]{0:T(128)S(1)}, f32[2]{0:T(128)S(1)}, u32[]{:S(2)}, u32[]{:S(2)}) collective-permute-start(f32[2]{0:T(128)S(1)} %copy-done.18), channel_id=1, source_target_pairs={{0,3},{1,0},{2,1},{3,2},{4,7},{5,4},{6,5},{7,6},{8,11},{9,8},{10,9... | collective-permute-start | bytes 32 | tf_op jit(solution)/shard_map/ppermute | solution.py:422
  48.3 11.6 %collective-permute-start.15 = (bf16[3,35,16,128]{3,2,1,0:T(8,128)(2,1)}, bf16[3,35,16,128]{3,2,1,0:T(8,128)(2,1)}, u32[]{:S(2)}, u32[]{:S(2)}) collective-permute-start(bf16[3,35,16,128]{3,2,1,0:T(8,128)(2,1)} %pad_maximum_fusion.refs_1_), channel_id=1, source_target_pairs={{0,16},{4,20},{8,24},{12,28},{16,0},{20,4},{24,8},{28,12},{1,17},{... | collective-permute-start | bytes 1290248 | tf_op jit(solution)/shard_map/ppermute | solution.py:140
  49.8 10.1 %collective-permute-start.9 = (bf16[3,35,16,128]{3,2,1,0:T(8,128)(2,1)}, bf16[3,35,16,128]{3,2,1,0:T(8,128)(2,1)}, u32[]{:S(2)}, u32[]{:S(2)}) collective-permute-start(bf16[3,35,16,128]{3,2,1,0:T(8,128)(2,1)} %pad_maximum_fusion.refs_1_), channel_id=1, source_target_pairs={{0,4},{4,0},{8,12},{12,8},{16,20},{20,16},{24,28},{28,24},{1,5},{5... | collective-permute-start | bytes 1290248 | tf_op jit(solution)/shard_map/ppermute | solution.py:140
  49.8 12.6 %collective-permute-start.20 = (bf16[3,35,16,128]{3,2,1,0:T(8,128)(2,1)}, bf16[3,35,16,128]{3,2,1,0:T(8,128)(2,1)}, u32[]{:S(2)}, u32[]{:S(2)}) collective-permute-start(bf16[3,35,16,128]{3,2,1,0:T(8,128)(2,1)} %collective-permute-done.16.refs_10_), channel_id=1, source_target_pairs={{0,8},{4,12},{8,0},{12,4},{16,24},{20,28},{24,16},{28,20},{1,9},{5... | collective-permute-start | bytes 1290248 | tf_op jit(solution)/shard_map/ppermute | solution.py:140
  50.4 12.0 %collective-permute-start.14 = (bf16[3,35,16,128]{3,2,1,0:T(8,128)(2,1)}, bf16[3,35,16,128]{3,2,1,0:T(8,128)(2,1)}, u32[]{:S(2)}, u32[]{:S(2)}) collective-permute-start(bf16[3,35,16,128]{3,2,1,0:T(8,128)(2,1)} %collective-permute-done.12.refs_6_), channel_id=1, source_target_pairs={{0,4},{4,0},{8,12},{12,8},{16,20},{20,16},{24,28},{28,24},{1,5},{5... | collective-permute-start | bytes 1290248 | tf_op jit(solution)/shard_map/ppermute | solution.py:140
  50.6 15.4 %collective-permute-start.19 = (bf16[3,35,16,128]{3,2,1,0:T(8,128)(2,1)}, bf16[3,35,16,128]{3,2,1,0:T(8,128)(2,1)}, u32[]{:S(2)}, u32[]{:S(2)}) collective-permute-start(bf16[3,35,16,128]{3,2,1,0:T(8,128)(2,1)} %collective-permute-done.11.refs_5_), channel_id=1, source_target_pairs={{0,16},{4,20},{8,24},{12,28},{16,0},{20,4},{24,8},{28,12},{1,17},{... | collective-permute-start | bytes 1290248 | tf_op jit(solution)/shard_map/ppermute | solution.py:140
  59.9 19.7 %collective-permute-start.18 = (bf16[3,35,16,128]{3,2,1,0:T(8,128)(2,1)}, bf16[3,35,16,128]{3,2,1,0:T(8,128)(2,1)S(1)}, u32[]{:S(2)}, u32[]{:S(2)}) collective-permute-start(bf16[3,35,16,128]{3,2,1,0:T(8,128)(2,1)} %collective-permute-done.16.refs_10_), channel_id=1, source_target_pairs={{0,4},{4,0},{8,12},{12,8},{16,20},{20,16},{24,28},{28,24},{1,5},{5... | collective-permute-start | bytes 1290248 | tf_op jit(solution)/shard_map/ppermute | solution.py:140
  59.9 19.7 %collective-permute-start.13 = (bf16[3,35,16,128]{3,2,1,0:T(8,128)(2,1)}, bf16[3,35,16,128]{3,2,1,0:T(8,128)(2,1)S(1)}, u32[]{:S(2)}, u32[]{:S(2)}) collective-permute-start(bf16[3,35,16,128]{3,2,1,0:T(8,128)(2,1)} %collective-permute-done.11.refs_5_), channel_id=1, source_target_pairs={{0,4},{4,0},{8,12},{12,8},{16,20},{20,16},{24,28},{28,24},{1,5},{5... | collective-permute-start | bytes 1290248 | tf_op jit(solution)/shard_map/ppermute | solution.py:140
  62.5 17.2 %collective-permute-start.17 = (bf16[3,35,16,128]{3,2,1,0:T(8,128)(2,1)}, bf16[3,35,16,128]{3,2,1,0:T(8,128)(2,1)S(1)}, u32[]{:S(2)}, u32[]{:S(2)}) collective-permute-start(bf16[3,35,16,128]{3,2,1,0:T(8,128)(2,1)} %collective-permute-done.15.refs_9_), channel_id=1, source_target_pairs={{0,4},{4,0},{8,12},{12,8},{16,20},{20,16},{24,28},{28,24},{1,5},{5... | collective-permute-start | bytes 1290248 | tf_op jit(solution)/shard_map/ppermute | solution.py:140
  62.5 17.2 %collective-permute-start.22 = (bf16[3,35,16,128]{3,2,1,0:T(8,128)(2,1)}, bf16[3,35,16,128]{3,2,1,0:T(8,128)(2,1)S(1)}, u32[]{:S(2)}, u32[]{:S(2)}) collective-permute-start(bf16[3,35,16,128]{3,2,1,0:T(8,128)(2,1)} %collective-permute-done.20.refs_14_), channel_id=1, source_target_pairs={{0,4},{4,0},{8,12},{12,8},{16,20},{20,16},{24,28},{28,24},{1,5},{5... | collective-permute-start | bytes 1290248 | tf_op jit(solution)/shard_map/ppermute | solution.py:140
  66.1 13.6 %collective-permute-start.21 = (bf16[3,35,16,128]{3,2,1,0:T(8,128)(2,1)}, bf16[3,35,16,128]{3,2,1,0:T(8,128)(2,1)S(1)}, u32[]{:S(2)}, u32[]{:S(2)}) collective-permute-start(bf16[3,35,16,128]{3,2,1,0:T(8,128)(2,1)} %collective-permute-done.19.refs_13_), channel_id=1, source_target_pairs={{0,4},{4,0},{8,12},{12,8},{16,20},{20,16},{24,28},{28,24},{1,5},{5... | collective-permute-start | bytes 1290248 | tf_op jit(solution)/shard_map/ppermute | solution.py:140
  75.0 3.3 %copy-start.2 = (bf16[8,1024,512]{2,1,0:T(8,128)(2,1)}, bf16[8,1024,512]{2,1,0:T(8,128)(2,1)S(1)}, u32[]{:S(2)}) copy-start(bf16[8,1024,512]{2,1,0:T(8,128)(2,1)S(1)} %get-tuple-element.10.refs_19_) | copy-start | bytes 25165828
  78.3 1.3 copy-start.4
  79.6 0.8 copy-start.9
  79.6 0.9 copy-start.10
  79.6 1.1 copy-start.11
  79.7 1.2 copy-start.12
  79.7 1.3 copy-start.13

commit v3 on v2

--- a/solution.py
+++ b/solution.py
@@ -159,80 +159,112 @@
     return got
 
 
-def field_kernel(sizes, place_ref, where_ref, inverse_ref, *refs):
-    positions, rows, modes, waves, half, slabs, keys = sizes
+def path_kernel(sizes, place_ref, where_ref, *refs):
+    positions, modes, waves, half, slabs, keys = sizes
     parts = refs[: 1 + len(keys)]
-    spread_ref, row_ref, column_ref, image_ref, sum_ref = refs[1 + len(keys) : 6 + len(keys)]
-    basis, path, opening, even, odd, total, first, sems = refs[6 + len(keys) :]
+    spread_ref = refs[1 + len(keys)]
+    path, opening, basis, sems = refs[-4:]
     wave = where_ref[0]
     share = where_ref[1]
-
-    @pl.when(pl.program_id(0) == 0)
-    def _():
-        copies = [
-            pltpu.make_async_copy(parts[0], basis.at[pl.ds(wave * slabs, slabs)], sems.at[0])
+    copies = [pltpu.make_async_copy(parts[0], basis.at[pl.ds(wave * slabs, slabs)], sems.at[0])]
+    n = 1
+    for key, part in zip(keys, parts[1:]):
+        mask, h = key
+        for s in range(1, waves):
+            source = lax.rem(wave + (waves - s), waves)
+            start = source * slabs + (share ^ mask) * (2 * half) + h * half
+            copies.append(
+                pltpu.make_async_copy(part.at[s - 1], basis.at[pl.ds(start, half)], sems.at[n])
+            )
+            n += 1
+    for copy in copies:
+        copy.start()
+    for copy in copies:
+        copy.wait()
+
+    lane = lax.broadcasted_iota(jnp.int32, (ROWS, LANES), 1)
+    line = lax.broadcasted_iota(jnp.int32, (ROWS, LANES), 0)
+
+    def chunk(c, carry):
+        values = jnp.concatenate(
+            [
+                basis[pl.ds(place_ref[c * UNITS + j, 0], modes)].reshape(modes * ROWS, LANES)
+                for j in range(UNITS)
+            ],
+            axis=1,
+        )
+        found = jnp.dot(spread_ref[...], values, preferred_element_type=jnp.float32)
+        for j in range(UNITS):
+            u = c * UNITS + j
+            a = 2 * (line + place_ref[u, 1]) - (PUP - 1)
+            b = 2 * (lane + jnp.where(lane < 64, place_ref[u, 2], place_ref[u, 3])) - (PUP - 1)
+            radius = a * a + b * b
+            inside = (radius <= PUP * PUP) & (radius >= INNER * INNER)
+            opening[u] = jnp.where(inside, 1.0, 0.0)
+            for f in range(positions):
+                path[u, f * ROWS : (f + 1) * ROWS] = jnp.where(
+                    inside, found[f * ROWS : (f + 1) * ROWS, j * LANES : (j + 1) * LANES], 0.0
+                )
+        return carry
+
+    lax.fori_loop(0, len(CHUNKS), chunk, 0)
+
+
+def paths(own, got, spread, place, after, positions, sizes):
+    modes, waves, half, slabs = sizes
+    keys = sorted(got)
+    units = place.shape[0]
+    where = jnp.stack(
+        [
+            lax.axis_index("wave"),
+            (lax.axis_index("groups") % 2) * 4 + lax.axis_index("field") % 4,
         ]
-        n = 1
-        for key, part in zip(keys, parts[1:]):
-            mask, h = key
-            for s in range(1, waves):
-                source = lax.rem(wave + (waves - s), waves)
-                start = source * slabs + (share ^ mask) * (2 * half) + h * half
-                copies.append(
-                    pltpu.make_async_copy(part.at[s - 1], basis.at[pl.ds(start, half)], sems.at[n])
-                )
-                n += 1
-        for copy in copies:
-            copy.start()
-        for copy in copies:
-            copy.wait()
-
-        lane = lax.broadcasted_iota(jnp.int32, (ROWS, LANES), 1)
-        line = lax.broadcasted_iota(jnp.int32, (ROWS, LANES), 0)
-
-        def chunk(c, carry):
-            values = jnp.concatenate(
-                [
-                    basis[pl.ds(place_ref[c * UNITS + j, 0], modes)].reshape(modes * ROWS, LANES)
-                    for j in range(UNITS)
-                ],
-                axis=1,
-            )
-            found = jnp.dot(spread_ref[...], values, preferred_element_type=jnp.float32)
-            for j in range(UNITS):
-                u = c * UNITS + j
-                a = 2 * (line + place_ref[u, 1]) - (PUP - 1)
-                b = 2 * (lane + jnp.where(lane < 64, place_ref[u, 2], place_ref[u, 3])) - (PUP - 1)
-                radius = a * a + b * b
-                inside = (radius <= PUP * PUP) & (radius >= INNER * INNER)
-                opening[u] = jnp.where(inside, 1.0, 0.0)
-                for f in range(positions):
-                    path[u, f * ROWS : (f + 1) * ROWS] = jnp.where(
-                        inside, found[f * ROWS : (f + 1) * ROWS, j * LANES : (j + 1) * LANES], 0.0
-                    )
-            return carry
-
-        lax.fori_loop(0, len(CHUNKS), chunk, 0)
-
+    ).astype(jnp.int32)
+    smem = pl.BlockSpec(memory_space=pltpu.SMEM)
+    hbm = pl.BlockSpec(memory_space=pl.ANY)
+    vmem = pl.BlockSpec(memory_space=pltpu.VMEM)
+    return pl.pallas_call(
+        functools.partial(path_kernel, (positions, modes, waves, half, slabs, tuple(keys))),
+        out_shape=(
+            jax.ShapeDtypeStruct((units, positions * ROWS, LANES), jnp.float32),
+            jax.ShapeDtypeStruct((units, ROWS, LANES), jnp.float32),
+        ),
+        in_specs=[smem, smem, hbm] + [hbm] * len(keys) + [vmem] + [hbm] * len(after),
+        out_specs=(vmem, vmem),
+        scratch_shapes=[
+            pltpu.VMEM((waves * slabs, ROWS, LANES), jnp.bfloat16),
+            pltpu.SemaphoreType.DMA((1 + len(keys) * (waves - 1),)),
+        ],
+        compiler_params=pltpu.CompilerParams(vmem_limit_bytes=32 * 2**20),
+    )(place, where, own, *[got[key] for key in keys], spread, *after)
+
+
+def field_kernel(sizes, inverse_ref, path, opening, row_ref, column_ref, *refs):
+    positions, rows, parts = sizes
+    image_ref = refs[0]
+    even, odd, total, first = refs[-4:]
     inverse = inverse_ref[pl.program_id(0)]
     total[...] = jnp.zeros_like(total)
     odd[...] = jnp.zeros_like(odd)
-
-    def form(c, pupil, before, held):
-        band, rows_band = place_ref[before * UNITS, 4], place_ref[before * UNITS, 5]
+    batch = max(1, positions // 2)
+
+    def form(c, pupil, band, rows_band, held):
         for j in range(UNITS):
             u = c * UNITS + j
             inside = opening[u]
-            for f in range(positions):
-                turns = path[u, f * ROWS : (f + 1) * ROWS] * inverse
-                s, k = half_turn(turns)
-                columns = slice(f * LANES, (f + 1) * LANES)
-                pupil[2 * ROWS * j : 2 * ROWS * j + ROWS, columns] = (inside - s * s).astype(
-                    jnp.bfloat16
-                )
-                pupil[2 * ROWS * j + ROWS : 2 * ROWS * (j + 1), columns] = (s * k).astype(
-                    jnp.bfloat16
-                )
+            for f0 in range(0, positions, batch):
+                s, k = half_turn(path[u, f0 * ROWS : (f0 + batch) * ROWS] * inverse)
+                sine = s * k
+                square = s * s
+                for f in range(f0, f0 + batch):
+                    columns = slice(f * LANES, (f + 1) * LANES)
+                    lines = slice((f - f0) * ROWS, (f - f0 + 1) * ROWS)
+                    pupil[2 * ROWS * j : 2 * ROWS * j + ROWS, columns] = (
+                        inside - square[lines]
+                    ).astype(jnp.bfloat16)
+                    pupil[2 * ROWS * j + ROWS : 2 * ROWS * (j + 1), columns] = sine[lines].astype(
+                        jnp.bfloat16
+                    )
             width = positions * LANES // UNITS
             if j % 2 == 1:
                 columns = slice((j - 1) * width, (j + 1) * width)
@@ -240,9 +272,16 @@
                     row_ref[0, rows_band], held[:, columns], preferred_element_type=jnp.float32
                 )
 
+    def chunk_bands(c):
+        band, rows_band = jnp.int32(CHUNKS[0][0]), jnp.int32(CHUNKS[0][1])
+        for n, (one, two) in enumerate(CHUNKS[1:]):
+            band = jnp.where(c > n, one, band)
+            rows_band = jnp.where(c > n, two, rows_band)
+        return band, rows_band
+
     def pair(i, carry):
-        form(2 * i, even, jnp.maximum(2 * i - 1, 0), odd)
-        form(2 * i + 1, odd, 2 * i, even)
+        form(2 * i, even, *chunk_bands(2 * i - 1), odd)
+        form(2 * i + 1, odd, *chunk_bands(2 * i), even)
         return carry
 
     lax.fori_loop(0, len(CHUNKS) // 2, pair, 0)
@@ -258,91 +297,107 @@
                 ] = total[
                     band, part * rows : (part + 1) * rows, f * LANES : (f + 1) * LANES
                 ].astype(jnp.bfloat16)
-    real = jnp.dot(first[...], column_ref[0, :, :PIX], preferred_element_type=jnp.float32)
-    imag = jnp.dot(first[...], column_ref[0, :, PIX:], preferred_element_type=jnp.float32)
-    intensity = real * real + imag * imag
-    image_ref[0] = intensity.astype(jnp.bfloat16)
-    sum_ref[0] = jnp.sum(intensity.reshape(positions, rows, PIX), axis=1)
-
-
-def fields(own, got, spread, place, inverse, row_table, column_table, positions, rows, sizes):
-    modes, waves, half, slabs = sizes
-    keys = sorted(got)
+    if parts == 1:
+        sum_ref = refs[1]
+        real = jnp.dot(first[...], column_ref[0, :, :PIX], preferred_element_type=jnp.float32)
+        imag = jnp.dot(first[...], column_ref[0, :, PIX:], preferred_element_type=jnp.float32)
+        intensity = real * real + imag * imag
+        image_ref[0] = intensity
+        sum_ref[0] = jnp.sum(intensity.reshape(positions, rows, PIX), axis=1)
+    else:
+        share = rows // parts
+        for f in range(positions):
+            lines = first[f * rows : (f + 1) * rows]
+            real = jnp.dot(lines, column_ref[0, :, :PIX], preferred_element_type=jnp.float32)
+            imag = jnp.dot(lines, column_ref[0, :, PIX:], preferred_element_type=jnp.float32)
+            intensity = real * real + imag * imag
+            level = jnp.sum(
+                jnp.sum(intensity, axis=0, keepdims=True), axis=1, keepdims=True
+            ) / (rows * PIX)
+            spectra = (intensity / (level + EPSILON)).astype(jnp.bfloat16)
+            for part in range(parts):
+                image_ref[part, 0, f * share : (f + 1) * share] = spectra[
+                    part * share : (part + 1) * share
+                ]
+
+
+def fields(path, opening, inverse, row_table, column_table, positions, parts):
     lengths = row_table.shape[0]
-    units = place.shape[0]
-    where = jnp.stack(
-        [
-            lax.axis_index("wave"),
-            (lax.axis_index("groups") % 2) * 4 + lax.axis_index("field") % 4,
-        ]
-    ).astype(jnp.int32)
-    place = jnp.concatenate(
-        [place, np.repeat(np.array(CHUNKS, np.int32), UNITS, axis=0)], axis=1
-    )
-    smem = pl.BlockSpec(memory_space=pltpu.SMEM)
-    hbm = pl.BlockSpec(memory_space=pl.ANY)
+    rows = row_table.shape[2] // 2
+    if parts == 1:
+        out_shape = (
+            jax.ShapeDtypeStruct((lengths, positions * rows, PIX), jnp.float32),
+            jax.ShapeDtypeStruct((lengths, positions, PIX), jnp.float32),
+        )
+        out_specs = (
+            pl.BlockSpec((1, positions * rows, PIX), lambda l: (l, 0, 0)),
+            pl.BlockSpec((1, positions, PIX), lambda l: (l, 0, 0)),
+        )
+    else:
+        share = positions * rows // parts
+        out_shape = jax.ShapeDtypeStruct((parts, lengths, share, PIX), jnp.bfloat16)
+        out_specs = pl.BlockSpec((parts, 1, share, PIX), lambda l: (0, l, 0, 0))
     return pl.pallas_call(
-        functools.partial(
-            field_kernel, (positions, rows, modes, waves, half, slabs, tuple(keys))
-        ),
+        functools.partial(field_kernel, (positions, rows, parts)),
         grid=(lengths,),
-        out_shape=(
-            jax.ShapeDtypeStruct((lengths, positions * rows, PIX), jnp.bfloat16),
-            jax.ShapeDtypeStruct((lengths, positions, PIX), jnp.float32),
-        ),
-        in_specs=[smem, smem, smem, hbm]
-        + [hbm] * len(keys)
-        + [
-            pl.BlockSpec(spread.shape, lambda l: (0, 0)),
+        out_shape=out_shape,
+        in_specs=[
+            pl.BlockSpec(memory_space=pltpu.SMEM),
+            pl.BlockSpec(memory_space=pltpu.VMEM),
+            pl.BlockSpec(memory_space=pltpu.VMEM),
             pl.BlockSpec((1,) + row_table.shape[1:], lambda l: (l, 0, 0, 0)),
             pl.BlockSpec((1,) + column_table.shape[1:], lambda l: (l, 0, 0)),
         ],
-        out_specs=(
-            pl.BlockSpec((1, positions * rows, PIX), lambda l: (l, 0, 0)),
-            pl.BlockSpec((1, positions, PIX), lambda l: (l, 0, 0)),
-        ),
+        out_specs=out_specs,
         scratch_shapes=[
-            pltpu.VMEM((waves * slabs, ROWS, LANES), jnp.bfloat16),
-            pltpu.VMEM((units, positions * ROWS, LANES), jnp.float32),
-            pltpu.VMEM((units, ROWS, LANES), jnp.float32),
             pltpu.VMEM((2 * BAND, positions * LANES), jnp.bfloat16),
             pltpu.VMEM((2 * BAND, positions * LANES), jnp.bfloat16),
             pltpu.VMEM((BANDS, 2 * rows, positions * LANES), jnp.float32),
             pltpu.VMEM((positions * rows, 2 * PUP), jnp.bfloat16),
-            pltpu.SemaphoreType.DMA((1 + len(keys) * (waves - 1),)),
         ],
-        compiler_params=pltpu.CompilerParams(vmem_limit_bytes=56 * 2**20),
-    )(place, where, inverse, own, *[got[key] for key in keys], spread, row_table, column_table)
-
-
-def mix_kernel(weight_ref, image_ref, out_ref):
+        cost_estimate=pl.CostEstimate(
+            flops=lengths * positions * (rows * 8 * PUP * PUP + rows * 8 * PUP * PIX + 10**8),
+            bytes_accessed=8 * 2**20,
+            transcendentals=0,
+        ),
+        compiler_params=pltpu.CompilerParams(vmem_limit_bytes=44 * 2**20),
+    )(inverse, path, opening, row_table, column_table)
+
+
+def mix_kernel(inverse_ref, weight_ref, sent_ref, image_ref, out_ref):
     f = pl.program_id(0)
-    templates = out_ref.shape[1]
-    lengths = image_ref.shape[0]
-    for start in range(0, image_ref.shape[1], ROWS):
-        rows = slice(start, start + ROWS)
-        sums = [None] * templates
-        for l in range(lengths):
-            values = image_ref[l, rows].astype(jnp.float32)
-            for j in range(templates):
-                term = weight_ref[f, j * lengths + l] * values
-                sums[j] = term if l == 0 else sums[j] + term
+    templates, rows = out_ref.shape[1], out_ref.shape[2]
+    for start in range(0, rows, ROWS):
+        lines = slice(start, start + ROWS)
+        values = [sent_ref[l, lines] for l in range(sent_ref.shape[0])] + [
+            (image_ref[l, lines] * inverse_ref[l, f]).astype(jnp.bfloat16)
+            for l in range(image_ref.shape[0])
+        ]
+        mixed = jnp.dot(
+            weight_ref[0], jnp.concatenate(values, axis=0), preferred_element_type=jnp.float32
+        )
         for j in range(templates):
-            out_ref[0, j, rows] = sums[j].astype(jnp.bfloat16)
-
-
-def mix(weights, images, rows):
+            out_ref[0, j, lines] = mixed[j * ROWS : (j + 1) * ROWS].astype(jnp.bfloat16)
+
+
+def mix(weights, inverse, sent, images, rows):
     positions, templates, lengths = weights.shape
+    spread = (
+        weights[:, :, None, :, None].astype(jnp.float32)
+        * np.eye(ROWS, dtype=np.float32)[None, None, :, None, :]
+    ).reshape(positions, templates * ROWS, lengths * ROWS).astype(jnp.bfloat16)
     return pl.pallas_call(
         mix_kernel,
         grid=(positions,),
         out_shape=jax.ShapeDtypeStruct((positions, templates, rows, PIX), jnp.bfloat16),
         in_specs=[
             pl.BlockSpec(memory_space=pltpu.SMEM),
-            pl.BlockSpec((lengths, rows, PIX), lambda f: (0, f, 0)),
+            pl.BlockSpec((1,) + spread.shape[1:], lambda f: (f, 0, 0)),
+            pl.BlockSpec((sent.shape[0], rows, PIX), lambda f: (0, f, 0)),
+            pl.BlockSpec((images.shape[0], rows, PIX), lambda f: (0, f, 0)),
         ],
         out_specs=pl.BlockSpec((1, templates, rows, PIX), lambda f: (f, 0, 0, 0)),
-    )(weights.reshape(positions, templates * lengths), images)
+    )(inverse, spread, sent, images)
 
 
 def table_kernel(scale_ref, y_ref, v_ref, u_ref, x_ref, row_ref, column_ref):
@@ -370,12 +425,12 @@
             ).astype(jnp.bfloat16)
 
 
-def tables(wave_lengths, rows):
+def tables(wave_lengths, first_row, rows):
     lengths = wave_lengths.shape[0]
     scale = (SAMPLING / (2.0 * PUP)) / wave_lengths
     y = 2 * np.concatenate([band_columns(band) for band in range(BANDS)]) - PUP + 1
     v = np.arange(PIX) - PIX // 2
-    u = lax.axis_index("wave") * rows + jnp.arange(rows, dtype=jnp.int32) - PIX // 2
+    u = first_row + jnp.arange(rows, dtype=jnp.int32) - PIX // 2
     x = np.array(
         [[row + i for row in band_rows(band) for i in range(ROWS)] for band in range(BANDS)]
     )
@@ -412,31 +467,32 @@
     )
 
 
-def every_length(wave_lengths, waves):
-    mine = lax.axis_index("wave")
-    count = wave_lengths.shape[0]
-    out = jnp.zeros((waves * count,), wave_lengths.dtype)
-    for s in range(waves):
-        part = wave_lengths
-        if s > 0:
-            part = lax.ppermute(part, "wave", [(i, (i + s) % waves) for i in range(waves)])
-        out = lax.dynamic_update_slice(out, part, (((mine - s) % waves) * count,))
-    return out
+def shifts(x, waves):
+    return [x] + [
+        lax.ppermute(x, "wave", [(i, (i + s) % waves) for i in range(waves)])
+        for s in range(1, waves)
+    ]
 
 
 def local(mode_basis, coef_table, table_index, wave_lengths, sed_table, template_ids):
     waves = lax.axis_size("wave")
+    mine = lax.axis_index("wave")
     modes = mode_basis.shape[0]
     positions = table_index.shape[0]
     rows = PIX // waves
     count, half, slabs, pack, place = layout(waves, modes)
-
-    every = every_length(wave_lengths, waves)
-    table = jnp.asarray(pack)[lax.axis_index("wave")]
+    sent_lengths = wave_lengths.shape[0] // 2
+    kept = wave_lengths.shape[0] - sent_lengths
+
+    table = jnp.asarray(pack)[mine]
     own = pack_rows(mode_basis, table, slabs)
     got = gather_rows(own, half, waves)
 
-    row_table, column_table = tables(every, rows)
+    own_tables = tables(wave_lengths[:sent_lengths], 0, PIX)
+    every = jnp.zeros((waves * kept,), wave_lengths.dtype)
+    for s, part in enumerate(shifts(wave_lengths[sent_lengths:], waves)):
+        every = lax.dynamic_update_slice(every, part, (((mine - s) % waves) * kept,))
+    all_tables = tables(every, mine * rows, rows)
 
     selector = (
         table_index[:, None] == jnp.arange(coef_table.shape[0], dtype=jnp.int32)[None, :]
@@ -447,29 +503,33 @@
         .reshape(positions * ROWS, modes * ROWS)
         .astype(jnp.bfloat16)
     )
-
-    images, sums = fields(
-        own,
-        got,
-        spread,
-        place,
-        1.0 / every,
-        row_table,
-        column_table,
-        positions,
-        rows,
-        (modes, waves, half, slabs),
-    )
-    level = lax.psum(jnp.sum(sums, axis=2), "wave") / (PIX * PIX)
-
     one_hot = (
         template_ids[:, :, None]
         == jnp.arange(sed_table.shape[0], dtype=jnp.int32)[None, None, :]
     ).astype(jnp.float32)
     raw_weights = jnp.einsum("fjn,nl->fjl", one_hot, sed_table, precision=lax.Precision.HIGHEST)
     weights = (raw_weights / jnp.sum(raw_weights, axis=2, keepdims=True)).astype(jnp.bfloat16)
-    weights = weights.astype(jnp.float32) / (level.T[:, None, :] + EPSILON)
-    return mix(weights, images, rows)
+    order = weights.reshape(weights.shape[:2] + (waves, sent_lengths + kept))
+    weights = jnp.concatenate(
+        [
+            order[..., :sent_lengths].reshape(weights.shape[:2] + (-1,)),
+            order[..., sent_lengths:].reshape(weights.shape[:2] + (-1,)),
+        ],
+        axis=2,
+    )
+
+    path, opening = paths(
+        own, got, spread, place, own_tables + all_tables, positions, (modes, waves, half, slabs)
+    )
+    spectra = fields(
+        path, opening, 1.0 / wave_lengths[:sent_lengths], *own_tables, positions, waves
+    )
+    sent = lax.all_to_all(spectra, "wave", split_axis=0, concat_axis=0, tiled=True)
+    sent = sent.reshape(waves * sent_lengths, positions * rows, PIX)
+
+    images, sums = fields(path, opening, 1.0 / every, *all_tables, positions, 1)
+    level = sum(shifts(jnp.sum(sums, axis=2), waves)) / (PIX * PIX)
+    return mix(weights, 1.0 / (level + EPSILON), sent, images, rows)
 
 
 def solution(mesh):

time: 180 us -> 195 us (1.083)
  local copies, waits for them, and re-layouts: 12.9 us -> 35.9 us
  Pallas kernels: 93 us -> 77.8 us
  blocking collectives: 12.1 us -> 0 us
  waiting for transfers between devices: 29.9 us -> 37 us
  starting transfers between devices: 26.9 us -> 31.5 us
  other arithmetic: 3.71 us -> 7.03 us
    pallas_call x1 -> x3, Pallas kernels: 77.8 us -> 64.3 us  [the longest x2 51.4 us: fields(): pl.pallas_call(functools.partial(field_kernel, (positions, rows, parts)),...]
    unnamed x38 -> x70, local copies, waits for them, and re-layouts: 7.72 us -> 20.3 us
    psum x1 -> x0, blocking collectives: 12.1 us -> none  [local(): level = lax.psum(jnp.sum(sums, axis=2), 'wave') / (PIX * PIX)]
    mul x0 -> x4, local copies, waits for them, and re-layouts: none -> 8.52 us  [mix(): weights[:, :, None, :, None].astype(jnp.float32)]
    all_to_all x0 -> x1, starting transfers between devices: none -> 4.5 us  [local(): lax.all_to_all(spectra, 'wave', split_axis=0, concat_axis=0, tiled=True)]
    ppermute x6, waiting for transfers between devices: 11.8 us -> 15.4 us  [gather_rows(): lax.ppermute(piece, 'wave', [(i, (i + s) % waves) for i in range(waves)])]
    ppermute x3 -> x6, starting transfers between devices: 5.96 us -> 8.49 us  [shifts(): lax.ppermute(x, 'wave', [(i, (i + s) % waves) for i in range(waves)])]
    ppermute x14, waiting for transfers between devices: 10.2 us -> 12.3 us  [swap(): return lax.ppermute(x, ('groups', 'field'), pairs)]
  transfers between devices with their start and end apart: 23 -> 27, of which waited for: 10 -> 10; matrix products, arithmetic and copies ran while one was open for 4% -> 13% of each run, Pallas kernels for 4% -> 22%
where the time goes in v3:
time: 195 us; the launch traced here: 194 us
  Pallas kernels  77.8 us (40%)
  waiting for transfers between devices  37 us (19%)
  local copies, waits for them, and re-layouts  35.9 us (18%)
  starting transfers between devices  31.5 us (16%)
  other arithmetic  7.03 us (4%)
  matrix products  2.69 us (1%)
    pallas_call x2, Pallas kernels, fields(): pl.pallas_call(functools.partial(field_kernel, (positions, rows, parts)),...  51.4 us
    unnamed x70, local copies, waits for them, and re-layouts  20.3 us
    ppermute x6, waiting for transfers between devices, gather_rows(): lax.ppermute(piece, 'wave', [(i, (i + s) % waves) for i in range(waves)])  15.4 us
    pallas_call x1, Pallas kernels, paths(): pl.pallas_call(functools.partial(path_kernel, (positions, modes, waves, h...  12.8 us
    ppermute x14, waiting for transfers between devices, swap(): return lax.ppermute(x, ('groups', 'field'), pairs)  12.3 us
    ppermute x6, starting transfers between devices, gather_rows(): lax.ppermute(piece, 'wave', [(i, (i + s) % waves) for i in range(waves)])  10.1 us
    ppermute x6, waiting for transfers between devices, shifts(): lax.ppermute(x, 'wave', [(i, (i + s) % waves) for i in range(waves)])  9.33 us
    mul x4, local copies, waits for them, and re-layouts, mix(): weights[:, :, None, :, None].astype(jnp.float32)  8.52 us
  transfers between devices with their start and end apart: 27, of which 10 were waited for; matrix products, arithmetic and copies ran while one was open for 13% of the time, Pallas kernels for 22%

profile of v3, /device:TPU:0, one launch (start us, length us, event | category | flops | bytes accessed | tf_op | source)
XLA Modules:
  0.0 193.6 jit_solution(2855700617442429695)
XLA Ops:
  0.0 0.7 dynamic-slice_bitcast_fusion
  0.8 1.8 copy-done.3
  2.6 1.6 shard_map.154.refs_0_
  4.4 5.1 %collective-permute-start.5 = (bf16[35,16,128]{2,1,0:T(8,128)(2,1)S(1)}, bf16[35,16,128]{2,1,0:T(8,128)(2,1)S(1)}, u32[]{:S(2)}, u32[]{:S(2)}) collective-permute-start(bf16[35,16,128]{2,1,0:T(8,128)(2,1)S(1)} %get-tuple-element.22), channel_id=1, source_target_pairs={{0,3},{1,0},{2,1},{3,2},{4,7},{5,4},{6,5},{7,6},{8,11},{9,8},{10,9... | collective-permute-start | bytes 430088 | tf_op jit(solution)/shard_map/ppermute | solution.py:146
  9.5 1.0 collective-permute-start.3
  10.5 2.8 %collective-permute-start.8 = (bf16[35,16,128]{2,1,0:T(8,128)(2,1)S(1)}, bf16[35,16,128]{2,1,0:T(8,128)(2,1)S(1)}, u32[]{:S(2)}, u32[]{:S(2)}) collective-permute-start(bf16[35,16,128]{2,1,0:T(8,128)(2,1)S(1)} %get-tuple-element.21), channel_id=1, source_target_pairs={{0,3},{1,0},{2,1},{3,2},{4,7},{5,4},{6,5},{7,6},{8,11},{9,8},{10,9... | collective-permute-start | bytes 430088 | tf_op jit(solution)/shard_map/ppermute | solution.py:146
  13.3 1.1 collective-permute-start.7
  14.5 0.6 fusion.9
  15.1 8.2 %collective-permute-done.4 = bf16[35,16,128]{2,1,0:T(8,128)(2,1)S(1)} collective-permute-done((bf16[35,16,128]{2,1,0:T(8,128)(2,1)S(1)}, bf16[35,16,128]{2,1,0:T(8,128)(2,1)S(1)}, u32[]{:S(2)}, u32[]{:S(2)}) %collective-permute-start.4) | collective-permute-done | bytes 143392 | tf_op jit(solution)/shard_map/ppermute | solution.py:146
  23.3 0.6 copy-done.26
  24.0 1.1 pad_maximum_fusion.refs_1_
  25.2 1.6 collective-permute-start.11
  26.8 7.2 %collective-permute-done.7 = bf16[35,16,128]{2,1,0:T(8,128)(2,1)S(1)} collective-permute-done((bf16[35,16,128]{2,1,0:T(8,128)(2,1)S(1)}, bf16[35,16,128]{2,1,0:T(8,128)(2,1)S(1)}, u32[]{:S(2)}, u32[]{:S(2)}) %collective-permute-start.7) | collective-permute-done | bytes 143392 | tf_op jit(solution)/shard_map/ppermute | solution.py:146
  34.0 0.7 copy-done.24
  34.6 1.0 pad_maximum_fusion.1.refs_2_
  35.7 1.6 collective-permute-start.16
  37.3 0.9 fusion.5
  38.1 1.8 multiply_convert_fusion
  39.9 2.3 %convert_element_type.42 = bf16[128,352]{0,1:T(8,128)(2,1)} reshape(bf16[8,16,22,16]{1,0,3,2:T(8,128)(2,1)} %multiply_convert_fusion) | data formatting | bytes 180224 | tf_op jit(solution)/shard_map/convert_element_type | solution.py:504
  42.2 1.0 copy.39.refs_17_
  44.5 0.9 copy-done.13
  45.4 1.5 shard_map.155
  46.9 1.0 copy-done.5
  47.9 1.0 copy-done.8
  48.9 2.1 %collective-permute-start.1 = (f32[1]{0:T(128)}, f32[1]{0:T(128)}, u32[]{:S(2)}, u32[]{:S(2)}) collective-permute-start(f32[1]{0:T(128)} %get-tuple-element.29), channel_id=1, source_target_pairs={{0,2},{1,3},{2,0},{3,1},{4,6},{5,7},{6,4},{7,5},{8,10},{9,11},{10,... | collective-permute-start | bytes 20 | tf_op jit(solution)/shard_map/ppermute | solution.py:472
  51.0 2.7 %collective-permute-done.1 = f32[1]{0:T(128)} collective-permute-done((f32[1]{0:T(128)}, f32[1]{0:T(128)}, u32[]{:S(2)}, u32[]{:S(2)}) %collective-permute-start.1) | collective-permute-done | bytes 36 | tf_op jit(solution)/shard_map/ppermute | solution.py:472
  53.6 1.4 collective-permute-start.2
  55.1 2.4 %collective-permute-done.2 = f32[1]{0:T(128)} collective-permute-done((f32[1]{0:T(128)}, f32[1]{0:T(128)}, u32[]{:S(2)}, u32[]{:S(2)}) %collective-permute-start.2) | collective-permute-done | bytes 36 | tf_op jit(solution)/shard_map/ppermute | solution.py:472
  57.5 1.5 collective-permute-start.12
  59.5 1.6 collective-permute-start.19
  61.7 1.8 fusion.3
  63.5 5.6 %collective-permute-done.12.refs_6_ = bf16[3,35,16,128]{3,2,1,0:T(8,128)(2,1)} collective-permute-done((bf16[3,35,16,128]{3,2,1,0:T(8,128)(2,1)S(1)}, bf16[3,35,16,128]{3,2,1,0:T(8,128)(2,1)}, u32[]{:S(2)}, u32[]{:S(2)}) %collective-permute-start.12) | collective-permute-done | bytes 430112 | tf_op jit(solution)/shard_map/ppermute | solution.py:140
  69.1 2.8 %collective-permute-done.15.refs_9_ = bf16[3,35,16,128]{3,2,1,0:T(8,128)(2,1)} collective-permute-done((bf16[3,35,16,128]{3,2,1,0:T(8,128)(2,1)S(1)}, bf16[3,35,16,128]{3,2,1,0:T(8,128)(2,1)}, u32[]{:S(2)}, u32[]{:S(2)}) %collective-permute-start.15) | collective-permute-done | bytes 430112 | tf_op jit(solution)/shard_map/ppermute | solution.py:140
  71.9 0.8 copy-done.15
  73.2 3.9 %collective-permute-done.19.refs_13_ = bf16[3,35,16,128]{3,2,1,0:T(8,128)(2,1)} collective-permute-done((bf16[3,35,16,128]{3,2,1,0:T(8,128)(2,1)}, bf16[3,35,16,128]{3,2,1,0:T(8,128)(2,1)}, u32[]{:S(2)}, u32[]{:S(2)}) %collective-permute-start.19) | collective-permute-done | bytes 430112 | tf_op jit(solution)/shard_map/ppermute | solution.py:140
  77.6 0.6 fusion.2
  78.2 0.7 dynamic_update_slice.13
  79.0 0.7 dynamic_update_slice.14
  79.7 0.8 dynamic_update_slice.15
  80.5 0.9 copy-done.14
  81.5 3.6 %shard_map.156 = (bf16[4,4,128,256]{3,2,1,0:T(8,128)(2,1)S(1)}, bf16[4,1024,512]{2,1,0:T(8,128)(2,1)S(1)}) custom-call(f32[4]{0:T(128)S(1)} %get-tuple-element.25.scale_ref, f32[512,1]{1,0:T(8,128)S(1)} %copy-done.14, f32[1,256]{1,0:T(1,128)S(1)} %copy-done.19, f32[64,1]{1,0:T(8,128)S(1)} %add_convert_fusion.1.u_ref, f32[4,1,256]{2,1,0:T(1,128)S(1)} %copy-done.18), custom_call_target="tpu_custom_call" | custom-call | flops 15728640 | bytes 4194304 | tf_op jit(solution)/shard_map/pallas_call | solution.py:439
  85.2 2.0 %copy-done.6 = bf16[1,4,512,256]{3,2,1,0:T(8,128)(2,1)S(1)} copy-done((bf16[1,4,512,256]{3,2,1,0:T(8,128)(2,1)S(1)}, bf16[1,4,512,256]{3,2,1,0:T(8,128)(2,1)}, u32[]{:S(2)}) %copy-start.6) | copy-done | bytes 1048600
  87.2 1.2 copy-done.9
  88.4 1.0 copy-done.16
  89.5 12.8 %shard_map.157 = (f32[96,128,128]{2,1,0:T(8,128)}, f32[96,16,128]{2,1,0:T(8,128)S(1)}) custom-call(s32[96,4]{1,0:T(8,128)S(1)} %copy-done.17, s32[2]{0:T(128)S(1)} %pad_add_fusion.where_ref, bf16[560,16,128]{2,1,0:T(8,128)(2,1)S(1)} %shard_map.154.refs_0_, bf16[3,35,16,128]{3,2,1,0:T(8,128)(2,1)S(1)} %pad_maximum_fusion.refs_1_, ...), custom_call_target="tpu_custom_call" | custom-call | tf_op jit(solution)/shard_map/pallas_call | solution.py:226
  102.3 2.8 %copy-done.20 = f32[96,128,128]{2,1,0:T(8,128)S(1)} copy-done((f32[96,128,128]{2,1,0:T(8,128)S(1)}, f32[96,128,128]{2,1,0:T(8,128)}, u32[]{:S(2)}) %copy-start.20) | copy-done | bytes 6291480
  105.1 14.1 %shard_map.159 = bf16[4,1,512,256]{3,2,1,0:T(8,128)(2,1)} custom-call(f32[1]{0:T(128)S(6)} %div.41.inverse_ref, f32[96,128,128]{2,1,0:T(8,128)S(1)} %copy-done.20, f32[96,16,128]{2,1,0:T(8,128)S(1)} %get-tuple-element.18.opening, bf16[1,4,512,256]{3,2,1,0:T(8,128)(2,1)S(1)} %copy-done.7, bf16[1,1024,512]{2,1,0:T(8,128)(2,1)S(1)} %copy-done.10), custom_call_target="tpu_custom_call" | custom-call | flops 7242450944 | bytes 8388608 | tf_op jit(solution)/shard_map/pallas_call | solution.py:340
  119.2 0.9 copy-done.21
  120.1 4.5 %all-to-all-start = ((bf16[4,1,512,256]{3,2,1,0:T(8,128)(2,1)}), bf16[4,1,512,256]{3,2,1,0:T(8,128)(2,1)S(1)}, u32[]{:S(2)}, u32[]{:S(2)}) async-start(bf16[4,1,512,256]{3,2,1,0:T(8,128)(2,1)} %shard_map.159), calls=%async_computation | async-start | bytes 2097152 | tf_op jit(solution)/shard_map/all_to_all | solution.py:527
  124.8 2.4 %mul.65 = f32[8,8,16,8,16]{4,3,2,1,0:T(8,128)} broadcast(f32[8,8,8]{2,1,0:T(8,128)S(1)} %copy.42), dimensions={0,1,3} | broadcast | bytes 526336 | tf_op jit(solution)/shard_map/mul | solution.py:386
  127.2 4.1 %mul.66 = f32[8,128,128]{2,1,0:T(8,128)} reshape(f32[8,8,16,8,16]{4,3,2,1,0:T(8,128)} %mul.65) | data formatting | bytes 1048576 | tf_op jit(solution)/shard_map/mul | solution.py:386
  131.3 0.8 mul.68
  132.1 1.2 mul.69
  133.3 1.8 multiply_convert_fusion.1.weight_ref
  135.1 2.2 %copy-done.2 = bf16[4,1024,512]{2,1,0:T(8,128)(2,1)S(1)} copy-done((bf16[4,1024,512]{2,1,0:T(8,128)(2,1)S(1)}, bf16[4,1024,512]{2,1,0:T(8,128)(2,1)}, u32[]{:S(2)}) %copy-start.2) | copy-done | bytes 4194328
  137.3 37.3 %shard_map.158 = (f32[4,512,256]{2,1,0:T(8,128)S(1)}, f32[4,8,256]{2,1,0:T(8,128)S(1)}) custom-call(f32[4]{0:T(128)S(1)} %get-tuple-element.26.inverse_ref, f32[96,128,128]{2,1,0:T(8,128)} %get-tuple-element.17.path, f32[96,16,128]{2,1,0:T(8,128)S(1)} %copy-done.22, bf16[4,4,128,256]{3,2,1,0:T(8,128)(2,1)S(1)} %copy-done.12, bf16[4,1024,512]{2,1,0:T(8,128)(2,1)S(1)} %copy-done.2), custom_call_target="tpu_custom_call" | custom-call | flops 9642450944 | bytes 8388608 | tf_op jit(solution)/shard_map/pallas_call | solution.py:340
  174.6 1.3 copy-done.4
  176.1 3.8 %collective-permute-start.25 = (f32[4,8]{1,0:T(4,128)S(1)}, f32[4,8]{1,0:T(4,128)S(1)}, u32[]{:S(2)}, u32[]{:S(2)}) collective-permute-start(f32[4,8]{1,0:T(4,128)S(1)} %reduce_sum.18), channel_id=1, source_target_pairs={{0,3},{1,0},{2,1},{3,2},{4,7},{5,4},{6,5},{7,6},{8,11},{9,8},{10,9... | collective-permute-start | bytes 392 | tf_op jit(solution)/shard_map/ppermute | solution.py:472
  179.9 1.1 collective-permute-start.23
  181.2 3.2 %collective-permute-done.24 = f32[4,8]{1,0:T(4,128)S(1)} collective-permute-done((f32[4,8]{1,0:T(4,128)S(1)}, f32[4,8]{1,0:T(4,128)S(1)}, u32[]{:S(2)}, u32[]{:S(2)}) %collective-permute-start.24) | collective-permute-done | bytes 160 | tf_op jit(solution)/shard_map/ppermute | solution.py:472
  184.4 0.9 collective-permute-done.23
  185.3 0.6 add_divide_fusion.inverse_ref
  185.9 1.0 copy-done.23
  186.9 6.8 %shard_map.160 = bf16[8,8,64,256]{3,2,1,0:T(8,128)(2,1)} custom-call(f32[4,8]{1,0:T(4,128)} %add_divide_fusion.inverse_ref, bf16[8,128,128]{2,1,0:T(8,128)(2,1)} %multiply_convert_fusion.1.weight_ref, bf16[4,512,256]{2,1,0:T(8,128)(2,1)} %bitcast.31, f32[4,512,256]{2,1,0:T(8,128)} %copy-done.4), custom_call_target="tpu_custom_call" | custom-call | tf_op jit(solution)/shard_map/pallas_call | solution.py:389
  (97 shorter events, 3.1 us)
Async XLA Ops:
  0.0 37.3 %copy-start = (bf16[4096,22]{0,1:T(8,128)(2,1)S(1)}, bf16[4096,22]{0,1:T(8,128)(2,1)}, u32[]{:S(2)}) copy-start(bf16[4096,22]{0,1:T(8,128)(2,1)} %param.17) | copy-start | bytes 540676
  0.8 1.8 copy-start.3
  2.6 11.8 %copy-start.30 = (f32[2]{0:T(128)S(1)}, f32[2]{0:T(128)}, u32[]{:S(2)}) copy-start(f32[2]{0:T(128)} %param.19) | copy-start | bytes 28
  4.3 40.2 %copy-start.18 = (f32[4,1,256]{2,1,0:T(1,128)S(1)}, f32[4,1,256]{2,1,0:T(1,128)}, u32[]{:S(2)}) copy-start(f32[4,1,256]{2,1,0:T(1,128)} %constant.112.clone.x_ref) | copy-start | bytes 12292
  4.3 40.1 %copy-start.19 = (f32[1,256]{1,0:T(1,128)S(1)}, f32[1,256]{1,0:T(1,128)}, u32[]{:S(2)}) copy-start(f32[1,256]{1,0:T(1,128)} %constant.111.clone.v_ref) | copy-start | bytes 3076
  4.4 57.3 %copy-start.31 = (s32[8,8]{1,0:T(8,128)S(1)}, s32[8,8]{1,0:T(8,128)}, u32[]{:S(2)}) copy-start(s32[8,8]{1,0:T(8,128)} %param.21) | copy-start | bytes 772
  4.4 10.1 %collective-permute-start.5 = (bf16[35,16,128]{2,1,0:T(8,128)(2,1)S(1)}, bf16[35,16,128]{2,1,0:T(8,128)(2,1)S(1)}, u32[]{:S(2)}, u32[]{:S(2)}) collective-permute-start(bf16[35,16,128]{2,1,0:T(8,128)(2,1)S(1)} %get-tuple-element.22), channel_id=1, source_target_pairs={{0,3},{1,0},{2,1},{3,2},{4,7},{5,4},{6,5},{7,6},{8,11},{9,8},{10,9... | collective-permute-start | bytes 430088 | tf_op jit(solution)/shard_map/ppermute | solution.py:146
  9.5 13.8 %collective-permute-start.4 = (bf16[35,16,128]{2,1,0:T(8,128)(2,1)S(1)}, bf16[35,16,128]{2,1,0:T(8,128)(2,1)S(1)}, u32[]{:S(2)}, u32[]{:S(2)}) collective-permute-start(bf16[35,16,128]{2,1,0:T(8,128)(2,1)S(1)} %get-tuple-element.22), channel_id=1, source_target_pairs={{0,2},{1,3},{2,0},{3,1},{4,6},{5,7},{6,4},{7,5},{8,10},{9,11},{10,... | collective-permute-start | bytes 430088 | tf_op jit(solution)/shard_map/ppermute | solution.py:146
  9.5 13.8 %collective-permute-start.3 = (bf16[35,16,128]{2,1,0:T(8,128)(2,1)S(1)}, bf16[35,16,128]{2,1,0:T(8,128)(2,1)S(1)}, u32[]{:S(2)}, u32[]{:S(2)}) collective-permute-start(bf16[35,16,128]{2,1,0:T(8,128)(2,1)S(1)} %get-tuple-element.22), channel_id=1, source_target_pairs={{0,1},{1,2},{2,3},{3,0},{4,5},{5,6},{6,7},{7,4},{8,9},{9,10},{10,1... | collective-permute-start | bytes 430088 | tf_op jit(solution)/shard_map/ppermute | solution.py:146
  10.5 14.7 %collective-permute-start.8 = (bf16[35,16,128]{2,1,0:T(8,128)(2,1)S(1)}, bf16[35,16,128]{2,1,0:T(8,128)(2,1)S(1)}, u32[]{:S(2)}, u32[]{:S(2)}) collective-permute-start(bf16[35,16,128]{2,1,0:T(8,128)(2,1)S(1)} %get-tuple-element.21), channel_id=1, source_target_pairs={{0,3},{1,0},{2,1},{3,2},{4,7},{5,4},{6,5},{7,6},{8,11},{9,8},{10,9... | collective-permute-start | bytes 430088 | tf_op jit(solution)/shard_map/ppermute | solution.py:146
  13.3 20.6 %collective-permute-start.7 = (bf16[35,16,128]{2,1,0:T(8,128)(2,1)S(1)}, bf16[35,16,128]{2,1,0:T(8,128)(2,1)S(1)}, u32[]{:S(2)}, u32[]{:S(2)}) collective-permute-start(bf16[35,16,128]{2,1,0:T(8,128)(2,1)S(1)} %get-tuple-element.21), channel_id=1, source_target_pairs={{0,2},{1,3},{2,0},{3,1},{4,6},{5,7},{6,4},{7,5},{8,10},{9,11},{10,... | collective-permute-start | bytes 430088 | tf_op jit(solution)/shard_map/ppermute | solution.py:146
  14.4 8.9 %copy-start.25 = (bf16[35,16,128]{2,1,0:T(8,128)(2,1)}, bf16[35,16,128]{2,1,0:T(8,128)(2,1)S(1)}, u32[]{:S(2)}) copy-start(bf16[35,16,128]{2,1,0:T(8,128)(2,1)S(1)} %collective-permute-done.5) | copy-start | bytes 430084
  14.4 19.5 %collective-permute-start.6 = (bf16[35,16,128]{2,1,0:T(8,128)(2,1)S(1)}, bf16[35,16,128]{2,1,0:T(8,128)(2,1)S(1)}, u32[]{:S(2)}, u32[]{:S(2)}) collective-permute-start(bf16[35,16,128]{2,1,0:T(8,128)(2,1)S(1)} %get-tuple-element.21), channel_id=1, source_target_pairs={{0,1},{1,2},{2,3},{3,0},{4,5},{5,6},{6,7},{7,4},{8,9},{9,10},{10,1... | collective-permute-start | bytes 430088 | tf_op jit(solution)/shard_map/ppermute | solution.py:146
  15.1 8.2 %copy-start.32 = (f32[4]{0:T(128)}, f32[4]{0:T(128)S(1)}, u32[]{:S(2)}) copy-start(f32[4]{0:T(128)S(1)} %get-tuple-element.28) | copy-start | bytes 52
  23.3 0.7 copy-start.26
  23.3 25.6 %collective-permute-start = (f32[1]{0:T(128)}, f32[1]{0:T(128)}, u32[]{:S(2)}, u32[]{:S(2)}) collective-permute-start(f32[1]{0:T(128)} %get-tuple-element.29), channel_id=1, source_target_pairs={{0,1},{1,2},{2,3},{3,0},{4,5},{5,6},{6,7},{7,4},{8,9},{9,10},{10,1... | collective-permute-start | bytes 20 | tf_op jit(solution)/shard_map/ppermute | solution.py:472
  23.3 0.7 copy-start.27
  24.0 61.2 %copy-start.17 = (s32[96,4]{1,0:T(8,128)S(1)}, s32[96,4]{1,0:T(8,128)}, u32[]{:S(2)}) copy-start(s32[96,4]{1,0:T(8,128)} %constant.114.clone.place_ref) | copy-start | bytes 4612
  25.1 33.8 %collective-permute-start.9 = (bf16[3,35,16,128]{3,2,1,0:T(8,128)(2,1)S(1)}, bf16[3,35,16,128]{3,2,1,0:T(8,128)(2,1)}, u32[]{:S(2)}, u32[]{:S(2)}) collective-permute-start(bf16[3,35,16,128]{3,2,1,0:T(8,128)(2,1)S(1)} %pad_maximum_fusion.refs_1_), channel_id=1, source_target_pairs={{0,4},{4,0},{8,12},{12,8},{16,20},{20,16},{24,28},{28,24},{1,5},{5... | collective-permute-start | bytes 1290248 | tf_op jit(solution)/shard_map/ppermute | solution.py:140
  25.2 34.3 %collective-permute-start.11 = (bf16[3,35,16,128]{3,2,1,0:T(8,128)(2,1)S(1)}, bf16[3,35,16,128]{3,2,1,0:T(8,128)(2,1)}, u32[]{:S(2)}, u32[]{:S(2)}) collective-permute-start(bf16[3,35,16,128]{3,2,1,0:T(8,128)(2,1)S(1)} %pad_maximum_fusion.refs_1_), channel_id=1, source_target_pairs={{0,8},{4,12},{8,0},{12,4},{16,24},{20,28},{24,16},{28,20},{1,9},{5... | collective-permute-start | bytes 1290248 | tf_op jit(solution)/shard_map/ppermute | solution.py:140
  34.0 0.7 copy-start.24
  35.6 42.6 %copy-start.33 = (f32[4]{0:T(128)S(1)}, f32[4]{0:T(128)}, u32[]{:S(2)}) copy-start(f32[4]{0:T(128)} %copy-done.32) | copy-start | bytes 52
  35.6 23.9 %collective-permute-start.10 = (bf16[3,35,16,128]{3,2,1,0:T(8,128)(2,1)S(1)}, bf16[3,35,16,128]{3,2,1,0:T(8,128)(2,1)}, u32[]{:S(2)}, u32[]{:S(2)}) collective-permute-start(bf16[3,35,16,128]{3,2,1,0:T(8,128)(2,1)S(1)} %pad_maximum_fusion.1.refs_2_), channel_id=1, source_target_pairs={{0,4},{4,0},{8,12},{12,8},{16,20},{20,16},{24,28},{28,24},{1,5},{5... | collective-permute-start | bytes 1290248 | tf_op jit(solution)/shard_map/ppermute | solution.py:140
  35.7 25.4 %collective-permute-start.16 = (bf16[3,35,16,128]{3,2,1,0:T(8,128)(2,1)S(1)}, bf16[3,35,16,128]{3,2,1,0:T(8,128)(2,1)}, u32[]{:S(2)}, u32[]{:S(2)}) collective-permute-start(bf16[3,35,16,128]{3,2,1,0:T(8,128)(2,1)S(1)} %pad_maximum_fusion.1.refs_2_), channel_id=1, source_target_pairs={{0,16},{4,20},{8,24},{12,28},{16,0},{20,4},{24,8},{28,12},{1,17},{... | collective-permute-start | bytes 1290248 | tf_op jit(solution)/shard_map/ppermute | solution.py:140
  44.5 1.0 copy-start.13
  46.9 1.0 copy-start.5
  47.9 1.0 copy-start.8
  48.9 4.8 %collective-permute-start.1 = (f32[1]{0:T(128)}, f32[1]{0:T(128)}, u32[]{:S(2)}, u32[]{:S(2)}) collective-permute-start(f32[1]{0:T(128)} %get-tuple-element.29), channel_id=1, source_target_pairs={{0,2},{1,3},{2,0},{3,1},{4,6},{5,7},{6,4},{7,5},{8,10},{9,11},{10,... | collective-permute-start | bytes 20 | tf_op jit(solution)/shard_map/ppermute | solution.py:472
  53.6 3.9 %collective-permute-start.2 = (f32[1]{0:T(128)}, f32[1]{0:T(128)}, u32[]{:S(2)}, u32[]{:S(2)}) collective-permute-start(f32[1]{0:T(128)} %get-tuple-element.29), channel_id=1, source_target_pairs={{0,3},{1,0},{2,1},{3,2},{4,7},{5,4},{6,5},{7,6},{8,11},{9,8},{10,9... | collective-permute-start | bytes 20 | tf_op jit(solution)/shard_map/ppermute | solution.py:472
  57.5 11.6 %collective-permute-start.12 = (bf16[3,35,16,128]{3,2,1,0:T(8,128)(2,1)S(1)}, bf16[3,35,16,128]{3,2,1,0:T(8,128)(2,1)}, u32[]{:S(2)}, u32[]{:S(2)}) collective-permute-start(bf16[3,35,16,128]{3,2,1,0:T(8,128)(2,1)S(1)} %pad_maximum_fusion.1.refs_2_), channel_id=1, source_target_pairs={{0,8},{4,12},{8,0},{12,4},{16,24},{20,28},{24,16},{28,20},{1,9},{5... | collective-permute-start | bytes 1290248 | tf_op jit(solution)/shard_map/ppermute | solution.py:140
  59.0 13.0 %collective-permute-start.15 = (bf16[3,35,16,128]{3,2,1,0:T(8,128)(2,1)S(1)}, bf16[3,35,16,128]{3,2,1,0:T(8,128)(2,1)}, u32[]{:S(2)}, u32[]{:S(2)}) collective-permute-start(bf16[3,35,16,128]{3,2,1,0:T(8,128)(2,1)S(1)} %pad_maximum_fusion.refs_1_), channel_id=1, source_target_pairs={{0,16},{4,20},{8,24},{12,28},{16,0},{20,4},{24,8},{28,12},{1,17},{... | collective-permute-start | bytes 1290248 | tf_op jit(solution)/shard_map/ppermute | solution.py:140
  59.5 12.4 %collective-permute-start.13 = (bf16[3,35,16,128]{3,2,1,0:T(8,128)(2,1)}, bf16[3,35,16,128]{3,2,1,0:T(8,128)(2,1)S(1)}, u32[]{:S(2)}, u32[]{:S(2)}) collective-permute-start(bf16[3,35,16,128]{3,2,1,0:T(8,128)(2,1)} %collective-permute-done.11.refs_5_), channel_id=1, source_target_pairs={{0,4},{4,0},{8,12},{12,8},{16,20},{20,16},{24,28},{28,24},{1,5},{5... | collective-permute-start | bytes 1290248 | tf_op jit(solution)/shard_map/ppermute | solution.py:140
  59.5 17.6 %collective-permute-start.19 = (bf16[3,35,16,128]{3,2,1,0:T(8,128)(2,1)}, bf16[3,35,16,128]{3,2,1,0:T(8,128)(2,1)}, u32[]{:S(2)}, u32[]{:S(2)}) collective-permute-start(bf16[3,35,16,128]{3,2,1,0:T(8,128)(2,1)} %collective-permute-done.11.refs_5_), channel_id=1, source_target_pairs={{0,16},{4,20},{8,24},{12,28},{16,0},{20,4},{24,8},{28,12},{1,17},{... | collective-permute-start | bytes 1290248 | tf_op jit(solution)/shard_map/ppermute | solution.py:140
  61.1 16.0 %collective-permute-start.20 = (bf16[3,35,16,128]{3,2,1,0:T(8,128)(2,1)}, bf16[3,35,16,128]{3,2,1,0:T(8,128)(2,1)}, u32[]{:S(2)}, u32[]{:S(2)}) collective-permute-start(bf16[3,35,16,128]{3,2,1,0:T(8,128)(2,1)} %collective-permute-done.16.refs_10_), channel_id=1, source_target_pairs={{0,8},{4,12},{8,0},{12,4},{16,24},{20,28},{24,16},{28,20},{1,9},{5... | collective-permute-start | bytes 1290248 | tf_op jit(solution)/shard_map/ppermute | solution.py:140
  69.1 16.1 %collective-permute-start.18 = (bf16[3,35,16,128]{3,2,1,0:T(8,128)(2,1)}, bf16[3,35,16,128]{3,2,1,0:T(8,128)(2,1)}, u32[]{:S(2)}, u32[]{:S(2)}) collective-permute-start(bf16[3,35,16,128]{3,2,1,0:T(8,128)(2,1)} %collective-permute-done.16.refs_10_), channel_id=1, source_target_pairs={{0,4},{4,0},{8,12},{12,8},{16,20},{20,16},{24,28},{28,24},{1,5},{5... | collective-permute-start | bytes 1290248 | tf_op jit(solution)/shard_map/ppermute | solution.py:140
  71.9 13.2 %collective-permute-start.14 = (bf16[3,35,16,128]{3,2,1,0:T(8,128)(2,1)}, bf16[3,35,16,128]{3,2,1,0:T(8,128)(2,1)}, u32[]{:S(2)}, u32[]{:S(2)}) collective-permute-start(bf16[3,35,16,128]{3,2,1,0:T(8,128)(2,1)} %collective-permute-done.12.refs_6_), channel_id=1, source_target_pairs={{0,4},{4,0},{8,12},{12,8},{16,20},{20,16},{24,28},{28,24},{1,5},{5... | collective-permute-start | bytes 1290248 | tf_op jit(solution)/shard_map/ppermute | solution.py:140
  71.9 0.8 copy-start.15
  72.7 12.5 %collective-permute-start.17 = (bf16[3,35,16,128]{3,2,1,0:T(8,128)(2,1)}, bf16[3,35,16,128]{3,2,1,0:T(8,128)(2,1)}, u32[]{:S(2)}, u32[]{:S(2)}) collective-permute-start(bf16[3,35,16,128]{3,2,1,0:T(8,128)(2,1)} %collective-permute-done.15.refs_9_), channel_id=1, source_target_pairs={{0,4},{4,0},{8,12},{12,8},{16,20},{20,16},{24,28},{28,24},{1,5},{5... | collective-permute-start | bytes 1290248 | tf_op jit(solution)/shard_map/ppermute | solution.py:140
  77.1 8.1 %collective-permute-start.21 = (bf16[3,35,16,128]{3,2,1,0:T(8,128)(2,1)}, bf16[3,35,16,128]{3,2,1,0:T(8,128)(2,1)}, u32[]{:S(2)}, u32[]{:S(2)}) collective-permute-start(bf16[3,35,16,128]{3,2,1,0:T(8,128)(2,1)} %collective-permute-done.19.refs_13_), channel_id=1, source_target_pairs={{0,4},{4,0},{8,12},{12,8},{16,20},{20,16},{24,28},{28,24},{1,5},{5... | collective-permute-start | bytes 1290248 | tf_op jit(solution)/shard_map/ppermute | solution.py:140
  77.1 8.1 %collective-permute-start.22 = (bf16[3,35,16,128]{3,2,1,0:T(8,128)(2,1)}, bf16[3,35,16,128]{3,2,1,0:T(8,128)(2,1)}, u32[]{:S(2)}, u32[]{:S(2)}) collective-permute-start(bf16[3,35,16,128]{3,2,1,0:T(8,128)(2,1)} %collective-permute-done.20.refs_14_), channel_id=1, source_target_pairs={{0,4},{4,0},{8,12},{12,8},{16,20},{20,16},{24,28},{28,24},{1,5},{5... | collective-permute-start | bytes 1290248 | tf_op jit(solution)/shard_map/ppermute | solution.py:140
  80.5 1.0 copy-start.14
  85.1 17.2 %copy-start.1 = (bf16[4,1024,512]{2,1,0:T(8,128)(2,1)}, bf16[4,1024,512]{2,1,0:T(8,128)(2,1)S(1)}, u32[]{:S(2)}) copy-start(bf16[4,1024,512]{2,1,0:T(8,128)(2,1)S(1)} %get-tuple-element.16.refs_21_.column_ref) | copy-start | bytes 12582916
  85.1 17.2 %copy-start.11 = (bf16[4,4,128,256]{3,2,1,0:T(8,128)(2,1)}, bf16[4,4,128,256]{3,2,1,0:T(8,128)(2,1)S(1)}, u32[]{:S(2)}) copy-start(bf16[4,4,128,256]{3,2,1,0:T(8,128)(2,1)S(1)} %get-tuple-element.15.refs_20_.row_ref) | copy-start | bytes 3145732
  85.2 2.0 %copy-start.6 = (bf16[1,4,512,256]{3,2,1,0:T(8,128)(2,1)S(1)}, bf16[1,4,512,256]{3,2,1,0:T(8,128)(2,1)}, u32[]{:S(2)}) copy-start(bf16[1,4,512,256]{3,2,1,0:T(8,128)(2,1)} %copy-done.5) | copy-start | bytes 3145732
  87.2 1.2 copy-start.9
  88.4 1.0 copy-start.16
  89.5 12.9 %copy-start.7 = (bf16[1,4,512,256]{3,2,1,0:T(8,128)(2,1)S(1)}, bf16[1,4,512,256]{3,2,1,0:T(8,128)(2,1)}, u32[]{:S(2)}) copy-start(bf16[1,4,512,256]{3,2,1,0:T(8,128)(2,1)} %copy-done.5) | copy-start | bytes 3145732
  89.5 12.9 %copy-start.10 = (bf16[1,1024,512]{2,1,0:T(8,128)(2,1)S(1)}, bf16[1,1024,512]{2,1,0:T(8,128)(2,1)}, u32[]{:S(2)}) copy-start(bf16[1,1024,512]{2,1,0:T(8,128)(2,1)} %copy-done.8) | copy-start | bytes 3145732
  102.3 2.8 %copy-start.20 = (f32[96,128,128]{2,1,0:T(8,128)S(1)}, f32[96,128,128]{2,1,0:T(8,128)}, u32[]{:S(2)}) copy-start(f32[96,128,128]{2,1,0:T(8,128)} %get-tuple-element.17.path) | copy-start | bytes 18874372
  105.1 19.5 %copy-start.28 = (bf16[8,8,8]{1,2,0:T(8,128)(2,1)S(1)}, bf16[8,8,8]{1,2,0:T(8,128)(2,1)}, u32[]{:S(2)}) copy-start(bf16[8,8,8]{1,2,0:T(8,128)(2,1)} %fusion.2) | copy-start | bytes 3076
  119.2 0.9 copy-start.21
  120.1 65.7 %all-to-all-start = ((bf16[4,1,512,256]{3,2,1,0:T(8,128)(2,1)}), bf16[4,1,512,256]{3,2,1,0:T(8,128)(2,1)S(1)}, u32[]{:S(2)}, u32[]{:S(2)}) async-start(bf16[4,1,512,256]{3,2,1,0:T(8,128)(2,1)} %shard_map.159), calls=%async_computation | async-start | bytes 2097152 | tf_op jit(solution)/shard_map/all_to_all | solution.py:527
  127.2 4.1 %copy-start.29 = (f32[16,16]{1,0:T(8,128)S(1)}, f32[16,16]{1,0:T(8,128)}, u32[]{:S(2)}) copy-start(f32[16,16]{1,0:T(8,128)} %constant.119) | copy-start | bytes 3076
  127.2 7.9 %copy-start.12 = (bf16[4,4,128,256]{3,2,1,0:T(8,128)(2,1)S(1)}, bf16[4,4,128,256]{3,2,1,0:T(8,128)(2,1)}, u32[]{:S(2)}) copy-start(bf16[4,4,128,256]{3,2,1,0:T(8,128)(2,1)} %copy-done.11) | copy-start | bytes 3145732
  127.2 7.9 %copy-start.22 = (f32[96,16,128]{2,1,0:T(8,128)S(1)}, f32[96,16,128]{2,1,0:T(8,128)}, u32[]{:S(2)}) copy-start(f32[96,16,128]{2,1,0:T(8,128)} %copy-done.21) | copy-start | bytes 2359300
  135.1 2.2 %copy-start.2 = (bf16[4,1024,512]{2,1,0:T(8,128)(2,1)S(1)}, bf16[4,1024,512]{2,1,0:T(8,128)(2,1)}, u32[]{:S(2)}) copy-start(bf16[4,1024,512]{2,1,0:T(8,128)(2,1)} %copy-done.1) | copy-start | bytes 12582916
  174.6 1.3 copy-start.4
  176.1 5.1 %collective-permute-start.25 = (f32[4,8]{1,0:T(4,128)S(1)}, f32[4,8]{1,0:T(4,128)S(1)}, u32[]{:S(2)}, u32[]{:S(2)}) collective-permute-start(f32[4,8]{1,0:T(4,128)S(1)} %reduce_sum.18), channel_id=1, source_target_pairs={{0,3},{1,0},{2,1},{3,2},{4,7},{5,4},{6,5},{7,6},{8,11},{9,8},{10,9... | collective-permute-start | bytes 392 | tf_op jit(solution)/shard_map/ppermute | solution.py:472
  179.9 4.5 %collective-permute-start.24 = (f32[4,8]{1,0:T(4,128)S(1)}, f32[4,8]{1,0:T(4,128)S(1)}, u32[]{:S(2)}, u32[]{:S(2)}) collective-permute-start(f32[4,8]{1,0:T(4,128)S(1)} %reduce_sum.18), channel_id=1, source_target_pairs={{0,2},{1,3},{2,0},{3,1},{4,6},{5,7},{6,4},{7,5},{8,10},{9,11},{10,... | collective-permute-start | bytes 392 | tf_op jit(solution)/shard_map/ppermute | solution.py:472
  179.9 5.4 %collective-permute-start.23 = (f32[4,8]{1,0:T(4,128)S(1)}, f32[4,8]{1,0:T(4,128)S(1)}, u32[]{:S(2)}, u32[]{:S(2)}) collective-permute-start(f32[4,8]{1,0:T(4,128)S(1)} %reduce_sum.18), channel_id=1, source_target_pairs={{0,1},{1,2},{2,3},{3,0},{4,5},{5,6},{6,7},{7,4},{8,9},{9,10},{10,1... | collective-permute-start | bytes 392 | tf_op jit(solution)/shard_map/ppermute | solution.py:472
  185.9 1.0 copy-start.23

commit v4 on v2

v4 whole, which is shorter than its diff:
```python
import functools
import math

import jax
import jax.numpy as jnp
import numpy as np
from jax import lax
from jax.experimental import pallas as pl
from jax.experimental.pallas import tpu as pltpu
from jax.sharding import PartitionSpec as P

PUP = 512
PIX = 256
TWO_PI = 2.0 * math.pi
SAMPLING = 0.25
EPSILON = 1e-06
INNER = 61 * PUP // 100
BAND = 128
BANDS = PUP // BAND
ROWS = 16
LANES = 128
UNITS = BAND // ROWS
SHARES = 8

SIN_POLY = (4.4428679, -7.30744341, 3.59478797, -0.78437376)
COS_POLY = (1.4142135, -6.97885099, 5.73946117, -1.88356298, 0.31069817)


def half_turn(turns):
    magic = jnp.float32(12582912.0)
    r = turns - ((turns + magic) - magic)
    z = r * r
    s = jnp.float32(SIN_POLY[-1])
    for value in SIN_POLY[-2::-1]:
        s = s * z + value
    k = jnp.float32(COS_POLY[-1])
    for value in COS_POLY[-2::-1]:
        k = k * z + value
    return s * r, k


def band_rows(band):
    low, high = PUP // 2 - 64 * (band + 1), PUP // 2 + 64 * band
    return [low + ROWS * i for i in range(4)] + [high + ROWS * i for i in range(4)]


def band_columns(band):
    low, high = PUP // 2 - 64 * (band + 1), PUP // 2 + 64 * band
    sides = (high, low) if band % 2 == 0 else (low, high)
    return np.concatenate([side + np.arange(64) for side in sides])


def unit_open(row, band):
    a = 2 * (row + np.arange(ROWS)) - PUP + 1
    b = 2 * band_columns(band) - PUP + 1
    radius = a[:, None] ** 2 + b[None, :] ** 2
    return bool(np.any((radius <= PUP * PUP) & (radius >= INNER * INNER)))


CHUNKS = [
    (band, rows)
    for band in range(BANDS)
    for rows in range(BANDS)
    if any(unit_open(row, band) for row in band_rows(rows))
]


@functools.lru_cache(None)
def layout(waves, modes):
    per = PUP // waves
    lists = []
    for wave in range(waves):
        lists.append(
            [
                (band, row)
                for band in range(BANDS)
                for row in range(wave * per, (wave + 1) * per, ROWS)
                if unit_open(row, band)
            ]
        )
    count = max(len(one) for one in lists)
    half = -(-count * modes // (2 * SHARES))
    slabs = 2 * SHARES * half
    pack = np.zeros((waves, count, 3), np.int32)
    for wave, one in enumerate(lists):
        for i, (band, row) in enumerate(one):
            columns = band_columns(band)
            pack[wave, i] = (columns[0] // LANES * LANES, columns[64] // LANES * LANES, row - wave * per)
    place = np.zeros((len(CHUNKS) * UNITS, 4), np.int32)
    for c, (band, rows) in enumerate(CHUNKS):
        columns = band_columns(band)
        for j, row in enumerate(band_rows(rows)):
            wave = row // per
            slab = 0
            if (band, row) in lists[wave]:
                slab = wave * slabs + lists[wave].index((band, row)) * modes
            place[c * UNITS + j] = (slab, row, columns[0], columns[64] - 64)
    return count, half, slabs, pack, place


def pack_kernel(count, modes, half, where, table, lengths, basis, own, piece):
    left = lax.broadcasted_iota(jnp.int32, (ROWS, LANES), 1) < 64
    wave, share = where[0], where[1]

    def unit(i, carry):
        first = pl.multiple_of(table[wave * count + i, 0], LANES)
        second = pl.multiple_of(table[wave * count + i, 1], LANES)
        row = pl.multiple_of(table[wave * count + i, 2], ROWS)
        for k in range(modes):
            one = basis[k, pl.ds(row, ROWS), pl.ds(first, LANES)].astype(jnp.float32)
            two = basis[k, pl.ds(row, ROWS), pl.ds(second, LANES)].astype(jnp.float32)
            own[i * modes + k] = jnp.where(left, one, two).astype(own.dtype)
        return carry

    lax.fori_loop(0, count, unit, 0)
    for n in range(count * modes, own.shape[0]):
        own[n] = jnp.zeros((ROWS, LANES), own.dtype)
    piece[: 2 * half] = own[pl.ds(share * (2 * half), 2 * half)]
    line = lax.broadcasted_iota(jnp.int32, (ROWS, LANES), 0)
    slab = jnp.zeros((ROWS, LANES), jnp.float32)
    for i in range(lengths.shape[0]):
        rest = jnp.full((ROWS, LANES), lengths[i], jnp.float32)
        for limb in range(3):
            value = rest.astype(jnp.bfloat16).astype(jnp.float32)
            slab = jnp.where(line == 3 * i + limb, value, slab)
            rest = rest - value
    piece[2 * half] = slab.astype(piece.dtype)


def pack_rows(basis, wave_lengths, table, where, half, slabs):
    modes = basis.shape[0]
    waves, count, _ = table.shape
    smem = pl.BlockSpec(memory_space=pltpu.SMEM)
    vmem = pl.BlockSpec(memory_space=pltpu.VMEM)
    return pl.pallas_call(
        functools.partial(pack_kernel, count, modes, half),
        out_shape=(
            jax.ShapeDtypeStruct((slabs, ROWS, LANES), basis.dtype),
            jax.ShapeDtypeStruct((2 * half + 1, ROWS, LANES), basis.dtype),
        ),
        in_specs=[smem, smem, smem, vmem],
        out_specs=(vmem, vmem),
        compiler_params=pltpu.CompilerParams(vmem_limit_bytes=24 * 2**20),
    )(where, table.reshape(waves * count, 3), wave_lengths, basis)


def gather_rows(piece, half, waves):
    groups, fields = lax.axis_size("groups"), lax.axis_size("field")

    def swap(x, mask):
        pairs = [
            (g * fields + f, (g ^ (mask >> 2)) * fields + (f ^ (mask & 3)))
            for g in range(groups)
            for f in range(fields)
        ]
        return lax.ppermute(x, ("groups", "field"), pairs)

    parts = [
        lax.ppermute(piece, "wave", [(i, (i + s) % waves) for i in range(waves)])
        for s in range(1, waves)
    ]
    got = []
    for h, (one, two) in enumerate(((2, 4), (4, 2))):
        mine = jnp.concatenate([part[h * half : (h + 1) * half] for part in parts])
        both = jnp.concatenate([mine, swap(mine, one)])
        far = swap(both, two)
        got.append((h, both, (0, one)))
        got.append((h, far, (two, one | two)))
        got.append((h, swap(both, 1), (1, one | 1)))
        got.append((h, swap(far, 1), (two | 1, one | two | 1)))
    return parts, got


def spread_kernel(*refs):
    count = len(refs) // 2
    for small_ref, big_ref in zip(refs[:count], refs[count:]):
        _, many, wide = small_ref.shape
        tall, long = many * ROWS, wide * ROWS
        down = lax.broadcasted_iota(jnp.int32, (tall, many), 0) // ROWS
        down = (down == lax.broadcasted_iota(jnp.int32, (tall, many), 1)).astype(jnp.float32)
        along = lax.broadcasted_iota(jnp.int32, (wide, long), 1) // ROWS
        along = (along == lax.broadcasted_iota(jnp.int32, (wide, long), 0)).astype(jnp.float32)
        same = (lax.broadcasted_iota(jnp.int32, (tall, long), 0) % ROWS) == (
            lax.broadcasted_iota(jnp.int32, (tall, long), 1) % ROWS
        )
        down, along = down.astype(jnp.bfloat16), along.astype(jnp.bfloat16)
        for i in range(small_ref.shape[0]):
            half = jnp.dot(down, small_ref[i], preferred_element_type=jnp.float32)
            whole = jnp.dot(half.astype(jnp.bfloat16), along, preferred_element_type=jnp.float32)
            big_ref[i] = jnp.where(same, whole, 0.0).astype(jnp.bfloat16)


def spreads(*matrices):
    return pl.pallas_call(
        spread_kernel,
        out_shape=tuple(
            jax.ShapeDtypeStruct((m.shape[0], m.shape[1] * ROWS, m.shape[2] * ROWS), jnp.bfloat16)
            for m in matrices
        ),
    )(*matrices)


def form_paths(sizes, where, place, parts, spread, path, opening, basis, sems):
    positions, modes, waves, half, slabs, keys = sizes
    wave, share = where[0], where[1]
    copies = [pltpu.make_async_copy(parts[0], basis.at[pl.ds(wave * slabs, slabs)], sems.at[0])]
    n = 1
    for (h, masks), part in zip(keys, parts[1:]):
        for m, mask in enumerate(masks):
            for s in range(1, waves):
                source = lax.rem(wave + (waves - s), waves)
                start = source * slabs + (share ^ mask) * (2 * half) + h * half
                copies.append(
                    pltpu.make_async_copy(
                        part.at[pl.ds((m * (waves - 1) + s - 1) * half, half)],
                        basis.at[pl.ds(start, half)],
                        sems.at[n],
                    )
                )
                n += 1
    for copy in copies:
        copy.start()
    for copy in copies:
        copy.wait()

    lane = lax.broadcasted_iota(jnp.int32, (ROWS, LANES), 1)
    line = lax.broadcasted_iota(jnp.int32, (ROWS, LANES), 0)

    def chunk(c, carry):
        values = jnp.concatenate(
            [
                basis[pl.ds(place[c * UNITS + j, 0], modes)].reshape(modes * ROWS, LANES)
                for j in range(UNITS)
            ],
            axis=1,
        )
        found = jnp.dot(spread[0], values, preferred_element_type=jnp.float32)
        for j in range(UNITS):
            u = c * UNITS + j
            a = 2 * (line + place[u, 1]) - (PUP - 1)
            b = 2 * (lane + jnp.where(lane < 64, place[u, 2], place[u, 3])) - (PUP - 1)
            radius = a * a + b * b
            inside = (radius <= PUP * PUP) & (radius >= INNER * INNER)
            opening[u] = jnp.where(inside, 1.0, 0.0)
            for f in range(positions):
                path[u, f * ROWS : (f + 1) * ROWS] = jnp.where(
                    inside, found[f * ROWS : (f + 1) * ROWS, j * LANES : (j + 1) * LANES], 0.0
                )
        return carry

    lax.fori_loop(0, len(CHUNKS), chunk, 0)


def transform(positions, rows, inverse, path, opening, row_ref, column_ref, scratch):
    pupils, total, first = scratch[:2], scratch[2], scratch[3]
    batch = max(1, positions // 2)
    width = 2 * positions * LANES // UNITS

    def finish(band, columns, value):
        for f in range(columns.start // LANES, columns.stop // LANES):
            lanes = slice(f * LANES - columns.start, (f + 1) * LANES - columns.start)
            for part in range(2):
                first[
                    f * rows : (f + 1) * rows,
                    part * PUP + band * LANES : part * PUP + (band + 1) * LANES,
                ] = value[part * rows : (part + 1) * rows, lanes].astype(jnp.bfloat16)

    def product(c, columns):
        band, rows_band = CHUNKS[c]
        value = jnp.dot(
            row_ref[0, rows_band], pupils[c % 2][:, columns], preferred_element_type=jnp.float32
        )
        if c > 0 and CHUNKS[c - 1][0] == band:
            value = value + total[:, columns]
        if c + 1 < len(CHUNKS) and CHUNKS[c + 1][0] == band:
            total[:, columns] = value
        else:
            finish(band, columns, value)

    for c, (band, rows_band) in enumerate(CHUNKS):
        pupil = pupils[c % 2]
        for j, row in enumerate(band_rows(rows_band)):
            real_lines = slice(2 * ROWS * j, 2 * ROWS * j + ROWS)
            imag_lines = slice(2 * ROWS * j + ROWS, 2 * ROWS * (j + 1))
            if unit_open(row, band):
                u = c * UNITS + j
                inside = opening[u]
                for f0 in range(0, positions, batch):
                    s, k = half_turn(path[u, f0 * ROWS : (f0 + batch) * ROWS] * inverse)
                    sine = s * k
                    square = s * s
                    for f in range(f0, f0 + batch):
                        columns = slice(f * LANES, (f + 1) * LANES)
                        lines = slice((f - f0) * ROWS, (f - f0 + 1) * ROWS)
                        pupil[real_lines, columns] = (inside - square[lines]).astype(jnp.bfloat16)
                        pupil[imag_lines, columns] = sine[lines].astype(jnp.bfloat16)
            else:
                empty = jnp.zeros((ROWS, positions * LANES), jnp.bfloat16)
                pupil[real_lines] = empty
                pupil[imag_lines] = empty
            if c > 0 and j % 2 == 1:
                product(c - 1, slice(j // 2 * width, (j // 2 + 1) * width))
    for n in range(positions * LANES // width):
        product(len(CHUNKS) - 1, slice(n * width, (n + 1) * width))


def whole_kernel(sizes, tokens, inverse_ref, place, where, *refs):
    positions, modes, waves, half, slabs, keys = sizes
    parts, refs = refs[: 1 + len(keys)], refs[1 + len(keys) :]
    spread, row_ref, column_ref = refs[:3]
    image_ref, path, opening = refs[3 + tokens : 6 + tokens]
    basis, sems = refs[6 + tokens : 8 + tokens]
    scratch = refs[8 + tokens :]

    @pl.when(pl.program_id(0) == 0)
    def _():
        form_paths(sizes, where, place, parts, spread, path, opening, basis, sems)

    inverse = inverse_ref[pl.program_id(0)]
    rows = PIX
    transform(positions, rows, inverse, path, opening, row_ref, column_ref, scratch)
    first = scratch[3]
    share = rows // waves
    for f in range(positions):
        lines = first[f * rows : (f + 1) * rows]
        real = jnp.dot(lines, column_ref[0, :, :PIX], preferred_element_type=jnp.float32)
        imag = jnp.dot(lines, column_ref[0, :, PIX:], preferred_element_type=jnp.float32)
        intensity = real * real + imag * imag
        level = jnp.sum(
            jnp.sum(intensity, axis=0, keepdims=True), axis=1, keepdims=True
        ) / (rows * PIX)
        spectra = (intensity / (level + EPSILON)).astype(jnp.bfloat16)
        for part in range(waves):
            image_ref[part, 0, f * share : (f + 1) * share] = spectra[
                part * share : (part + 1) * share
            ]


def rows_kernel(positions, rows, inverse_ref, path, opening, row_ref, column_ref, *refs):
    image_ref, sum_ref = refs[:2]
    scratch = refs[2:]
    inverse = inverse_ref[pl.program_id(0)]
    transform(positions, rows, inverse, path, opening, row_ref, column_ref, scratch)
    first = scratch[3]
    real = jnp.dot(first[...], column_ref[0, :, :PIX], preferred_element_type=jnp.float32)
    imag = jnp.dot(first[...], column_ref[0, :, PIX:], preferred_element_type=jnp.float32)
    intensity = real * real + imag * imag
    image_ref[0] = intensity
    sum_ref[0] = jnp.sum(intensity.reshape(positions, rows, PIX), axis=1)


def transform_scratch(positions, rows):
    return [
        pltpu.VMEM((2 * BAND, positions * LANES), jnp.bfloat16),
        pltpu.VMEM((2 * BAND, positions * LANES), jnp.bfloat16),
        pltpu.VMEM((2 * rows, positions * LANES), jnp.float32),
        pltpu.VMEM((positions * rows, 2 * PUP), jnp.bfloat16),
    ]


def transform_cost(lengths, positions, rows):
    return pl.CostEstimate(
        flops=lengths * positions * (rows * 8 * PUP * PUP + rows * 8 * PUP * PIX + 10**8),
        bytes_accessed=8 * 2**20,
        transcendentals=0,
    )


SMEM = pl.BlockSpec(memory_space=pltpu.SMEM)
VMEM = pl.BlockSpec(memory_space=pltpu.VMEM)


def table_specs(row_table, column_table):
    return [
        pl.BlockSpec((1,) + row_table.shape[1:], lambda l: (l, 0, 0, 0)),
        pl.BlockSpec((1,) + column_table.shape[1:], lambda l: (l, 0, 0)),
    ]


def whole_fields(own, got, spread, place, where, inverse, row_table, column_table, tokens, sizes):
    positions, modes, waves, half, slabs = sizes
    keys = tuple((h, masks) for h, _, masks in got)
    arrays = [array for _, array, _ in got]
    lengths = row_table.shape[0]
    units = place.shape[0]
    share = positions * PIX // waves
    any_memory = pl.BlockSpec(memory_space=pl.ANY)
    return pl.pallas_call(
        functools.partial(
            whole_kernel, (positions, modes, waves, half, slabs, keys), len(tokens)
        ),
        grid=(lengths,),
        out_shape=(
            jax.ShapeDtypeStruct((waves, lengths, share, PIX), jnp.bfloat16),
            jax.ShapeDtypeStruct((units, positions * ROWS, LANES), jnp.float32),
            jax.ShapeDtypeStruct((units, ROWS, LANES), jnp.float32),
        ),
        in_specs=[SMEM, SMEM, SMEM]
        + [any_memory] * (1 + len(keys))
        + [VMEM]
        + table_specs(row_table, column_table)
        + [VMEM] * len(tokens),
        out_specs=(pl.BlockSpec((waves, 1, share, PIX), lambda l: (0, l, 0, 0)), VMEM, VMEM),
        scratch_shapes=[
            pltpu.VMEM((waves * slabs, ROWS, LANES), jnp.bfloat16),
            pltpu.SemaphoreType.DMA((1 + sum(len(masks) for _, masks in keys) * (waves - 1),)),
        ]
        + transform_scratch(positions, PIX),
        cost_estimate=transform_cost(lengths, positions, PIX),
        compiler_params=pltpu.CompilerParams(vmem_limit_bytes=48 * 2**20),
    )(inverse, place, where, own, *arrays, spread, row_table, column_table, *tokens)


def row_fields(path, opening, inverse, row_table, column_table, positions):
    lengths = row_table.shape[0]
    rows = row_table.shape[2] // 2
    return pl.pallas_call(
        functools.partial(rows_kernel, positions, rows),
        grid=(lengths,),
        out_shape=(
            jax.ShapeDtypeStruct((lengths, positions * rows, PIX), jnp.float32),
            jax.ShapeDtypeStruct((lengths, positions, PIX), jnp.float32),
        ),
        in_specs=[SMEM, VMEM, VMEM] + table_specs(row_table, column_table),
        out_specs=(
            pl.BlockSpec((1, positions * rows, PIX), lambda l: (l, 0, 0)),
            pl.BlockSpec((1, positions, PIX), lambda l: (l, 0, 0)),
        ),
        scratch_shapes=transform_scratch(positions, rows),
        cost_estimate=transform_cost(lengths, positions, rows),
        compiler_params=pltpu.CompilerParams(vmem_limit_bytes=30 * 2**20),
    )(inverse, path, opening, row_table, column_table)


def mix_kernel(inverse_ref, weight_ref, sent_ref, image_ref, out_ref):
    f = pl.program_id(0)
    templates, rows = out_ref.shape[1], out_ref.shape[2]
    blocks = []
    for start in range(0, rows, ROWS):
        lines = slice(start, start + ROWS)
        blocks.append(
            jnp.concatenate(
                [sent_ref[l, lines] for l in range(sent_ref.shape[0])]
                + [
                    (image_ref[l, lines] * inverse_ref[l, f]).astype(jnp.bfloat16)
                    for l in range(image_ref.shape[0])
                ],
                axis=0,
            )
        )
    mixed = jnp.dot(
        weight_ref[0], jnp.concatenate(blocks, axis=1), preferred_element_type=jnp.float32
    ).astype(jnp.bfloat16)
    for n in range(len(blocks)):
        for j in range(templates):
            out_ref[0, j, n * ROWS : (n + 1) * ROWS] = mixed[
                j * ROWS : (j + 1) * ROWS, n * PIX : (n + 1) * PIX
            ]


def mix(spread, inverse, sent, images, templates, rows):
    positions = spread.shape[0]
    return pl.pallas_call(
        mix_kernel,
        grid=(positions,),
        out_shape=jax.ShapeDtypeStruct((positions, templates, rows, PIX), jnp.bfloat16),
        in_specs=[
            SMEM,
            pl.BlockSpec((1,) + spread.shape[1:], lambda f: (f, 0, 0)),
            pl.BlockSpec((sent.shape[0], rows, PIX), lambda f: (0, f, 0)),
            pl.BlockSpec((images.shape[0], rows, PIX), lambda f: (0, f, 0)),
        ],
        out_specs=pl.BlockSpec((1, templates, rows, PIX), lambda f: (f, 0, 0, 0)),
    )(inverse, spread, sent, images)


def table_kernel(scale_ref, y_ref, v_ref, u_ref, x_ref, row_ref, column_ref, token_ref):
    scale = scale_ref[pl.program_id(0)]
    token_ref[...] = jnp.zeros_like(token_ref)
    for start in range(0, PUP, ROWS):
        s, k = half_turn((y_ref[start : start + ROWS] * v_ref[...]) * scale)
        cosine, sine = 1.0 - s * s, s * k
        lower = slice(start, start + ROWS)
        upper = slice(PUP + start, PUP + start + ROWS)
        column_ref[0, lower, :PIX] = cosine.astype(jnp.bfloat16)
        column_ref[0, lower, PIX:] = (-sine).astype(jnp.bfloat16)
        column_ref[0, upper, :PIX] = sine.astype(jnp.bfloat16)
        column_ref[0, upper, PIX:] = cosine.astype(jnp.bfloat16)
    rows = u_ref.shape[0]
    imag = (lax.broadcasted_iota(jnp.int32, (ROWS, 2 * BAND), 1) // ROWS) % 2 == 1
    for band in range(BANDS):
        for start in range(0, rows, ROWS):
            s, k = half_turn((u_ref[start : start + ROWS] * x_ref[band]) * scale)
            cosine, sine = 1.0 - s * s, s * k
            row_ref[0, band, start : start + ROWS] = jnp.where(imag, sine, cosine).astype(
                jnp.bfloat16
            )
            row_ref[0, band, rows + start : rows + start + ROWS] = jnp.where(
                imag, cosine, -sine
            ).astype(jnp.bfloat16)


def tables(wave_lengths, first_row, rows):
    lengths = wave_lengths.shape[0]
    scale = (SAMPLING / (2.0 * PUP)) / wave_lengths
    y = 2 * np.concatenate([band_columns(band) for band in range(BANDS)]) - PUP + 1
    v = np.arange(PIX) - PIX // 2
    u = first_row + jnp.arange(rows, dtype=jnp.int32) - PIX // 2
    x = np.array(
        [[row + i for row in band_rows(band) for i in range(ROWS)] for band in range(BANDS)]
    )
    x = np.repeat(x.reshape(BANDS, UNITS, 1, ROWS), 2, axis=2).reshape(BANDS, 1, 2 * BAND)
    whole = lambda *shape: pl.BlockSpec(shape, lambda l: (0,) * len(shape))
    return pl.pallas_call(
        table_kernel,
        grid=(lengths,),
        out_shape=(
            jax.ShapeDtypeStruct((lengths, BANDS, 2 * rows, 2 * BAND), jnp.bfloat16),
            jax.ShapeDtypeStruct((lengths, 2 * PUP, 2 * PIX), jnp.bfloat16),
            jax.ShapeDtypeStruct((8, LANES), jnp.float32),
        ),
        in_specs=[
            SMEM,
            whole(PUP, 1),
            whole(1, PIX),
            whole(rows, 1),
            whole(BANDS, 1, 2 * BAND),
        ],
        out_specs=(
            pl.BlockSpec((1, BANDS, 2 * rows, 2 * BAND), lambda l: (l, 0, 0, 0)),
            pl.BlockSpec((1, 2 * PUP, 2 * PIX), lambda l: (l, 0, 0)),
            whole(8, LANES),
        ),
        cost_estimate=pl.CostEstimate(
            flops=lengths * 30 * PUP * PIX, bytes_accessed=lengths * 4 * PUP * PIX * 2, transcendentals=0
        ),
        compiler_params=pltpu.CompilerParams(vmem_limit_bytes=24 * 2**20),
    )(
        scale,
        jnp.asarray(y[:, None].astype(np.float32)),
        jnp.asarray(v[None, :].astype(np.float32)),
        u.astype(jnp.float32)[:, None],
        jnp.asarray((2 * x - PUP + 1).astype(np.float32)),
    )


def add_over_wave(x, waves):
    step = 1
    while step < waves:
        x = x + lax.ppermute(x, "wave", [(i, i ^ step) for i in range(waves)])
        step *= 2
    return x


def local(mode_basis, coef_table, table_index, wave_lengths, sed_table, template_ids):
    waves = lax.axis_size("wave")
    mine = lax.axis_index("wave")
    modes = mode_basis.shape[0]
    positions = table_index.shape[0]
    rows = PIX // waves
    count, half, slabs, pack, place = layout(waves, modes)
    lengths = wave_lengths.shape[0]
    sent_lengths = lengths // 2

    share = (lax.axis_index("groups") % 2) * 4 + lax.axis_index("field") % 4
    where = jnp.stack([mine, share]).astype(jnp.int32)
    own, piece = pack_rows(mode_basis, wave_lengths, pack, where, half, slabs)
    parts, got = gather_rows(piece, half, waves)

    limbs = jnp.stack([part[2 * half, : 3 * lengths, 0] for part in parts])
    others = jnp.sum(limbs.astype(jnp.float32).reshape(waves - 1, lengths, 3), axis=2)
    known = jnp.concatenate([wave_lengths[None], others])
    order = (mine - jnp.arange(waves)) % waves
    every = jnp.sum(
        jnp.where((order[:, None] == jnp.arange(waves)[None, :])[:, :, None], known[None], 0.0),
        axis=1,
    )[:, sent_lengths:].reshape(-1)
    own_row, own_column, own_token = tables(wave_lengths[:sent_lengths], 0, PIX)
    all_row, all_column, all_token = tables(every, mine * rows, rows)

    selector = (
        table_index[:, None] == jnp.arange(coef_table.shape[0], dtype=jnp.int32)[None, :]
    ).astype(jnp.bfloat16)
    coeffs = jnp.dot(selector, coef_table, preferred_element_type=jnp.float32)
    one_hot = (
        template_ids[:, :, None]
        == jnp.arange(sed_table.shape[0], dtype=jnp.int32)[None, None, :]
    ).astype(jnp.float32)
    raw_weights = jnp.einsum("fjn,nl->fjl", one_hot, sed_table, precision=lax.Precision.HIGHEST)
    weights = (raw_weights / jnp.sum(raw_weights, axis=2, keepdims=True)).astype(jnp.bfloat16)
    templates = weights.shape[1]
    split = weights.reshape(positions, templates, waves, lengths)
    weights = jnp.concatenate(
        [
            split[..., :sent_lengths].reshape(positions, templates, -1),
            split[..., sent_lengths:].reshape(positions, templates, -1),
        ],
        axis=2,
    )
    path_spread, mix_spread = spreads(coeffs.astype(jnp.bfloat16)[None], weights)

    spectra, path, opening = whole_fields(
        own,
        got,
        path_spread,
        place,
        where,
        1.0 / wave_lengths[:sent_lengths],
        own_row,
        own_column,
        (all_token,),
        (positions, modes, waves, half, slabs),
    )
    sent = lax.all_to_all(spectra, "wave", split_axis=0, concat_axis=0, tiled=True)
    sent = sent.reshape(waves * sent_lengths, positions * rows, PIX)

    images, sums = row_fields(path, opening, 1.0 / every, all_row, all_column, positions)
    level = add_over_wave(jnp.sum(sums, axis=2), waves) / (PIX * PIX)
    return mix(mix_spread, 1.0 / (level + EPSILON), sent, images, templates, rows)


def solution(mesh):
    return jax.shard_map(
        local,
        mesh=mesh,
        in_specs=(
            P(None, "wave", None),
            P(),
            P(("groups", "field")),
            P("wave"),
            P(),
            P(("groups", "field"), None),
        ),
        out_specs=P(("groups", "field"), None, "wave", None),
        check_vma=False,
    )
```

time: 180 us -> 158 us (0.88)
  Pallas kernels: 93 us -> 65.5 us
  waiting for transfers between devices: 29.9 us -> 43.3 us
  blocking collectives: 12.1 us -> 0 us
  local copies, waits for them, and re-layouts: 12.9 us -> 22.7 us
  starting transfers between devices: 26.9 us -> 21.3 us
    pallas_call x2 -> x4, Pallas kernels: 79.5 us -> 52.9 us  [the longest x1 27.6 us: row_fields(): pl.pallas_call(functools.partial(rows_kernel, positions, rows), grid=(len...]
    unnamed x38 -> x54, local copies, waits for them, and re-layouts: 7.72 us -> 19.9 us
    psum x1 -> x0, blocking collectives: 12.1 us -> none  [local(): level = lax.psum(jnp.sum(sums, axis=2), 'wave') / (PIX * PIX)]
    ppermute x6 -> x3, waiting for transfers between devices: 11.8 us -> 23.7 us  [gather_rows(): lax.ppermute(piece, 'wave', [(i, (i + s) % waves) for i in range(waves)])]
    ppermute x14 -> x8, waiting for transfers between devices: 10.2 us -> 16.5 us  [swap(): return lax.ppermute(x, ('groups', 'field'), pairs)]
    ppermute x3 -> x2, waiting for transfers between devices: 7.9 us -> 3.13 us  [add_over_wave(): x = x + lax.ppermute(x, 'wave', [(i, i ^ step) for i in range(waves)])]
    ppermute x6 -> x3, starting transfers between devices: 10.6 us -> 6.06 us  [gather_rows(): lax.ppermute(piece, 'wave', [(i, (i + s) % waves) for i in range(waves)])]
    ppermute x14 -> x8, starting transfers between devices: 10.4 us -> 5.93 us  [swap(): return lax.ppermute(x, ('groups', 'field'), pairs)]
  transfers between devices with their start and end apart: 23 -> 14, of which waited for: 10 -> 7; matrix products, arithmetic and copies ran while one was open for 4% -> 4% of each run, Pallas kernels for 4% -> 23%
where the time goes in v4:
time: 158 us; the launch traced here: 157 us
  Pallas kernels  65.5 us (41%)
  waiting for transfers between devices  43.3 us (27%)
  local copies, waits for them, and re-layouts  22.7 us (14%)
  starting transfers between devices  21.3 us (13%)
  other arithmetic  2.06 us (1%)
  matrix products  1.83 us (1%)
    pallas_call x1, Pallas kernels, row_fields(): pl.pallas_call(functools.partial(rows_kernel, positions, rows), grid=(len...  27.6 us
    ppermute x3, waiting for transfers between devices, gather_rows(): lax.ppermute(piece, 'wave', [(i, (i + s) % waves) for i in range(waves)])  23.7 us
    pallas_call x1, Pallas kernels, whole_fields(): pl.pallas_call(functools.partial(whole_kernel, (positions, modes, waves,...  20.9 us
    unnamed x54, local copies, waits for them, and re-layouts  19.9 us
    ppermute x8, waiting for transfers between devices, swap(): return lax.ppermute(x, ('groups', 'field'), pairs)  16.5 us
    pallas_call x1, Pallas kernels, mix(): pl.pallas_call(mix_kernel, grid=(positions,), out_shape=jax.ShapeDtypeStr...  6.76 us
    ppermute x3, starting transfers between devices, gather_rows(): lax.ppermute(piece, 'wave', [(i, (i + s) % waves) for i in range(waves)])  6.06 us
    ppermute x8, starting transfers between devices, swap(): return lax.ppermute(x, ('groups', 'field'), pairs)  5.93 us
  transfers between devices with their start and end apart: 14, of which 7 were waited for; matrix products, arithmetic and copies ran while one was open for 4% of the time, Pallas kernels for 23%

profile of v4, /device:TPU:0, one launch (start us, length us, event | category | flops | bytes accessed | tf_op | source)
XLA Modules:
  0.0 157.2 jit_solution(689603404235766882)
XLA Ops:
  0.0 0.1 pad_add_fusion.where
  0.1 1.8 %copy-done.1 = bf16[22,128,512]{2,1,0:T(8,128)(2,1)S(1)} copy-done((bf16[22,128,512]{2,1,0:T(8,128)(2,1)S(1)}, bf16[22,128,512]{2,1,0:T(8,128)(2,1)}, u32[]{:S(2)}) %copy-start.1) | copy-done | bytes 2883608
  1.9 0.8 copy-done.4
  2.7 0.7 copy-done.7
  3.4 2.3 %shard_map.136 = (bf16[560,16,128]{2,1,0:T(8,128)(2,1)S(1)}, bf16[71,16,128]{2,1,0:T(8,128)(2,1)S(1)}) custom-call(s32[2]{0:T(128)S(1)} %pad_add_fusion.where, s32[100,3]{1,0:T(8,128)S(1)} %copy-done.4, f32[2]{0:T(128)S(1)} %copy-done.7, bf16[22,128,512]{2,1,0:T(8,128)(2,1)S(1)} %copy-done.1), custom_call_target="tpu_custom_call" | custom-call | tf_op jit(solution)/shard_map/pallas_call | solution.py:135
  5.8 1.4 copy-done.11
  7.2 5.0 %collective-permute-start.2 = (bf16[71,16,128]{2,1,0:T(8,128)(2,1)S(1)}, bf16[71,16,128]{2,1,0:T(8,128)(2,1)S(1)}, u32[]{:S(2)}, u32[]{:S(2)}) collective-permute-start(bf16[71,16,128]{2,1,0:T(8,128)(2,1)S(1)} %get-tuple-element.19), channel_id=1, source_target_pairs={{0,3},{1,0},{2,1},{3,2},{4,7},{5,4},{6,5},{7,6},{8,11},{9,8},{10,9... | collective-permute-start | bytes 872456 | tf_op jit(solution)/shard_map/ppermute | solution.py:159
  12.2 0.0 collective-permute-start.1
  12.2 1.0 collective-permute-start
  13.2 6.4 %collective-permute-done.2 = bf16[71,16,128]{2,1,0:T(8,128)(2,1)S(1)} collective-permute-done((bf16[71,16,128]{2,1,0:T(8,128)(2,1)S(1)}, bf16[71,16,128]{2,1,0:T(8,128)(2,1)S(1)}, u32[]{:S(2)}, u32[]{:S(2)}) %collective-permute-start.2) | collective-permute-done | bytes 290848 | tf_op jit(solution)/shard_map/ppermute | solution.py:159
  19.6 17.4 %collective-permute-done.1 = bf16[71,16,128]{2,1,0:T(8,128)(2,1)S(1)} collective-permute-done((bf16[71,16,128]{2,1,0:T(8,128)(2,1)S(1)}, bf16[71,16,128]{2,1,0:T(8,128)(2,1)S(1)}, u32[]{:S(2)}, u32[]{:S(2)}) %collective-permute-start.1) | collective-permute-done | bytes 290848 | tf_op jit(solution)/shard_map/ppermute | solution.py:159
  37.0 0.0 collective-permute-done
  37.1 0.0 copy-start.25
  37.1 0.6 copy-done.21
  37.8 1.6 collective-permute-start.3
  39.4 1.6 %collective-permute-start.7 = (bf16[105,16,128]{2,1,0:T(8,128)(2,1)S(1)}, bf16[105,16,128]{2,1,0:T(8,128)(2,1)S(1)}, u32[]{:S(2)}, u32[]{:S(2)}) collective-permute-start(bf16[105,16,128]{2,1,0:T(8,128)(2,1)S(1)} %pad_maximum_fusion.3), channel_id=1, source_target_pairs={{0,16},{4,20},{8,24},{12,28},{16,0},{20,4},{24,8},{28,12},{1,17},{... | collective-permute-start | bytes 1290248 | tf_op jit(solution)/shard_map/ppermute | solution.py:156
  41.0 1.1 fusion.10
  42.2 7.7 %collective-permute-done.7 = bf16[105,16,128]{2,1,0:T(8,128)(2,1)S(1)} collective-permute-done((bf16[105,16,128]{2,1,0:T(8,128)(2,1)S(1)}, bf16[105,16,128]{2,1,0:T(8,128)(2,1)S(1)}, u32[]{:S(2)}, u32[]{:S(2)}) %collective-permute-start.7) | collective-permute-done | bytes 430112 | tf_op jit(solution)/shard_map/ppermute | solution.py:156
  50.0 0.1 pad_maximum_fusion.1.refs_5_
  50.0 0.6 collective-permute-start.8
  50.6 0.1 pad_maximum_fusion.refs_1_
  50.7 1.6 %collective-permute-start.4 = (bf16[210,16,128]{2,1,0:T(8,128)(2,1)S(1)}, bf16[210,16,128]{2,1,0:T(8,128)(2,1)}, u32[]{:S(2)}, u32[]{:S(2)}) collective-permute-start(bf16[210,16,128]{2,1,0:T(8,128)(2,1)S(1)} %pad_maximum_fusion.refs_1_), channel_id=1, source_target_pairs={{0,16},{4,20},{8,24},{12,28},{16,0},{20,4},{24,8},{28,12},{1,17},{... | collective-permute-start | bytes 2580488 | tf_op jit(solution)/shard_map/ppermute | solution.py:156
  52.3 0.1 copy.36
  52.5 0.1 copy.37
  52.6 0.7 pad_maximum_fusion.4.refs_1_
  53.3 0.8 fusion.refs_0_
  54.1 2.0 %shard_map.137 = (bf16[1,128,352]{2,1,0:T(8,128)(2,1)}, bf16[8,128,128]{2,1,0:T(8,128)(2,1)}) custom-call(bf16[1,8,22]{2,1,0:T(8,128)(2,1)} %fusion.refs_0_, bf16[8,8,8]{2,1,0:T(8,128)(2,1)} %pad_maximum_fusion.4.refs_1_), custom_call_target="tpu_custom_call" | custom-call | tf_op jit(solution)/shard_map/pallas_call | solution.py:194
  56.1 2.0 %shard_map.138 = (bf16[1,4,512,256]{3,2,1,0:T(8,128)(2,1)S(1)}, bf16[1,1024,512]{2,1,0:T(8,128)(2,1)S(1)}, f32[8,128]{1,0:T(8,128)}) custom-call(f32[1]{0:T(128)S(6)} %div.42.scale_ref, f32[512,1]{1,0:T(8,128)S(1)} %copy-done.3, f32[1,256]{1,0:T(1,128)S(1)} %copy-done.6, f32[256,1]{1,0:T(8,128)S(1)} %add_convert_fusion.u_ref, f32[4,1,256]{2,1,0:T(1,128)S(1)} %copy-done.5), custom_call_target="tpu_custom_call" | custom-call | flops 3932160 | bytes 1048576 | tf_op jit(solution)/shard_map/pallas_call | solution.py:514
  58.1 1.0 copy-done.12
  59.1 1.0 copy-done.13
  60.1 0.1 iota_compare_fusion.4
  60.2 0.5 collective-permute-start.5
  60.7 8.3 %collective-permute-done.8.refs_6_ = bf16[210,16,128]{2,1,0:T(8,128)(2,1)} collective-permute-done((bf16[210,16,128]{2,1,0:T(8,128)(2,1)S(1)}, bf16[210,16,128]{2,1,0:T(8,128)(2,1)}, u32[]{:S(2)}, u32[]{:S(2)}) %collective-permute-start.8) | collective-permute-done | bytes 860192 | tf_op jit(solution)/shard_map/ppermute | solution.py:156
  69.0 0.4 collective-permute-done.4.refs_2_
  69.4 0.1 collective-permute-start.6
  69.5 0.8 slice_reduce_fusion
  70.3 0.1 stack.23
  70.4 0.8 slice_reduce_fusion.1
  71.2 0.1 stack.22
  71.3 0.8 slice_reduce_fusion.2
  72.1 0.1 stack.21
  72.2 0.1 convert_reduce_fusion
  72.3 0.1 copy.31
  72.4 0.1 select_reduce_fusion
  72.5 3.8 %shard_map.139 = (bf16[4,4,128,256]{3,2,1,0:T(8,128)(2,1)S(1)}, bf16[4,1024,512]{2,1,0:T(8,128)(2,1)S(1)}, f32[8,128]{1,0:T(8,128)S(1)}) custom-call(f32[4]{0:T(128)S(1)} %get-tuple-element.41.scale_ref, f32[512,1]{1,0:T(8,128)S(1)} %copy-done.3, f32[1,256]{1,0:T(1,128)S(1)} %copy-done.6, f32[64,1]{1,0:T(8,128)S(1)} %add_convert_fusion.1.u_ref, ...), custom_call_target="tpu_custom_call" | custom-call | flops 15728640 | bytes 4194304 | tf_op jit(solution)/shard_map/pallas_call | solution.py:514
  76.3 2.0 %copy-done.9 = bf16[4,1024,512]{2,1,0:T(8,128)(2,1)} copy-done((bf16[4,1024,512]{2,1,0:T(8,128)(2,1)}, bf16[4,1024,512]{2,1,0:T(8,128)(2,1)S(1)}, u32[]{:S(2)}) %copy-start.9) | copy-done | bytes 4194328
  78.4 0.9 copy-done.14
  79.3 20.9 %shard_map.140 = (bf16[4,1,512,256]{3,2,1,0:T(8,128)(2,1)}, f32[96,128,128]{2,1,0:T(8,128)}, f32[96,16,128]{2,1,0:T(8,128)S(1)}) custom-call(f32[1]{0:T(128)S(6)} %div.39.inverse_ref, s32[96,4]{1,0:T(8,128)S(1)} %copy-done.15, s32[2]{0:T(128)S(1)} %pad_add_fusion.where, bf16[560,16,128]{2,1,0:T(8,128)(2,1)} %copy-done.11, ...), custom_call_target="tpu_custom_call" | custom-call | flops 7242450944 | bytes 8388608 | tf_op jit(solution)/shard_map/pallas_call | solution.py:388
  100.3 0.0 copy-start.17
  100.3 0.9 copy-done.17
  101.1 4.4 %all-to-all-start = ((bf16[4,1,512,256]{3,2,1,0:T(8,128)(2,1)}), bf16[4,1,512,256]{3,2,1,0:T(8,128)(2,1)S(1)}, u32[]{:S(2)}, u32[]{:S(2)}) async-start(bf16[4,1,512,256]{3,2,1,0:T(8,128)(2,1)} %get-tuple-element.31), calls=%async_computation | async-start | bytes 2097152 | tf_op jit(solution)/shard_map/all_to_all | solution.py:614
  105.6 2.2 %copy-done.10 = bf16[4,1024,512]{2,1,0:T(8,128)(2,1)S(1)} copy-done((bf16[4,1024,512]{2,1,0:T(8,128)(2,1)S(1)}, bf16[4,1024,512]{2,1,0:T(8,128)(2,1)}, u32[]{:S(2)}) %copy-start.10) | copy-done | bytes 4194328
  107.7 2.8 %copy-done.16 = f32[96,128,128]{2,1,0:T(8,128)S(1)} copy-done((f32[96,128,128]{2,1,0:T(8,128)S(1)}, f32[96,128,128]{2,1,0:T(8,128)}, u32[]{:S(2)}) %copy-start.16) | copy-done | bytes 6291480
  110.5 1.1 copy-done.18
  111.7 27.6 %shard_map.141 = (f32[4,512,256]{2,1,0:T(8,128)S(1)}, f32[4,8,256]{2,1,0:T(8,128)S(1)}) custom-call(f32[4]{0:T(128)S(1)} %get-tuple-element.42.inverse_ref, f32[96,128,128]{2,1,0:T(8,128)S(1)} %copy-done.16, f32[96,16,128]{2,1,0:T(8,128)S(1)} %copy-done.18, bf16[4,4,128,256]{3,2,1,0:T(8,128)(2,1)S(1)} %get-tuple-element.27.row_ref, ...), custom_call_target="tpu_custom_call" | custom-call | flops 9642450944 | bytes 8388608 | tf_op jit(solution)/shard_map/pallas_call | solution.py:417
  139.3 1.4 copy-done.2
  140.7 0.1 reduce_sum.39
  140.7 2.0 %collective-permute-start.11 = (f32[4,8]{1,0:T(4,128)S(1)}, f32[4,8]{1,0:T(4,128)S(1)}, u32[]{:S(2)}, u32[]{:S(2)}) collective-permute-start(f32[4,8]{1,0:T(4,128)S(1)} %reduce_sum.39), channel_id=1, source_target_pairs={{0,1},{1,0},{2,3},{3,2},{4,5},{5,4},{6,7},{7,6},{8,9},{9,8},{10,11... | collective-permute-start | bytes 392 | tf_op jit(solution)/shard_map/ppermute | solution.py:550
  142.8 1.6 collective-permute-done.11
  144.3 2.9 %collective-permute-start.12 = (f32[4,8]{1,0:T(4,128)S(1)}, f32[4,8]{1,0:T(4,128)S(1)}, u32[]{:S(2)}, u32[]{:S(2)}) collective-permute-start(f32[4,8]{1,0:T(4,128)S(1)} %add.67), channel_id=1, source_target_pairs={{0,2},{1,3},{2,0},{3,1},{4,6},{5,7},{6,4},{7,5},{8,10},{9,11},{10,... | collective-permute-start | bytes 392 | tf_op jit(solution)/shard_map/ppermute | solution.py:550
  147.3 1.6 collective-permute-done.12
  148.8 0.6 add_divide_fusion.inverse_ref
  149.4 1.0 copy-done.19
  150.4 6.8 %shard_map.142 = bf16[8,8,64,256]{3,2,1,0:T(8,128)(2,1)} custom-call(f32[4,8]{1,0:T(4,128)} %add_divide_fusion.inverse_ref, bf16[8,128,128]{2,1,0:T(8,128)(2,1)} %get-tuple-element.30.weight_ref, bf16[4,512,256]{2,1,0:T(8,128)(2,1)} %bitcast.23, f32[4,512,256]{2,1,0:T(8,128)} %copy-done.2), custom_call_target="tpu_custom_call" | custom-call | tf_op jit(solution)/shard_map/pallas_call | solution.py:463
  (57 shorter events, 0.3 us)
Async XLA Ops:
  0.0 53.3 %copy-start = (bf16[4096,22]{0,1:T(8,128)(2,1)S(1)}, bf16[4096,22]{0,1:T(8,128)(2,1)}, u32[]{:S(2)}) copy-start(bf16[4096,22]{0,1:T(8,128)(2,1)} %param.15) | copy-start | bytes 540676
  0.1 1.8 %copy-start.1 = (bf16[22,128,512]{2,1,0:T(8,128)(2,1)S(1)}, bf16[22,128,512]{2,1,0:T(8,128)(2,1)}, u32[]{:S(2)}) copy-start(bf16[22,128,512]{2,1,0:T(8,128)(2,1)} %basis.1) | copy-start | bytes 8650756
  1.9 0.8 copy-start.4
  2.7 0.7 copy-start.7
  3.4 37.6 %copy-start.23 = (f32[1024,8]{0,1:T(8,128)S(1)}, f32[1024,8]{0,1:T(8,128)}, u32[]{:S(2)}) copy-start(f32[1024,8]{0,1:T(8,128)} %param.18) | copy-start | bytes 98308
  3.4 37.6 %copy-start.24 = (s32[8,8]{1,0:T(8,128)S(1)}, s32[8,8]{1,0:T(8,128)}, u32[]{:S(2)}) copy-start(s32[8,8]{1,0:T(8,128)} %param.19) | copy-start | bytes 772
  3.4 38.7 %copy-start.8 = (f32[2]{0:T(128)S(1)}, f32[2]{0:T(128)}, u32[]{:S(2)}) copy-start(f32[2]{0:T(128)} %lengths.1) | copy-start | bytes 28
  5.7 1.4 copy-start.11
  7.2 12.4 %collective-permute-start.2 = (bf16[71,16,128]{2,1,0:T(8,128)(2,1)S(1)}, bf16[71,16,128]{2,1,0:T(8,128)(2,1)S(1)}, u32[]{:S(2)}, u32[]{:S(2)}) collective-permute-start(bf16[71,16,128]{2,1,0:T(8,128)(2,1)S(1)} %get-tuple-element.19), channel_id=1, source_target_pairs={{0,3},{1,0},{2,1},{3,2},{4,7},{5,4},{6,5},{7,6},{8,11},{9,8},{10,9... | collective-permute-start | bytes 872456 | tf_op jit(solution)/shard_map/ppermute | solution.py:159
  12.2 24.8 %collective-permute-start.1 = (bf16[71,16,128]{2,1,0:T(8,128)(2,1)S(1)}, bf16[71,16,128]{2,1,0:T(8,128)(2,1)S(1)}, u32[]{:S(2)}, u32[]{:S(2)}) collective-permute-start(bf16[71,16,128]{2,1,0:T(8,128)(2,1)S(1)} %get-tuple-element.19), channel_id=1, source_target_pairs={{0,2},{1,3},{2,0},{3,1},{4,6},{5,7},{6,4},{7,5},{8,10},{9,11},{10,... | collective-permute-start | bytes 872456 | tf_op jit(solution)/shard_map/ppermute | solution.py:159
  12.2 24.8 %collective-permute-start = (bf16[71,16,128]{2,1,0:T(8,128)(2,1)S(1)}, bf16[71,16,128]{2,1,0:T(8,128)(2,1)S(1)}, u32[]{:S(2)}, u32[]{:S(2)}) collective-permute-start(bf16[71,16,128]{2,1,0:T(8,128)(2,1)S(1)} %get-tuple-element.19), channel_id=1, source_target_pairs={{0,1},{1,2},{2,3},{3,0},{4,5},{5,6},{6,7},{7,4},{8,9},{9,10},{10,1... | collective-permute-start | bytes 872456 | tf_op jit(solution)/shard_map/ppermute | solution.py:159
  19.6 17.5 %copy-start.20 = (bf16[71,16,128]{2,1,0:T(8,128)(2,1)}, bf16[71,16,128]{2,1,0:T(8,128)(2,1)S(1)}, u32[]{:S(2)}) copy-start(bf16[71,16,128]{2,1,0:T(8,128)(2,1)S(1)} %collective-permute-done.2) | copy-start | bytes 872452
  37.0 0.7 copy-start.21
  37.0 2.3 %copy-start.22 = (bf16[71,16,128]{2,1,0:T(8,128)(2,1)}, bf16[71,16,128]{2,1,0:T(8,128)(2,1)S(1)}, u32[]{:S(2)}) copy-start(bf16[71,16,128]{2,1,0:T(8,128)(2,1)S(1)} %collective-permute-done) | copy-start | bytes 872452
  37.1 16.2 %copy-start.25 = (s32[8]{0:T(128)S(1)}, s32[8]{0:T(128)}, u32[]{:S(2)}) copy-start(s32[8]{0:T(128)} %param.16) | copy-start | bytes 100
  37.7 18.3 %copy-start.3 = (f32[512,1]{1,0:T(8,128)S(1)}, f32[512,1]{1,0:T(8,128)}, u32[]{:S(2)}) copy-start(f32[512,1]{1,0:T(8,128)} %constant.78.clone.y_ref) | copy-start | bytes 6148
  37.7 18.3 %copy-start.5 = (f32[4,1,256]{2,1,0:T(1,128)S(1)}, f32[4,1,256]{2,1,0:T(1,128)}, u32[]{:S(2)}) copy-start(f32[4,1,256]{2,1,0:T(1,128)} %constant.80.clone.x_ref) | copy-start | bytes 12292
  37.7 18.4 %copy-start.6 = (f32[1,256]{1,0:T(1,128)S(1)}, f32[1,256]{1,0:T(1,128)}, u32[]{:S(2)}) copy-start(f32[1,256]{1,0:T(1,128)} %constant.79.clone.v_ref) | copy-start | bytes 3076
  37.8 12.9 %collective-permute-start.3 = (bf16[105,16,128]{2,1,0:T(8,128)(2,1)S(1)}, bf16[105,16,128]{2,1,0:T(8,128)(2,1)S(1)}, u32[]{:S(2)}, u32[]{:S(2)}) collective-permute-start(bf16[105,16,128]{2,1,0:T(8,128)(2,1)S(1)} %pad_maximum_fusion.2), channel_id=1, source_target_pairs={{0,8},{4,12},{8,0},{12,4},{16,24},{20,28},{24,16},{28,20},{1,9},{5... | collective-permute-start | bytes 1290248 | tf_op jit(solution)/shard_map/ppermute | solution.py:156
  39.3 39.1 %copy-start.15 = (s32[96,4]{1,0:T(8,128)S(1)}, s32[96,4]{1,0:T(8,128)}, u32[]{:S(2)}) copy-start(s32[96,4]{1,0:T(8,128)} %constant.81.clone.place) | copy-start | bytes 4612
  39.4 10.6 %collective-permute-start.7 = (bf16[105,16,128]{2,1,0:T(8,128)(2,1)S(1)}, bf16[105,16,128]{2,1,0:T(8,128)(2,1)S(1)}, u32[]{:S(2)}, u32[]{:S(2)}) collective-permute-start(bf16[105,16,128]{2,1,0:T(8,128)(2,1)S(1)} %pad_maximum_fusion.3), channel_id=1, source_target_pairs={{0,16},{4,20},{8,24},{12,28},{16,0},{20,4},{24,8},{28,12},{1,17},{... | collective-permute-start | bytes 1290248 | tf_op jit(solution)/shard_map/ppermute | solution.py:156
  50.0 19.0 %collective-permute-start.8 = (bf16[210,16,128]{2,1,0:T(8,128)(2,1)S(1)}, bf16[210,16,128]{2,1,0:T(8,128)(2,1)}, u32[]{:S(2)}, u32[]{:S(2)}) collective-permute-start(bf16[210,16,128]{2,1,0:T(8,128)(2,1)S(1)} %pad_maximum_fusion.1.refs_5_), channel_id=1, source_target_pairs={{0,8},{4,12},{8,0},{12,4},{16,24},{20,28},{24,16},{28,20},{1,9},{5... | collective-permute-start | bytes 2580488 | tf_op jit(solution)/shard_map/ppermute | solution.py:156
  50.7 18.7 %collective-permute-start.4 = (bf16[210,16,128]{2,1,0:T(8,128)(2,1)S(1)}, bf16[210,16,128]{2,1,0:T(8,128)(2,1)}, u32[]{:S(2)}, u32[]{:S(2)}) collective-permute-start(bf16[210,16,128]{2,1,0:T(8,128)(2,1)S(1)} %pad_maximum_fusion.refs_1_), channel_id=1, source_target_pairs={{0,16},{4,20},{8,24},{12,28},{16,0},{20,4},{24,8},{28,12},{1,17},{... | collective-permute-start | bytes 2580488 | tf_op jit(solution)/shard_map/ppermute | solution.py:156
  58.1 1.0 copy-start.12
  59.1 1.0 copy-start.13
  60.2 18.2 %collective-permute-start.9 = (bf16[210,16,128]{2,1,0:T(8,128)(2,1)S(1)}, bf16[210,16,128]{2,1,0:T(8,128)(2,1)}, u32[]{:S(2)}, u32[]{:S(2)}) collective-permute-start(bf16[210,16,128]{2,1,0:T(8,128)(2,1)S(1)} %pad_maximum_fusion.1.refs_5_), channel_id=1, source_target_pairs={{0,4},{4,0},{8,12},{12,8},{16,20},{20,16},{24,28},{28,24},{1,5},{5... | collective-permute-start | bytes 2580488 | tf_op jit(solution)/shard_map/ppermute | solution.py:156
  60.2 18.2 %collective-permute-start.5 = (bf16[210,16,128]{2,1,0:T(8,128)(2,1)S(1)}, bf16[210,16,128]{2,1,0:T(8,128)(2,1)}, u32[]{:S(2)}, u32[]{:S(2)}) collective-permute-start(bf16[210,16,128]{2,1,0:T(8,128)(2,1)S(1)} %pad_maximum_fusion.refs_1_), channel_id=1, source_target_pairs={{0,4},{4,0},{8,12},{12,8},{16,20},{20,16},{24,28},{28,24},{1,5},{5... | collective-permute-start | bytes 2580488 | tf_op jit(solution)/shard_map/ppermute | solution.py:156
  69.0 9.4 %collective-permute-start.10 = (bf16[210,16,128]{2,1,0:T(8,128)(2,1)}, bf16[210,16,128]{2,1,0:T(8,128)(2,1)}, u32[]{:S(2)}, u32[]{:S(2)}) collective-permute-start(bf16[210,16,128]{2,1,0:T(8,128)(2,1)} %collective-permute-done.8.refs_6_), channel_id=1, source_target_pairs={{0,4},{4,0},{8,12},{12,8},{16,20},{20,16},{24,28},{28,24},{1,5},{5... | collective-permute-start | bytes 2580488 | tf_op jit(solution)/shard_map/ppermute | solution.py:156
  69.4 9.0 %collective-permute-start.6 = (bf16[210,16,128]{2,1,0:T(8,128)(2,1)}, bf16[210,16,128]{2,1,0:T(8,128)(2,1)}, u32[]{:S(2)}, u32[]{:S(2)}) collective-permute-start(bf16[210,16,128]{2,1,0:T(8,128)(2,1)} %collective-permute-done.4.refs_2_), channel_id=1, source_target_pairs={{0,4},{4,0},{8,12},{12,8},{16,20},{20,16},{24,28},{28,24},{1,5},{5... | collective-permute-start | bytes 2580488 | tf_op jit(solution)/shard_map/ppermute | solution.py:156
  76.3 2.1 %copy-start.9 = (bf16[4,1024,512]{2,1,0:T(8,128)(2,1)}, bf16[4,1024,512]{2,1,0:T(8,128)(2,1)S(1)}, u32[]{:S(2)}) copy-start(bf16[4,1024,512]{2,1,0:T(8,128)(2,1)S(1)} %get-tuple-element.28.column_ref) | copy-start | bytes 12582916
  78.4 0.9 copy-start.14
  100.3 0.9 copy-start.17
  101.1 48.3 %all-to-all-start = ((bf16[4,1,512,256]{3,2,1,0:T(8,128)(2,1)}), bf16[4,1,512,256]{3,2,1,0:T(8,128)(2,1)S(1)}, u32[]{:S(2)}, u32[]{:S(2)}) async-start(bf16[4,1,512,256]{3,2,1,0:T(8,128)(2,1)} %get-tuple-element.31), calls=%async_computation | async-start | bytes 2097152 | tf_op jit(solution)/shard_map/all_to_all | solution.py:614
  105.5 2.2 %copy-start.10 = (bf16[4,1024,512]{2,1,0:T(8,128)(2,1)S(1)}, bf16[4,1024,512]{2,1,0:T(8,128)(2,1)}, u32[]{:S(2)}) copy-start(bf16[4,1024,512]{2,1,0:T(8,128)(2,1)} %copy-done.9) | copy-start | bytes 12582916
  107.7 2.8 %copy-start.16 = (f32[96,128,128]{2,1,0:T(8,128)S(1)}, f32[96,128,128]{2,1,0:T(8,128)}, u32[]{:S(2)}) copy-start(f32[96,128,128]{2,1,0:T(8,128)} %get-tuple-element.25.path) | copy-start | bytes 18874372
  110.5 1.1 copy-start.18
  139.3 1.4 copy-start.2
  140.7 3.6 %collective-permute-start.11 = (f32[4,8]{1,0:T(4,128)S(1)}, f32[4,8]{1,0:T(4,128)S(1)}, u32[]{:S(2)}, u32[]{:S(2)}) collective-permute-start(f32[4,8]{1,0:T(4,128)S(1)} %reduce_sum.39), channel_id=1, source_target_pairs={{0,1},{1,0},{2,3},{3,2},{4,5},{5,4},{6,7},{7,6},{8,9},{9,8},{10,11... | collective-permute-start | bytes 392 | tf_op jit(solution)/shard_map/ppermute | solution.py:550
  144.3 4.5 %collective-permute-start.12 = (f32[4,8]{1,0:T(4,128)S(1)}, f32[4,8]{1,0:T(4,128)S(1)}, u32[]{:S(2)}, u32[]{:S(2)}) collective-permute-start(f32[4,8]{1,0:T(4,128)S(1)} %add.67), channel_id=1, source_target_pairs={{0,2},{1,3},{2,0},{3,1},{4,6},{5,7},{6,4},{7,5},{8,10},{9,11},{10,... | collective-permute-start | bytes 392 | tf_op jit(solution)/shard_map/ppermute | solution.py:550
  149.4 1.0 copy-start.19

commit v5 on v4

--- a/solution.py
+++ b/solution.py
@@ -20,7 +20,12 @@
 ROWS = 16
 LANES = 128
 UNITS = BAND // ROWS
+VMEM_BYTES = 60 * 2**20
 SHARES = 8
+
+SMEM = pl.BlockSpec(memory_space=pltpu.SMEM)
+VMEM = pl.BlockSpec(memory_space=pltpu.VMEM)
+LENGTH = pl.BlockSpec((1, 8, LANES), lambda l: (l, 0, 0))
 
 SIN_POLY = (4.4428679, -7.30744341, 3.59478797, -0.78437376)
 COS_POLY = (1.4142135, -6.97885099, 5.73946117, -1.88356298, 0.31069817)
@@ -140,11 +145,67 @@
         ),
         in_specs=[smem, smem, smem, vmem],
         out_specs=(vmem, vmem),
-        compiler_params=pltpu.CompilerParams(vmem_limit_bytes=24 * 2**20),
+        compiler_params=pltpu.CompilerParams(vmem_limit_bytes=VMEM_BYTES),
     )(where, table.reshape(waves * count, 3), wave_lengths, basis)
 
 
-def gather_rows(piece, half, waves):
+def split_kernel(half, sent, where, own_lengths, *refs):
+    parts, (low_ref, high_ref, length_ref) = refs[:-3], refs[-3:]
+    wave, waves = where[0], len(parts) + 1
+    kept = own_lengths.shape[0] - sent
+    for s in range(waves):
+        for i in range(kept):
+            if s == 0:
+                value = jnp.full((8, LANES), own_lengths[sent + i], jnp.float32)
+            else:
+                slab = parts[s - 1][2 * half].astype(jnp.float32)
+                line = 3 * (sent + i)
+                value = (slab[line : line + 1] + slab[line + 1 : line + 2]) + slab[
+                    line + 2 : line + 3
+                ]
+                value = jnp.broadcast_to(value, (8, LANES))
+            length_ref[lax.rem(wave + (waves - s), waves) * kept + i] = value
+    for s, part in enumerate(parts):
+        low_ref[s * half : (s + 1) * half] = part[:half]
+        high_ref[s * half : (s + 1) * half] = part[half : 2 * half]
+
+
+def split_parts(parts, where, wave_lengths, half, sent):
+    count = (len(parts) + 1) * (wave_lengths.shape[0] - sent)
+    slabs = jax.ShapeDtypeStruct((len(parts) * half, ROWS, LANES), parts[0].dtype)
+    return pl.pallas_call(
+        functools.partial(split_kernel, half, sent),
+        out_shape=(slabs, slabs, jax.ShapeDtypeStruct((count, 8, LANES), jnp.float32)),
+        in_specs=[SMEM, SMEM] + [VMEM] * len(parts),
+        out_specs=(VMEM,) * 3,
+        compiler_params=pltpu.CompilerParams(vmem_limit_bytes=VMEM_BYTES),
+    )(where, wave_lengths, *parts)
+
+
+def join_kernel(one_ref, two_ref, token_ref, out_ref):
+    count = one_ref.shape[0]
+    out_ref[:count] = one_ref[...]
+    out_ref[count:] = two_ref[...]
+
+
+def join(one, two, token):
+    return pl.pallas_call(
+        join_kernel,
+        out_shape=jax.ShapeDtypeStruct((2 * one.shape[0],) + one.shape[1:], one.dtype),
+        in_specs=[VMEM] * 3,
+        out_specs=VMEM,
+        compiler_params=pltpu.CompilerParams(vmem_limit_bytes=VMEM_BYTES),
+    )(one, two, token)
+
+
+def along_wave(piece, waves):
+    return [
+        lax.ppermute(piece, "wave", [(i, (i + s) % waves) for i in range(waves)])
+        for s in range(1, waves)
+    ]
+
+
+def gather_rows(halves, token):
     groups, fields = lax.axis_size("groups"), lax.axis_size("field")
 
     def swap(x, mask):
@@ -155,20 +216,16 @@
         ]
         return lax.ppermute(x, ("groups", "field"), pairs)
 
-    parts = [
-        lax.ppermute(piece, "wave", [(i, (i + s) % waves) for i in range(waves)])
-        for s in range(1, waves)
-    ]
     got = []
     for h, (one, two) in enumerate(((2, 4), (4, 2))):
-        mine = jnp.concatenate([part[h * half : (h + 1) * half] for part in parts])
-        both = jnp.concatenate([mine, swap(mine, one)])
+        mine = halves[h]
+        both = join(mine, swap(mine, one), token)
         far = swap(both, two)
         got.append((h, both, (0, one)))
         got.append((h, far, (two, one | two)))
         got.append((h, swap(both, 1), (1, one | 1)))
         got.append((h, swap(far, 1), (two | 1, one | two | 1)))
-    return parts, got
+    return got
 
 
 def spread_kernel(*refs):
@@ -197,6 +254,7 @@
             jax.ShapeDtypeStruct((m.shape[0], m.shape[1] * ROWS, m.shape[2] * ROWS), jnp.bfloat16)
             for m in matrices
         ),
+        compiler_params=pltpu.CompilerParams(vmem_limit_bytes=VMEM_BYTES),
     )(*matrices)
 
 
@@ -304,19 +362,19 @@
         product(len(CHUNKS) - 1, slice(n * width, (n + 1) * width))
 
 
-def whole_kernel(sizes, tokens, inverse_ref, place, where, *refs):
+def whole_kernel(sizes, length_ref, place, where, *refs):
     positions, modes, waves, half, slabs, keys = sizes
     parts, refs = refs[: 1 + len(keys)], refs[1 + len(keys) :]
     spread, row_ref, column_ref = refs[:3]
-    image_ref, path, opening = refs[3 + tokens : 6 + tokens]
-    basis, sems = refs[6 + tokens : 8 + tokens]
-    scratch = refs[8 + tokens :]
+    image_ref, path, opening = refs[3:6]
+    basis, sems = refs[6:8]
+    scratch = refs[8:]
 
     @pl.when(pl.program_id(0) == 0)
     def _():
         form_paths(sizes, where, place, parts, spread, path, opening, basis, sems)
 
-    inverse = inverse_ref[pl.program_id(0)]
+    inverse = 1.0 / length_ref[0, :1]
     rows = PIX
     transform(positions, rows, inverse, path, opening, row_ref, column_ref, scratch)
     first = scratch[3]
@@ -336,10 +394,10 @@
             ]
 
 
-def rows_kernel(positions, rows, inverse_ref, path, opening, row_ref, column_ref, *refs):
+def rows_kernel(positions, rows, length_ref, path, opening, row_ref, column_ref, *refs):
     image_ref, sum_ref = refs[:2]
     scratch = refs[2:]
-    inverse = inverse_ref[pl.program_id(0)]
+    inverse = 1.0 / length_ref[0, :1]
     transform(positions, rows, inverse, path, opening, row_ref, column_ref, scratch)
     first = scratch[3]
     real = jnp.dot(first[...], column_ref[0, :, :PIX], preferred_element_type=jnp.float32)
@@ -366,10 +424,6 @@
     )
 
 
-SMEM = pl.BlockSpec(memory_space=pltpu.SMEM)
-VMEM = pl.BlockSpec(memory_space=pltpu.VMEM)
-
-
 def table_specs(row_table, column_table):
     return [
         pl.BlockSpec((1,) + row_table.shape[1:], lambda l: (l, 0, 0, 0)),
@@ -377,7 +431,7 @@
     ]
 
 
-def whole_fields(own, got, spread, place, where, inverse, row_table, column_table, tokens, sizes):
+def whole_fields(own, got, spread, place, where, length, row_table, column_table, sizes):
     positions, modes, waves, half, slabs = sizes
     keys = tuple((h, masks) for h, _, masks in got)
     arrays = [array for _, array, _ in got]
@@ -387,7 +441,7 @@
     any_memory = pl.BlockSpec(memory_space=pl.ANY)
     return pl.pallas_call(
         functools.partial(
-            whole_kernel, (positions, modes, waves, half, slabs, keys), len(tokens)
+            whole_kernel, (positions, modes, waves, half, slabs, keys)
         ),
         grid=(lengths,),
         out_shape=(
@@ -395,11 +449,10 @@
             jax.ShapeDtypeStruct((units, positions * ROWS, LANES), jnp.float32),
             jax.ShapeDtypeStruct((units, ROWS, LANES), jnp.float32),
         ),
-        in_specs=[SMEM, SMEM, SMEM]
+        in_specs=[LENGTH, SMEM, SMEM]
         + [any_memory] * (1 + len(keys))
         + [VMEM]
-        + table_specs(row_table, column_table)
-        + [VMEM] * len(tokens),
+        + table_specs(row_table, column_table),
         out_specs=(pl.BlockSpec((waves, 1, share, PIX), lambda l: (0, l, 0, 0)), VMEM, VMEM),
         scratch_shapes=[
             pltpu.VMEM((waves * slabs, ROWS, LANES), jnp.bfloat16),
@@ -407,11 +460,11 @@
         ]
         + transform_scratch(positions, PIX),
         cost_estimate=transform_cost(lengths, positions, PIX),
-        compiler_params=pltpu.CompilerParams(vmem_limit_bytes=48 * 2**20),
-    )(inverse, place, where, own, *arrays, spread, row_table, column_table, *tokens)
-
-
-def row_fields(path, opening, inverse, row_table, column_table, positions):
+        compiler_params=pltpu.CompilerParams(vmem_limit_bytes=VMEM_BYTES),
+    )(length, place, where, own, *arrays, spread, row_table, column_table)
+
+
+def row_fields(path, opening, length, row_table, column_table, positions):
     lengths = row_table.shape[0]
     rows = row_table.shape[2] // 2
     return pl.pallas_call(
@@ -421,61 +474,65 @@
             jax.ShapeDtypeStruct((lengths, positions * rows, PIX), jnp.float32),
             jax.ShapeDtypeStruct((lengths, positions, PIX), jnp.float32),
         ),
-        in_specs=[SMEM, VMEM, VMEM] + table_specs(row_table, column_table),
+        in_specs=[LENGTH, VMEM, VMEM] + table_specs(row_table, column_table),
         out_specs=(
             pl.BlockSpec((1, positions * rows, PIX), lambda l: (l, 0, 0)),
             pl.BlockSpec((1, positions, PIX), lambda l: (l, 0, 0)),
         ),
         scratch_shapes=transform_scratch(positions, rows),
         cost_estimate=transform_cost(lengths, positions, rows),
-        compiler_params=pltpu.CompilerParams(vmem_limit_bytes=30 * 2**20),
-    )(inverse, path, opening, row_table, column_table)
+        compiler_params=pltpu.CompilerParams(vmem_limit_bytes=VMEM_BYTES),
+    )(length, path, opening, row_table, column_table)
 
 
 def mix_kernel(inverse_ref, weight_ref, sent_ref, image_ref, out_ref):
-    f = pl.program_id(0)
-    templates, rows = out_ref.shape[1], out_ref.shape[2]
-    blocks = []
-    for start in range(0, rows, ROWS):
-        lines = slice(start, start + ROWS)
-        blocks.append(
-            jnp.concatenate(
-                [sent_ref[l, lines] for l in range(sent_ref.shape[0])]
-                + [
-                    (image_ref[l, lines] * inverse_ref[l, f]).astype(jnp.bfloat16)
-                    for l in range(image_ref.shape[0])
-                ],
-                axis=0,
+    count, templates, rows = out_ref.shape[:3]
+    for i in range(count):
+        f = pl.program_id(0) * count + i
+        blocks = []
+        for start in range(i * rows, (i + 1) * rows, ROWS):
+            lines = slice(start, start + ROWS)
+            blocks.append(
+                jnp.concatenate(
+                    [sent_ref[l, lines] for l in range(sent_ref.shape[0])]
+                    + [
+                        (image_ref[l, lines] * inverse_ref[l, f]).astype(jnp.bfloat16)
+                        for l in range(image_ref.shape[0])
+                    ],
+                    axis=0,
+                )
             )
-        )
-    mixed = jnp.dot(
-        weight_ref[0], jnp.concatenate(blocks, axis=1), preferred_element_type=jnp.float32
-    ).astype(jnp.bfloat16)
-    for n in range(len(blocks)):
-        for j in range(templates):
-            out_ref[0, j, n * ROWS : (n + 1) * ROWS] = mixed[
-                j * ROWS : (j + 1) * ROWS, n * PIX : (n + 1) * PIX
-            ]
+        mixed = jnp.dot(
+            weight_ref[i], jnp.concatenate(blocks, axis=1), preferred_element_type=jnp.float32
+        ).astype(jnp.bfloat16)
+        for n in range(len(blocks)):
+            for j in range(templates):
+                out_ref[i, j, n * ROWS : (n + 1) * ROWS] = mixed[
+                    j * ROWS : (j + 1) * ROWS, n * PIX : (n + 1) * PIX
+                ]
 
 
 def mix(spread, inverse, sent, images, templates, rows):
     positions = spread.shape[0]
+    count = 2 if positions % 2 == 0 else 1
     return pl.pallas_call(
         mix_kernel,
-        grid=(positions,),
+        grid=(positions // count,),
         out_shape=jax.ShapeDtypeStruct((positions, templates, rows, PIX), jnp.bfloat16),
         in_specs=[
             SMEM,
-            pl.BlockSpec((1,) + spread.shape[1:], lambda f: (f, 0, 0)),
-            pl.BlockSpec((sent.shape[0], rows, PIX), lambda f: (0, f, 0)),
-            pl.BlockSpec((images.shape[0], rows, PIX), lambda f: (0, f, 0)),
+            pl.BlockSpec((count,) + spread.shape[1:], lambda f: (f, 0, 0)),
+            pl.BlockSpec((sent.shape[0], count * rows, PIX), lambda f: (0, f, 0)),
+            pl.BlockSpec((images.shape[0], count * rows, PIX), lambda f: (0, f, 0)),
         ],
-        out_specs=pl.BlockSpec((1, templates, rows, PIX), lambda f: (f, 0, 0, 0)),
+        out_specs=pl.BlockSpec((count, templates, rows, PIX), lambda f: (f, 0, 0, 0)),
+        compiler_params=pltpu.CompilerParams(vmem_limit_bytes=VMEM_BYTES),
     )(inverse, spread, sent, images)
 
 
-def table_kernel(scale_ref, y_ref, v_ref, u_ref, x_ref, row_ref, column_ref, token_ref):
-    scale = scale_ref[pl.program_id(0)]
+def table_kernel(length_ref, y_ref, v_ref, u_ref, x_ref, row_ref, column_ref, token_ref):
+    scale = (SAMPLING / (2.0 * PUP)) / length_ref[0, :1]
+    scale = jnp.concatenate([scale] * (PIX // LANES), axis=1)
     token_ref[...] = jnp.zeros_like(token_ref)
     for start in range(0, PUP, ROWS):
         s, k = half_turn((y_ref[start : start + ROWS] * v_ref[...]) * scale)
@@ -500,9 +557,8 @@
             ).astype(jnp.bfloat16)
 
 
-def tables(wave_lengths, first_row, rows):
-    lengths = wave_lengths.shape[0]
-    scale = (SAMPLING / (2.0 * PUP)) / wave_lengths
+def tables(length, first_row, rows):
+    lengths = length.shape[0]
     y = 2 * np.concatenate([band_columns(band) for band in range(BANDS)]) - PUP + 1
     v = np.arange(PIX) - PIX // 2
     u = first_row + jnp.arange(rows, dtype=jnp.int32) - PIX // 2
@@ -520,7 +576,7 @@
             jax.ShapeDtypeStruct((8, LANES), jnp.float32),
         ),
         in_specs=[
-            SMEM,
+            LENGTH,
             whole(PUP, 1),
             whole(1, PIX),
             whole(rows, 1),
@@ -534,9 +590,9 @@
         cost_estimate=pl.CostEstimate(
             flops=lengths * 30 * PUP * PIX, bytes_accessed=lengths * 4 * PUP * PIX * 2, transcendentals=0
         ),
-        compiler_params=pltpu.CompilerParams(vmem_limit_bytes=24 * 2**20),
+        compiler_params=pltpu.CompilerParams(vmem_limit_bytes=VMEM_BYTES),
     )(
-        scale,
+        length,
         jnp.asarray(y[:, None].astype(np.float32)),
         jnp.asarray(v[None, :].astype(np.float32)),
         u.astype(jnp.float32)[:, None],
@@ -545,11 +601,8 @@
 
 
 def add_over_wave(x, waves):
-    step = 1
-    while step < waves:
-        x = x + lax.ppermute(x, "wave", [(i, i ^ step) for i in range(waves)])
-        step *= 2
-    return x
+    copies = jnp.broadcast_to(x[None], (waves,) + x.shape)
+    return jnp.sum(lax.all_to_all(copies, "wave", split_axis=0, concat_axis=0, tiled=True), axis=0)
 
 
 def local(mode_basis, coef_table, table_index, wave_lengths, sed_table, template_ids):
@@ -565,18 +618,14 @@
     share = (lax.axis_index("groups") % 2) * 4 + lax.axis_index("field") % 4
     where = jnp.stack([mine, share]).astype(jnp.int32)
     own, piece = pack_rows(mode_basis, wave_lengths, pack, where, half, slabs)
-    parts, got = gather_rows(piece, half, waves)
-
-    limbs = jnp.stack([part[2 * half, : 3 * lengths, 0] for part in parts])
-    others = jnp.sum(limbs.astype(jnp.float32).reshape(waves - 1, lengths, 3), axis=2)
-    known = jnp.concatenate([wave_lengths[None], others])
-    order = (mine - jnp.arange(waves)) % waves
-    every = jnp.sum(
-        jnp.where((order[:, None] == jnp.arange(waves)[None, :])[:, :, None], known[None], 0.0),
-        axis=1,
-    )[:, sent_lengths:].reshape(-1)
-    own_row, own_column, own_token = tables(wave_lengths[:sent_lengths], 0, PIX)
-    all_row, all_column, all_token = tables(every, mine * rows, rows)
+    parts = along_wave(piece, waves)
+    low, high, every = split_parts(parts, where, wave_lengths, half, sent_lengths)
+    own_length = jnp.broadcast_to(
+        wave_lengths[:sent_lengths, None, None], (sent_lengths, 8, LANES)
+    )
+    own_row, own_column, _ = tables(own_length, 0, PIX)
+    all_row, all_column, token = tables(every, mine * rows, rows)
+    got = gather_rows((low, high), token)
 
     selector = (
         table_index[:, None] == jnp.arange(coef_table.shape[0], dtype=jnp.int32)[None, :]
@@ -605,16 +654,15 @@
         path_spread,
         place,
         where,
-        1.0 / wave_lengths[:sent_lengths],
+        own_length,
         own_row,
         own_column,
-        (all_token,),
         (positions, modes, waves, half, slabs),
     )
     sent = lax.all_to_all(spectra, "wave", split_axis=0, concat_axis=0, tiled=True)
     sent = sent.reshape(waves * sent_lengths, positions * rows, PIX)
 
-    images, sums = row_fields(path, opening, 1.0 / every, all_row, all_column, positions)
+    images, sums = row_fields(path, opening, every, all_row, all_column, positions)
     level = add_over_wave(jnp.sum(sums, axis=2), waves) / (PIX * PIX)
     return mix(mix_spread, 1.0 / (level + EPSILON), sent, images, templates, rows)
 

time: 158 us -> 182 us (1.15)
  waiting for transfers between devices: 43.3 us -> 67.9 us
  local copies, waits for them, and re-layouts: 22.7 us -> 4.89 us
  Pallas kernels: 65.5 us -> 77.2 us
  blocking collectives: 0 us -> 9.28 us
  starting transfers between devices: 21.3 us -> 16.2 us
  other arithmetic: 2.06 us -> 3.99 us
    all_to_all x1, waiting for transfers between devices: 0.01 us -> 24.6 us  [local(): lax.all_to_all(spectra, 'wave', split_axis=0, concat_axis=0, tiled=True)]
    unnamed x54 -> x28, local copies, waits for them, and re-layouts: 19.9 us -> 4.25 us
    all_to_all x0 -> x1, blocking collectives: none -> 9.28 us  [add_over_wave(): lax.all_to_all(copies, 'wave', split_axis=0, concat_axis=0, tiled=True)]
    ppermute x5 -> x3, starting transfers between devices: 11 us -> 6.11 us  [along_wave(): lax.ppermute(piece, 'wave', [(i, (i + s) % waves) for i in range(waves)])]
    pallas_call x1 -> x4, Pallas kernels: 6.76 us -> 10.9 us  [the longest x1 4.54 us: mix(): pl.pallas_call(mix_kernel, grid=(positions // count,), out_shape=jax.Shap...]
    pallas_call x1, Pallas kernels: 27.6 us -> 31.2 us  [row_fields(): pl.pallas_call(functools.partial(rows_kernel, positions, rows), grid=(len...]
    ppermute x5 -> x3, waiting for transfers between devices: 26.9 us -> 24 us  [along_wave(): lax.ppermute(piece, 'wave', [(i, (i + s) % waves) for i in range(waves)])]
    ppermute x8, waiting for transfers between devices: 16.5 us -> 19.4 us  [swap(): return lax.ppermute(x, ('groups', 'field'), pairs)]
  transfers between devices with their start and end apart: 14 -> 12, of which waited for: 7 -> 6; matrix products, arithmetic and copies ran while one was open for 4% -> 3% of each run, Pallas kernels for 23% -> 8%
where the time goes in v5:
time: 182 us; the launch traced here: 181 us
  Pallas kernels  77.2 us (42%)
  waiting for transfers between devices  67.9 us (37%)
  starting transfers between devices  16.2 us (9%)
  blocking collectives  9.28 us (5%)
  local copies, waits for them, and re-layouts  4.89 us (3%)
  other arithmetic  3.99 us (2%)
  matrix products  1.86 us (1%)
    pallas_call x1, Pallas kernels, row_fields(): pl.pallas_call(functools.partial(rows_kernel, positions, rows), grid=(len...  31.2 us
    all_to_all x1, waiting for transfers between devices, local(): lax.all_to_all(spectra, 'wave', split_axis=0, concat_axis=0, tiled=True)  24.6 us
    ppermute x3, waiting for transfers between devices, along_wave(): lax.ppermute(piece, 'wave', [(i, (i + s) % waves) for i in range(waves)])  24 us
    pallas_call x1, Pallas kernels, whole_fields(): pl.pallas_call(functools.partial(whole_kernel, (positions, modes, waves,...  20.5 us
    ppermute x8, waiting for transfers between devices, swap(): return lax.ppermute(x, ('groups', 'field'), pairs)  19.4 us
    all_to_all x1, blocking collectives, add_over_wave(): lax.all_to_all(copies, 'wave', split_axis=0, concat_axis=0, tiled=True)  9.28 us
    pallas_call x2, Pallas kernels, tables(): pl.pallas_call(table_kernel, grid=(lengths,), out_shape=(jax.ShapeDtypeSt...  8.44 us
    ppermute x8, starting transfers between devices, swap(): return lax.ppermute(x, ('groups', 'field'), pairs)  6.54 us
  transfers between devices with their start and end apart: 12, of which 6 were waited for; matrix products, arithmetic and copies ran while one was open for 3% of the time, Pallas kernels for 8%

profile of v5, /device:TPU:0, one launch (start us, length us, event | category | flops | bytes accessed | tf_op | source)
XLA Modules:
  0.0 181.4 jit_solution(6168548377137736889)
XLA Ops:
  0.0 0.0 copy-start
  0.0 0.6 pad_add_fusion.where
  0.6 4.2 %shard_map.136 = (bf16[560,16,128]{2,1,0:T(8,128)(2,1)}, bf16[71,16,128]{2,1,0:T(8,128)(2,1)}) custom-call(s32[2]{0:T(128)} %pad_add_fusion.where, s32[100,3]{1,0:T(8,128)} %constant.62.clone.table, f32[2]{0:T(128)} %own_lengths.1, bf16[22,128,512]{2,1,0:T(8,128)(2,1)} %basis.1), custom_call_target="tpu_custom_call" | custom-call | tf_op jit(solution)/shard_map/pallas_call | solution.py:140
  4.8 0.0 copy-start.10
  4.8 0.0 copy-start.11
  4.8 0.0 copy-start.12
  4.8 0.0 copy-start.7
  4.8 5.1 %collective-permute-start.2 = (bf16[71,16,128]{2,1,0:T(8,128)(2,1)}, bf16[71,16,128]{2,1,0:T(8,128)(2,1)S(1)}, u32[]{:S(2)}, u32[]{:S(2)}) collective-permute-start(bf16[71,16,128]{2,1,0:T(8,128)(2,1)} %get-tuple-element.22), channel_id=1, source_target_pairs={{0,3},{1,0},{2,1},{3,2},{4,7},{5,4},{6,5},{7,6},{8,11},{9,8},{10,9... | collective-permute-start | bytes 872456 | tf_op jit(solution)/shard_map/ppermute | solution.py:203
  9.9 0.0 collective-permute-start.1
  9.9 1.0 collective-permute-start
  10.9 6.7 %collective-permute-done.2.refs_2_ = bf16[71,16,128]{2,1,0:T(8,128)(2,1)S(1)} collective-permute-done((bf16[71,16,128]{2,1,0:T(8,128)(2,1)}, bf16[71,16,128]{2,1,0:T(8,128)(2,1)S(1)}, u32[]{:S(2)}, u32[]{:S(2)}) %collective-permute-start.2) | collective-permute-done | bytes 290848 | tf_op jit(solution)/shard_map/ppermute | solution.py:203
  17.6 17.3 %collective-permute-done.1.refs_1_ = bf16[71,16,128]{2,1,0:T(8,128)(2,1)S(1)} collective-permute-done((bf16[71,16,128]{2,1,0:T(8,128)(2,1)}, bf16[71,16,128]{2,1,0:T(8,128)(2,1)S(1)}, u32[]{:S(2)}, u32[]{:S(2)}) %collective-permute-start.1) | collective-permute-done | bytes 290848 | tf_op jit(solution)/shard_map/ppermute | solution.py:203
  34.9 0.0 collective-permute-done.refs_0_
  34.9 0.0 copy-done.4
  34.9 0.7 copy-done.5
  35.6 0.7 copy-done.6
  36.3 2.1 %shard_map.137 = (bf16[105,16,128]{2,1,0:T(8,128)(2,1)}, bf16[105,16,128]{2,1,0:T(8,128)(2,1)}, f32[4,8,128]{2,1,0:T(8,128)}) custom-call(s32[2]{0:T(128)} %pad_add_fusion.where, f32[2]{0:T(128)} %own_lengths.1, bf16[71,16,128]{2,1,0:T(8,128)(2,1)} %copy-done.6, bf16[71,16,128]{2,1,0:T(8,128)(2,1)} %copy-done.5, bf16[71,16,128]{2,1,0:T(8,128)(2,1)} %copy-done.4), custom_call_target="tpu_custom_call" | custom-call | tf_op jit(solution)/shard_map/pallas_call | solution.py:176
  38.4 1.5 collective-permute-start.3
  39.9 1.5 collective-permute-start.7
  41.4 0.6 add_convert_fusion.1.u_ref
  42.0 5.0 %shard_map.138 = (bf16[4,4,128,256]{3,2,1,0:T(8,128)(2,1)}, bf16[4,1024,512]{2,1,0:T(8,128)(2,1)}, f32[8,128]{1,0:T(8,128)}) custom-call(f32[4,8,128]{2,1,0:T(8,128)} %get-tuple-element.23.length_ref, f32[512,1]{1,0:T(8,128)} %constant.63.clone.y_ref, f32[1,256]{1,0:T(1,128)} %constant.64.clone.v_ref, f32[64,1]{1,0:T(8,128)} %add_convert_fusion.1.u_ref, ...), custom_call_target="tpu_custom_call" | custom-call | flops 15728640 | bytes 4194304 | tf_op jit(solution)/shard_map/pallas_call | solution.py:570
  47.0 2.4 %collective-permute-done.3.two_ref = bf16[105,16,128]{2,1,0:T(8,128)(2,1)S(1)} collective-permute-done((bf16[105,16,128]{2,1,0:T(8,128)(2,1)}, bf16[105,16,128]{2,1,0:T(8,128)(2,1)S(1)}, u32[]{:S(2)}, u32[]{:S(2)}) %collective-permute-start.3) | collective-permute-done | bytes 430112 | tf_op jit(solution)/shard_map/ppermute | solution.py:217
  49.4 0.7 copy-done.3
  50.1 2.1 %shard_map.139.refs_1_ = bf16[210,16,128]{2,1,0:T(8,128)(2,1)} custom-call(bf16[105,16,128]{2,1,0:T(8,128)(2,1)} %get-tuple-element.25.one_ref, bf16[105,16,128]{2,1,0:T(8,128)(2,1)} %copy-done.3, f32[8,128]{1,0:T(8,128)} %get-tuple-element.26.token_ref), custom_call_target="tpu_custom_call" | custom-call | tf_op jit(solution)/shard_map/pallas_call | solution.py:192
  52.2 1.5 collective-permute-start.4
  53.8 0.0 collective-permute-done.7.two_ref
  53.8 0.8 copy-done.2
  54.5 2.1 %shard_map.140.refs_5_ = bf16[210,16,128]{2,1,0:T(8,128)(2,1)} custom-call(bf16[105,16,128]{2,1,0:T(8,128)(2,1)} %get-tuple-element.27.one_ref, bf16[105,16,128]{2,1,0:T(8,128)(2,1)} %copy-done.2, f32[8,128]{1,0:T(8,128)} %get-tuple-element.26.token_ref), custom_call_target="tpu_custom_call" | custom-call | tf_op jit(solution)/shard_map/pallas_call | solution.py:192
  56.6 1.5 collective-permute-start.8
  58.1 0.0 collective-permute-start.5
  58.1 0.5 collective-permute-start.9
  58.6 12.9 %collective-permute-done.4.refs_2_ = bf16[210,16,128]{2,1,0:T(8,128)(2,1)S(1)} collective-permute-done((bf16[210,16,128]{2,1,0:T(8,128)(2,1)}, bf16[210,16,128]{2,1,0:T(8,128)(2,1)S(1)}, u32[]{:S(2)}, u32[]{:S(2)}) %collective-permute-start.4) | collective-permute-done | bytes 860192 | tf_op jit(solution)/shard_map/ppermute | solution.py:217
  71.5 0.0 collective-permute-start.6
  71.5 4.1 %collective-permute-done.8.refs_6_ = bf16[210,16,128]{2,1,0:T(8,128)(2,1)S(1)} collective-permute-done((bf16[210,16,128]{2,1,0:T(8,128)(2,1)}, bf16[210,16,128]{2,1,0:T(8,128)(2,1)S(1)}, u32[]{:S(2)}, u32[]{:S(2)}) %collective-permute-start.8) | collective-permute-done | bytes 860192 | tf_op jit(solution)/shard_map/ppermute | solution.py:217
  75.6 0.0 collective-permute-start.10
  75.6 0.0 copy-done.10
  75.6 0.0 copy-done.11
  75.7 1.1 fusion.6
  76.8 0.1 copy.30
  76.9 0.1 copy.31
  77.0 0.7 pad_maximum_fusion.refs_1_
  77.7 0.0 copy-done
  77.7 0.0 copy-done.12
  77.7 0.8 fusion.refs_0_
  78.5 2.0 %shard_map.141 = (bf16[1,128,352]{2,1,0:T(8,128)(2,1)}, bf16[8,128,128]{2,1,0:T(8,128)(2,1)}) custom-call(bf16[1,8,22]{2,1,0:T(8,128)(2,1)} %fusion.refs_0_, bf16[8,8,8]{2,1,0:T(8,128)(2,1)} %pad_maximum_fusion.refs_1_), custom_call_target="tpu_custom_call" | custom-call | tf_op jit(solution)/shard_map/pallas_call | solution.py:251
  80.5 0.7 add_convert_fusion.u_ref
  81.2 0.0 copy-done.7
  81.2 0.6 broadcast_in_dim.9.length_ref
  81.8 3.5 %shard_map.142 = (bf16[1,4,512,256]{3,2,1,0:T(8,128)(2,1)}, bf16[1,1024,512]{2,1,0:T(8,128)(2,1)}, f32[8,128]{1,0:T(8,128)}) custom-call(f32[1,8,128]{2,1,0:T(8,128)} %broadcast_in_dim.9.length_ref, f32[512,1]{1,0:T(8,128)} %constant.63.clone.y_ref, f32[1,256]{1,0:T(1,128)} %constant.64.clone.v_ref, f32[256,1]{1,0:T(8,128)} %add_convert_fusion.u_ref, ...), custom_call_target="tpu_custom_call" | custom-call | flops 3932160 | bytes 1048576 | tf_op jit(solution)/shard_map/pallas_call | solution.py:570
  85.2 0.0 collective-permute-done.5.refs_3_
  85.3 0.0 collective-permute-done.9.refs_7_
  85.3 0.0 collective-permute-done.6.refs_4_
  85.3 0.0 collective-permute-done.10.refs_8_
  85.3 0.0 copy-done.8
  85.3 0.0 copy-done.9
  85.3 20.5 %shard_map.143 = (bf16[4,1,512,256]{3,2,1,0:T(8,128)(2,1)}, f32[96,128,128]{2,1,0:T(8,128)}, f32[96,16,128]{2,1,0:T(8,128)}) custom-call(f32[1,8,128]{2,1,0:T(8,128)} %broadcast_in_dim.9.length_ref, s32[96,4]{1,0:T(8,128)} %constant.66.clone.place, s32[2]{0:T(128)} %pad_add_fusion.where, bf16[560,16,128]{2,1,0:T(8,128)(2,1)} %get-tuple-element.24.refs_0_, ...), custom_call_target="tpu_custom_call" | custom-call | flops 7242450944 | bytes 8388608 | tf_op jit(solution)/shard_map/pallas_call | solution.py:442
  105.8 31.2 %shard_map.144 = (f32[4,512,256]{2,1,0:T(8,128)}, f32[4,8,256]{2,1,0:T(8,128)}) custom-call(f32[4,8,128]{2,1,0:T(8,128)} %get-tuple-element.23.length_ref, f32[96,128,128]{2,1,0:T(8,128)} %get-tuple-element.31.path, f32[96,16,128]{2,1,0:T(8,128)} %get-tuple-element.32.opening, bf16[4,4,128,256]{3,2,1,0:T(8,128)(2,1)} %get-tuple-element.33.row_ref, ...), custom_call_target="tpu_custom_call" | custom-call | flops 9642450944 | bytes 8388608 | tf_op jit(solution)/shard_map/pallas_call | solution.py:470
  137.0 0.8 reduce_sum.28
  137.8 9.3 %all_to_all.10 = f32[4,4,8]{2,1,0:T(4,128)S(1)} all-to-all(f32[4,4,8]{2,1,0:T(4,128)S(1)} %broadcast_in_dim.11), channel_id=1, replica_groups=mesh['groups'=2,'field'=4,'wave'=4] {'wave'}, dimensions={0} | all-to-all | bytes 1024 | tf_op jit(solution)/shard_map/all_to_all | solution.py:605
  147.1 3.5 %all-to-all-start.1 = ((bf16[4,1,512,256]{3,2,1,0:T(8,128)(2,1)}), bf16[4,1,512,256]{3,2,1,0:T(8,128)(2,1)S(1)}, u32[]{:S(2)}, u32[]{:S(2)}) async-start(bf16[4,1,512,256]{3,2,1,0:T(8,128)(2,1)} %get-tuple-element.37), calls=%async_computation.1 | async-start | bytes 2097152 | tf_op jit(solution)/shard_map/all_to_all | solution.py:662
  150.7 0.6 add_divide_fusion.inverse_ref
  151.3 24.6 %all-to-all-done.1 = bf16[4,1,512,256]{3,2,1,0:T(8,128)(2,1)S(1)} async-done(((bf16[4,1,512,256]{3,2,1,0:T(8,128)(2,1)}), bf16[4,1,512,256]{3,2,1,0:T(8,128)(2,1)S(1)}, u32[]{:S(2)}, u32[]{:S(2)}) %all-to-all-start.1) | async-done | bytes 1048608 | tf_op jit(solution)/shard_map/all_to_all | solution.py:662
  175.8 1.0 copy-done.1
  176.9 4.5 %shard_map.145 = bf16[8,8,64,256]{3,2,1,0:T(8,128)(2,1)} custom-call(f32[4,8]{1,0:T(4,128)} %add_divide_fusion.inverse_ref, bf16[8,128,128]{2,1,0:T(8,128)(2,1)} %get-tuple-element.36.weight_ref, bf16[4,512,256]{2,1,0:T(8,128)(2,1)} %bitcast.16, f32[4,512,256]{2,1,0:T(8,128)} %get-tuple-element.38.image_ref), custom_call_target="tpu_custom_call" | custom-call | tf_op jit(solution)/shard_map/pallas_call | solution.py:518
  (13 shorter events, 0.1 us)
Async XLA Ops:
  0.0 77.7 %copy-start = (bf16[4096,22]{0,1:T(8,128)(2,1)S(1)}, bf16[4096,22]{0,1:T(8,128)(2,1)}, u32[]{:S(2)}) copy-start(bf16[4096,22]{0,1:T(8,128)(2,1)} %param.15) | copy-start | bytes 540676
  4.8 70.9 %copy-start.10 = (f32[1024,8]{0,1:T(8,128)S(1)}, f32[1024,8]{0,1:T(8,128)}, u32[]{:S(2)}) copy-start(f32[1024,8]{0,1:T(8,128)} %param.18) | copy-start | bytes 98308
  4.8 70.9 %copy-start.11 = (s32[8,8]{1,0:T(8,128)S(1)}, s32[8,8]{1,0:T(8,128)}, u32[]{:S(2)}) copy-start(s32[8,8]{1,0:T(8,128)} %param.19) | copy-start | bytes 772
  4.8 73.0 %copy-start.12 = (s32[8]{0:T(128)S(1)}, s32[8]{0:T(128)}, u32[]{:S(2)}) copy-start(s32[8]{0:T(128)} %param.16) | copy-start | bytes 100
  4.8 76.4 %copy-start.7 = (f32[2]{0:T(128)S(1)}, f32[2]{0:T(128)}, u32[]{:S(2)}) copy-start(f32[2]{0:T(128)} %own_lengths.1) | copy-start | bytes 28
  4.8 12.8 %collective-permute-start.2 = (bf16[71,16,128]{2,1,0:T(8,128)(2,1)}, bf16[71,16,128]{2,1,0:T(8,128)(2,1)S(1)}, u32[]{:S(2)}, u32[]{:S(2)}) collective-permute-start(bf16[71,16,128]{2,1,0:T(8,128)(2,1)} %get-tuple-element.22), channel_id=1, source_target_pairs={{0,3},{1,0},{2,1},{3,2},{4,7},{5,4},{6,5},{7,6},{8,11},{9,8},{10,9... | collective-permute-start | bytes 872456 | tf_op jit(solution)/shard_map/ppermute | solution.py:203
  9.9 25.0 %collective-permute-start.1 = (bf16[71,16,128]{2,1,0:T(8,128)(2,1)}, bf16[71,16,128]{2,1,0:T(8,128)(2,1)S(1)}, u32[]{:S(2)}, u32[]{:S(2)}) collective-permute-start(bf16[71,16,128]{2,1,0:T(8,128)(2,1)} %get-tuple-element.22), channel_id=1, source_target_pairs={{0,2},{1,3},{2,0},{3,1},{4,6},{5,7},{6,4},{7,5},{8,10},{9,11},{10,... | collective-permute-start | bytes 872456 | tf_op jit(solution)/shard_map/ppermute | solution.py:203
  9.9 25.0 %collective-permute-start = (bf16[71,16,128]{2,1,0:T(8,128)(2,1)}, bf16[71,16,128]{2,1,0:T(8,128)(2,1)S(1)}, u32[]{:S(2)}, u32[]{:S(2)}) collective-permute-start(bf16[71,16,128]{2,1,0:T(8,128)(2,1)} %get-tuple-element.22), channel_id=1, source_target_pairs={{0,1},{1,2},{2,3},{3,0},{4,5},{5,6},{6,7},{7,4},{8,9},{9,10},{10,1... | collective-permute-start | bytes 872456 | tf_op jit(solution)/shard_map/ppermute | solution.py:203
  17.6 17.3 %copy-start.4 = (bf16[71,16,128]{2,1,0:T(8,128)(2,1)}, bf16[71,16,128]{2,1,0:T(8,128)(2,1)S(1)}, u32[]{:S(2)}) copy-start(bf16[71,16,128]{2,1,0:T(8,128)(2,1)S(1)} %collective-permute-done.2.refs_2_) | copy-start | bytes 872452
  34.9 0.7 copy-start.5
  35.6 0.7 copy-start.6
  38.4 11.0 %collective-permute-start.3 = (bf16[105,16,128]{2,1,0:T(8,128)(2,1)}, bf16[105,16,128]{2,1,0:T(8,128)(2,1)S(1)}, u32[]{:S(2)}, u32[]{:S(2)}) collective-permute-start(bf16[105,16,128]{2,1,0:T(8,128)(2,1)} %get-tuple-element.25.one_ref), channel_id=1, source_target_pairs={{0,8},{4,12},{8,0},{12,4},{16,24},{20,28},{24,16},{28,20},{1,9},{5... | collective-permute-start | bytes 1290248 | tf_op jit(solution)/shard_map/ppermute | solution.py:217
  39.9 13.9 %collective-permute-start.7 = (bf16[105,16,128]{2,1,0:T(8,128)(2,1)}, bf16[105,16,128]{2,1,0:T(8,128)(2,1)S(1)}, u32[]{:S(2)}, u32[]{:S(2)}) collective-permute-start(bf16[105,16,128]{2,1,0:T(8,128)(2,1)} %get-tuple-element.27.one_ref), channel_id=1, source_target_pairs={{0,16},{4,20},{8,24},{12,28},{16,0},{20,4},{24,8},{28,12},{1,17},{... | collective-permute-start | bytes 1290248 | tf_op jit(solution)/shard_map/ppermute | solution.py:217
  49.4 0.7 copy-start.3
  52.2 19.3 %collective-permute-start.4 = (bf16[210,16,128]{2,1,0:T(8,128)(2,1)}, bf16[210,16,128]{2,1,0:T(8,128)(2,1)S(1)}, u32[]{:S(2)}, u32[]{:S(2)}) collective-permute-start(bf16[210,16,128]{2,1,0:T(8,128)(2,1)} %shard_map.139.refs_1_), channel_id=1, source_target_pairs={{0,16},{4,20},{8,24},{12,28},{16,0},{20,4},{24,8},{28,12},{1,17},{... | collective-permute-start | bytes 2580488 | tf_op jit(solution)/shard_map/ppermute | solution.py:217
  53.8 0.8 copy-start.2
  56.6 19.0 %collective-permute-start.8 = (bf16[210,16,128]{2,1,0:T(8,128)(2,1)}, bf16[210,16,128]{2,1,0:T(8,128)(2,1)S(1)}, u32[]{:S(2)}, u32[]{:S(2)}) collective-permute-start(bf16[210,16,128]{2,1,0:T(8,128)(2,1)} %shard_map.140.refs_5_), channel_id=1, source_target_pairs={{0,8},{4,12},{8,0},{12,4},{16,24},{20,28},{24,16},{28,20},{1,9},{5... | collective-permute-start | bytes 2580488 | tf_op jit(solution)/shard_map/ppermute | solution.py:217
  58.1 27.1 %collective-permute-start.5 = (bf16[210,16,128]{2,1,0:T(8,128)(2,1)}, bf16[210,16,128]{2,1,0:T(8,128)(2,1)}, u32[]{:S(2)}, u32[]{:S(2)}) collective-permute-start(bf16[210,16,128]{2,1,0:T(8,128)(2,1)} %shard_map.139.refs_1_), channel_id=1, source_target_pairs={{0,4},{4,0},{8,12},{12,8},{16,20},{20,16},{24,28},{28,24},{1,5},{5... | collective-permute-start | bytes 2580488 | tf_op jit(solution)/shard_map/ppermute | solution.py:217
  58.1 27.1 %collective-permute-start.9 = (bf16[210,16,128]{2,1,0:T(8,128)(2,1)}, bf16[210,16,128]{2,1,0:T(8,128)(2,1)}, u32[]{:S(2)}, u32[]{:S(2)}) collective-permute-start(bf16[210,16,128]{2,1,0:T(8,128)(2,1)} %shard_map.140.refs_5_), channel_id=1, source_target_pairs={{0,4},{4,0},{8,12},{12,8},{16,20},{20,16},{24,28},{28,24},{1,5},{5... | collective-permute-start | bytes 2580488 | tf_op jit(solution)/shard_map/ppermute | solution.py:217
  71.5 13.8 %copy-start.8 = (bf16[210,16,128]{2,1,0:T(8,128)(2,1)}, bf16[210,16,128]{2,1,0:T(8,128)(2,1)S(1)}, u32[]{:S(2)}) copy-start(bf16[210,16,128]{2,1,0:T(8,128)(2,1)S(1)} %collective-permute-done.4.refs_2_) | copy-start | bytes 2580484
  71.5 13.7 %collective-permute-start.6 = (bf16[210,16,128]{2,1,0:T(8,128)(2,1)S(1)}, bf16[210,16,128]{2,1,0:T(8,128)(2,1)}, u32[]{:S(2)}, u32[]{:S(2)}) collective-permute-start(bf16[210,16,128]{2,1,0:T(8,128)(2,1)S(1)} %collective-permute-done.4.refs_2_), channel_id=1, source_target_pairs={{0,4},{4,0},{8,12},{12,8},{16,20},{20,16},{24,28},{28,24},{1,5},{5... | collective-permute-start | bytes 2580488 | tf_op jit(solution)/shard_map/ppermute | solution.py:217
  75.6 9.7 %copy-start.9 = (bf16[210,16,128]{2,1,0:T(8,128)(2,1)}, bf16[210,16,128]{2,1,0:T(8,128)(2,1)S(1)}, u32[]{:S(2)}) copy-start(bf16[210,16,128]{2,1,0:T(8,128)(2,1)S(1)} %collective-permute-done.8.refs_6_) | copy-start | bytes 2580484
  75.6 9.6 %collective-permute-start.10 = (bf16[210,16,128]{2,1,0:T(8,128)(2,1)S(1)}, bf16[210,16,128]{2,1,0:T(8,128)(2,1)}, u32[]{:S(2)}, u32[]{:S(2)}) collective-permute-start(bf16[210,16,128]{2,1,0:T(8,128)(2,1)S(1)} %collective-permute-done.8.refs_6_), channel_id=1, source_target_pairs={{0,4},{4,0},{8,12},{12,8},{16,20},{20,16},{24,28},{28,24},{1,5},{5... | collective-permute-start | bytes 2580488 | tf_op jit(solution)/shard_map/ppermute | solution.py:217
  147.1 28.7 %all-to-all-start.1 = ((bf16[4,1,512,256]{3,2,1,0:T(8,128)(2,1)}), bf16[4,1,512,256]{3,2,1,0:T(8,128)(2,1)S(1)}, u32[]{:S(2)}, u32[]{:S(2)}) async-start(bf16[4,1,512,256]{3,2,1,0:T(8,128)(2,1)} %get-tuple-element.37), calls=%async_computation.1 | async-start | bytes 2097152 | tf_op jit(solution)/shard_map/all_to_all | solution.py:662
  175.8 1.0 copy-start.1

commit v6 on v5

--- a/solution.py
+++ b/solution.py
@@ -25,7 +25,6 @@
 
 SMEM = pl.BlockSpec(memory_space=pltpu.SMEM)
 VMEM = pl.BlockSpec(memory_space=pltpu.VMEM)
-LENGTH = pl.BlockSpec((1, 8, LANES), lambda l: (l, 0, 0))
 
 SIN_POLY = (4.4428679, -7.30744341, 3.59478797, -0.78437376)
 COS_POLY = (1.4142135, -6.97885099, 5.73946117, -1.88356298, 0.31069817)
@@ -62,23 +61,28 @@
     return bool(np.any((radius <= PUP * PUP) & (radius >= INNER * INNER)))
 
 
-CHUNKS = [
-    (band, rows)
-    for band in range(BANDS)
-    for rows in range(BANDS)
-    if any(unit_open(row, band) for row in band_rows(rows))
-]
+STAGES = ((0, 3), (1, 2))
+WIDE = BANDS // len(STAGES) * LANES
+
+
+def chunks_of(stage):
+    return [
+        (band, rows)
+        for band in STAGES[stage]
+        for rows in range(BANDS)
+        if any(unit_open(row, band) for row in band_rows(rows))
+    ]
 
 
 @functools.lru_cache(None)
-def layout(waves, modes):
+def layout(waves, modes, stage):
     per = PUP // waves
     lists = []
     for wave in range(waves):
         lists.append(
             [
                 (band, row)
-                for band in range(BANDS)
+                for band in STAGES[stage]
                 for row in range(wave * per, (wave + 1) * per, ROWS)
                 if unit_open(row, band)
             ]
@@ -91,8 +95,9 @@
         for i, (band, row) in enumerate(one):
             columns = band_columns(band)
             pack[wave, i] = (columns[0] // LANES * LANES, columns[64] // LANES * LANES, row - wave * per)
-    place = np.zeros((len(CHUNKS) * UNITS, 4), np.int32)
-    for c, (band, rows) in enumerate(CHUNKS):
+    chunks = chunks_of(stage)
+    place = np.zeros((len(chunks) * UNITS, 4), np.int32)
+    for c, (band, rows) in enumerate(chunks):
         columns = band_columns(band)
         for j, row in enumerate(band_rows(rows)):
             wave = row // per
@@ -100,10 +105,10 @@
             if (band, row) in lists[wave]:
                 slab = wave * slabs + lists[wave].index((band, row)) * modes
             place[c * UNITS + j] = (slab, row, columns[0], columns[64] - 64)
-    return count, half, slabs, pack, place
-
-
-def pack_kernel(count, modes, half, where, table, lengths, basis, own, piece):
+    return half, slabs, pack, place
+
+
+def pack_kernel(count, modes, half, with_lengths, where, table, lengths, basis, own, piece):
     left = lax.broadcasted_iota(jnp.int32, (ROWS, LANES), 1) < 64
     wave, share = where[0], where[1]
 
@@ -121,6 +126,8 @@
     for n in range(count * modes, own.shape[0]):
         own[n] = jnp.zeros((ROWS, LANES), own.dtype)
     piece[: 2 * half] = own[pl.ds(share * (2 * half), 2 * half)]
+    if not with_lengths:
+        return
     line = lax.broadcasted_iota(jnp.int32, (ROWS, LANES), 0)
     slab = jnp.zeros((ROWS, LANES), jnp.float32)
     for i in range(lengths.shape[0]):
@@ -132,16 +139,16 @@
     piece[2 * half] = slab.astype(piece.dtype)
 
 
-def pack_rows(basis, wave_lengths, table, where, half, slabs):
+def pack_rows(basis, wave_lengths, table, where, half, slabs, with_lengths):
     modes = basis.shape[0]
     waves, count, _ = table.shape
     smem = pl.BlockSpec(memory_space=pltpu.SMEM)
     vmem = pl.BlockSpec(memory_space=pltpu.VMEM)
     return pl.pallas_call(
-        functools.partial(pack_kernel, count, modes, half),
+        functools.partial(pack_kernel, count, modes, half, with_lengths),
         out_shape=(
             jax.ShapeDtypeStruct((slabs, ROWS, LANES), basis.dtype),
-            jax.ShapeDtypeStruct((2 * half + 1, ROWS, LANES), basis.dtype),
+            jax.ShapeDtypeStruct((2 * half + int(with_lengths), ROWS, LANES), basis.dtype),
         ),
         in_specs=[smem, smem, smem, vmem],
         out_specs=(vmem, vmem),
@@ -149,9 +156,9 @@
     )(where, table.reshape(waves * count, 3), wave_lengths, basis)
 
 
-def split_kernel(half, sent, where, own_lengths, *refs):
-    parts, (low_ref, high_ref, length_ref) = refs[:-3], refs[-3:]
-    wave, waves = where[0], len(parts) + 1
+def split_kernel(half, sent, parts_count, where, own_lengths, *refs):
+    parts, (low_ref, high_ref, length_ref) = refs[:parts_count], refs[-3:]
+    wave, waves = where[0], parts_count + 1
     kept = own_lengths.shape[0] - sent
     for s in range(waves):
         for i in range(kept):
@@ -170,32 +177,38 @@
         high_ref[s * half : (s + 1) * half] = part[half : 2 * half]
 
 
-def split_parts(parts, where, wave_lengths, half, sent):
+def split_parts(parts, where, wave_lengths, half, sent, tokens):
     count = (len(parts) + 1) * (wave_lengths.shape[0] - sent)
     slabs = jax.ShapeDtypeStruct((len(parts) * half, ROWS, LANES), parts[0].dtype)
     return pl.pallas_call(
-        functools.partial(split_kernel, half, sent),
+        functools.partial(split_kernel, half, sent, len(parts)),
         out_shape=(slabs, slabs, jax.ShapeDtypeStruct((count, 8, LANES), jnp.float32)),
-        in_specs=[SMEM, SMEM] + [VMEM] * len(parts),
+        in_specs=[SMEM, SMEM] + [VMEM] * (len(parts) + len(tokens)),
         out_specs=(VMEM,) * 3,
         compiler_params=pltpu.CompilerParams(vmem_limit_bytes=VMEM_BYTES),
-    )(where, wave_lengths, *parts)
-
-
-def join_kernel(one_ref, two_ref, token_ref, out_ref):
-    count = one_ref.shape[0]
-    out_ref[:count] = one_ref[...]
-    out_ref[count:] = two_ref[...]
-
-
-def join(one, two, token):
+    )(where, wave_lengths, *parts, *tokens)
+
+
+def join_kernel(count, *refs):
+    start = 0
+    for one in refs[:count]:
+        refs[-2][start : start + one.shape[0]] = one[...]
+        start += one.shape[0]
+    refs[-1][...] = jnp.zeros_like(refs[-1])
+
+
+def join(arrays, tokens):
+    long = sum(one.shape[0] for one in arrays)
     return pl.pallas_call(
-        join_kernel,
-        out_shape=jax.ShapeDtypeStruct((2 * one.shape[0],) + one.shape[1:], one.dtype),
-        in_specs=[VMEM] * 3,
-        out_specs=VMEM,
+        functools.partial(join_kernel, len(arrays)),
+        out_shape=(
+            jax.ShapeDtypeStruct((long,) + arrays[0].shape[1:], arrays[0].dtype),
+            jax.ShapeDtypeStruct((8, LANES), jnp.float32),
+        ),
+        in_specs=[VMEM] * (len(arrays) + len(tokens)),
+        out_specs=(VMEM, VMEM),
         compiler_params=pltpu.CompilerParams(vmem_limit_bytes=VMEM_BYTES),
-    )(one, two, token)
+    )(*arrays, *tokens)
 
 
 def along_wave(piece, waves):
@@ -205,21 +218,22 @@
     ]
 
 
-def gather_rows(halves, token):
+def swap(x, mask):
     groups, fields = lax.axis_size("groups"), lax.axis_size("field")
-
-    def swap(x, mask):
-        pairs = [
-            (g * fields + f, (g ^ (mask >> 2)) * fields + (f ^ (mask & 3)))
-            for g in range(groups)
-            for f in range(fields)
-        ]
-        return lax.ppermute(x, ("groups", "field"), pairs)
-
+    pairs = [
+        (g * fields + f, (g ^ (mask >> 2)) * fields + (f ^ (mask & 3)))
+        for g in range(groups)
+        for f in range(fields)
+    ]
+    return lax.ppermute(x, ("groups", "field"), pairs)
+
+
+def gather_halves(halves, token):
     got = []
+    tokens = []
     for h, (one, two) in enumerate(((2, 4), (4, 2))):
         mine = halves[h]
-        both = join(mine, swap(mine, one), token)
+        both, done = join([mine, swap(mine, one)], [token])
         far = swap(both, two)
         got.append((h, both, (0, one)))
         got.append((h, far, (two, one | two)))
@@ -228,9 +242,19 @@
     return got
 
 
+def gather_direct(mine):
+    got = [(None, mine, (0,)), (None, swap(mine, 1), (1,))]
+    for mask in (6, 2, 4):
+        there = swap(mine, mask)
+        got.append((None, there, (mask,)))
+        got.append((None, swap(there, 1), (mask | 1,)))
+    return got
+
+
 def spread_kernel(*refs):
     count = len(refs) // 2
-    for small_ref, big_ref in zip(refs[:count], refs[count:]):
+    refs[-1][...] = jnp.zeros_like(refs[-1])
+    for small_ref, big_ref in zip(refs[:count], refs[count:-1]):
         _, many, wide = small_ref.shape
         tall, long = many * ROWS, wide * ROWS
         down = lax.broadcasted_iota(jnp.int32, (tall, many), 0) // ROWS
@@ -253,13 +277,15 @@
         out_shape=tuple(
             jax.ShapeDtypeStruct((m.shape[0], m.shape[1] * ROWS, m.shape[2] * ROWS), jnp.bfloat16)
             for m in matrices
-        ),
+        )
+        + (jax.ShapeDtypeStruct((8, LANES), jnp.float32),),
         compiler_params=pltpu.CompilerParams(vmem_limit_bytes=VMEM_BYTES),
     )(*matrices)
 
 
 def form_paths(sizes, where, place, parts, spread, path, opening, basis, sems):
     positions, modes, waves, half, slabs, keys = sizes
+    length = 2 * half if keys[0][0] is None else half
     wave, share = where[0], where[1]
     copies = [pltpu.make_async_copy(parts[0], basis.at[pl.ds(wave * slabs, slabs)], sems.at[0])]
     n = 1
@@ -267,11 +293,11 @@
         for m, mask in enumerate(masks):
             for s in range(1, waves):
                 source = lax.rem(wave + (waves - s), waves)
-                start = source * slabs + (share ^ mask) * (2 * half) + h * half
+                start = source * slabs + (share ^ mask) * (2 * half) + (h or 0) * half
                 copies.append(
                     pltpu.make_async_copy(
-                        part.at[pl.ds((m * (waves - 1) + s - 1) * half, half)],
-                        basis.at[pl.ds(start, half)],
+                        part.at[pl.ds((m * (waves - 1) + s - 1) * length, length)],
+                        basis.at[pl.ds(start, length)],
                         sems.at[n],
                     )
                 )
@@ -306,36 +332,38 @@
                 )
         return carry
 
-    lax.fori_loop(0, len(CHUNKS), chunk, 0)
-
-
-def transform(positions, rows, inverse, path, opening, row_ref, column_ref, scratch):
-    pupils, total, first = scratch[:2], scratch[2], scratch[3]
+    lax.fori_loop(0, place.shape[0] // UNITS, chunk, 0)
+
+
+def transform(stage, positions, rows, inverse, path, opening, row_ref, first, scratch):
+    pupils, total = scratch[:2], scratch[2]
+    chunks = chunks_of(stage)
     batch = max(1, positions // 2)
     width = 2 * positions * LANES // UNITS
 
     def finish(band, columns, value):
+        start = STAGES[stage].index(band) * LANES
         for f in range(columns.start // LANES, columns.stop // LANES):
             lanes = slice(f * LANES - columns.start, (f + 1) * LANES - columns.start)
             for part in range(2):
                 first[
                     f * rows : (f + 1) * rows,
-                    part * PUP + band * LANES : part * PUP + (band + 1) * LANES,
+                    part * WIDE + start : part * WIDE + start + LANES,
                 ] = value[part * rows : (part + 1) * rows, lanes].astype(jnp.bfloat16)
 
     def product(c, columns):
-        band, rows_band = CHUNKS[c]
+        band, rows_band = chunks[c]
         value = jnp.dot(
             row_ref[0, rows_band], pupils[c % 2][:, columns], preferred_element_type=jnp.float32
         )
-        if c > 0 and CHUNKS[c - 1][0] == band:
+        if c > 0 and chunks[c - 1][0] == band:
             value = value + total[:, columns]
-        if c + 1 < len(CHUNKS) and CHUNKS[c + 1][0] == band:
+        if c + 1 < len(chunks) and chunks[c + 1][0] == band:
             total[:, columns] = value
         else:
             finish(band, columns, value)
 
-    for c, (band, rows_band) in enumerate(CHUNKS):
+    for c, (band, rows_band) in enumerate(chunks):
         pupil = pupils[c % 2]
         for j, row in enumerate(band_rows(rows_band)):
             real_lines = slice(2 * ROWS * j, 2 * ROWS * j + ROWS)
@@ -359,16 +387,31 @@
             if c > 0 and j % 2 == 1:
                 product(c - 1, slice(j // 2 * width, (j // 2 + 1) * width))
     for n in range(positions * LANES // width):
-        product(len(CHUNKS) - 1, slice(n * width, (n + 1) * width))
-
-
-def whole_kernel(sizes, length_ref, place, where, *refs):
+        product(len(chunks) - 1, slice(n * width, (n + 1) * width))
+
+
+def columns_of(first_a, first_b, column_ref):
+    out = []
+    for part in range(2):
+        lanes = slice(part * PIX, (part + 1) * PIX)
+        out.append(
+            jnp.dot(first_a, column_ref[0, : 2 * WIDE, lanes], preferred_element_type=jnp.float32)
+            + jnp.dot(
+                first_b, column_ref[0, 2 * WIDE :, lanes], preferred_element_type=jnp.float32
+            )
+        )
+    return out
+
+
+def whole_kernel(stage, sizes, tokens, length_ref, place, where, *refs):
     positions, modes, waves, half, slabs, keys = sizes
+    last = stage == len(STAGES) - 1
     parts, refs = refs[: 1 + len(keys)], refs[1 + len(keys) :]
-    spread, row_ref, column_ref = refs[:3]
-    image_ref, path, opening = refs[3:6]
-    basis, sems = refs[6:8]
-    scratch = refs[8:]
+    spread, row_ref, refs = refs[0], refs[1], refs[2:]
+    if last:
+        column_ref, before, refs = refs[0], refs[1], refs[2:]
+    out_ref, path, opening, basis, sems = refs[tokens : tokens + 5]
+    scratch = refs[tokens + 5 :]
 
     @pl.when(pl.program_id(0) == 0)
     def _():
@@ -376,32 +419,37 @@
 
     inverse = 1.0 / length_ref[0, :1]
     rows = PIX
-    transform(positions, rows, inverse, path, opening, row_ref, column_ref, scratch)
-    first = scratch[3]
+    first = scratch[3] if last else out_ref.at[0]
+    transform(stage, positions, rows, inverse, path, opening, row_ref, first, scratch)
+    if not last:
+        return
     share = rows // waves
     for f in range(positions):
-        lines = first[f * rows : (f + 1) * rows]
-        real = jnp.dot(lines, column_ref[0, :, :PIX], preferred_element_type=jnp.float32)
-        imag = jnp.dot(lines, column_ref[0, :, PIX:], preferred_element_type=jnp.float32)
+        lines = slice(f * rows, (f + 1) * rows)
+        real, imag = columns_of(before[0, lines], first[lines], column_ref)
         intensity = real * real + imag * imag
         level = jnp.sum(
             jnp.sum(intensity, axis=0, keepdims=True), axis=1, keepdims=True
         ) / (rows * PIX)
         spectra = (intensity / (level + EPSILON)).astype(jnp.bfloat16)
         for part in range(waves):
-            image_ref[part, 0, f * share : (f + 1) * share] = spectra[
+            out_ref[part, 0, f * share : (f + 1) * share] = spectra[
                 part * share : (part + 1) * share
             ]
 
 
-def rows_kernel(positions, rows, length_ref, path, opening, row_ref, column_ref, *refs):
-    image_ref, sum_ref = refs[:2]
-    scratch = refs[2:]
+def rows_kernel(stage, positions, rows, length_ref, path, opening, row_ref, *refs):
     inverse = 1.0 / length_ref[0, :1]
-    transform(positions, rows, inverse, path, opening, row_ref, column_ref, scratch)
-    first = scratch[3]
-    real = jnp.dot(first[...], column_ref[0, :, :PIX], preferred_element_type=jnp.float32)
-    imag = jnp.dot(first[...], column_ref[0, :, PIX:], preferred_element_type=jnp.float32)
+    if stage < len(STAGES) - 1:
+        refs[1][...] = jnp.zeros_like(refs[1])
+        transform(
+            stage, positions, rows, inverse, path, opening, row_ref, refs[0].at[0], refs[2:]
+        )
+        return
+    column_ref, before, image_ref, sum_ref = refs[:4]
+    scratch = refs[4:]
+    transform(stage, positions, rows, inverse, path, opening, row_ref, scratch[3], scratch)
+    real, imag = columns_of(before[0], scratch[3][...], column_ref)
     intensity = real * real + imag * imag
     image_ref[0] = intensity
     sum_ref[0] = jnp.sum(intensity.reshape(positions, rows, PIX), axis=1)
@@ -412,77 +460,88 @@
         pltpu.VMEM((2 * BAND, positions * LANES), jnp.bfloat16),
         pltpu.VMEM((2 * BAND, positions * LANES), jnp.bfloat16),
         pltpu.VMEM((2 * rows, positions * LANES), jnp.float32),
-        pltpu.VMEM((positions * rows, 2 * PUP), jnp.bfloat16),
+        pltpu.VMEM((positions * rows, 2 * WIDE), jnp.bfloat16),
     ]
 
 
-def transform_cost(lengths, positions, rows):
+def transform_cost(stage, lengths, positions, rows):
+    share = len(chunks_of(stage))
     return pl.CostEstimate(
-        flops=lengths * positions * (rows * 8 * PUP * PUP + rows * 8 * PUP * PIX + 10**8),
+        flops=lengths * positions * share * (rows * PUP * PUP + rows * PUP * PIX + 10**7),
         bytes_accessed=8 * 2**20,
         transcendentals=0,
     )
 
 
-def table_specs(row_table, column_table):
-    return [
-        pl.BlockSpec((1,) + row_table.shape[1:], lambda l: (l, 0, 0, 0)),
-        pl.BlockSpec((1,) + column_table.shape[1:], lambda l: (l, 0, 0)),
-    ]
-
-
-def whole_fields(own, got, spread, place, where, length, row_table, column_table, sizes):
+def by_length(array):
+    return pl.BlockSpec((1,) + array.shape[1:], lambda l: (l,) + (0,) * (array.ndim - 1))
+
+
+def whole_fields(stage, own, got, spread, place, where, length, tables, sizes, tokens):
     positions, modes, waves, half, slabs = sizes
     keys = tuple((h, masks) for h, _, masks in got)
     arrays = [array for _, array, _ in got]
-    lengths = row_table.shape[0]
+    lengths = length.shape[0]
     units = place.shape[0]
     share = positions * PIX // waves
     any_memory = pl.BlockSpec(memory_space=pl.ANY)
+    if stage < len(STAGES) - 1:
+        out_shape = jax.ShapeDtypeStruct((lengths, positions * PIX, 2 * WIDE), jnp.bfloat16)
+        out_spec = by_length(out_shape)
+    else:
+        out_shape = jax.ShapeDtypeStruct((waves, lengths, share, PIX), jnp.bfloat16)
+        out_spec = pl.BlockSpec((waves, 1, share, PIX), lambda l: (0, l, 0, 0))
     return pl.pallas_call(
         functools.partial(
-            whole_kernel, (positions, modes, waves, half, slabs, keys)
+            whole_kernel, stage, (positions, modes, waves, half, slabs, keys), len(tokens)
         ),
         grid=(lengths,),
         out_shape=(
-            jax.ShapeDtypeStruct((waves, lengths, share, PIX), jnp.bfloat16),
+            out_shape,
             jax.ShapeDtypeStruct((units, positions * ROWS, LANES), jnp.float32),
             jax.ShapeDtypeStruct((units, ROWS, LANES), jnp.float32),
         ),
-        in_specs=[LENGTH, SMEM, SMEM]
+        in_specs=[by_length(length), SMEM, SMEM]
         + [any_memory] * (1 + len(keys))
         + [VMEM]
-        + table_specs(row_table, column_table),
-        out_specs=(pl.BlockSpec((waves, 1, share, PIX), lambda l: (0, l, 0, 0)), VMEM, VMEM),
+        + [by_length(table) for table in tables]
+        + [VMEM] * len(tokens),
+        out_specs=(out_spec, VMEM, VMEM),
         scratch_shapes=[
             pltpu.VMEM((waves * slabs, ROWS, LANES), jnp.bfloat16),
             pltpu.SemaphoreType.DMA((1 + sum(len(masks) for _, masks in keys) * (waves - 1),)),
         ]
         + transform_scratch(positions, PIX),
-        cost_estimate=transform_cost(lengths, positions, PIX),
+        cost_estimate=transform_cost(stage, lengths, positions, PIX),
         compiler_params=pltpu.CompilerParams(vmem_limit_bytes=VMEM_BYTES),
-    )(length, place, where, own, *arrays, spread, row_table, column_table)
-
-
-def row_fields(path, opening, length, row_table, column_table, positions):
-    lengths = row_table.shape[0]
-    rows = row_table.shape[2] // 2
-    return pl.pallas_call(
-        functools.partial(rows_kernel, positions, rows),
-        grid=(lengths,),
-        out_shape=(
+    )(length, place, where, own, *arrays, spread, *tables, *tokens)
+
+
+def row_fields(stage, path, opening, length, tables, positions):
+    lengths = length.shape[0]
+    rows = tables[0].shape[2] // 2
+    if stage < len(STAGES) - 1:
+        out_shape = (
+            jax.ShapeDtypeStruct((lengths, positions * rows, 2 * WIDE), jnp.bfloat16),
+            jax.ShapeDtypeStruct((8, LANES), jnp.float32),
+        )
+        out_specs = (by_length(out_shape[0]), pl.BlockSpec((8, LANES), lambda l: (0, 0)))
+    else:
+        out_shape = (
             jax.ShapeDtypeStruct((lengths, positions * rows, PIX), jnp.float32),
             jax.ShapeDtypeStruct((lengths, positions, PIX), jnp.float32),
-        ),
-        in_specs=[LENGTH, VMEM, VMEM] + table_specs(row_table, column_table),
-        out_specs=(
-            pl.BlockSpec((1, positions * rows, PIX), lambda l: (l, 0, 0)),
-            pl.BlockSpec((1, positions, PIX), lambda l: (l, 0, 0)),
-        ),
+        )
+        out_specs = tuple(by_length(one) for one in out_shape)
+    return pl.pallas_call(
+        functools.partial(rows_kernel, stage, positions, rows),
+        grid=(lengths,),
+        out_shape=out_shape,
+        in_specs=[by_length(length), VMEM, VMEM] + [by_length(table) for table in tables],
+        out_specs=out_specs,
         scratch_shapes=transform_scratch(positions, rows),
-        cost_estimate=transform_cost(lengths, positions, rows),
+        cost_estimate=transform_cost(stage, lengths, positions, rows),
         compiler_params=pltpu.CompilerParams(vmem_limit_bytes=VMEM_BYTES),
-    )(length, path, opening, row_table, column_table)
+    )(length, path, opening, *tables)
 
 
 def mix_kernel(inverse_ref, weight_ref, sent_ref, image_ref, out_ref):
@@ -537,8 +596,8 @@
     for start in range(0, PUP, ROWS):
         s, k = half_turn((y_ref[start : start + ROWS] * v_ref[...]) * scale)
         cosine, sine = 1.0 - s * s, s * k
-        lower = slice(start, start + ROWS)
-        upper = slice(PUP + start, PUP + start + ROWS)
+        lower = start // WIDE * 2 * WIDE + start % WIDE
+        lower, upper = slice(lower, lower + ROWS), slice(lower + WIDE, lower + WIDE + ROWS)
         column_ref[0, lower, :PIX] = cosine.astype(jnp.bfloat16)
         column_ref[0, lower, PIX:] = (-sine).astype(jnp.bfloat16)
         column_ref[0, upper, :PIX] = sine.astype(jnp.bfloat16)
@@ -559,7 +618,7 @@
 
 def tables(length, first_row, rows):
     lengths = length.shape[0]
-    y = 2 * np.concatenate([band_columns(band) for band in range(BANDS)]) - PUP + 1
+    y = 2 * np.concatenate([band_columns(band) for stage in STAGES for band in stage]) - PUP + 1
     v = np.arange(PIX) - PIX // 2
     u = first_row + jnp.arange(rows, dtype=jnp.int32) - PIX // 2
     x = np.array(
@@ -576,7 +635,7 @@
             jax.ShapeDtypeStruct((8, LANES), jnp.float32),
         ),
         in_specs=[
-            LENGTH,
+            pl.BlockSpec((1, 8, LANES), lambda l: (l, 0, 0)),
             whole(PUP, 1),
             whole(1, PIX),
             whole(rows, 1),
@@ -601,8 +660,11 @@
 
 
 def add_over_wave(x, waves):
-    copies = jnp.broadcast_to(x[None], (waves,) + x.shape)
-    return jnp.sum(lax.all_to_all(copies, "wave", split_axis=0, concat_axis=0, tiled=True), axis=0)
+    step = 1
+    while step < waves:
+        x = x + lax.ppermute(x, "wave", [(i, i ^ step) for i in range(waves)])
+        step *= 2
+    return x
 
 
 def local(mode_basis, coef_table, table_index, wave_lengths, sed_table, template_ids):
@@ -611,21 +673,17 @@
     modes = mode_basis.shape[0]
     positions = table_index.shape[0]
     rows = PIX // waves
-    count, half, slabs, pack, place = layout(waves, modes)
     lengths = wave_lengths.shape[0]
     sent_lengths = lengths // 2
 
     share = (lax.axis_index("groups") % 2) * 4 + lax.axis_index("field") % 4
     where = jnp.stack([mine, share]).astype(jnp.int32)
-    own, piece = pack_rows(mode_basis, wave_lengths, pack, where, half, slabs)
-    parts = along_wave(piece, waves)
-    low, high, every = split_parts(parts, where, wave_lengths, half, sent_lengths)
-    own_length = jnp.broadcast_to(
-        wave_lengths[:sent_lengths, None, None], (sent_lengths, 8, LANES)
-    )
-    own_row, own_column, _ = tables(own_length, 0, PIX)
-    all_row, all_column, token = tables(every, mine * rows, rows)
-    got = gather_rows((low, high), token)
+    plans = [layout(waves, modes, stage) for stage in range(len(STAGES))]
+    owns, parts = [], []
+    for stage, (half, slabs, pack, _) in enumerate(plans):
+        own, piece = pack_rows(mode_basis, wave_lengths, pack, where, half, slabs, stage == 0)
+        owns.append(own)
+        parts.append(along_wave(piece, waves))
 
     selector = (
         table_index[:, None] == jnp.arange(coef_table.shape[0], dtype=jnp.int32)[None, :]
@@ -646,23 +704,38 @@
         ],
         axis=2,
     )
-    path_spread, mix_spread = spreads(coeffs.astype(jnp.bfloat16)[None], weights)
-
+    path_spread, mix_spread, spread_token = spreads(coeffs.astype(jnp.bfloat16)[None], weights)
+    own_length = jnp.broadcast_to(
+        wave_lengths[:sent_lengths, None, None], (sent_lengths, 8, LANES)
+    )
+    own_row, own_column, own_token = tables(own_length, 0, PIX)
+
+    low, high, every = split_parts(
+        parts[0], where, wave_lengths, plans[0][0], sent_lengths, (spread_token, own_token)
+    )
+    all_row, all_column, all_token = tables(every, mine * rows, rows)
+    got = gather_halves((low, high), all_token)
+    second, second_token = join(parts[1], [array[0, :8] for _, array, masks in got if masks in ((2, 6), (4, 6))])
+
+    def sizes(stage):
+        half, slabs, _, _ = plans[stage]
+        return positions, modes, waves, half, slabs
+
+    before, path, opening = whole_fields(
+        0, owns[0], got, path_spread, plans[0][3], where, own_length, (own_row,), sizes(0),
+        (second_token,),
+    )
+    got = gather_direct(second)
+    rows_before, rows_token = row_fields(0, path, opening, every, (all_row,), positions)
     spectra, path, opening = whole_fields(
-        own,
-        got,
-        path_spread,
-        place,
-        where,
-        own_length,
-        own_row,
-        own_column,
-        (positions, modes, waves, half, slabs),
+        1, owns[1], got, path_spread, plans[1][3], where, own_length,
+        (own_row, own_column, before), sizes(1), (rows_token,),
     )
     sent = lax.all_to_all(spectra, "wave", split_axis=0, concat_axis=0, tiled=True)
     sent = sent.reshape(waves * sent_lengths, positions * rows, PIX)
-
-    images, sums = row_fields(path, opening, every, all_row, all_column, positions)
+    images, sums = row_fields(
+        1, path, opening, every, (all_row, all_column, rows_before), positions
+    )
     level = add_over_wave(jnp.sum(sums, axis=2), waves) / (PIX * PIX)
     return mix(mix_spread, 1.0 / (level + EPSILON), sent, images, templates, rows)
 

time: 182 us -> 158 us (0.87)
  waiting for transfers between devices: 67.9 us -> 28 us
  Pallas kernels: 77.2 us -> 89.5 us
  starting transfers between devices: 16.2 us -> 26.6 us
  blocking collectives: 9.28 us -> 0 us
  local copies, waits for them, and re-layouts: 4.89 us -> 7.16 us
    all_to_all x1, waiting for transfers between devices: 24.6 us -> 0.01 us  [local(): lax.all_to_all(spectra, 'wave', split_axis=0, concat_axis=0, tiled=True)]
    pallas_call x6 -> x10, Pallas kernels: 62.2 us -> 74.5 us  [the longest x2 34.8 us: row_fields(): pl.pallas_call(functools.partial(rows_kernel, stage, positions, rows), gr...]
    ppermute x8 -> x15, waiting for transfers between devices: 19.4 us -> 8.53 us  [swap(): return lax.ppermute(x, ('groups', 'field'), pairs)]
    all_to_all x1 -> x0, blocking collectives: 9.28 us -> none  [add_over_wave(): lax.all_to_all(copies, 'wave', split_axis=0, concat_axis=0, tiled=True)]
    ppermute x3 -> x6, waiting for transfers between devices: 24 us -> 16.1 us  [along_wave(): lax.ppermute(piece, 'wave', [(i, (i + s) % waves) for i in range(waves)])]
    ppermute x0 -> x2, starting transfers between devices: none -> 4.8 us  [add_over_wave(): x = x + lax.ppermute(x, 'wave', [(i, i ^ step) for i in range(waves)])]
    ppermute x0 -> x2, waiting for transfers between devices: none -> 3.42 us  [add_over_wave(): x = x + lax.ppermute(x, 'wave', [(i, i ^ step) for i in range(waves)])]
    ppermute x3 -> x6, starting transfers between devices: 6.11 us -> 8.95 us  [along_wave(): lax.ppermute(piece, 'wave', [(i, (i + s) % waves) for i in range(waves)])]
  transfers between devices with their start and end apart: 12 -> 24, of which waited for: 6 -> 8; matrix products, arithmetic and copies ran while one was open for 3% -> 5% of each run, Pallas kernels for 8% -> 41%
where the time goes in v6:
time: 158 us; the launch traced here: 157 us
  Pallas kernels  89.5 us (57%)
  waiting for transfers between devices  28 us (18%)
  starting transfers between devices  26.6 us (17%)
  local copies, waits for them, and re-layouts  7.16 us (5%)
  other arithmetic  4 us (3%)
  matrix products  1.87 us (1%)
    pallas_call x2, Pallas kernels, row_fields(): pl.pallas_call(functools.partial(rows_kernel, stage, positions, rows), gr...  34.8 us
    pallas_call x2, Pallas kernels, whole_fields(): pl.pallas_call(functools.partial(whole_kernel, stage, (positions, modes,...  25.7 us
    ppermute x6, waiting for transfers between devices, along_wave(): lax.ppermute(piece, 'wave', [(i, (i + s) % waves) for i in range(waves)])  16.1 us
    ppermute x6, starting transfers between devices, along_wave(): lax.ppermute(piece, 'wave', [(i, (i + s) % waves) for i in range(waves)])  8.95 us
    ppermute x15, starting transfers between devices, swap(): return lax.ppermute(x, ('groups', 'field'), pairs)  8.69 us
    ppermute x15, waiting for transfers between devices, swap(): return lax.ppermute(x, ('groups', 'field'), pairs)  8.53 us
    pallas_call x2, Pallas kernels, tables(): pl.pallas_call(table_kernel, grid=(lengths,), out_shape=(jax.ShapeDtypeSt...  8.51 us
    pallas_call x2, Pallas kernels, pack_rows(): pl.pallas_call(functools.partial(pack_kernel, count, modes, half, with_le...  6.74 us
  transfers between devices with their start and end apart: 24, of which 8 were waited for; matrix products, arithmetic and copies ran while one was open for 5% of the time, Pallas kernels for 41%

profile of v6, /device:TPU:0, one launch (start us, length us, event | category | flops | bytes accessed | tf_op | source)
XLA Modules:
  0.0 157.3 jit_solution(14063606098982057153)
XLA Ops:
  0.0 0.6 pad_add_fusion.where
  0.6 3.3 %shard_map.154 = (bf16[256,16,128]{2,1,0:T(8,128)(2,1)}, bf16[33,16,128]{2,1,0:T(8,128)(2,1)}) custom-call(s32[2]{0:T(128)} %pad_add_fusion.where, s32[44,3]{1,0:T(8,128)} %constant.66.clone.table, f32[2]{0:T(128)} %lengths.3, bf16[22,128,512]{2,1,0:T(8,128)(2,1)} %basis.3), custom_call_target="tpu_custom_call" | custom-call | tf_op jit(solution)/shard_map/pallas_call | solution.py:147
  3.9 5.1 %collective-permute-start.2 = (bf16[33,16,128]{2,1,0:T(8,128)(2,1)}, bf16[33,16,128]{2,1,0:T(8,128)(2,1)S(1)}, u32[]{:S(2)}, u32[]{:S(2)}) collective-permute-start(bf16[33,16,128]{2,1,0:T(8,128)(2,1)} %get-tuple-element.35), channel_id=1, source_target_pairs={{0,3},{1,0},{2,1},{3,2},{4,7},{5,4},{6,5},{7,6},{8,11},{9,8},{10,9... | collective-permute-start | bytes 405512 | tf_op jit(solution)/shard_map/ppermute | solution.py:216
  9.0 0.0 collective-permute-start.1
  9.0 1.0 collective-permute-start
  10.0 1.1 fusion.6
  11.1 0.1 copy.29
  11.3 0.1 copy.30
  11.4 0.8 fusion.refs_0_
  12.2 0.7 pad_maximum_fusion.refs_1_
  12.9 1.9 %shard_map.155 = (bf16[1,128,352]{2,1,0:T(8,128)(2,1)}, bf16[8,128,128]{2,1,0:T(8,128)(2,1)}, f32[8,128]{1,0:T(8,128)}) custom-call(bf16[1,8,22]{2,1,0:T(8,128)(2,1)} %fusion.refs_0_, bf16[8,8,8]{2,1,0:T(8,128)(2,1)} %pad_maximum_fusion.refs_1_), custom_call_target="tpu_custom_call" | custom-call | tf_op jit(solution)/shard_map/pallas_call | solution.py:275
  14.8 0.7 add_convert_fusion.u_ref
  15.5 0.6 broadcast_in_dim.8.length_ref
  16.1 3.5 %shard_map.156 = (bf16[1,4,512,256]{3,2,1,0:T(8,128)(2,1)}, bf16[1,1024,512]{2,1,0:T(8,128)(2,1)}, f32[8,128]{1,0:T(8,128)}) custom-call(f32[1,8,128]{2,1,0:T(8,128)} %broadcast_in_dim.8.length_ref, f32[512,1]{1,0:T(8,128)} %constant.68.clone.y_ref, f32[1,256]{1,0:T(1,128)} %constant.69.clone.v_ref, f32[256,1]{1,0:T(8,128)} %add_convert_fusion.u_ref, ...), custom_call_target="tpu_custom_call" | custom-call | flops 3932160 | bytes 1048576 | tf_op jit(solution)/shard_map/pallas_call | solution.py:629
  19.6 1.1 collective-permute-done.1.refs_1_
  20.7 0.7 copy-done.8
  21.4 0.1 copy-done.9
  21.5 1.8 %shard_map.157 = (bf16[48,16,128]{2,1,0:T(8,128)(2,1)}, bf16[48,16,128]{2,1,0:T(8,128)(2,1)}, f32[4,8,128]{2,1,0:T(8,128)}) custom-call(s32[2]{0:T(128)} %pad_add_fusion.where, f32[2]{0:T(128)} %lengths.3, bf16[33,16,128]{2,1,0:T(8,128)(2,1)} %copy-done.9, bf16[33,16,128]{2,1,0:T(8,128)(2,1)} %copy-done.8, bf16[33,16,128]{2,1,0:T(8,128)(2,1)} %copy-done.7, ...), custom_call_target="tpu_custom_call" | custom-call | tf_op jit(solution)/shard_map/pallas_call | solution.py:183
  23.3 1.5 collective-permute-start.6
  24.8 1.5 collective-permute-start.8
  26.3 0.6 add_convert_fusion.1.u_ref
  26.9 5.1 %shard_map.159 = (bf16[4,4,128,256]{3,2,1,0:T(8,128)(2,1)}, bf16[4,1024,512]{2,1,0:T(8,128)(2,1)}, f32[8,128]{1,0:T(8,128)}) custom-call(f32[4,8,128]{2,1,0:T(8,128)} %get-tuple-element.38.length_ref, f32[512,1]{1,0:T(8,128)} %constant.68.clone.y_ref, f32[1,256]{1,0:T(1,128)} %constant.69.clone.v_ref, f32[64,1]{1,0:T(8,128)} %add_convert_fusion.1.u_ref, ...), custom_call_target="tpu_custom_call" | custom-call | flops 15728640 | bytes 4194304 | tf_op jit(solution)/shard_map/pallas_call | solution.py:629
  32.0 0.7 copy-done.3
  32.6 1.8 %shard_map.160 = (bf16[96,16,128]{2,1,0:T(8,128)(2,1)}, f32[8,128]{1,0:T(8,128)}) custom-call(bf16[48,16,128]{2,1,0:T(8,128)(2,1)} %get-tuple-element.41.refs_0_, bf16[48,16,128]{2,1,0:T(8,128)(2,1)} %copy-done.3, f32[8,128]{1,0:T(8,128)} %get-tuple-element.42.refs_2_), custom_call_target="tpu_custom_call" | custom-call | tf_op jit(solution)/shard_map/pallas_call | solution.py:202
  34.4 0.5 collective-permute-start.7
  34.9 0.7 copy-done.2
  35.6 1.8 %shard_map.161 = (bf16[96,16,128]{2,1,0:T(8,128)(2,1)}, f32[8,128]{1,0:T(8,128)}) custom-call(bf16[48,16,128]{2,1,0:T(8,128)(2,1)} %get-tuple-element.44.refs_0_, bf16[48,16,128]{2,1,0:T(8,128)(2,1)} %copy-done.2, f32[8,128]{1,0:T(8,128)} %get-tuple-element.42.refs_2_), custom_call_target="tpu_custom_call" | custom-call | tf_op jit(solution)/shard_map/pallas_call | solution.py:202
  37.4 0.5 collective-permute-start.9
  38.0 3.4 %shard_map.158 = (bf16[320,16,128]{2,1,0:T(8,128)(2,1)}, bf16[40,16,128]{2,1,0:T(8,128)(2,1)}) custom-call(s32[2]{0:T(128)} %pad_add_fusion.where, s32[56,3]{1,0:T(8,128)} %constant.67.clone.table, f32[2]{0:T(128)} %lengths.3, bf16[22,128,512]{2,1,0:T(8,128)(2,1)} %basis.3), custom_call_target="tpu_custom_call" | custom-call | tf_op jit(solution)/shard_map/pallas_call | solution.py:147
  41.4 1.7 %collective-permute-start.5 = (bf16[40,16,128]{2,1,0:T(8,128)(2,1)}, bf16[40,16,128]{2,1,0:T(8,128)(2,1)S(1)}, u32[]{:S(2)}, u32[]{:S(2)}) collective-permute-start(bf16[40,16,128]{2,1,0:T(8,128)(2,1)} %get-tuple-element.40), channel_id=1, source_target_pairs={{0,3},{1,0},{2,1},{3,2},{4,7},{5,4},{6,5},{7,6},{8,11},{9,8},{10,9... | collective-permute-start | bytes 491528 | tf_op jit(solution)/shard_map/ppermute | solution.py:216
  43.1 1.1 collective-permute-start.4
  44.3 3.8 %collective-permute-done.5.refs_2_ = bf16[40,16,128]{2,1,0:T(8,128)(2,1)S(1)} collective-permute-done((bf16[40,16,128]{2,1,0:T(8,128)(2,1)}, bf16[40,16,128]{2,1,0:T(8,128)(2,1)S(1)}, u32[]{:S(2)}, u32[]{:S(2)}) %collective-permute-start.5) | collective-permute-done | bytes 163872 | tf_op jit(solution)/shard_map/ppermute | solution.py:216
  48.1 0.5 collective-permute-start.18
  48.6 0.1 collective-permute-start.20
  48.7 0.6 slice_bitcast_fusion.1.refs_3_
  49.2 4.5 %collective-permute-done.4.refs_1_ = bf16[40,16,128]{2,1,0:T(8,128)(2,1)S(1)} collective-permute-done((bf16[40,16,128]{2,1,0:T(8,128)(2,1)}, bf16[40,16,128]{2,1,0:T(8,128)(2,1)S(1)}, u32[]{:S(2)}, u32[]{:S(2)}) %collective-permute-start.4) | collective-permute-done | bytes 163872 | tf_op jit(solution)/shard_map/ppermute | solution.py:216
  53.7 0.0 collective-permute-start.3
  53.7 0.6 slice_bitcast_fusion.refs_4_
  54.4 6.7 %collective-permute-done.3.refs_0_ = bf16[40,16,128]{2,1,0:T(8,128)(2,1)S(1)} collective-permute-done((bf16[40,16,128]{2,1,0:T(8,128)(2,1)}, bf16[40,16,128]{2,1,0:T(8,128)(2,1)S(1)}, u32[]{:S(2)}, u32[]{:S(2)}) %collective-permute-start.3) | collective-permute-done | bytes 163872 | tf_op jit(solution)/shard_map/ppermute | solution.py:216
  61.0 0.7 copy-done.6
  61.7 1.9 %shard_map.162 = (bf16[120,16,128]{2,1,0:T(8,128)(2,1)}, f32[8,128]{1,0:T(8,128)}) custom-call(bf16[40,16,128]{2,1,0:T(8,128)(2,1)} %copy-done.6, bf16[40,16,128]{2,1,0:T(8,128)(2,1)} %copy-done.5, bf16[40,16,128]{2,1,0:T(8,128)(2,1)} %copy-done.4, bf16[8,128]{1,0:T(8,128)(2,1)} %slice_bitcast_fusion.1.refs_3_, bf16[8,128]{1,0:T(8,128)(2,1)} %slice_bitcast_fusion.refs_4_), custom_call_target="tpu_custom_call" | custom-call | tf_op jit(solution)/shard_map/pallas_call | solution.py:202
  63.6 1.5 collective-permute-start.15
  65.1 1.5 collective-permute-start.13
  66.6 0.5 collective-permute-start.11
  67.2 10.5 %shard_map.163 = (bf16[1,2048,512]{2,1,0:T(8,128)(2,1)}, f32[40,128,128]{2,1,0:T(8,128)}, f32[40,16,128]{2,1,0:T(8,128)}) custom-call(f32[1,8,128]{2,1,0:T(8,128)} %broadcast_in_dim.8.length_ref, s32[40,4]{1,0:T(8,128)} %constant.71.clone.place, s32[2]{0:T(128)} %pad_add_fusion.where, bf16[256,16,128]{2,1,0:T(8,128)(2,1)} %get-tuple-element.50.refs_0_, ...), custom_call_target="tpu_custom_call" | custom-call | flops 4426531840 | bytes 8388608 | tf_op jit(solution)/shard_map/pallas_call | solution.py:494
  77.7 0.6 collective-permute-start.16
  78.2 1.3 collective-permute-done.13.refs_5_
  79.5 7.2 %collective-permute-done.11.refs_3_ = bf16[120,16,128]{2,1,0:T(8,128)(2,1)S(1)} collective-permute-done((bf16[120,16,128]{2,1,0:T(8,128)(2,1)}, bf16[120,16,128]{2,1,0:T(8,128)(2,1)S(1)}, u32[]{:S(2)}, u32[]{:S(2)}) %collective-permute-start.11) | collective-permute-done | bytes 491552 | tf_op jit(solution)/shard_map/ppermute | solution.py:228
  86.7 13.9 %shard_map.164 = (bf16[4,512,512]{2,1,0:T(8,128)(2,1)}, f32[8,128]{1,0:T(8,128)}) custom-call(f32[4,8,128]{2,1,0:T(8,128)} %get-tuple-element.38.length_ref, f32[40,128,128]{2,1,0:T(8,128)} %get-tuple-element.53.path, f32[40,16,128]{2,1,0:T(8,128)} %get-tuple-element.54.opening, bf16[4,4,128,256]{3,2,1,0:T(8,128)(2,1)} %get-tuple-element.55.row_ref), custom_call_target="tpu_custom_call" | custom-call | flops 5626531840 | bytes 8388608 | tf_op jit(solution)/shard_map/pallas_call | solution.py:535
  100.7 0.7 copy-done.16
  101.4 0.2 copy-done.17
  101.6 0.2 copy-done.18
  101.8 0.1 copy-done.19
  101.9 15.2 %shard_map.165 = (bf16[4,1,512,256]{3,2,1,0:T(8,128)(2,1)}, f32[56,128,128]{2,1,0:T(8,128)}, f32[56,16,128]{2,1,0:T(8,128)}) custom-call(f32[1,8,128]{2,1,0:T(8,128)} %broadcast_in_dim.8.length_ref, s32[56,4]{1,0:T(8,128)} %constant.72.clone.place, s32[2]{0:T(128)} %pad_add_fusion.where, bf16[320,16,128]{2,1,0:T(8,128)(2,1)} %get-tuple-element.39.refs_0_, ...), custom_call_target="tpu_custom_call" | custom-call | flops 6197144576 | bytes 8388608 | tf_op jit(solution)/shard_map/pallas_call | solution.py:494
  117.1 4.1 %all-to-all-start = ((bf16[4,1,512,256]{3,2,1,0:T(8,128)(2,1)}), bf16[4,1,512,256]{3,2,1,0:T(8,128)(2,1)S(1)}, u32[]{:S(2)}, u32[]{:S(2)}) async-start(bf16[4,1,512,256]{3,2,1,0:T(8,128)(2,1)} %get-tuple-element.63), calls=%async_computation | async-start | bytes 2097152 | tf_op jit(solution)/shard_map/all_to_all | solution.py:734
  121.2 20.9 %shard_map.166 = (f32[4,512,256]{2,1,0:T(8,128)}, f32[4,8,256]{2,1,0:T(8,128)}) custom-call(f32[4,8,128]{2,1,0:T(8,128)} %get-tuple-element.38.length_ref, f32[56,128,128]{2,1,0:T(8,128)} %get-tuple-element.57.path, f32[56,16,128]{2,1,0:T(8,128)} %get-tuple-element.58.opening, bf16[4,4,128,256]{3,2,1,0:T(8,128)(2,1)} %get-tuple-element.55.row_ref, ...), custom_call_target="tpu_custom_call" | custom-call | flops 7877144576 | bytes 8388608 | tf_op jit(solution)/shard_map/pallas_call | solution.py:535
  142.1 0.8 reduce_sum.19
  142.9 2.0 %collective-permute-start.21 = (f32[4,8]{1,0:T(4,128)S(1)}, f32[4,8]{1,0:T(4,128)S(1)}, u32[]{:S(2)}, u32[]{:S(2)}) collective-permute-start(f32[4,8]{1,0:T(4,128)S(1)} %reduce_sum.19), channel_id=1, source_target_pairs={{0,1},{1,0},{2,3},{3,2},{4,5},{5,4},{6,7},{7,6},{8,9},{9,8},{10,11... | collective-permute-start | bytes 392 | tf_op jit(solution)/shard_map/ppermute | solution.py:665
  145.0 1.7 %collective-permute-done.21 = f32[4,8]{1,0:T(4,128)S(1)} collective-permute-done((f32[4,8]{1,0:T(4,128)S(1)}, f32[4,8]{1,0:T(4,128)S(1)}, u32[]{:S(2)}, u32[]{:S(2)}) %collective-permute-start.21) | collective-permute-done | bytes 160 | tf_op jit(solution)/shard_map/ppermute | solution.py:665
  146.7 2.8 %collective-permute-start.22 = (f32[4,8]{1,0:T(4,128)S(1)}, f32[4,8]{1,0:T(4,128)S(1)}, u32[]{:S(2)}, u32[]{:S(2)}) collective-permute-start(f32[4,8]{1,0:T(4,128)S(1)} %add.56), channel_id=1, source_target_pairs={{0,2},{1,3},{2,0},{3,1},{4,6},{5,7},{6,4},{7,5},{8,10},{9,11},{10,... | collective-permute-start | bytes 392 | tf_op jit(solution)/shard_map/ppermute | solution.py:665
  149.4 1.7 %collective-permute-done.22 = f32[4,8]{1,0:T(4,128)S(1)} collective-permute-done((f32[4,8]{1,0:T(4,128)S(1)}, f32[4,8]{1,0:T(4,128)S(1)}, u32[]{:S(2)}, u32[]{:S(2)}) %collective-permute-start.22) | collective-permute-done | bytes 160 | tf_op jit(solution)/shard_map/ppermute | solution.py:665
  151.2 0.6 add_divide_fusion.inverse_ref
  151.8 1.0 copy-done.1
  152.8 4.5 %shard_map.167 = bf16[8,8,64,256]{3,2,1,0:T(8,128)(2,1)} custom-call(f32[4,8]{1,0:T(4,128)} %add_divide_fusion.inverse_ref, bf16[8,128,128]{2,1,0:T(8,128)(2,1)} %get-tuple-element.62.weight_ref, bf16[4,512,256]{2,1,0:T(8,128)(2,1)} %bitcast.20, f32[4,512,256]{2,1,0:T(8,128)} %get-tuple-element.64.image_ref), custom_call_target="tpu_custom_call" | custom-call | tf_op jit(solution)/shard_map/pallas_call | solution.py:577
  (65 shorter events, 0.2 us)
Async XLA Ops:
  0.0 11.4 %copy-start = (bf16[4096,22]{0,1:T(8,128)(2,1)S(1)}, bf16[4096,22]{0,1:T(8,128)(2,1)}, u32[]{:S(2)}) copy-start(bf16[4096,22]{0,1:T(8,128)(2,1)} %param.17) | copy-start | bytes 540676
  0.0 15.5 %copy-start.10 = (f32[2]{0:T(128)S(1)}, f32[2]{0:T(128)}, u32[]{:S(2)}) copy-start(f32[2]{0:T(128)} %lengths.3) | copy-start | bytes 28
  0.0 10.0 %copy-start.23 = (s32[8,8]{1,0:T(8,128)S(1)}, s32[8,8]{1,0:T(8,128)}, u32[]{:S(2)}) copy-start(s32[8,8]{1,0:T(8,128)} %param.21) | copy-start | bytes 772
  0.0 10.0 %copy-start.22 = (f32[1024,8]{0,1:T(8,128)S(1)}, f32[1024,8]{0,1:T(8,128)}, u32[]{:S(2)}) copy-start(f32[1024,8]{0,1:T(8,128)} %param.20) | copy-start | bytes 98308
  0.0 11.4 %copy-start.24 = (s32[8]{0:T(128)S(1)}, s32[8]{0:T(128)}, u32[]{:S(2)}) copy-start(s32[8]{0:T(128)} %param.18) | copy-start | bytes 100
  3.9 15.7 %collective-permute-start.2 = (bf16[33,16,128]{2,1,0:T(8,128)(2,1)}, bf16[33,16,128]{2,1,0:T(8,128)(2,1)S(1)}, u32[]{:S(2)}, u32[]{:S(2)}) collective-permute-start(bf16[33,16,128]{2,1,0:T(8,128)(2,1)} %get-tuple-element.35), channel_id=1, source_target_pairs={{0,3},{1,0},{2,1},{3,2},{4,7},{5,4},{6,5},{7,6},{8,11},{9,8},{10,9... | collective-permute-start | bytes 405512 | tf_op jit(solution)/shard_map/ppermute | solution.py:216
  9.0 11.7 %collective-permute-start.1 = (bf16[33,16,128]{2,1,0:T(8,128)(2,1)}, bf16[33,16,128]{2,1,0:T(8,128)(2,1)S(1)}, u32[]{:S(2)}, u32[]{:S(2)}) collective-permute-start(bf16[33,16,128]{2,1,0:T(8,128)(2,1)} %get-tuple-element.35), channel_id=1, source_target_pairs={{0,2},{1,3},{2,0},{3,1},{4,6},{5,7},{6,4},{7,5},{8,10},{9,11},{10,... | collective-permute-start | bytes 405512 | tf_op jit(solution)/shard_map/ppermute | solution.py:216
  9.0 11.7 %collective-permute-start = (bf16[33,16,128]{2,1,0:T(8,128)(2,1)}, bf16[33,16,128]{2,1,0:T(8,128)(2,1)S(1)}, u32[]{:S(2)}, u32[]{:S(2)}) collective-permute-start(bf16[33,16,128]{2,1,0:T(8,128)(2,1)} %get-tuple-element.35), channel_id=1, source_target_pairs={{0,1},{1,2},{2,3},{3,0},{4,5},{5,6},{6,7},{7,4},{8,9},{9,10},{10,1... | collective-permute-start | bytes 405512 | tf_op jit(solution)/shard_map/ppermute | solution.py:216
  19.6 1.1 copy-start.7
  20.7 0.7 copy-start.8
  20.7 0.7 copy-start.9
  23.3 8.7 %collective-permute-start.6 = (bf16[48,16,128]{2,1,0:T(8,128)(2,1)}, bf16[48,16,128]{2,1,0:T(8,128)(2,1)S(1)}, u32[]{:S(2)}, u32[]{:S(2)}) collective-permute-start(bf16[48,16,128]{2,1,0:T(8,128)(2,1)} %get-tuple-element.41.refs_0_), channel_id=1, source_target_pairs={{0,8},{4,12},{8,0},{12,4},{16,24},{20,28},{24,16},{28,20},{1,9},{5... | collective-permute-start | bytes 589832 | tf_op jit(solution)/shard_map/ppermute | solution.py:228
  24.8 10.2 %collective-permute-start.8 = (bf16[48,16,128]{2,1,0:T(8,128)(2,1)}, bf16[48,16,128]{2,1,0:T(8,128)(2,1)S(1)}, u32[]{:S(2)}, u32[]{:S(2)}) collective-permute-start(bf16[48,16,128]{2,1,0:T(8,128)(2,1)} %get-tuple-element.44.refs_0_), channel_id=1, source_target_pairs={{0,16},{4,20},{8,24},{12,28},{16,0},{20,4},{24,8},{28,12},{1,17},{... | collective-permute-start | bytes 589832 | tf_op jit(solution)/shard_map/ppermute | solution.py:228
  32.0 0.7 copy-start.3
  34.4 9.8 %copy-start.20 = (bf16[96,16,128]{2,1,0:T(8,128)(2,1)S(1)}, bf16[96,16,128]{2,1,0:T(8,128)(2,1)}, u32[]{:S(2)}) copy-start(bf16[96,16,128]{2,1,0:T(8,128)(2,1)} %get-tuple-element.43.refs_1_) | copy-start | bytes 1179652
  34.4 13.6 %collective-permute-start.7 = (bf16[96,16,128]{2,1,0:T(8,128)(2,1)}, bf16[96,16,128]{2,1,0:T(8,128)(2,1)S(1)}, u32[]{:S(2)}, u32[]{:S(2)}) collective-permute-start(bf16[96,16,128]{2,1,0:T(8,128)(2,1)} %get-tuple-element.43.refs_1_), channel_id=1, source_target_pairs={{0,16},{4,20},{8,24},{12,28},{16,0},{20,4},{24,8},{28,12},{1,17},{... | collective-permute-start | bytes 1179656 | tf_op jit(solution)/shard_map/ppermute | solution.py:228
  34.9 0.7 copy-start.2
  37.4 10.6 %copy-start.21 = (bf16[96,16,128]{2,1,0:T(8,128)(2,1)S(1)}, bf16[96,16,128]{2,1,0:T(8,128)(2,1)}, u32[]{:S(2)}) copy-start(bf16[96,16,128]{2,1,0:T(8,128)(2,1)} %get-tuple-element.45.refs_5_) | copy-start | bytes 1179652
  37.4 11.2 %collective-permute-start.9 = (bf16[96,16,128]{2,1,0:T(8,128)(2,1)}, bf16[96,16,128]{2,1,0:T(8,128)(2,1)S(1)}, u32[]{:S(2)}, u32[]{:S(2)}) collective-permute-start(bf16[96,16,128]{2,1,0:T(8,128)(2,1)} %get-tuple-element.45.refs_5_), channel_id=1, source_target_pairs={{0,8},{4,12},{8,0},{12,4},{16,24},{20,28},{24,16},{28,20},{1,9},{5... | collective-permute-start | bytes 1179656 | tf_op jit(solution)/shard_map/ppermute | solution.py:228
  41.4 6.7 %collective-permute-start.5 = (bf16[40,16,128]{2,1,0:T(8,128)(2,1)}, bf16[40,16,128]{2,1,0:T(8,128)(2,1)S(1)}, u32[]{:S(2)}, u32[]{:S(2)}) collective-permute-start(bf16[40,16,128]{2,1,0:T(8,128)(2,1)} %get-tuple-element.40), channel_id=1, source_target_pairs={{0,3},{1,0},{2,1},{3,2},{4,7},{5,4},{6,5},{7,6},{8,11},{9,8},{10,9... | collective-permute-start | bytes 491528 | tf_op jit(solution)/shard_map/ppermute | solution.py:216
  43.1 10.6 %collective-permute-start.4 = (bf16[40,16,128]{2,1,0:T(8,128)(2,1)}, bf16[40,16,128]{2,1,0:T(8,128)(2,1)S(1)}, u32[]{:S(2)}, u32[]{:S(2)}) collective-permute-start(bf16[40,16,128]{2,1,0:T(8,128)(2,1)} %get-tuple-element.40), channel_id=1, source_target_pairs={{0,2},{1,3},{2,0},{3,1},{4,6},{5,7},{6,4},{7,5},{8,10},{9,11},{10,... | collective-permute-start | bytes 491528 | tf_op jit(solution)/shard_map/ppermute | solution.py:216
  44.3 20.9 %collective-permute-start.17 = (bf16[96,16,128]{2,1,0:T(8,128)(2,1)S(1)}, bf16[96,16,128]{2,1,0:T(8,128)(2,1)}, u32[]{:S(2)}, u32[]{:S(2)}) collective-permute-start(bf16[96,16,128]{2,1,0:T(8,128)(2,1)S(1)} %copy-done.20), channel_id=1, source_target_pairs={{0,4},{4,0},{8,12},{12,8},{16,20},{20,16},{24,28},{28,24},{1,5},{5... | collective-permute-start | bytes 1179656 | tf_op jit(solution)/shard_map/ppermute | solution.py:228
  48.1 13.0 %copy-start.4 = (bf16[40,16,128]{2,1,0:T(8,128)(2,1)}, bf16[40,16,128]{2,1,0:T(8,128)(2,1)S(1)}, u32[]{:S(2)}) copy-start(bf16[40,16,128]{2,1,0:T(8,128)(2,1)S(1)} %collective-permute-done.5.refs_2_) | copy-start | bytes 491524
  48.1 18.6 %collective-permute-start.19 = (bf16[96,16,128]{2,1,0:T(8,128)(2,1)S(1)}, bf16[96,16,128]{2,1,0:T(8,128)(2,1)}, u32[]{:S(2)}, u32[]{:S(2)}) collective-permute-start(bf16[96,16,128]{2,1,0:T(8,128)(2,1)S(1)} %copy-done.21), channel_id=1, source_target_pairs={{0,4},{4,0},{8,12},{12,8},{16,20},{20,16},{24,28},{28,24},{1,5},{5... | collective-permute-start | bytes 1179656 | tf_op jit(solution)/shard_map/ppermute | solution.py:228
  48.1 19.1 %copy-start.11 = (bf16[96,16,128]{2,1,0:T(8,128)(2,1)}, bf16[96,16,128]{2,1,0:T(8,128)(2,1)S(1)}, u32[]{:S(2)}) copy-start(bf16[96,16,128]{2,1,0:T(8,128)(2,1)S(1)} %collective-permute-done.7.refs_2_) | copy-start | bytes 1179652
  48.1 19.0 %collective-permute-start.18 = (bf16[96,16,128]{2,1,0:T(8,128)(2,1)S(1)}, bf16[96,16,128]{2,1,0:T(8,128)(2,1)}, u32[]{:S(2)}, u32[]{:S(2)}) collective-permute-start(bf16[96,16,128]{2,1,0:T(8,128)(2,1)S(1)} %collective-permute-done.7.refs_2_), channel_id=1, source_target_pairs={{0,4},{4,0},{8,12},{12,8},{16,20},{20,16},{24,28},{28,24},{1,5},{5... | collective-permute-start | bytes 1179656 | tf_op jit(solution)/shard_map/ppermute | solution.py:228
  48.6 18.6 %copy-start.12 = (bf16[96,16,128]{2,1,0:T(8,128)(2,1)}, bf16[96,16,128]{2,1,0:T(8,128)(2,1)S(1)}, u32[]{:S(2)}) copy-start(bf16[96,16,128]{2,1,0:T(8,128)(2,1)S(1)} %collective-permute-done.9.refs_6_) | copy-start | bytes 1179652
  48.6 18.5 %collective-permute-start.20 = (bf16[96,16,128]{2,1,0:T(8,128)(2,1)S(1)}, bf16[96,16,128]{2,1,0:T(8,128)(2,1)}, u32[]{:S(2)}, u32[]{:S(2)}) collective-permute-start(bf16[96,16,128]{2,1,0:T(8,128)(2,1)S(1)} %collective-permute-done.9.refs_6_), channel_id=1, source_target_pairs={{0,4},{4,0},{8,12},{12,8},{16,20},{20,16},{24,28},{28,24},{1,5},{5... | collective-permute-start | bytes 1179656 | tf_op jit(solution)/shard_map/ppermute | solution.py:228
  53.7 7.3 %copy-start.5 = (bf16[40,16,128]{2,1,0:T(8,128)(2,1)}, bf16[40,16,128]{2,1,0:T(8,128)(2,1)S(1)}, u32[]{:S(2)}) copy-start(bf16[40,16,128]{2,1,0:T(8,128)(2,1)S(1)} %collective-permute-done.4.refs_1_) | copy-start | bytes 491524
  53.7 7.3 %collective-permute-start.3 = (bf16[40,16,128]{2,1,0:T(8,128)(2,1)}, bf16[40,16,128]{2,1,0:T(8,128)(2,1)S(1)}, u32[]{:S(2)}, u32[]{:S(2)}) collective-permute-start(bf16[40,16,128]{2,1,0:T(8,128)(2,1)} %get-tuple-element.40), channel_id=1, source_target_pairs={{0,1},{1,2},{2,3},{3,0},{4,5},{5,6},{6,7},{7,4},{8,9},{9,10},{10,1... | collective-permute-start | bytes 491528 | tf_op jit(solution)/shard_map/ppermute | solution.py:216
  61.0 0.7 copy-start.6
  63.6 14.0 %collective-permute-start.15 = (bf16[120,16,128]{2,1,0:T(8,128)(2,1)}, bf16[120,16,128]{2,1,0:T(8,128)(2,1)S(1)}, u32[]{:S(2)}, u32[]{:S(2)}) collective-permute-start(bf16[120,16,128]{2,1,0:T(8,128)(2,1)} %get-tuple-element.46.refs_1_), channel_id=1, source_target_pairs={{0,16},{4,20},{8,24},{12,28},{16,0},{20,4},{24,8},{28,12},{1,17},{... | collective-permute-start | bytes 1474568 | tf_op jit(solution)/shard_map/ppermute | solution.py:228
  65.1 14.4 %collective-permute-start.13 = (bf16[120,16,128]{2,1,0:T(8,128)(2,1)}, bf16[120,16,128]{2,1,0:T(8,128)(2,1)S(1)}, u32[]{:S(2)}, u32[]{:S(2)}) collective-permute-start(bf16[120,16,128]{2,1,0:T(8,128)(2,1)} %get-tuple-element.46.refs_1_), channel_id=1, source_target_pairs={{0,8},{4,12},{8,0},{12,4},{16,24},{20,28},{24,16},{28,20},{1,9},{5... | collective-permute-start | bytes 1474568 | tf_op jit(solution)/shard_map/ppermute | solution.py:228
  66.6 20.1 %collective-permute-start.11 = (bf16[120,16,128]{2,1,0:T(8,128)(2,1)}, bf16[120,16,128]{2,1,0:T(8,128)(2,1)S(1)}, u32[]{:S(2)}, u32[]{:S(2)}) collective-permute-start(bf16[120,16,128]{2,1,0:T(8,128)(2,1)} %get-tuple-element.46.refs_1_), channel_id=1, source_target_pairs={{0,24},{4,28},{8,16},{12,20},{16,8},{20,12},{24,0},{28,4},{1,25},{... | collective-permute-start | bytes 1474568 | tf_op jit(solution)/shard_map/ppermute | solution.py:228
  67.1 33.5 %collective-permute-start.10 = (bf16[120,16,128]{2,1,0:T(8,128)(2,1)}, bf16[120,16,128]{2,1,0:T(8,128)(2,1)S(1)}, u32[]{:S(2)}, u32[]{:S(2)}) collective-permute-start(bf16[120,16,128]{2,1,0:T(8,128)(2,1)} %get-tuple-element.46.refs_1_), channel_id=1, source_target_pairs={{0,4},{4,0},{8,12},{12,8},{16,20},{20,16},{24,28},{28,24},{1,5},{5... | collective-permute-start | bytes 1474568 | tf_op jit(solution)/shard_map/ppermute | solution.py:228
  77.6 23.0 %copy-start.13 = (bf16[120,16,128]{2,1,0:T(8,128)(2,1)}, bf16[120,16,128]{2,1,0:T(8,128)(2,1)S(1)}, u32[]{:S(2)}) copy-start(bf16[120,16,128]{2,1,0:T(8,128)(2,1)S(1)} %collective-permute-done.15.refs_7_) | copy-start | bytes 1474564
  77.7 23.0 %collective-permute-start.16 = (bf16[120,16,128]{2,1,0:T(8,128)(2,1)S(1)}, bf16[120,16,128]{2,1,0:T(8,128)(2,1)S(1)}, u32[]{:S(2)}, u32[]{:S(2)}) collective-permute-start(bf16[120,16,128]{2,1,0:T(8,128)(2,1)S(1)} %collective-permute-done.15.refs_7_), channel_id=1, source_target_pairs={{0,4},{4,0},{8,12},{12,8},{16,20},{20,16},{24,28},{28,24},{1,5},{5... | collective-permute-start | bytes 1474568 | tf_op jit(solution)/shard_map/ppermute | solution.py:228
  79.5 21.1 %copy-start.14 = (bf16[120,16,128]{2,1,0:T(8,128)(2,1)}, bf16[120,16,128]{2,1,0:T(8,128)(2,1)S(1)}, u32[]{:S(2)}) copy-start(bf16[120,16,128]{2,1,0:T(8,128)(2,1)S(1)} %collective-permute-done.13.refs_5_) | copy-start | bytes 1474564
  79.5 21.1 %collective-permute-start.14 = (bf16[120,16,128]{2,1,0:T(8,128)(2,1)S(1)}, bf16[120,16,128]{2,1,0:T(8,128)(2,1)S(1)}, u32[]{:S(2)}, u32[]{:S(2)}) collective-permute-start(bf16[120,16,128]{2,1,0:T(8,128)(2,1)S(1)} %collective-permute-done.13.refs_5_), channel_id=1, source_target_pairs={{0,4},{4,0},{8,12},{12,8},{16,20},{20,16},{24,28},{28,24},{1,5},{5... | collective-permute-start | bytes 1474568 | tf_op jit(solution)/shard_map/ppermute | solution.py:228
  86.7 13.9 %copy-start.15 = (bf16[120,16,128]{2,1,0:T(8,128)(2,1)}, bf16[120,16,128]{2,1,0:T(8,128)(2,1)S(1)}, u32[]{:S(2)}) copy-start(bf16[120,16,128]{2,1,0:T(8,128)(2,1)S(1)} %collective-permute-done.11.refs_3_) | copy-start | bytes 1474564
  86.7 14.0 %collective-permute-start.12 = (bf16[120,16,128]{2,1,0:T(8,128)(2,1)S(1)}, bf16[120,16,128]{2,1,0:T(8,128)(2,1)S(1)}, u32[]{:S(2)}, u32[]{:S(2)}) collective-permute-start(bf16[120,16,128]{2,1,0:T(8,128)(2,1)S(1)} %collective-permute-done.11.refs_3_), channel_id=1, source_target_pairs={{0,4},{4,0},{8,12},{12,8},{16,20},{20,16},{24,28},{28,24},{1,5},{5... | collective-permute-start | bytes 1474568 | tf_op jit(solution)/shard_map/ppermute | solution.py:228
  100.6 0.8 copy-start.16
  100.7 0.9 copy-start.17
  100.7 1.1 copy-start.18
  100.7 1.2 copy-start.19
  117.1 34.7 %all-to-all-start = ((bf16[4,1,512,256]{3,2,1,0:T(8,128)(2,1)}), bf16[4,1,512,256]{3,2,1,0:T(8,128)(2,1)S(1)}, u32[]{:S(2)}, u32[]{:S(2)}) async-start(bf16[4,1,512,256]{3,2,1,0:T(8,128)(2,1)} %get-tuple-element.63), calls=%async_computation | async-start | bytes 2097152 | tf_op jit(solution)/shard_map/all_to_all | solution.py:734
  142.9 3.7 %collective-permute-start.21 = (f32[4,8]{1,0:T(4,128)S(1)}, f32[4,8]{1,0:T(4,128)S(1)}, u32[]{:S(2)}, u32[]{:S(2)}) collective-permute-start(f32[4,8]{1,0:T(4,128)S(1)} %reduce_sum.19), channel_id=1, source_target_pairs={{0,1},{1,0},{2,3},{3,2},{4,5},{5,4},{6,7},{7,6},{8,9},{9,8},{10,11... | collective-permute-start | bytes 392 | tf_op jit(solution)/shard_map/ppermute | solution.py:665
  146.7 4.5 %collective-permute-start.22 = (f32[4,8]{1,0:T(4,128)S(1)}, f32[4,8]{1,0:T(4,128)S(1)}, u32[]{:S(2)}, u32[]{:S(2)}) collective-permute-start(f32[4,8]{1,0:T(4,128)S(1)} %add.56), channel_id=1, source_target_pairs={{0,2},{1,3},{2,0},{3,1},{4,6},{5,7},{6,4},{7,5},{8,10},{9,11},{10,... | collective-permute-start | bytes 392 | tf_op jit(solution)/shard_map/ppermute | solution.py:665
  151.8 1.0 copy-start.1

commit v7 on v6

--- a/solution.py
+++ b/solution.py
@@ -108,26 +108,29 @@
     return half, slabs, pack, place
 
 
-def pack_kernel(count, modes, half, with_lengths, where, table, lengths, basis, own, piece):
+def pack_kernel(counts, halves, modes, where, table, lengths, basis, *refs):
+    owns, piece = refs[:-1], refs[-1]
     left = lax.broadcasted_iota(jnp.int32, (ROWS, LANES), 1) < 64
     wave, share = where[0], where[1]
-
-    def unit(i, carry):
-        first = pl.multiple_of(table[wave * count + i, 0], LANES)
-        second = pl.multiple_of(table[wave * count + i, 1], LANES)
-        row = pl.multiple_of(table[wave * count + i, 2], ROWS)
-        for k in range(modes):
-            one = basis[k, pl.ds(row, ROWS), pl.ds(first, LANES)].astype(jnp.float32)
-            two = basis[k, pl.ds(row, ROWS), pl.ds(second, LANES)].astype(jnp.float32)
-            own[i * modes + k] = jnp.where(left, one, two).astype(own.dtype)
-        return carry
-
-    lax.fori_loop(0, count, unit, 0)
-    for n in range(count * modes, own.shape[0]):
-        own[n] = jnp.zeros((ROWS, LANES), own.dtype)
-    piece[: 2 * half] = own[pl.ds(share * (2 * half), 2 * half)]
-    if not with_lengths:
-        return
+    start, line = 0, wave * sum(counts)
+    for count, half, own in zip(counts, halves, owns):
+
+        def unit(i, carry, own=own, line=line):
+            first = pl.multiple_of(table[line + i, 0], LANES)
+            second = pl.multiple_of(table[line + i, 1], LANES)
+            row = pl.multiple_of(table[line + i, 2], ROWS)
+            for k in range(modes):
+                one = basis[k, pl.ds(row, ROWS), pl.ds(first, LANES)].astype(jnp.float32)
+                two = basis[k, pl.ds(row, ROWS), pl.ds(second, LANES)].astype(jnp.float32)
+                own[i * modes + k] = jnp.where(left, one, two).astype(own.dtype)
+            return carry
+
+        lax.fori_loop(0, count, unit, 0)
+        for n in range(count * modes, own.shape[0]):
+            own[n] = jnp.zeros((ROWS, LANES), own.dtype)
+        piece[start : start + 2 * half] = own[pl.ds(share * (2 * half), 2 * half)]
+        start += 2 * half
+        line = line + count
     line = lax.broadcasted_iota(jnp.int32, (ROWS, LANES), 0)
     slab = jnp.zeros((ROWS, LANES), jnp.float32)
     for i in range(lengths.shape[0]):
@@ -136,28 +139,27 @@
             value = rest.astype(jnp.bfloat16).astype(jnp.float32)
             slab = jnp.where(line == 3 * i + limb, value, slab)
             rest = rest - value
-    piece[2 * half] = slab.astype(piece.dtype)
-
-
-def pack_rows(basis, wave_lengths, table, where, half, slabs, with_lengths):
-    modes = basis.shape[0]
-    waves, count, _ = table.shape
-    smem = pl.BlockSpec(memory_space=pltpu.SMEM)
-    vmem = pl.BlockSpec(memory_space=pltpu.VMEM)
-    return pl.pallas_call(
-        functools.partial(pack_kernel, count, modes, half, with_lengths),
-        out_shape=(
-            jax.ShapeDtypeStruct((slabs, ROWS, LANES), basis.dtype),
-            jax.ShapeDtypeStruct((2 * half + int(with_lengths), ROWS, LANES), basis.dtype),
-        ),
-        in_specs=[smem, smem, smem, vmem],
-        out_specs=(vmem, vmem),
+    piece[start] = slab.astype(piece.dtype)
+
+
+def pack_rows(basis, wave_lengths, plans, where):
+    table = np.concatenate([pack for _, _, pack, _ in plans], axis=1)
+    counts = tuple(pack.shape[1] for _, _, pack, _ in plans)
+    halves = tuple(half for half, _, _, _ in plans)
+    tile = (ROWS, LANES)
+    return pl.pallas_call(
+        functools.partial(pack_kernel, counts, halves, basis.shape[0]),
+        out_shape=tuple(jax.ShapeDtypeStruct((slabs,) + tile, basis.dtype) for _, slabs, _, _ in plans)
+        + (jax.ShapeDtypeStruct((2 * sum(halves) + 1,) + tile, basis.dtype),),
+        in_specs=[SMEM, SMEM, SMEM, VMEM],
+        out_specs=(VMEM,) * (len(plans) + 1),
         compiler_params=pltpu.CompilerParams(vmem_limit_bytes=VMEM_BYTES),
-    )(where, table.reshape(waves * count, 3), wave_lengths, basis)
-
-
-def split_kernel(half, sent, parts_count, where, own_lengths, *refs):
-    parts, (low_ref, high_ref, length_ref) = refs[:parts_count], refs[-3:]
+    )(where, table.reshape(-1, 3), wave_lengths, basis)
+
+
+def split_kernel(halves, sent, parts_count, where, own_lengths, *refs):
+    parts, (low_ref, high_ref, second_ref, length_ref) = refs[:parts_count], refs[-4:]
+    half, other = halves
     wave, waves = where[0], parts_count + 1
     kept = own_lengths.shape[0] - sent
     for s in range(waves):
@@ -165,7 +167,7 @@
             if s == 0:
                 value = jnp.full((8, LANES), own_lengths[sent + i], jnp.float32)
             else:
-                slab = parts[s - 1][2 * half].astype(jnp.float32)
+                slab = parts[s - 1][2 * (half + other)].astype(jnp.float32)
                 line = 3 * (sent + i)
                 value = (slab[line : line + 1] + slab[line + 1 : line + 2]) + slab[
                     line + 2 : line + 3
@@ -175,40 +177,38 @@
     for s, part in enumerate(parts):
         low_ref[s * half : (s + 1) * half] = part[:half]
         high_ref[s * half : (s + 1) * half] = part[half : 2 * half]
-
-
-def split_parts(parts, where, wave_lengths, half, sent, tokens):
+        second_ref[s * 2 * other : (s + 1) * 2 * other] = part[2 * half : 2 * (half + other)]
+
+
+def split_parts(parts, where, wave_lengths, halves, sent, tokens):
     count = (len(parts) + 1) * (wave_lengths.shape[0] - sent)
-    slabs = jax.ShapeDtypeStruct((len(parts) * half, ROWS, LANES), parts[0].dtype)
-    return pl.pallas_call(
-        functools.partial(split_kernel, half, sent, len(parts)),
-        out_shape=(slabs, slabs, jax.ShapeDtypeStruct((count, 8, LANES), jnp.float32)),
+    slabs = lambda n: jax.ShapeDtypeStruct((len(parts) * n, ROWS, LANES), parts[0].dtype)
+    return pl.pallas_call(
+        functools.partial(split_kernel, halves, sent, len(parts)),
+        out_shape=(slabs(halves[0]), slabs(halves[0]), slabs(2 * halves[1]), jax.ShapeDtypeStruct((count, 8, LANES), jnp.float32)),
         in_specs=[SMEM, SMEM] + [VMEM] * (len(parts) + len(tokens)),
-        out_specs=(VMEM,) * 3,
+        out_specs=(VMEM,) * 4,
         compiler_params=pltpu.CompilerParams(vmem_limit_bytes=VMEM_BYTES),
     )(where, wave_lengths, *parts, *tokens)
 
 
-def join_kernel(count, *refs):
-    start = 0
-    for one in refs[:count]:
-        refs[-2][start : start + one.shape[0]] = one[...]
-        start += one.shape[0]
-    refs[-1][...] = jnp.zeros_like(refs[-1])
-
-
-def join(arrays, tokens):
-    long = sum(one.shape[0] for one in arrays)
-    return pl.pallas_call(
-        functools.partial(join_kernel, len(arrays)),
-        out_shape=(
-            jax.ShapeDtypeStruct((long,) + arrays[0].shape[1:], arrays[0].dtype),
-            jax.ShapeDtypeStruct((8, LANES), jnp.float32),
+def join_kernel(pairs, *refs):
+    for i in range(pairs):
+        one, two, out = refs[2 * i], refs[2 * i + 1], refs[i - pairs]
+        out[: one.shape[0]] = one[...]
+        out[one.shape[0] :] = two[...]
+
+
+def join(pairs, token):
+    return pl.pallas_call(
+        functools.partial(join_kernel, len(pairs)),
+        out_shape=tuple(
+            jax.ShapeDtypeStruct((2 * one.shape[0],) + one.shape[1:], one.dtype) for one, _ in pairs
         ),
-        in_specs=[VMEM] * (len(arrays) + len(tokens)),
-        out_specs=(VMEM, VMEM),
+        in_specs=[VMEM] * (2 * len(pairs) + 1),
+        out_specs=(VMEM,) * len(pairs),
         compiler_params=pltpu.CompilerParams(vmem_limit_bytes=VMEM_BYTES),
-    )(*arrays, *tokens)
+    )(*[one for pair in pairs for one in pair], token)
 
 
 def along_wave(piece, waves):
@@ -228,12 +228,22 @@
     return lax.ppermute(x, ("groups", "field"), pairs)
 
 
+def after(arrays, tokens):
+    any_memory = pl.BlockSpec(memory_space=pl.ANY)
+    return pl.pallas_call(
+        lambda *refs: None,
+        out_shape=tuple(jax.ShapeDtypeStruct(x.shape, x.dtype) for x in arrays),
+        in_specs=[any_memory] * len(arrays) + [VMEM] * len(tokens),
+        out_specs=(any_memory,) * len(arrays),
+        input_output_aliases={i: i for i in range(len(arrays))},
+    )(*arrays, *tokens)
+
+
 def gather_halves(halves, token):
     got = []
-    tokens = []
-    for h, (one, two) in enumerate(((2, 4), (4, 2))):
-        mine = halves[h]
-        both, done = join([mine, swap(mine, one)], [token])
+    routes = ((2, 4), (4, 2))
+    joined = join([(mine, swap(mine, one)) for mine, (one, _) in zip(halves, routes)], token)
+    for h, (both, (one, two)) in enumerate(zip(joined, routes)):
         far = swap(both, two)
         got.append((h, both, (0, one)))
         got.append((h, far, (two, one | two)))
@@ -242,12 +252,16 @@
     return got
 
 
-def gather_direct(mine):
-    got = [(None, mine, (0,)), (None, swap(mine, 1), (1,))]
-    for mask in (6, 2, 4):
-        there = swap(mine, mask)
-        got.append((None, there, (mask,)))
-        got.append((None, swap(there, 1), (mask | 1,)))
+def send_direct(mine):
+    return [(None, mine, (0,)), (None, swap(mine, 1), (1,))], [
+        (mask, swap(mine, mask)) for mask in (6, 2, 4)
+    ]
+
+
+def end_direct(got, there, token):
+    arrays = after([array for _, array in there], [token])
+    for (mask, _), array in zip(there, arrays):
+        got = got + [(None, array, (mask,)), (None, swap(array, 1), (mask | 1,))]
     return got
 
 
@@ -452,7 +466,8 @@
     real, imag = columns_of(before[0], scratch[3][...], column_ref)
     intensity = real * real + imag * imag
     image_ref[0] = intensity
-    sum_ref[0] = jnp.sum(intensity.reshape(positions, rows, PIX), axis=1)
+    sums = jnp.sum(intensity.reshape(positions, rows, PIX), axis=1)
+    sum_ref[0] = jnp.broadcast_to(jnp.sum(sums, axis=1, keepdims=True), (positions, LANES))
 
 
 def transform_scratch(positions, rows):
@@ -473,8 +488,10 @@
     )
 
 
-def by_length(array):
-    return pl.BlockSpec((1,) + array.shape[1:], lambda l: (l,) + (0,) * (array.ndim - 1))
+def by_length(array, start=0):
+    return pl.BlockSpec(
+        (1,) + array.shape[1:], lambda l: (l + start,) + (0,) * (len(array.shape) - 1)
+    )
 
 
 def whole_fields(stage, own, got, spread, place, where, length, tables, sizes, tokens):
@@ -517,8 +534,9 @@
     )(length, place, where, own, *arrays, spread, *tables, *tokens)
 
 
-def row_fields(stage, path, opening, length, tables, positions):
-    lengths = length.shape[0]
+def row_fields(stage, path, opening, length, tables, positions, part):
+    start, stop, _ = part.indices(length.shape[0])
+    lengths = stop - start
     rows = tables[0].shape[2] // 2
     if stage < len(STAGES) - 1:
         out_shape = (
@@ -529,14 +547,15 @@
     else:
         out_shape = (
             jax.ShapeDtypeStruct((lengths, positions * rows, PIX), jnp.float32),
-            jax.ShapeDtypeStruct((lengths, positions, PIX), jnp.float32),
+            jax.ShapeDtypeStruct((lengths, positions, LANES), jnp.float32),
         )
         out_specs = tuple(by_length(one) for one in out_shape)
     return pl.pallas_call(
         functools.partial(rows_kernel, stage, positions, rows),
         grid=(lengths,),
         out_shape=out_shape,
-        in_specs=[by_length(length), VMEM, VMEM] + [by_length(table) for table in tables],
+        in_specs=[by_length(length, start), VMEM, VMEM]
+        + [by_length(table, start) for table in tables],
         out_specs=out_specs,
         scratch_shapes=transform_scratch(positions, rows),
         cost_estimate=transform_cost(stage, lengths, positions, rows),
@@ -544,10 +563,15 @@
     )(length, path, opening, *tables)
 
 
-def mix_kernel(inverse_ref, weight_ref, sent_ref, image_ref, out_ref):
+def mix_kernel(sum_ref, weight_ref, sent_ref, image_ref, out_ref):
     count, templates, rows = out_ref.shape[:3]
     for i in range(count):
         f = pl.program_id(0) * count + i
+        inverse = [
+            1.0 / (sum_ref[l, pl.ds(f, 1)] / (PIX * PIX) + EPSILON)
+            for l in range(image_ref.shape[0])
+        ]
+        inverse = [jnp.concatenate([one] * (PIX // LANES), axis=1) for one in inverse]
         blocks = []
         for start in range(i * rows, (i + 1) * rows, ROWS):
             lines = slice(start, start + ROWS)
@@ -555,7 +579,7 @@
                 jnp.concatenate(
                     [sent_ref[l, lines] for l in range(sent_ref.shape[0])]
                     + [
-                        (image_ref[l, lines] * inverse_ref[l, f]).astype(jnp.bfloat16)
+                        (image_ref[l, lines] * inverse[l]).astype(jnp.bfloat16)
                         for l in range(image_ref.shape[0])
                     ],
                     axis=0,
@@ -571,7 +595,7 @@
                 ]
 
 
-def mix(spread, inverse, sent, images, templates, rows):
+def mix(spread, sums, sent, images, templates, rows):
     positions = spread.shape[0]
     count = 2 if positions % 2 == 0 else 1
     return pl.pallas_call(
@@ -579,14 +603,14 @@
         grid=(positions // count,),
         out_shape=jax.ShapeDtypeStruct((positions, templates, rows, PIX), jnp.bfloat16),
         in_specs=[
-            SMEM,
+            VMEM,
             pl.BlockSpec((count,) + spread.shape[1:], lambda f: (f, 0, 0)),
             pl.BlockSpec((sent.shape[0], count * rows, PIX), lambda f: (0, f, 0)),
             pl.BlockSpec((images.shape[0], count * rows, PIX), lambda f: (0, f, 0)),
         ],
         out_specs=pl.BlockSpec((count, templates, rows, PIX), lambda f: (f, 0, 0, 0)),
-        compiler_params=pltpu.CompilerParams(vmem_limit_bytes=VMEM_BYTES),
-    )(inverse, spread, sent, images)
+        compiler_params=pltpu.CompilerParams(vmem_limit_bytes=24 * 2**20),
+    )(sums, spread, sent, images)
 
 
 def table_kernel(length_ref, y_ref, v_ref, u_ref, x_ref, row_ref, column_ref, token_ref):
@@ -679,11 +703,8 @@
     share = (lax.axis_index("groups") % 2) * 4 + lax.axis_index("field") % 4
     where = jnp.stack([mine, share]).astype(jnp.int32)
     plans = [layout(waves, modes, stage) for stage in range(len(STAGES))]
-    owns, parts = [], []
-    for stage, (half, slabs, pack, _) in enumerate(plans):
-        own, piece = pack_rows(mode_basis, wave_lengths, pack, where, half, slabs, stage == 0)
-        owns.append(own)
-        parts.append(along_wave(piece, waves))
+    *owns, piece = pack_rows(mode_basis, wave_lengths, plans, where)
+    parts = along_wave(piece, waves)
 
     selector = (
         table_index[:, None] == jnp.arange(coef_table.shape[0], dtype=jnp.int32)[None, :]
@@ -710,12 +731,19 @@
     )
     own_row, own_column, own_token = tables(own_length, 0, PIX)
 
-    low, high, every = split_parts(
-        parts[0], where, wave_lengths, plans[0][0], sent_lengths, (spread_token, own_token)
+    low, high, second, every = split_parts(
+        parts,
+        where,
+        wave_lengths,
+        (plans[0][0], plans[1][0]),
+        sent_lengths,
+        (spread_token, own_token),
     )
     all_row, all_column, all_token = tables(every, mine * rows, rows)
     got = gather_halves((low, high), all_token)
-    second, second_token = join(parts[1], [array[0, :8] for _, array, masks in got if masks in ((2, 6), (4, 6))])
+    (second,) = after(
+        [second], [array[0, :8] for _, array, masks in got if masks in ((2, 6), (4, 6))]
+    )
 
     def sizes(stage):
         half, slabs, _, _ = plans[stage]
@@ -723,10 +751,16 @@
 
     before, path, opening = whole_fields(
         0, owns[0], got, path_spread, plans[0][3], where, own_length, (own_row,), sizes(0),
-        (second_token,),
-    )
-    got = gather_direct(second)
-    rows_before, rows_token = row_fields(0, path, opening, every, (all_row,), positions)
+        (second[0, :8],),
+    )
+    got, there = send_direct(second)
+    cut = every.shape[0] // 2
+    rows_before = []
+    for n, part in enumerate((slice(0, cut), slice(cut, None))):
+        one, rows_token = row_fields(0, path, opening, every, (all_row,), positions, part)
+        rows_before.append(one)
+        if n == 0:
+            got = end_direct(got, there, rows_token)
     spectra, path, opening = whole_fields(
         1, owns[1], got, path_spread, plans[1][3], where, own_length,
         (own_row, own_column, before), sizes(1), (rows_token,),
@@ -734,10 +768,15 @@
     sent = lax.all_to_all(spectra, "wave", split_axis=0, concat_axis=0, tiled=True)
     sent = sent.reshape(waves * sent_lengths, positions * rows, PIX)
     images, sums = row_fields(
-        1, path, opening, every, (all_row, all_column, rows_before), positions
-    )
-    level = add_over_wave(jnp.sum(sums, axis=2), waves) / (PIX * PIX)
-    return mix(mix_spread, 1.0 / (level + EPSILON), sent, images, templates, rows)
+        1,
+        path,
+        opening,
+        every,
+        (all_row, all_column, jnp.concatenate(rows_before)),
+        positions,
+        slice(None),
+    )
+    return mix(mix_spread, add_over_wave(sums, waves), sent, images, templates, rows)
 
 
 def solution(mesh):

time: 158 us -> 157 us (level)
  Pallas kernels: 89.5 us -> 85.9 us
  starting transfers between devices: 26.6 us -> 24.2 us
  waiting for transfers between devices: 28 us -> 30.2 us
    pallas_call x6 -> x5, Pallas kernels: 14.1 us -> 9.81 us  [the longest x1 4.21 us: pack_rows(): pl.pallas_call(functools.partial(pack_kernel, counts, halves, basis.shape...]
    ppermute x6 -> x3, starting transfers between devices: 8.95 us -> 6.07 us  [along_wave(): lax.ppermute(piece, 'wave', [(i, (i + s) % waves) for i in range(waves)])]
    pallas_call x2 -> x3, Pallas kernels: 34.8 us -> 37.4 us  [row_fields(): pl.pallas_call(functools.partial(rows_kernel, stage, positions, rows), gr...]
    ppermute x15, waiting for transfers between devices: 8.53 us -> 11.2 us  [swap(): return lax.ppermute(x, ('groups', 'field'), pairs)]
    pallas_call x1, Pallas kernels: 4.54 us -> 2.65 us  [mix(): pl.pallas_call(mix_kernel, grid=(positions // count,), out_shape=jax.Shap...]
    ppermute x6 -> x3, waiting for transfers between devices: 16.1 us -> 15 us  [along_wave(): lax.ppermute(piece, 'wave', [(i, (i + s) % waves) for i in range(waves)])]
    unnamed x52 -> x50, local copies, waits for them, and re-layouts: 5.3 us -> 5.45 us
  transfers between devices with their start and end apart: 24 -> 21, of which waited for: 8 -> 5; matrix products, arithmetic and copies ran while one was open for 5% -> 6% of each run, Pallas kernels for 41% -> 38%
where the time goes in v7:
time: 157 us; the launch traced here: 156 us
  Pallas kernels  85.9 us (55%)
  waiting for transfers between devices  30.2 us (19%)
  starting transfers between devices  24.2 us (15%)
  local copies, waits for them, and re-layouts  8.59 us (5%)
  other arithmetic  4.83 us (3%)
  matrix products  1.88 us (1%)
    pallas_call x3, Pallas kernels, row_fields(): pl.pallas_call(functools.partial(rows_kernel, stage, positions, rows), gr...  37.4 us
    pallas_call x2, Pallas kernels, whole_fields(): pl.pallas_call(functools.partial(whole_kernel, stage, (positions, modes,...  25.6 us
    ppermute x3, waiting for transfers between devices, along_wave(): lax.ppermute(piece, 'wave', [(i, (i + s) % waves) for i in range(waves)])  15 us
    ppermute x15, waiting for transfers between devices, swap(): return lax.ppermute(x, ('groups', 'field'), pairs)  11.2 us
    ppermute x15, starting transfers between devices, swap(): return lax.ppermute(x, ('groups', 'field'), pairs)  9.04 us
    pallas_call x2, Pallas kernels, tables(): pl.pallas_call(table_kernel, grid=(lengths,), out_shape=(jax.ShapeDtypeSt...  8.53 us
    ppermute x3, starting transfers between devices, along_wave(): lax.ppermute(piece, 'wave', [(i, (i + s) % waves) for i in range(waves)])  6.07 us
    unnamed x50, local copies, waits for them, and re-layouts  5.45 us
  transfers between devices with their start and end apart: 21, of which 5 were waited for; matrix products, arithmetic and copies ran while one was open for 6% of the time, Pallas kernels for 38%

profile of v7, /device:TPU:0, one launch (start us, length us, event | category | flops | bytes accessed | tf_op | source)
XLA Modules:
  0.0 156.0 jit_solution(6358039238434707295)
XLA Ops:
  0.0 0.6 pad_add_fusion.where
  0.7 4.2 %shard_map.145 = (bf16[256,16,128]{2,1,0:T(8,128)(2,1)}, bf16[320,16,128]{2,1,0:T(8,128)(2,1)}, bf16[73,16,128]{2,1,0:T(8,128)(2,1)}) custom-call(s32[2]{0:T(128)} %pad_add_fusion.where, s32[100,3]{1,0:T(8,128)} %constant.57.clone.table, f32[2]{0:T(128)} %own_lengths.1, bf16[22,128,512]{2,1,0:T(8,128)(2,1)} %basis.1), custom_call_target="tpu_custom_call" | custom-call | tf_op jit(solution)/shard_map/pallas_call | solution.py:150
  4.9 5.1 %collective-permute-start.2 = (bf16[73,16,128]{2,1,0:T(8,128)(2,1)}, bf16[73,16,128]{2,1,0:T(8,128)(2,1)S(1)}, u32[]{:S(2)}, u32[]{:S(2)}) collective-permute-start(bf16[73,16,128]{2,1,0:T(8,128)(2,1)} %get-tuple-element.38), channel_id=1, source_target_pairs={{0,3},{1,0},{2,1},{3,2},{4,7},{5,4},{6,5},{7,6},{8,11},{9,8},{10,9... | collective-permute-start | bytes 897032 | tf_op jit(solution)/shard_map/ppermute | solution.py:216
  9.9 0.0 collective-permute-start.1
  9.9 1.0 collective-permute-start
  10.9 1.1 fusion.6
  12.1 0.1 copy.32
  12.2 0.1 copy.33
  12.3 0.7 pad_maximum_fusion.1.refs_1_
  13.0 0.8 fusion.refs_0_
  13.8 1.9 %shard_map.146 = (bf16[1,128,352]{2,1,0:T(8,128)(2,1)}, bf16[8,128,128]{2,1,0:T(8,128)(2,1)}, f32[8,128]{1,0:T(8,128)}) custom-call(bf16[1,8,22]{2,1,0:T(8,128)(2,1)} %fusion.refs_0_, bf16[8,8,8]{2,1,0:T(8,128)(2,1)} %pad_maximum_fusion.1.refs_1_), custom_call_target="tpu_custom_call" | custom-call | tf_op jit(solution)/shard_map/pallas_call | solution.py:289
  15.8 0.7 add_convert_fusion.u_ref
  16.5 0.6 broadcast_in_dim.8.length_ref
  17.1 3.5 %shard_map.147 = (bf16[1,4,512,256]{3,2,1,0:T(8,128)(2,1)}, bf16[1,1024,512]{2,1,0:T(8,128)(2,1)}, f32[8,128]{1,0:T(8,128)}) custom-call(f32[1,8,128]{2,1,0:T(8,128)} %broadcast_in_dim.8.length_ref, f32[512,1]{1,0:T(8,128)} %constant.58.clone.y_ref, f32[1,256]{1,0:T(1,128)} %constant.59.clone.v_ref, f32[256,1]{1,0:T(8,128)} %add_convert_fusion.u_ref, ...), custom_call_target="tpu_custom_call" | custom-call | flops 3932160 | bytes 1048576 | tf_op jit(solution)/shard_map/pallas_call | solution.py:653
  20.6 15.0 %collective-permute-done.1.refs_1_ = bf16[73,16,128]{2,1,0:T(8,128)(2,1)S(1)} collective-permute-done((bf16[73,16,128]{2,1,0:T(8,128)(2,1)}, bf16[73,16,128]{2,1,0:T(8,128)(2,1)S(1)}, u32[]{:S(2)}, u32[]{:S(2)}) %collective-permute-start.1) | collective-permute-done | bytes 299040 | tf_op jit(solution)/shard_map/ppermute | solution.py:216
  35.6 0.7 copy-done.9
  36.3 0.1 copy-done.10
  36.4 2.1 %shard_map.148 = (bf16[48,16,128]{2,1,0:T(8,128)(2,1)}, bf16[48,16,128]{2,1,0:T(8,128)(2,1)}, bf16[120,16,128]{2,1,0:T(8,128)(2,1)}, f32[4,8,128]{2,1,0:T(8,128)}) custom-call(s32[2]{0:T(128)} %pad_add_fusion.where, f32[2]{0:T(128)} %own_lengths.1, bf16[73,16,128]{2,1,0:T(8,128)(2,1)} %copy-done.10, bf16[73,16,128]{2,1,0:T(8,128)(2,1)} %copy-done.9, ...), custom_call_target="tpu_custom_call" | custom-call | tf_op jit(solution)/shard_map/pallas_call | solution.py:186
  38.5 1.5 collective-permute-start.3
  40.0 1.5 collective-permute-start.4
  41.5 0.6 add_convert_fusion.1.u_ref
  42.2 5.0 %shard_map.149 = (bf16[4,4,128,256]{3,2,1,0:T(8,128)(2,1)}, bf16[4,1024,512]{2,1,0:T(8,128)(2,1)}, f32[8,128]{1,0:T(8,128)}) custom-call(f32[4,8,128]{2,1,0:T(8,128)} %get-tuple-element.41.length_ref, f32[512,1]{1,0:T(8,128)} %constant.58.clone.y_ref, f32[1,256]{1,0:T(1,128)} %constant.59.clone.v_ref, f32[64,1]{1,0:T(8,128)} %add_convert_fusion.1.u_ref, ...), custom_call_target="tpu_custom_call" | custom-call | flops 15728640 | bytes 4194304 | tf_op jit(solution)/shard_map/pallas_call | solution.py:653
  47.2 0.0 collective-permute-done.3.refs_1_
  47.2 0.0 copy-start.11
  47.2 0.6 copy-done.11
  47.8 0.1 copy-done.12
  47.9 2.1 %shard_map.150 = (bf16[96,16,128]{2,1,0:T(8,128)(2,1)}, bf16[96,16,128]{2,1,0:T(8,128)(2,1)}) custom-call(bf16[48,16,128]{2,1,0:T(8,128)(2,1)} %get-tuple-element.44.refs_0_, bf16[48,16,128]{2,1,0:T(8,128)(2,1)} %copy-done.11, bf16[48,16,128]{2,1,0:T(8,128)(2,1)} %get-tuple-element.45.refs_2_, bf16[48,16,128]{2,1,0:T(8,128)(2,1)} %copy-done.12, ...), custom_call_target="tpu_custom_call" | custom-call | tf_op jit(solution)/shard_map/pallas_call | solution.py:203
  50.0 0.5 collective-permute-start.5
  50.5 0.5 collective-permute-start.6
  51.1 0.5 collective-permute-start.13
  51.6 8.1 %collective-permute-done.5.refs_2_ = bf16[96,16,128]{2,1,0:T(8,128)(2,1)S(1)} collective-permute-done((bf16[96,16,128]{2,1,0:T(8,128)(2,1)}, bf16[96,16,128]{2,1,0:T(8,128)(2,1)S(1)}, u32[]{:S(2)}, u32[]{:S(2)}) %collective-permute-start.5) | collective-permute-done | bytes 393248 | tf_op jit(solution)/shard_map/ppermute | solution.py:228
  59.7 0.0 collective-permute-start.12
  59.7 0.6 slice_bitcast_fusion.2.refs_1_
  60.3 0.0 collective-permute-done.6.refs_6_
  60.3 0.5 collective-permute-start.14
  60.8 0.6 slice_bitcast_fusion.1.refs_2_
  61.4 0.7 shard_map.151.refs_1_
  62.1 0.7 collective-permute-start.10
  62.7 1.3 slice_bitcast_fusion.refs_11_
  64.0 0.5 collective-permute-start.9
  64.6 0.0 collective-permute-done.13.refs_7_
  64.6 2.3 %collective-permute-start.8 = (bf16[120,16,128]{2,1,0:T(8,128)(2,1)}, bf16[120,16,128]{2,1,0:T(8,128)(2,1)S(1)}, u32[]{:S(2)}, u32[]{:S(2)}) collective-permute-start(bf16[120,16,128]{2,1,0:T(8,128)(2,1)} %shard_map.151.refs_1_), channel_id=1, source_target_pairs={{0,24},{4,28},{8,16},{12,20},{16,8},{20,12},{24,0},{28,4},{1,25},{... | collective-permute-start | bytes 1474568 | tf_op jit(solution)/shard_map/ppermute | solution.py:228
  66.9 10.4 %shard_map.152 = (bf16[1,2048,512]{2,1,0:T(8,128)(2,1)}, f32[40,128,128]{2,1,0:T(8,128)}, f32[40,16,128]{2,1,0:T(8,128)}) custom-call(f32[1,8,128]{2,1,0:T(8,128)} %broadcast_in_dim.8.length_ref, s32[40,4]{1,0:T(8,128)} %constant.61.clone.place, s32[2]{0:T(128)} %pad_add_fusion.where, bf16[256,16,128]{2,1,0:T(8,128)(2,1)} %get-tuple-element.49.refs_0_, ...), custom_call_target="tpu_custom_call" | custom-call | flops 4426531840 | bytes 8388608 | tf_op jit(solution)/shard_map/pallas_call | solution.py:511
  77.3 8.2 %shard_map.153 = (bf16[2,512,512]{2,1,0:T(8,128)(2,1)}, f32[8,128]{1,0:T(8,128)}) custom-call(f32[4,8,128]{2,1,0:T(8,128)} %get-tuple-element.41.length_ref, f32[40,128,128]{2,1,0:T(8,128)} %get-tuple-element.52.path, f32[40,16,128]{2,1,0:T(8,128)} %get-tuple-element.53.opening, bf16[4,4,128,256]{3,2,1,0:T(8,128)(2,1)} %get-tuple-element.54.row_ref), custom_call_target="tpu_custom_call" | custom-call | flops 2813265920 | bytes 8388608 | tf_op jit(solution)/shard_map/pallas_call | solution.py:553
  85.5 3.0 %collective-permute-done.8.refs_0_ = bf16[120,16,128]{2,1,0:T(8,128)(2,1)S(1)} collective-permute-done((bf16[120,16,128]{2,1,0:T(8,128)(2,1)}, bf16[120,16,128]{2,1,0:T(8,128)(2,1)S(1)}, u32[]{:S(2)}, u32[]{:S(2)}) %collective-permute-start.8) | collective-permute-done | bytes 491552 | tf_op jit(solution)/shard_map/ppermute | solution.py:228
  88.5 0.8 copy-done.7
  89.3 0.7 shard_map.154
  90.0 0.5 collective-permute-start.16
  90.5 8.2 %shard_map.155 = (bf16[2,512,512]{2,1,0:T(8,128)(2,1)}, f32[8,128]{1,0:T(8,128)}) custom-call(f32[4,8,128]{2,1,0:T(8,128)} %get-tuple-element.41.length_ref, f32[40,128,128]{2,1,0:T(8,128)} %get-tuple-element.52.path, f32[40,16,128]{2,1,0:T(8,128)} %get-tuple-element.53.opening, bf16[4,4,128,256]{3,2,1,0:T(8,128)(2,1)} %get-tuple-element.54.row_ref), custom_call_target="tpu_custom_call" | custom-call | flops 2813265920 | bytes 8388608 | tf_op jit(solution)/shard_map/pallas_call | solution.py:553
  98.8 0.7 copy-done.16
  99.5 0.2 copy-done.17
  99.7 0.1 copy-done.18
  99.8 0.2 copy-done.19
  100.0 15.2 %shard_map.156 = (bf16[4,1,512,256]{3,2,1,0:T(8,128)(2,1)}, f32[56,128,128]{2,1,0:T(8,128)}, f32[56,16,128]{2,1,0:T(8,128)}) custom-call(f32[1,8,128]{2,1,0:T(8,128)} %broadcast_in_dim.8.length_ref, s32[56,4]{1,0:T(8,128)} %constant.62.clone.place, s32[2]{0:T(128)} %pad_add_fusion.where, bf16[320,16,128]{2,1,0:T(8,128)(2,1)} %get-tuple-element.42.refs_0_, ...), custom_call_target="tpu_custom_call" | custom-call | flops 6197144576 | bytes 8388608 | tf_op jit(solution)/shard_map/pallas_call | solution.py:511
  115.2 4.4 %all-to-all-start = ((bf16[4,1,512,256]{3,2,1,0:T(8,128)(2,1)}), bf16[4,1,512,256]{3,2,1,0:T(8,128)(2,1)S(1)}, u32[]{:S(2)}, u32[]{:S(2)}) async-start(bf16[4,1,512,256]{3,2,1,0:T(8,128)(2,1)} %get-tuple-element.69), calls=%async_computation | async-start | bytes 2097152 | tf_op jit(solution)/shard_map/all_to_all | solution.py:768
  119.6 1.5 pad_maximum_fusion.refs_1_
  121.1 21.0 %shard_map.157 = (f32[4,512,256]{2,1,0:T(8,128)}, f32[4,8,128]{2,1,0:T(8,128)}) custom-call(f32[4,8,128]{2,1,0:T(8,128)} %get-tuple-element.41.length_ref, f32[56,128,128]{2,1,0:T(8,128)} %get-tuple-element.62.path, f32[56,16,128]{2,1,0:T(8,128)} %get-tuple-element.63.opening, bf16[4,4,128,256]{3,2,1,0:T(8,128)(2,1)} %get-tuple-element.54.row_ref, ...), custom_call_target="tpu_custom_call" | custom-call | flops 7877144576 | bytes 8388608 | tf_op jit(solution)/shard_map/pallas_call | solution.py:553
  142.2 2.0 %collective-permute-start.18 = (f32[4,8,128]{2,1,0:T(8,128)}, f32[4,8,128]{2,1,0:T(8,128)S(1)}, u32[]{:S(2)}, u32[]{:S(2)}) collective-permute-start(f32[4,8,128]{2,1,0:T(8,128)} %get-tuple-element.67), channel_id=1, source_target_pairs={{0,1},{1,0},{2,3},{3,2},{4,5},{5,4},{6,7},{7,6},{8,9},{9,8},{10,11... | collective-permute-start | bytes 49160 | tf_op jit(solution)/shard_map/ppermute | solution.py:689
  144.2 2.1 %collective-permute-done.18 = f32[4,8,128]{2,1,0:T(8,128)S(1)} collective-permute-done((f32[4,8,128]{2,1,0:T(8,128)}, f32[4,8,128]{2,1,0:T(8,128)S(1)}, u32[]{:S(2)}, u32[]{:S(2)}) %collective-permute-start.18) | collective-permute-done | bytes 16416 | tf_op jit(solution)/shard_map/ppermute | solution.py:689
  146.3 0.7 add.50
  147.1 2.7 %collective-permute-start.19 = (f32[4,8,128]{2,1,0:T(8,128)S(1)}, f32[4,8,128]{2,1,0:T(8,128)S(1)}, u32[]{:S(2)}, u32[]{:S(2)}) collective-permute-start(f32[4,8,128]{2,1,0:T(8,128)S(1)} %add.50), channel_id=1, source_target_pairs={{0,2},{1,3},{2,0},{3,1},{4,6},{5,7},{6,4},{7,5},{8,10},{9,11},{10,... | collective-permute-start | bytes 49160 | tf_op jit(solution)/shard_map/ppermute | solution.py:689
  149.8 1.9 %collective-permute-done.19 = f32[4,8,128]{2,1,0:T(8,128)S(1)} collective-permute-done((f32[4,8,128]{2,1,0:T(8,128)S(1)}, f32[4,8,128]{2,1,0:T(8,128)S(1)}, u32[]{:S(2)}, u32[]{:S(2)}) %collective-permute-start.19) | collective-permute-done | bytes 16416 | tf_op jit(solution)/shard_map/ppermute | solution.py:689
  151.7 1.6 %copy-done.1 = f32[4,512,256]{2,1,0:T(8,128)S(1)} copy-done((f32[4,512,256]{2,1,0:T(8,128)S(1)}, f32[4,512,256]{2,1,0:T(8,128)}, u32[]{:S(2)}) %copy-start.1) | copy-done | bytes 2097176
  153.3 2.6 %shard_map.158 = bf16[8,8,64,256]{3,2,1,0:T(8,128)(2,1)} custom-call(f32[4,8,128]{2,1,0:T(8,128)S(1)} %add.51.sum_ref, bf16[8,128,128]{2,1,0:T(8,128)(2,1)S(1)} %copy-done.2, bf16[4,512,256]{2,1,0:T(8,128)(2,1)S(1)} %bitcast.22, f32[4,512,256]{2,1,0:T(8,128)S(1)} %copy-done.1), custom_call_target="tpu_custom_call" | custom-call | tf_op jit(solution)/shard_map/pallas_call | solution.py:601
  (58 shorter events, 0.1 us)
Async XLA Ops:
  0.0 13.0 %copy-start = (bf16[4096,22]{0,1:T(8,128)(2,1)S(1)}, bf16[4096,22]{0,1:T(8,128)(2,1)}, u32[]{:S(2)}) copy-start(bf16[4096,22]{0,1:T(8,128)(2,1)} %param.16) | copy-start | bytes 540676
  0.0 16.5 %copy-start.13 = (f32[2]{0:T(128)S(1)}, f32[2]{0:T(128)}, u32[]{:S(2)}) copy-start(f32[2]{0:T(128)} %own_lengths.1) | copy-start | bytes 28
  0.0 10.9 %copy-start.22 = (s32[8,8]{1,0:T(8,128)S(1)}, s32[8,8]{1,0:T(8,128)}, u32[]{:S(2)}) copy-start(s32[8,8]{1,0:T(8,128)} %param.20) | copy-start | bytes 772
  0.0 10.9 %copy-start.21 = (f32[1024,8]{0,1:T(8,128)S(1)}, f32[1024,8]{0,1:T(8,128)}, u32[]{:S(2)}) copy-start(f32[1024,8]{0,1:T(8,128)} %param.19) | copy-start | bytes 98308
  0.0 13.0 %copy-start.23 = (s32[8]{0:T(128)S(1)}, s32[8]{0:T(128)}, u32[]{:S(2)}) copy-start(s32[8]{0:T(128)} %param.17) | copy-start | bytes 100
  4.9 15.8 %collective-permute-start.2 = (bf16[73,16,128]{2,1,0:T(8,128)(2,1)}, bf16[73,16,128]{2,1,0:T(8,128)(2,1)S(1)}, u32[]{:S(2)}, u32[]{:S(2)}) collective-permute-start(bf16[73,16,128]{2,1,0:T(8,128)(2,1)} %get-tuple-element.38), channel_id=1, source_target_pairs={{0,3},{1,0},{2,1},{3,2},{4,7},{5,4},{6,5},{7,6},{8,11},{9,8},{10,9... | collective-permute-start | bytes 897032 | tf_op jit(solution)/shard_map/ppermute | solution.py:216
  9.9 25.7 %collective-permute-start.1 = (bf16[73,16,128]{2,1,0:T(8,128)(2,1)}, bf16[73,16,128]{2,1,0:T(8,128)(2,1)S(1)}, u32[]{:S(2)}, u32[]{:S(2)}) collective-permute-start(bf16[73,16,128]{2,1,0:T(8,128)(2,1)} %get-tuple-element.38), channel_id=1, source_target_pairs={{0,2},{1,3},{2,0},{3,1},{4,6},{5,7},{6,4},{7,5},{8,10},{9,11},{10,... | collective-permute-start | bytes 897032 | tf_op jit(solution)/shard_map/ppermute | solution.py:216
  9.9 25.7 %collective-permute-start = (bf16[73,16,128]{2,1,0:T(8,128)(2,1)}, bf16[73,16,128]{2,1,0:T(8,128)(2,1)S(1)}, u32[]{:S(2)}, u32[]{:S(2)}) collective-permute-start(bf16[73,16,128]{2,1,0:T(8,128)(2,1)} %get-tuple-element.38), channel_id=1, source_target_pairs={{0,1},{1,2},{2,3},{3,0},{4,5},{5,6},{6,7},{7,4},{8,9},{9,10},{10,1... | collective-permute-start | bytes 897032 | tf_op jit(solution)/shard_map/ppermute | solution.py:216
  20.6 15.0 %copy-start.8 = (bf16[73,16,128]{2,1,0:T(8,128)(2,1)}, bf16[73,16,128]{2,1,0:T(8,128)(2,1)S(1)}, u32[]{:S(2)}) copy-start(bf16[73,16,128]{2,1,0:T(8,128)(2,1)S(1)} %collective-permute-done.2.refs_2_) | copy-start | bytes 897028
  35.6 0.7 copy-start.9
  35.6 0.8 copy-start.10
  38.5 8.6 %collective-permute-start.3 = (bf16[48,16,128]{2,1,0:T(8,128)(2,1)}, bf16[48,16,128]{2,1,0:T(8,128)(2,1)S(1)}, u32[]{:S(2)}, u32[]{:S(2)}) collective-permute-start(bf16[48,16,128]{2,1,0:T(8,128)(2,1)} %get-tuple-element.44.refs_0_), channel_id=1, source_target_pairs={{0,8},{4,12},{8,0},{12,4},{16,24},{20,28},{24,16},{28,20},{1,9},{5... | collective-permute-start | bytes 589832 | tf_op jit(solution)/shard_map/ppermute | solution.py:228
  40.0 7.2 %collective-permute-start.4 = (bf16[48,16,128]{2,1,0:T(8,128)(2,1)}, bf16[48,16,128]{2,1,0:T(8,128)(2,1)S(1)}, u32[]{:S(2)}, u32[]{:S(2)}) collective-permute-start(bf16[48,16,128]{2,1,0:T(8,128)(2,1)} %get-tuple-element.45.refs_2_), channel_id=1, source_target_pairs={{0,16},{4,20},{8,24},{12,28},{16,0},{20,4},{24,8},{28,12},{1,17},{... | collective-permute-start | bytes 589832 | tf_op jit(solution)/shard_map/ppermute | solution.py:228
  47.2 0.7 copy-start.11
  47.2 0.7 copy-start.12
  50.0 9.6 %collective-permute-start.5 = (bf16[96,16,128]{2,1,0:T(8,128)(2,1)}, bf16[96,16,128]{2,1,0:T(8,128)(2,1)S(1)}, u32[]{:S(2)}, u32[]{:S(2)}) collective-permute-start(bf16[96,16,128]{2,1,0:T(8,128)(2,1)} %get-tuple-element.47.refs_1_), channel_id=1, source_target_pairs={{0,16},{4,20},{8,24},{12,28},{16,0},{20,4},{24,8},{28,12},{1,17},{... | collective-permute-start | bytes 1179656 | tf_op jit(solution)/shard_map/ppermute | solution.py:228
  50.5 9.8 %collective-permute-start.6 = (bf16[96,16,128]{2,1,0:T(8,128)(2,1)}, bf16[96,16,128]{2,1,0:T(8,128)(2,1)S(1)}, u32[]{:S(2)}, u32[]{:S(2)}) collective-permute-start(bf16[96,16,128]{2,1,0:T(8,128)(2,1)} %get-tuple-element.48.refs_5_), channel_id=1, source_target_pairs={{0,8},{4,12},{8,0},{12,4},{16,24},{20,28},{24,16},{28,20},{1,9},{5... | collective-permute-start | bytes 1179656 | tf_op jit(solution)/shard_map/ppermute | solution.py:228
  51.1 13.0 %collective-permute-start.11 = (bf16[96,16,128]{2,1,0:T(8,128)(2,1)}, bf16[96,16,128]{2,1,0:T(8,128)(2,1)S(1)}, u32[]{:S(2)}, u32[]{:S(2)}) collective-permute-start(bf16[96,16,128]{2,1,0:T(8,128)(2,1)} %get-tuple-element.47.refs_1_), channel_id=1, source_target_pairs={{0,4},{4,0},{8,12},{12,8},{16,20},{20,16},{24,28},{28,24},{1,5},{5... | collective-permute-start | bytes 1179656 | tf_op jit(solution)/shard_map/ppermute | solution.py:228
  51.1 13.5 %collective-permute-start.13 = (bf16[96,16,128]{2,1,0:T(8,128)(2,1)}, bf16[96,16,128]{2,1,0:T(8,128)(2,1)}, u32[]{:S(2)}, u32[]{:S(2)}) collective-permute-start(bf16[96,16,128]{2,1,0:T(8,128)(2,1)} %get-tuple-element.48.refs_5_), channel_id=1, source_target_pairs={{0,4},{4,0},{8,12},{12,8},{16,20},{20,16},{24,28},{28,24},{1,5},{5... | collective-permute-start | bytes 1179656 | tf_op jit(solution)/shard_map/ppermute | solution.py:228
  59.7 7.2 %copy-start.14 = (bf16[96,16,128]{2,1,0:T(8,128)(2,1)}, bf16[96,16,128]{2,1,0:T(8,128)(2,1)S(1)}, u32[]{:S(2)}) copy-start(bf16[96,16,128]{2,1,0:T(8,128)(2,1)S(1)} %collective-permute-done.5.refs_2_) | copy-start | bytes 1179652
  59.7 7.2 %collective-permute-start.12 = (bf16[96,16,128]{2,1,0:T(8,128)(2,1)S(1)}, bf16[96,16,128]{2,1,0:T(8,128)(2,1)}, u32[]{:S(2)}, u32[]{:S(2)}) collective-permute-start(bf16[96,16,128]{2,1,0:T(8,128)(2,1)S(1)} %collective-permute-done.5.refs_2_), channel_id=1, source_target_pairs={{0,4},{4,0},{8,12},{12,8},{16,20},{20,16},{24,28},{28,24},{1,5},{5... | collective-permute-start | bytes 1179656 | tf_op jit(solution)/shard_map/ppermute | solution.py:228
  60.3 6.6 %copy-start.15 = (bf16[96,16,128]{2,1,0:T(8,128)(2,1)}, bf16[96,16,128]{2,1,0:T(8,128)(2,1)S(1)}, u32[]{:S(2)}) copy-start(bf16[96,16,128]{2,1,0:T(8,128)(2,1)S(1)} %collective-permute-done.6.refs_6_) | copy-start | bytes 1179652
  60.3 6.5 %collective-permute-start.14 = (bf16[96,16,128]{2,1,0:T(8,128)(2,1)S(1)}, bf16[96,16,128]{2,1,0:T(8,128)(2,1)}, u32[]{:S(2)}, u32[]{:S(2)}) collective-permute-start(bf16[96,16,128]{2,1,0:T(8,128)(2,1)S(1)} %collective-permute-done.6.refs_6_), channel_id=1, source_target_pairs={{0,4},{4,0},{8,12},{12,8},{16,20},{20,16},{24,28},{28,24},{1,5},{5... | collective-permute-start | bytes 1179656 | tf_op jit(solution)/shard_map/ppermute | solution.py:228
  62.1 23.4 %collective-permute-start.10 = (bf16[120,16,128]{2,1,0:T(8,128)(2,1)}, bf16[120,16,128]{2,1,0:T(8,128)(2,1)S(1)}, u32[]{:S(2)}, u32[]{:S(2)}) collective-permute-start(bf16[120,16,128]{2,1,0:T(8,128)(2,1)} %shard_map.151.refs_1_), channel_id=1, source_target_pairs={{0,16},{4,20},{8,24},{12,28},{16,0},{20,4},{24,8},{28,12},{1,17},{... | collective-permute-start | bytes 1474568 | tf_op jit(solution)/shard_map/ppermute | solution.py:228
  64.0 2.8 %copy-start.20 = (bf16[96,16,128]{2,1,0:T(8,128)(2,1)}, bf16[96,16,128]{2,1,0:T(8,128)(2,1)S(1)}, u32[]{:S(2)}) copy-start(bf16[96,16,128]{2,1,0:T(8,128)(2,1)S(1)} %collective-permute-done.11.refs_3_) | copy-start | bytes 1179652
  64.0 21.4 %collective-permute-start.9 = (bf16[120,16,128]{2,1,0:T(8,128)(2,1)}, bf16[120,16,128]{2,1,0:T(8,128)(2,1)S(1)}, u32[]{:S(2)}, u32[]{:S(2)}) collective-permute-start(bf16[120,16,128]{2,1,0:T(8,128)(2,1)} %shard_map.151.refs_1_), channel_id=1, source_target_pairs={{0,8},{4,12},{8,0},{12,4},{16,24},{20,28},{24,16},{28,20},{1,9},{5... | collective-permute-start | bytes 1474568 | tf_op jit(solution)/shard_map/ppermute | solution.py:228
  64.6 23.9 %collective-permute-start.8 = (bf16[120,16,128]{2,1,0:T(8,128)(2,1)}, bf16[120,16,128]{2,1,0:T(8,128)(2,1)S(1)}, u32[]{:S(2)}, u32[]{:S(2)}) collective-permute-start(bf16[120,16,128]{2,1,0:T(8,128)(2,1)} %shard_map.151.refs_1_), channel_id=1, source_target_pairs={{0,24},{4,28},{8,16},{12,20},{16,8},{20,12},{24,0},{28,4},{1,25},{... | collective-permute-start | bytes 1474568 | tf_op jit(solution)/shard_map/ppermute | solution.py:228
  66.8 31.9 %collective-permute-start.7 = (bf16[120,16,128]{2,1,0:T(8,128)(2,1)}, bf16[120,16,128]{2,1,0:T(8,128)(2,1)S(1)}, u32[]{:S(2)}, u32[]{:S(2)}) collective-permute-start(bf16[120,16,128]{2,1,0:T(8,128)(2,1)} %shard_map.151.refs_1_), channel_id=1, source_target_pairs={{0,4},{4,0},{8,12},{12,8},{16,20},{20,16},{24,28},{28,24},{1,5},{5... | collective-permute-start | bytes 1474568 | tf_op jit(solution)/shard_map/ppermute | solution.py:228
  85.5 3.1 %copy-start.5 = (bf16[120,16,128]{2,1,0:T(8,128)(2,1)}, bf16[120,16,128]{2,1,0:T(8,128)(2,1)S(1)}, u32[]{:S(2)}) copy-start(bf16[120,16,128]{2,1,0:T(8,128)(2,1)S(1)} %collective-permute-done.10.refs_2_) | copy-start | bytes 1474564
  85.5 3.1 %copy-start.6 = (bf16[120,16,128]{2,1,0:T(8,128)(2,1)}, bf16[120,16,128]{2,1,0:T(8,128)(2,1)S(1)}, u32[]{:S(2)}) copy-start(bf16[120,16,128]{2,1,0:T(8,128)(2,1)S(1)} %collective-permute-done.9.refs_1_) | copy-start | bytes 1474564
  88.5 0.8 copy-start.7
  90.0 8.7 %collective-permute-start.15 = (bf16[120,16,128]{2,1,0:T(8,128)(2,1)}, bf16[120,16,128]{2,1,0:T(8,128)(2,1)S(1)}, u32[]{:S(2)}, u32[]{:S(2)}) collective-permute-start(bf16[120,16,128]{2,1,0:T(8,128)(2,1)} %get-tuple-element.56.refs_3_), channel_id=1, source_target_pairs={{0,4},{4,0},{8,12},{12,8},{16,20},{20,16},{24,28},{28,24},{1,5},{5... | collective-permute-start | bytes 1474568 | tf_op jit(solution)/shard_map/ppermute | solution.py:228
  90.0 8.7 %collective-permute-start.16 = (bf16[120,16,128]{2,1,0:T(8,128)(2,1)}, bf16[120,16,128]{2,1,0:T(8,128)(2,1)S(1)}, u32[]{:S(2)}, u32[]{:S(2)}) collective-permute-start(bf16[120,16,128]{2,1,0:T(8,128)(2,1)} %get-tuple-element.57.refs_5_), channel_id=1, source_target_pairs={{0,4},{4,0},{8,12},{12,8},{16,20},{20,16},{24,28},{28,24},{1,5},{5... | collective-permute-start | bytes 1474568 | tf_op jit(solution)/shard_map/ppermute | solution.py:228
  90.5 8.2 %collective-permute-start.17 = (bf16[120,16,128]{2,1,0:T(8,128)(2,1)}, bf16[120,16,128]{2,1,0:T(8,128)(2,1)S(1)}, u32[]{:S(2)}, u32[]{:S(2)}) collective-permute-start(bf16[120,16,128]{2,1,0:T(8,128)(2,1)} %get-tuple-element.58.refs_7_), channel_id=1, source_target_pairs={{0,4},{4,0},{8,12},{12,8},{16,20},{20,16},{24,28},{28,24},{1,5},{5... | collective-permute-start | bytes 1474568 | tf_op jit(solution)/shard_map/ppermute | solution.py:228
  98.7 0.8 copy-start.16
  98.7 1.0 copy-start.17
  98.7 1.1 copy-start.18
  98.8 1.2 copy-start.19
  115.2 4.4 %copy-start.3 = (bf16[2,512,512]{2,1,0:T(8,128)(2,1)S(1)}, bf16[2,512,512]{2,1,0:T(8,128)(2,1)}, u32[]{:S(2)}) copy-start(bf16[2,512,512]{2,1,0:T(8,128)(2,1)} %get-tuple-element.65) | copy-start | bytes 3145732
  115.2 4.4 %copy-start.4 = (bf16[2,512,512]{2,1,0:T(8,128)(2,1)S(1)}, bf16[2,512,512]{2,1,0:T(8,128)(2,1)}, u32[]{:S(2)}) copy-start(bf16[2,512,512]{2,1,0:T(8,128)(2,1)} %get-tuple-element.66) | copy-start | bytes 3145732
  115.2 36.5 %all-to-all-start = ((bf16[4,1,512,256]{3,2,1,0:T(8,128)(2,1)}), bf16[4,1,512,256]{3,2,1,0:T(8,128)(2,1)S(1)}, u32[]{:S(2)}, u32[]{:S(2)}) async-start(bf16[4,1,512,256]{3,2,1,0:T(8,128)(2,1)} %get-tuple-element.69), calls=%async_computation | async-start | bytes 2097152 | tf_op jit(solution)/shard_map/all_to_all | solution.py:768
  121.1 30.6 %copy-start.2 = (bf16[8,128,128]{2,1,0:T(8,128)(2,1)S(1)}, bf16[8,128,128]{2,1,0:T(8,128)(2,1)}, u32[]{:S(2)}) copy-start(bf16[8,128,128]{2,1,0:T(8,128)(2,1)} %get-tuple-element.68.weight_ref) | copy-start | bytes 786436
  142.2 4.2 %collective-permute-start.18 = (f32[4,8,128]{2,1,0:T(8,128)}, f32[4,8,128]{2,1,0:T(8,128)S(1)}, u32[]{:S(2)}, u32[]{:S(2)}) collective-permute-start(f32[4,8,128]{2,1,0:T(8,128)} %get-tuple-element.67), channel_id=1, source_target_pairs={{0,1},{1,0},{2,3},{3,2},{4,5},{5,4},{6,7},{7,6},{8,9},{9,8},{10,11... | collective-permute-start | bytes 49160 | tf_op jit(solution)/shard_map/ppermute | solution.py:689
  147.1 4.6 %collective-permute-start.19 = (f32[4,8,128]{2,1,0:T(8,128)S(1)}, f32[4,8,128]{2,1,0:T(8,128)S(1)}, u32[]{:S(2)}, u32[]{:S(2)}) collective-permute-start(f32[4,8,128]{2,1,0:T(8,128)S(1)} %add.50), channel_id=1, source_target_pairs={{0,2},{1,3},{2,0},{3,1},{4,6},{5,7},{6,4},{7,5},{8,10},{9,11},{10,... | collective-permute-start | bytes 49160 | tf_op jit(solution)/shard_map/ppermute | solution.py:689
  151.7 1.6 %copy-start.1 = (f32[4,512,256]{2,1,0:T(8,128)S(1)}, f32[4,512,256]{2,1,0:T(8,128)}, u32[]{:S(2)}) copy-start(f32[4,512,256]{2,1,0:T(8,128)} %get-tuple-element.70.image_ref) | copy-start | bytes 6291460

commit v8 on v5

--- a/solution.py
+++ b/solution.py
@@ -25,7 +25,6 @@
 
 SMEM = pl.BlockSpec(memory_space=pltpu.SMEM)
 VMEM = pl.BlockSpec(memory_space=pltpu.VMEM)
-LENGTH = pl.BlockSpec((1, 8, LANES), lambda l: (l, 0, 0))
 
 SIN_POLY = (4.4428679, -7.30744341, 3.59478797, -0.78437376)
 COS_POLY = (1.4142135, -6.97885099, 5.73946117, -1.88356298, 0.31069817)
@@ -100,10 +99,10 @@
             if (band, row) in lists[wave]:
                 slab = wave * slabs + lists[wave].index((band, row)) * modes
             place[c * UNITS + j] = (slab, row, columns[0], columns[64] - 64)
-    return count, half, slabs, pack, place
-
-
-def pack_kernel(count, modes, half, where, table, lengths, basis, own, piece):
+    return half, slabs, pack, place
+
+
+def pack_kernel(count, half, modes, where, table, lengths, basis, own, piece):
     left = lax.broadcasted_iota(jnp.int32, (ROWS, LANES), 1) < 64
     wave, share = where[0], where[1]
 
@@ -132,26 +131,24 @@
     piece[2 * half] = slab.astype(piece.dtype)
 
 
-def pack_rows(basis, wave_lengths, table, where, half, slabs):
-    modes = basis.shape[0]
-    waves, count, _ = table.shape
-    smem = pl.BlockSpec(memory_space=pltpu.SMEM)
-    vmem = pl.BlockSpec(memory_space=pltpu.VMEM)
+def pack_rows(basis, wave_lengths, plan, where):
+    half, slabs, table, _ = plan
+    tile = (ROWS, LANES)
     return pl.pallas_call(
-        functools.partial(pack_kernel, count, modes, half),
+        functools.partial(pack_kernel, table.shape[1], half, basis.shape[0]),
         out_shape=(
-            jax.ShapeDtypeStruct((slabs, ROWS, LANES), basis.dtype),
-            jax.ShapeDtypeStruct((2 * half + 1, ROWS, LANES), basis.dtype),
+            jax.ShapeDtypeStruct((slabs,) + tile, basis.dtype),
+            jax.ShapeDtypeStruct((2 * half + 1,) + tile, basis.dtype),
         ),
-        in_specs=[smem, smem, smem, vmem],
-        out_specs=(vmem, vmem),
+        in_specs=[SMEM, SMEM, SMEM, VMEM],
+        out_specs=(VMEM, VMEM),
         compiler_params=pltpu.CompilerParams(vmem_limit_bytes=VMEM_BYTES),
-    )(where, table.reshape(waves * count, 3), wave_lengths, basis)
-
-
-def split_kernel(half, sent, where, own_lengths, *refs):
-    parts, (low_ref, high_ref, length_ref) = refs[:-3], refs[-3:]
-    wave, waves = where[0], len(parts) + 1
+    )(where, table.reshape(-1, 3), wave_lengths, basis)
+
+
+def split_kernel(half, sent, parts_count, where, own_lengths, *refs):
+    parts, (low_ref, high_ref, length_ref) = refs[:parts_count], refs[-3:]
+    wave, waves = where[0], parts_count + 1
     kept = own_lengths.shape[0] - sent
     for s in range(waves):
         for i in range(kept):
@@ -170,32 +167,35 @@
         high_ref[s * half : (s + 1) * half] = part[half : 2 * half]
 
 
-def split_parts(parts, where, wave_lengths, half, sent):
+def split_parts(parts, where, wave_lengths, half, sent, tokens):
     count = (len(parts) + 1) * (wave_lengths.shape[0] - sent)
     slabs = jax.ShapeDtypeStruct((len(parts) * half, ROWS, LANES), parts[0].dtype)
     return pl.pallas_call(
-        functools.partial(split_kernel, half, sent),
+        functools.partial(split_kernel, half, sent, len(parts)),
         out_shape=(slabs, slabs, jax.ShapeDtypeStruct((count, 8, LANES), jnp.float32)),
-        in_specs=[SMEM, SMEM] + [VMEM] * len(parts),
+        in_specs=[SMEM, SMEM] + [VMEM] * (len(parts) + len(tokens)),
         out_specs=(VMEM,) * 3,
         compiler_params=pltpu.CompilerParams(vmem_limit_bytes=VMEM_BYTES),
-    )(where, wave_lengths, *parts)
-
-
-def join_kernel(one_ref, two_ref, token_ref, out_ref):
-    count = one_ref.shape[0]
-    out_ref[:count] = one_ref[...]
-    out_ref[count:] = two_ref[...]
-
-
-def join(one, two, token):
+    )(where, wave_lengths, *parts, *tokens)
+
+
+def join_kernel(pairs, *refs):
+    for i in range(pairs):
+        one, two, out = refs[2 * i], refs[2 * i + 1], refs[i - pairs]
+        out[: one.shape[0]] = one[...]
+        out[one.shape[0] :] = two[...]
+
+
+def join(pairs, token):
     return pl.pallas_call(
-        join_kernel,
-        out_shape=jax.ShapeDtypeStruct((2 * one.shape[0],) + one.shape[1:], one.dtype),
-        in_specs=[VMEM] * 3,
-        out_specs=VMEM,
+        functools.partial(join_kernel, len(pairs)),
+        out_shape=tuple(
+            jax.ShapeDtypeStruct((2 * one.shape[0],) + one.shape[1:], one.dtype) for one, _ in pairs
+        ),
+        in_specs=[VMEM] * (2 * len(pairs) + 1),
+        out_specs=(VMEM,) * len(pairs),
         compiler_params=pltpu.CompilerParams(vmem_limit_bytes=VMEM_BYTES),
-    )(one, two, token)
+    )(*[one for pair in pairs for one in pair], token)
 
 
 def along_wave(piece, waves):
@@ -205,21 +205,21 @@
     ]
 
 
-def gather_rows(halves, token):
+def swap(x, mask):
     groups, fields = lax.axis_size("groups"), lax.axis_size("field")
-
-    def swap(x, mask):
-        pairs = [
-            (g * fields + f, (g ^ (mask >> 2)) * fields + (f ^ (mask & 3)))
-            for g in range(groups)
-            for f in range(fields)
-        ]
-        return lax.ppermute(x, ("groups", "field"), pairs)
-
+    pairs = [
+        (g * fields + f, (g ^ (mask >> 2)) * fields + (f ^ (mask & 3)))
+        for g in range(groups)
+        for f in range(fields)
+    ]
+    return lax.ppermute(x, ("groups", "field"), pairs)
+
+
+def gather_halves(halves, token):
     got = []
-    for h, (one, two) in enumerate(((2, 4), (4, 2))):
-        mine = halves[h]
-        both = join(mine, swap(mine, one), token)
+    routes = ((2, 4), (4, 2))
+    joined = join([(mine, swap(mine, one)) for mine, (one, _) in zip(halves, routes)], token)
+    for h, (both, (one, two)) in enumerate(zip(joined, routes)):
         far = swap(both, two)
         got.append((h, both, (0, one)))
         got.append((h, far, (two, one | two)))
@@ -230,7 +230,8 @@
 
 def spread_kernel(*refs):
     count = len(refs) // 2
-    for small_ref, big_ref in zip(refs[:count], refs[count:]):
+    refs[-1][...] = jnp.zeros_like(refs[-1])
+    for small_ref, big_ref in zip(refs[:count], refs[count:-1]):
         _, many, wide = small_ref.shape
         tall, long = many * ROWS, wide * ROWS
         down = lax.broadcasted_iota(jnp.int32, (tall, many), 0) // ROWS
@@ -253,7 +254,8 @@
         out_shape=tuple(
             jax.ShapeDtypeStruct((m.shape[0], m.shape[1] * ROWS, m.shape[2] * ROWS), jnp.bfloat16)
             for m in matrices
-        ),
+        )
+        + (jax.ShapeDtypeStruct((8, LANES), jnp.float32),),
         compiler_params=pltpu.CompilerParams(vmem_limit_bytes=VMEM_BYTES),
     )(*matrices)
 
@@ -306,10 +308,10 @@
                 )
         return carry
 
-    lax.fori_loop(0, len(CHUNKS), chunk, 0)
-
-
-def transform(positions, rows, inverse, path, opening, row_ref, column_ref, scratch):
+    lax.fori_loop(0, place.shape[0] // UNITS, chunk, 0)
+
+
+def transform(positions, rows, inverse, path, opening, row_ref, scratch, wait=None):
     pupils, total, first = scratch[:2], scratch[2], scratch[3]
     batch = max(1, positions // 2)
     width = 2 * positions * LANES // UNITS
@@ -337,6 +339,8 @@
 
     for c, (band, rows_band) in enumerate(CHUNKS):
         pupil = pupils[c % 2]
+        if wait is not None:
+            wait(c)
         for j, row in enumerate(band_rows(rows_band)):
             real_lines = slice(2 * ROWS * j, 2 * ROWS * j + ROWS)
             imag_lines = slice(2 * ROWS * j + ROWS, 2 * ROWS * (j + 1))
@@ -362,49 +366,81 @@
         product(len(CHUNKS) - 1, slice(n * width, (n + 1) * width))
 
 
+def columns_of(first, column_ref):
+    return [
+        jnp.dot(
+            first, column_ref[0, :, part * PIX : (part + 1) * PIX], preferred_element_type=jnp.float32
+        )
+        for part in range(2)
+    ]
+
+
+def chunk_copies(source, target, sems):
+    return [
+        pltpu.make_async_copy(
+            source.at[pl.ds(c * UNITS, UNITS)], target.at[pl.ds(c * UNITS, UNITS)], sems.at[c]
+        )
+        for c in range(len(CHUNKS))
+    ]
+
+
 def whole_kernel(sizes, length_ref, place, where, *refs):
     positions, modes, waves, half, slabs, keys = sizes
     parts, refs = refs[: 1 + len(keys)], refs[1 + len(keys) :]
-    spread, row_ref, column_ref = refs[:3]
-    image_ref, path, opening = refs[3:6]
-    basis, sems = refs[6:8]
-    scratch = refs[8:]
+    spread, row_ref, column_ref, out_ref, path_out, opening, path, basis, sems, path_sems = refs[:10]
+    scratch = refs[10:]
+    copies = chunk_copies(path, path_out, path_sems)
 
     @pl.when(pl.program_id(0) == 0)
     def _():
         form_paths(sizes, where, place, parts, spread, path, opening, basis, sems)
-
-    inverse = 1.0 / length_ref[0, :1]
+        for copy in copies:
+            copy.start()
+
     rows = PIX
-    transform(positions, rows, inverse, path, opening, row_ref, column_ref, scratch)
+    transform(positions, rows, 1.0 / length_ref[0, :1], path, opening, row_ref, scratch)
     first = scratch[3]
     share = rows // waves
     for f in range(positions):
-        lines = first[f * rows : (f + 1) * rows]
-        real = jnp.dot(lines, column_ref[0, :, :PIX], preferred_element_type=jnp.float32)
-        imag = jnp.dot(lines, column_ref[0, :, PIX:], preferred_element_type=jnp.float32)
+        real, imag = columns_of(first[f * rows : (f + 1) * rows], column_ref)
         intensity = real * real + imag * imag
         level = jnp.sum(
             jnp.sum(intensity, axis=0, keepdims=True), axis=1, keepdims=True
         ) / (rows * PIX)
         spectra = (intensity / (level + EPSILON)).astype(jnp.bfloat16)
         for part in range(waves):
-            image_ref[part, 0, f * share : (f + 1) * share] = spectra[
+            out_ref[part, 0, f * share : (f + 1) * share] = spectra[
                 part * share : (part + 1) * share
             ]
 
-
-def rows_kernel(positions, rows, length_ref, path, opening, row_ref, column_ref, *refs):
-    image_ref, sum_ref = refs[:2]
-    scratch = refs[2:]
-    inverse = 1.0 / length_ref[0, :1]
-    transform(positions, rows, inverse, path, opening, row_ref, column_ref, scratch)
-    first = scratch[3]
-    real = jnp.dot(first[...], column_ref[0, :, :PIX], preferred_element_type=jnp.float32)
-    imag = jnp.dot(first[...], column_ref[0, :, PIX:], preferred_element_type=jnp.float32)
+    @pl.when(pl.program_id(0) == pl.num_programs(0) - 1)
+    def _():
+        for copy in copies:
+            copy.wait()
+
+
+def rows_kernel(positions, rows, length_ref, path_in, opening, row_ref, column_ref, *refs):
+    image_ref, sum_ref, path, path_sems = refs[:4]
+    scratch = refs[4:]
+    copies = chunk_copies(path_in, path, path_sems)
+    begin = pl.program_id(0) == 0
+
+    @pl.when(begin)
+    def _():
+        for copy in copies:
+            copy.start()
+
+    def wait(c):
+        @pl.when(begin)
+        def _():
+            copies[c].wait()
+
+    transform(positions, rows, 1.0 / length_ref[0, :1], path, opening, row_ref, scratch, wait)
+    real, imag = columns_of(scratch[3][...], column_ref)
     intensity = real * real + imag * imag
     image_ref[0] = intensity
-    sum_ref[0] = jnp.sum(intensity.reshape(positions, rows, PIX), axis=1)
+    sums = jnp.sum(intensity.reshape(positions, rows, PIX), axis=1)
+    sum_ref[0] = jnp.broadcast_to(jnp.sum(sums, axis=1, keepdims=True), (positions, LANES))
 
 
 def transform_scratch(positions, rows):
@@ -424,71 +460,83 @@
     )
 
 
-def table_specs(row_table, column_table):
-    return [
-        pl.BlockSpec((1,) + row_table.shape[1:], lambda l: (l, 0, 0, 0)),
-        pl.BlockSpec((1,) + column_table.shape[1:], lambda l: (l, 0, 0)),
-    ]
-
-
-def whole_fields(own, got, spread, place, where, length, row_table, column_table, sizes):
+def by_length(array):
+    return pl.BlockSpec((1,) + array.shape[1:], lambda l: (l,) + (0,) * (len(array.shape) - 1))
+
+
+def path_shape(positions):
+    return (len(CHUNKS) * UNITS, positions * ROWS, LANES)
+
+
+def whole_fields(own, got, spread, place, where, length, tables, sizes):
     positions, modes, waves, half, slabs = sizes
     keys = tuple((h, masks) for h, _, masks in got)
     arrays = [array for _, array, _ in got]
-    lengths = row_table.shape[0]
-    units = place.shape[0]
+    lengths = length.shape[0]
     share = positions * PIX // waves
     any_memory = pl.BlockSpec(memory_space=pl.ANY)
     return pl.pallas_call(
-        functools.partial(
-            whole_kernel, (positions, modes, waves, half, slabs, keys)
-        ),
+        functools.partial(whole_kernel, (positions, modes, waves, half, slabs, keys)),
         grid=(lengths,),
         out_shape=(
             jax.ShapeDtypeStruct((waves, lengths, share, PIX), jnp.bfloat16),
-            jax.ShapeDtypeStruct((units, positions * ROWS, LANES), jnp.float32),
-            jax.ShapeDtypeStruct((units, ROWS, LANES), jnp.float32),
+            jax.ShapeDtypeStruct(path_shape(positions), jnp.float32),
+            jax.ShapeDtypeStruct((place.shape[0], ROWS, LANES), jnp.float32),
         ),
-        in_specs=[LENGTH, SMEM, SMEM]
+        in_specs=[by_length(length), SMEM, SMEM]
         + [any_memory] * (1 + len(keys))
         + [VMEM]
-        + table_specs(row_table, column_table),
-        out_specs=(pl.BlockSpec((waves, 1, share, PIX), lambda l: (0, l, 0, 0)), VMEM, VMEM),
+        + [by_length(table) for table in tables],
+        out_specs=(
+            pl.BlockSpec((waves, 1, share, PIX), lambda l: (0, l, 0, 0)),
+            any_memory,
+            VMEM,
+        ),
         scratch_shapes=[
+            pltpu.VMEM(path_shape(positions), jnp.float32),
             pltpu.VMEM((waves * slabs, ROWS, LANES), jnp.bfloat16),
             pltpu.SemaphoreType.DMA((1 + sum(len(masks) for _, masks in keys) * (waves - 1),)),
+            pltpu.SemaphoreType.DMA((len(CHUNKS),)),
         ]
         + transform_scratch(positions, PIX),
         cost_estimate=transform_cost(lengths, positions, PIX),
         compiler_params=pltpu.CompilerParams(vmem_limit_bytes=VMEM_BYTES),
-    )(length, place, where, own, *arrays, spread, row_table, column_table)
-
-
-def row_fields(path, opening, length, row_table, column_table, positions):
-    lengths = row_table.shape[0]
-    rows = row_table.shape[2] // 2
+    )(length, place, where, own, *arrays, spread, *tables)
+
+
+def row_fields(path, opening, length, tables, positions):
+    lengths = length.shape[0]
+    rows = tables[0].shape[2] // 2
+    out_shape = (
+        jax.ShapeDtypeStruct((lengths, positions * rows, PIX), jnp.float32),
+        jax.ShapeDtypeStruct((lengths, positions, LANES), jnp.float32),
+    )
     return pl.pallas_call(
         functools.partial(rows_kernel, positions, rows),
         grid=(lengths,),
-        out_shape=(
-            jax.ShapeDtypeStruct((lengths, positions * rows, PIX), jnp.float32),
-            jax.ShapeDtypeStruct((lengths, positions, PIX), jnp.float32),
-        ),
-        in_specs=[LENGTH, VMEM, VMEM] + table_specs(row_table, column_table),
-        out_specs=(
-            pl.BlockSpec((1, positions * rows, PIX), lambda l: (l, 0, 0)),
-            pl.BlockSpec((1, positions, PIX), lambda l: (l, 0, 0)),
-        ),
-        scratch_shapes=transform_scratch(positions, rows),
+        out_shape=out_shape,
+        in_specs=[by_length(length), pl.BlockSpec(memory_space=pl.ANY), VMEM]
+        + [by_length(table) for table in tables],
+        out_specs=tuple(by_length(one) for one in out_shape),
+        scratch_shapes=[
+            pltpu.VMEM(path_shape(positions), jnp.float32),
+            pltpu.SemaphoreType.DMA((len(CHUNKS),)),
+        ]
+        + transform_scratch(positions, rows),
         cost_estimate=transform_cost(lengths, positions, rows),
         compiler_params=pltpu.CompilerParams(vmem_limit_bytes=VMEM_BYTES),
-    )(length, path, opening, row_table, column_table)
-
-
-def mix_kernel(inverse_ref, weight_ref, sent_ref, image_ref, out_ref):
+    )(length, path, opening, *tables)
+
+
+def mix_kernel(sum_ref, weight_ref, sent_ref, image_ref, out_ref):
     count, templates, rows = out_ref.shape[:3]
     for i in range(count):
         f = pl.program_id(0) * count + i
+        inverse = [
+            1.0 / (sum_ref[l, pl.ds(f, 1)] / (PIX * PIX) + EPSILON)
+            for l in range(image_ref.shape[0])
+        ]
+        inverse = [jnp.concatenate([one] * (PIX // LANES), axis=1) for one in inverse]
         blocks = []
         for start in range(i * rows, (i + 1) * rows, ROWS):
             lines = slice(start, start + ROWS)
@@ -496,7 +544,7 @@
                 jnp.concatenate(
                     [sent_ref[l, lines] for l in range(sent_ref.shape[0])]
                     + [
-                        (image_ref[l, lines] * inverse_ref[l, f]).astype(jnp.bfloat16)
+                        (image_ref[l, lines] * inverse[l]).astype(jnp.bfloat16)
                         for l in range(image_ref.shape[0])
                     ],
                     axis=0,
@@ -512,7 +560,7 @@
                 ]
 
 
-def mix(spread, inverse, sent, images, templates, rows):
+def mix(spread, sums, sent, images, templates, rows):
     positions = spread.shape[0]
     count = 2 if positions % 2 == 0 else 1
     return pl.pallas_call(
@@ -520,14 +568,14 @@
         grid=(positions // count,),
         out_shape=jax.ShapeDtypeStruct((positions, templates, rows, PIX), jnp.bfloat16),
         in_specs=[
-            SMEM,
+            VMEM,
             pl.BlockSpec((count,) + spread.shape[1:], lambda f: (f, 0, 0)),
             pl.BlockSpec((sent.shape[0], count * rows, PIX), lambda f: (0, f, 0)),
             pl.BlockSpec((images.shape[0], count * rows, PIX), lambda f: (0, f, 0)),
         ],
         out_specs=pl.BlockSpec((count, templates, rows, PIX), lambda f: (f, 0, 0, 0)),
-        compiler_params=pltpu.CompilerParams(vmem_limit_bytes=VMEM_BYTES),
-    )(inverse, spread, sent, images)
+        compiler_params=pltpu.CompilerParams(vmem_limit_bytes=24 * 2**20),
+    )(sums, spread, sent, images)
 
 
 def table_kernel(length_ref, y_ref, v_ref, u_ref, x_ref, row_ref, column_ref, token_ref):
@@ -537,8 +585,7 @@
     for start in range(0, PUP, ROWS):
         s, k = half_turn((y_ref[start : start + ROWS] * v_ref[...]) * scale)
         cosine, sine = 1.0 - s * s, s * k
-        lower = slice(start, start + ROWS)
-        upper = slice(PUP + start, PUP + start + ROWS)
+        lower, upper = slice(start, start + ROWS), slice(PUP + start, PUP + start + ROWS)
         column_ref[0, lower, :PIX] = cosine.astype(jnp.bfloat16)
         column_ref[0, lower, PIX:] = (-sine).astype(jnp.bfloat16)
         column_ref[0, upper, :PIX] = sine.astype(jnp.bfloat16)
@@ -576,7 +623,7 @@
             jax.ShapeDtypeStruct((8, LANES), jnp.float32),
         ),
         in_specs=[
-            LENGTH,
+            pl.BlockSpec((1, 8, LANES), lambda l: (l, 0, 0)),
             whole(PUP, 1),
             whole(1, PIX),
             whole(rows, 1),
@@ -601,8 +648,11 @@
 
 
 def add_over_wave(x, waves):
-    copies = jnp.broadcast_to(x[None], (waves,) + x.shape)
-    return jnp.sum(lax.all_to_all(copies, "wave", split_axis=0, concat_axis=0, tiled=True), axis=0)
+    step = 1
+    while step < waves:
+        x = x + lax.ppermute(x, "wave", [(i, i ^ step) for i in range(waves)])
+        step *= 2
+    return x
 
 
 def local(mode_basis, coef_table, table_index, wave_lengths, sed_table, template_ids):
@@ -611,21 +661,15 @@
     modes = mode_basis.shape[0]
     positions = table_index.shape[0]
     rows = PIX // waves
-    count, half, slabs, pack, place = layout(waves, modes)
     lengths = wave_lengths.shape[0]
     sent_lengths = lengths // 2
 
     share = (lax.axis_index("groups") % 2) * 4 + lax.axis_index("field") % 4
     where = jnp.stack([mine, share]).astype(jnp.int32)
-    own, piece = pack_rows(mode_basis, wave_lengths, pack, where, half, slabs)
+    plan = layout(waves, modes)
+    half, slabs, _, place = plan
+    own, piece = pack_rows(mode_basis, wave_lengths, plan, where)
     parts = along_wave(piece, waves)
-    low, high, every = split_parts(parts, where, wave_lengths, half, sent_lengths)
-    own_length = jnp.broadcast_to(
-        wave_lengths[:sent_lengths, None, None], (sent_lengths, 8, LANES)
-    )
-    own_row, own_column, _ = tables(own_length, 0, PIX)
-    all_row, all_column, token = tables(every, mine * rows, rows)
-    got = gather_rows((low, high), token)
 
     selector = (
         table_index[:, None] == jnp.arange(coef_table.shape[0], dtype=jnp.int32)[None, :]
@@ -646,7 +690,17 @@
         ],
         axis=2,
     )
-    path_spread, mix_spread = spreads(coeffs.astype(jnp.bfloat16)[None], weights)
+    path_spread, mix_spread, spread_token = spreads(coeffs.astype(jnp.bfloat16)[None], weights)
+    own_length = jnp.broadcast_to(
+        wave_lengths[:sent_lengths, None, None], (sent_lengths, 8, LANES)
+    )
+    own_row, own_column, own_token = tables(own_length, 0, PIX)
+
+    low, high, every = split_parts(
+        parts, where, wave_lengths, half, sent_lengths, (spread_token, own_token)
+    )
+    all_row, all_column, all_token = tables(every, mine * rows, rows)
+    got = gather_halves((low, high), all_token)
 
     spectra, path, opening = whole_fields(
         own,
@@ -655,16 +709,13 @@
         place,
         where,
         own_length,
-        own_row,
-        own_column,
+        (own_row, own_column),
         (positions, modes, waves, half, slabs),
     )
     sent = lax.all_to_all(spectra, "wave", split_axis=0, concat_axis=0, tiled=True)
     sent = sent.reshape(waves * sent_lengths, positions * rows, PIX)
-
-    images, sums = row_fields(path, opening, every, all_row, all_column, positions)
-    level = add_over_wave(jnp.sum(sums, axis=2), waves) / (PIX * PIX)
-    return mix(mix_spread, 1.0 / (level + EPSILON), sent, images, templates, rows)
+    images, sums = row_fields(path, opening, every, (all_row, all_column), positions)
+    return mix(mix_spread, add_over_wave(sums, waves), sent, images, templates, rows)
 
 
 def solution(mesh):

time: 182 us -> 149 us (0.82)
  waiting for transfers between devices: 67.9 us -> 41.5 us
  blocking collectives: 9.28 us -> 0 us
  starting transfers between devices: 16.2 us -> 21.2 us
    all_to_all x1, waiting for transfers between devices: 24.6 us -> 0.01 us  [local(): lax.all_to_all(spectra, 'wave', split_axis=0, concat_axis=0, tiled=True)]
    ppermute x3, waiting for transfers between devices: 24 us -> 14.4 us  [along_wave(): lax.ppermute(piece, 'wave', [(i, (i + s) % waves) for i in range(waves)])]
    all_to_all x1 -> x0, blocking collectives: 9.28 us -> none  [add_over_wave(): lax.all_to_all(copies, 'wave', split_axis=0, concat_axis=0, tiled=True)]
    ppermute x0 -> x2, starting transfers between devices: none -> 5.01 us  [add_over_wave(): x = x + lax.ppermute(x, 'wave', [(i, i ^ step) for i in range(waves)])]
    ppermute x8, waiting for transfers between devices: 19.4 us -> 23.5 us  [swap(): return lax.ppermute(x, ('groups', 'field'), pairs)]
    ppermute x0 -> x2, waiting for transfers between devices: none -> 3.65 us  [add_over_wave(): x = x + lax.ppermute(x, 'wave', [(i, i ^ step) for i in range(waves)])]
    pallas_call x1, Pallas kernels: 4.54 us -> 2.65 us  [mix(): pl.pallas_call(mix_kernel, grid=(positions // count,), out_shape=jax.Shap...]
    pallas_call x4 -> x3, Pallas kernels: 10.5 us -> 9.1 us  [the longest x1 4.33 us: pack_rows(): pl.pallas_call(functools.partial(pack_kernel, table.shape[1], half, basis...]
  transfers between devices with their start and end apart: 12 -> 14, of which waited for: 6 -> 9; matrix products, arithmetic and copies ran while one was open for 3% -> 4% of each run, Pallas kernels for 8% -> 29%
where the time goes in v8:
time: 149 us
  Pallas kernels  75.4 us (51%)
  waiting for transfers between devices  41.5 us (28%)
  starting transfers between devices  21.2 us (14%)
  local copies, waits for them, and re-layouts  5.03 us (3%)
  other arithmetic  3.37 us (2%)
  matrix products  1.87 us (1%)
    pallas_call x1, Pallas kernels, row_fields(): pl.pallas_call(functools.partial(rows_kernel, positions, rows), grid=(len...  32.4 us
    ppermute x8, waiting for transfers between devices, swap(): return lax.ppermute(x, ('groups', 'field'), pairs)  23.5 us
    pallas_call x1, Pallas kernels, whole_fields(): pl.pallas_call(functools.partial(whole_kernel, (positions, modes, waves,...  20.7 us
    ppermute x3, waiting for transfers between devices, along_wave(): lax.ppermute(piece, 'wave', [(i, (i + s) % waves) for i in range(waves)])  14.4 us
    pallas_call x2, Pallas kernels, tables(): pl.pallas_call(table_kernel, grid=(lengths,), out_shape=(jax.ShapeDtypeSt...  8.56 us
    ppermute x3, starting transfers between devices, along_wave(): lax.ppermute(piece, 'wave', [(i, (i + s) % waves) for i in range(waves)])  6.07 us
    ppermute x8, starting transfers between devices, swap(): return lax.ppermute(x, ('groups', 'field'), pairs)  5.58 us
    ppermute x2, starting transfers between devices, add_over_wave(): x = x + lax.ppermute(x, 'wave', [(i, i ^ step) for i in range(waves)])  5.01 us
  transfers between devices with their start and end apart: 14, of which 9 were waited for; matrix products, arithmetic and copies ran while one was open for 4% of the time, Pallas kernels for 29%

profile of v8, /device:TPU:0, one launch (start us, length us, event | category | flops | bytes accessed | tf_op | source)
XLA Modules:
  0.0 148.5 jit_solution(8620951539312469823)
XLA Ops:
  0.0 0.0 copy-start
  0.0 0.0 copy-start.17
  0.0 0.7 pad_add_fusion.where
  0.7 4.3 %shard_map.136 = (bf16[560,16,128]{2,1,0:T(8,128)(2,1)}, bf16[71,16,128]{2,1,0:T(8,128)(2,1)}) custom-call(s32[2]{0:T(128)} %pad_add_fusion.where, s32[100,3]{1,0:T(8,128)} %constant.55.clone.table, f32[2]{0:T(128)} %own_lengths.1, bf16[22,128,512]{2,1,0:T(8,128)(2,1)} %basis.1), custom_call_target="tpu_custom_call" | custom-call | tf_op jit(solution)/shard_map/pallas_call | solution.py:137
  5.0 5.1 %collective-permute-start.2 = (bf16[71,16,128]{2,1,0:T(8,128)(2,1)}, bf16[71,16,128]{2,1,0:T(8,128)(2,1)S(1)}, u32[]{:S(2)}, u32[]{:S(2)}) collective-permute-start(bf16[71,16,128]{2,1,0:T(8,128)(2,1)} %get-tuple-element.26), channel_id=1, source_target_pairs={{0,3},{1,0},{2,1},{3,2},{4,7},{5,4},{6,5},{7,6},{8,11},{9,8},{10,9... | collective-permute-start | bytes 872456 | tf_op jit(solution)/shard_map/ppermute | solution.py:203
  10.1 0.0 collective-permute-start.1
  10.1 1.0 collective-permute-start
  11.1 0.0 copy-done.16
  11.1 0.0 copy-done.15
  11.1 1.1 fusion.6
  12.2 0.1 copy.27
  12.3 0.1 copy.28
  12.5 0.7 pad_maximum_fusion.refs_1_
  13.2 0.0 copy-done
  13.2 0.0 copy-done.17
  13.2 0.8 fusion.refs_0_
  14.0 1.9 %shard_map.137 = (bf16[1,128,352]{2,1,0:T(8,128)(2,1)}, bf16[8,128,128]{2,1,0:T(8,128)(2,1)}, f32[8,128]{1,0:T(8,128)}) custom-call(bf16[1,8,22]{2,1,0:T(8,128)(2,1)} %fusion.refs_0_, bf16[8,8,8]{2,1,0:T(8,128)(2,1)} %pad_maximum_fusion.refs_1_), custom_call_target="tpu_custom_call" | custom-call | tf_op jit(solution)/shard_map/pallas_call | solution.py:252
  15.9 0.7 add_convert_fusion.u_ref
  16.6 0.0 copy-done.8
  16.6 0.6 broadcast_in_dim.8.length_ref
  17.2 3.4 %shard_map.138 = (bf16[1,4,512,256]{3,2,1,0:T(8,128)(2,1)}, bf16[1,1024,512]{2,1,0:T(8,128)(2,1)}, f32[8,128]{1,0:T(8,128)}) custom-call(f32[1,8,128]{2,1,0:T(8,128)} %broadcast_in_dim.8.length_ref, f32[512,1]{1,0:T(8,128)} %constant.56.clone.y_ref, f32[1,256]{1,0:T(1,128)} %constant.57.clone.v_ref, f32[256,1]{1,0:T(8,128)} %add_convert_fusion.u_ref, ...), custom_call_target="tpu_custom_call" | custom-call | flops 3932160 | bytes 1048576 | tf_op jit(solution)/shard_map/pallas_call | solution.py:617
  20.7 0.0 collective-permute-done.2.refs_2_
  20.7 14.4 %collective-permute-done.1.refs_1_ = bf16[71,16,128]{2,1,0:T(8,128)(2,1)S(1)} collective-permute-done((bf16[71,16,128]{2,1,0:T(8,128)(2,1)}, bf16[71,16,128]{2,1,0:T(8,128)(2,1)S(1)}, u32[]{:S(2)}, u32[]{:S(2)}) %collective-permute-start.1) | collective-permute-done | bytes 290848 | tf_op jit(solution)/shard_map/ppermute | solution.py:203
  35.1 0.0 collective-permute-done.refs_0_
  35.1 0.0 copy-done.5
  35.1 0.7 copy-done.6
  35.8 0.1 copy-done.7
  35.9 2.1 %shard_map.139 = (bf16[105,16,128]{2,1,0:T(8,128)(2,1)}, bf16[105,16,128]{2,1,0:T(8,128)(2,1)}, f32[4,8,128]{2,1,0:T(8,128)}) custom-call(s32[2]{0:T(128)} %pad_add_fusion.where, f32[2]{0:T(128)} %own_lengths.1, bf16[71,16,128]{2,1,0:T(8,128)(2,1)} %copy-done.7, bf16[71,16,128]{2,1,0:T(8,128)(2,1)} %copy-done.6, bf16[71,16,128]{2,1,0:T(8,128)(2,1)} %copy-done.5, ...), custom_call_target="tpu_custom_call" | custom-call | tf_op jit(solution)/shard_map/pallas_call | solution.py:173
  38.0 1.5 %collective-permute-start.3 = (bf16[105,16,128]{2,1,0:T(8,128)(2,1)}, bf16[105,16,128]{2,1,0:T(8,128)(2,1)S(1)}, u32[]{:S(2)}, u32[]{:S(2)}) collective-permute-start(bf16[105,16,128]{2,1,0:T(8,128)(2,1)} %get-tuple-element.31.refs_0_), channel_id=1, source_target_pairs={{0,8},{4,12},{8,0},{12,4},{16,24},{20,28},{24,16},{28,20},{1,9},{5... | collective-permute-start | bytes 1290248 | tf_op jit(solution)/shard_map/ppermute | solution.py:215
  39.5 1.5 %collective-permute-start.4 = (bf16[105,16,128]{2,1,0:T(8,128)(2,1)}, bf16[105,16,128]{2,1,0:T(8,128)(2,1)S(1)}, u32[]{:S(2)}, u32[]{:S(2)}) collective-permute-start(bf16[105,16,128]{2,1,0:T(8,128)(2,1)} %get-tuple-element.32.refs_2_), channel_id=1, source_target_pairs={{0,16},{4,20},{8,24},{12,28},{16,0},{20,4},{24,8},{28,12},{1,17},{... | collective-permute-start | bytes 1290248 | tf_op jit(solution)/shard_map/ppermute | solution.py:215
  41.0 0.6 add_convert_fusion.1.u_ref
  41.6 5.1 %shard_map.140 = (bf16[4,4,128,256]{3,2,1,0:T(8,128)(2,1)}, bf16[4,1024,512]{2,1,0:T(8,128)(2,1)}, f32[8,128]{1,0:T(8,128)}) custom-call(f32[4,8,128]{2,1,0:T(8,128)} %get-tuple-element.29.length_ref, f32[512,1]{1,0:T(8,128)} %constant.56.clone.y_ref, f32[1,256]{1,0:T(1,128)} %constant.57.clone.v_ref, f32[64,1]{1,0:T(8,128)} %add_convert_fusion.1.u_ref, ...), custom_call_target="tpu_custom_call" | custom-call | flops 15728640 | bytes 4194304 | tf_op jit(solution)/shard_map/pallas_call | solution.py:617
  46.7 2.2 %collective-permute-done.3.refs_1_ = bf16[105,16,128]{2,1,0:T(8,128)(2,1)S(1)} collective-permute-done((bf16[105,16,128]{2,1,0:T(8,128)(2,1)}, bf16[105,16,128]{2,1,0:T(8,128)(2,1)S(1)}, u32[]{:S(2)}, u32[]{:S(2)}) %collective-permute-start.3) | collective-permute-done | bytes 430112 | tf_op jit(solution)/shard_map/ppermute | solution.py:215
  49.0 1.2 collective-permute-done.4.refs_3_
  50.2 0.8 copy-done.4
  51.0 2.7 %shard_map.141 = (bf16[210,16,128]{2,1,0:T(8,128)(2,1)}, bf16[210,16,128]{2,1,0:T(8,128)(2,1)}) custom-call(bf16[105,16,128]{2,1,0:T(8,128)(2,1)} %get-tuple-element.31.refs_0_, bf16[105,16,128]{2,1,0:T(8,128)(2,1)} %copy-done.3, bf16[105,16,128]{2,1,0:T(8,128)(2,1)} %get-tuple-element.32.refs_2_, bf16[105,16,128]{2,1,0:T(8,128)(2,1)} %copy-done.4, ...), custom_call_target="tpu_custom_call" | custom-call | tf_op jit(solution)/shard_map/pallas_call | solution.py:190
  53.6 1.5 %collective-permute-start.5 = (bf16[210,16,128]{2,1,0:T(8,128)(2,1)}, bf16[210,16,128]{2,1,0:T(8,128)(2,1)S(1)}, u32[]{:S(2)}, u32[]{:S(2)}) collective-permute-start(bf16[210,16,128]{2,1,0:T(8,128)(2,1)} %get-tuple-element.34.refs_1_), channel_id=1, source_target_pairs={{0,16},{4,20},{8,24},{12,28},{16,0},{20,4},{24,8},{28,12},{1,17},{... | collective-permute-start | bytes 2580488 | tf_op jit(solution)/shard_map/ppermute | solution.py:215
  55.1 0.5 collective-permute-start.8
  55.7 0.0 collective-permute-start.6
  55.7 0.5 collective-permute-start.9
  56.2 16.4 %collective-permute-done.5.refs_2_ = bf16[210,16,128]{2,1,0:T(8,128)(2,1)S(1)} collective-permute-done((bf16[210,16,128]{2,1,0:T(8,128)(2,1)}, bf16[210,16,128]{2,1,0:T(8,128)(2,1)S(1)}, u32[]{:S(2)}, u32[]{:S(2)}) %collective-permute-start.5) | collective-permute-done | bytes 860192 | tf_op jit(solution)/shard_map/ppermute | solution.py:215
  72.6 0.0 collective-permute-start.7
  72.6 1.2 collective-permute-done.8.refs_6_
  73.9 0.0 collective-permute-start.10
  73.9 0.0 collective-permute-done.6.refs_3_
  73.9 0.0 collective-permute-done.9.refs_7_
  73.9 0.0 copy-start.12
  73.9 1.1 collective-permute-done.7.refs_4_
  75.0 1.2 collective-permute-done.10.refs_8_
  76.3 0.9 copy-done.14
  77.2 0.0 copy-done.9
  77.2 20.7 %shard_map.142 = (bf16[4,1,512,256]{3,2,1,0:T(8,128)(2,1)}, f32[96,128,128]{2,1,0:T(8,128)}, f32[96,16,128]{2,1,0:T(8,128)}) custom-call(f32[1,8,128]{2,1,0:T(8,128)} %broadcast_in_dim.8.length_ref, s32[96,4]{1,0:T(8,128)} %constant.59.clone.place, s32[2]{0:T(128)} %pad_add_fusion.where, bf16[560,16,128]{2,1,0:T(8,128)(2,1)} %get-tuple-element.30.refs_0_, ...), custom_call_target="tpu_custom_call" | custom-call | flops 7242450944 | bytes 8388608 | tf_op jit(solution)/shard_map/pallas_call | solution.py:478
  97.9 4.5 %all-to-all-start = ((bf16[4,1,512,256]{3,2,1,0:T(8,128)(2,1)}), bf16[4,1,512,256]{3,2,1,0:T(8,128)(2,1)S(1)}, u32[]{:S(2)}, u32[]{:S(2)}) async-start(bf16[4,1,512,256]{3,2,1,0:T(8,128)(2,1)} %get-tuple-element.45), calls=%async_computation | async-start | bytes 2097152 | tf_op jit(solution)/shard_map/all_to_all | solution.py:715
  102.4 32.4 %shard_map.143 = (f32[4,512,256]{2,1,0:T(8,128)}, f32[4,8,128]{2,1,0:T(8,128)}) custom-call(f32[4,8,128]{2,1,0:T(8,128)} %get-tuple-element.29.length_ref, f32[96,128,128]{2,1,0:T(8,128)} %get-tuple-element.39.path_in, f32[96,16,128]{2,1,0:T(8,128)} %get-tuple-element.40.opening, bf16[4,4,128,256]{3,2,1,0:T(8,128)(2,1)} %get-tuple-element.41.row_ref, ...), custom_call_target="tpu_custom_call" | custom-call | flops 9642450944 | bytes 8388608 | tf_op jit(solution)/shard_map/pallas_call | solution.py:514
  134.9 2.1 %collective-permute-start.11 = (f32[4,8,128]{2,1,0:T(8,128)}, f32[4,8,128]{2,1,0:T(8,128)S(1)}, u32[]{:S(2)}, u32[]{:S(2)}) collective-permute-start(f32[4,8,128]{2,1,0:T(8,128)} %get-tuple-element.43), channel_id=1, source_target_pairs={{0,1},{1,0},{2,3},{3,2},{4,5},{5,4},{6,7},{7,6},{8,9},{9,8},{10,11... | collective-permute-start | bytes 49160 | tf_op jit(solution)/shard_map/ppermute | solution.py:653
  136.9 1.9 %collective-permute-done.11 = f32[4,8,128]{2,1,0:T(8,128)S(1)} collective-permute-done((f32[4,8,128]{2,1,0:T(8,128)}, f32[4,8,128]{2,1,0:T(8,128)S(1)}, u32[]{:S(2)}, u32[]{:S(2)}) %collective-permute-start.11) | collective-permute-done | bytes 16416 | tf_op jit(solution)/shard_map/ppermute | solution.py:653
  138.9 0.7 add.50
  139.6 2.9 %collective-permute-start.12 = (f32[4,8,128]{2,1,0:T(8,128)S(1)}, f32[4,8,128]{2,1,0:T(8,128)S(1)}, u32[]{:S(2)}, u32[]{:S(2)}) collective-permute-start(f32[4,8,128]{2,1,0:T(8,128)S(1)} %add.50), channel_id=1, source_target_pairs={{0,2},{1,3},{2,0},{3,1},{4,6},{5,7},{6,4},{7,5},{8,10},{9,11},{10,... | collective-permute-start | bytes 49160 | tf_op jit(solution)/shard_map/ppermute | solution.py:653
  142.5 1.7 %collective-permute-done.12 = f32[4,8,128]{2,1,0:T(8,128)S(1)} collective-permute-done((f32[4,8,128]{2,1,0:T(8,128)S(1)}, f32[4,8,128]{2,1,0:T(8,128)S(1)}, u32[]{:S(2)}, u32[]{:S(2)}) %collective-permute-start.12) | collective-permute-done | bytes 16416 | tf_op jit(solution)/shard_map/ppermute | solution.py:653
  144.2 0.0 all-to-all-done
  144.2 0.0 copy-done.2
  144.3 0.0 copy-start.1
  144.3 1.6 %copy-done.1 = f32[4,512,256]{2,1,0:T(8,128)S(1)} copy-done((f32[4,512,256]{2,1,0:T(8,128)S(1)}, f32[4,512,256]{2,1,0:T(8,128)}, u32[]{:S(2)}) %copy-start.1) | copy-done | bytes 2097176
  145.8 2.7 %shard_map.144 = bf16[8,8,64,256]{3,2,1,0:T(8,128)(2,1)} custom-call(f32[4,8,128]{2,1,0:T(8,128)S(1)} %add.51.sum_ref, bf16[8,128,128]{2,1,0:T(8,128)(2,1)S(1)} %copy-done.2, bf16[4,512,256]{2,1,0:T(8,128)(2,1)S(1)} %bitcast.16, f32[4,512,256]{2,1,0:T(8,128)S(1)} %copy-done.1), custom_call_target="tpu_custom_call" | custom-call | tf_op jit(solution)/shard_map/pallas_call | solution.py:566
  (23 shorter events, 0.1 us)
Async XLA Ops:
  0.0 13.2 %copy-start = (bf16[4096,22]{0,1:T(8,128)(2,1)S(1)}, bf16[4096,22]{0,1:T(8,128)(2,1)}, u32[]{:S(2)}) copy-start(bf16[4096,22]{0,1:T(8,128)(2,1)} %param.15) | copy-start | bytes 540676
  0.0 16.6 %copy-start.8 = (f32[2]{0:T(128)S(1)}, f32[2]{0:T(128)}, u32[]{:S(2)}) copy-start(f32[2]{0:T(128)} %own_lengths.1) | copy-start | bytes 28
  0.0 11.1 %copy-start.16 = (s32[8,8]{1,0:T(8,128)S(1)}, s32[8,8]{1,0:T(8,128)}, u32[]{:S(2)}) copy-start(s32[8,8]{1,0:T(8,128)} %param.19) | copy-start | bytes 772
  0.0 11.1 %copy-start.15 = (f32[1024,8]{0,1:T(8,128)S(1)}, f32[1024,8]{0,1:T(8,128)}, u32[]{:S(2)}) copy-start(f32[1024,8]{0,1:T(8,128)} %param.18) | copy-start | bytes 98308
  0.0 13.2 %copy-start.17 = (s32[8]{0:T(128)S(1)}, s32[8]{0:T(128)}, u32[]{:S(2)}) copy-start(s32[8]{0:T(128)} %param.16) | copy-start | bytes 100
  5.0 15.6 %collective-permute-start.2 = (bf16[71,16,128]{2,1,0:T(8,128)(2,1)}, bf16[71,16,128]{2,1,0:T(8,128)(2,1)S(1)}, u32[]{:S(2)}, u32[]{:S(2)}) collective-permute-start(bf16[71,16,128]{2,1,0:T(8,128)(2,1)} %get-tuple-element.26), channel_id=1, source_target_pairs={{0,3},{1,0},{2,1},{3,2},{4,7},{5,4},{6,5},{7,6},{8,11},{9,8},{10,9... | collective-permute-start | bytes 872456 | tf_op jit(solution)/shard_map/ppermute | solution.py:203
  10.1 25.0 %collective-permute-start.1 = (bf16[71,16,128]{2,1,0:T(8,128)(2,1)}, bf16[71,16,128]{2,1,0:T(8,128)(2,1)S(1)}, u32[]{:S(2)}, u32[]{:S(2)}) collective-permute-start(bf16[71,16,128]{2,1,0:T(8,128)(2,1)} %get-tuple-element.26), channel_id=1, source_target_pairs={{0,2},{1,3},{2,0},{3,1},{4,6},{5,7},{6,4},{7,5},{8,10},{9,11},{10,... | collective-permute-start | bytes 872456 | tf_op jit(solution)/shard_map/ppermute | solution.py:203
  10.1 25.0 %collective-permute-start = (bf16[71,16,128]{2,1,0:T(8,128)(2,1)}, bf16[71,16,128]{2,1,0:T(8,128)(2,1)S(1)}, u32[]{:S(2)}, u32[]{:S(2)}) collective-permute-start(bf16[71,16,128]{2,1,0:T(8,128)(2,1)} %get-tuple-element.26), channel_id=1, source_target_pairs={{0,1},{1,2},{2,3},{3,0},{4,5},{5,6},{6,7},{7,4},{8,9},{9,10},{10,1... | collective-permute-start | bytes 872456 | tf_op jit(solution)/shard_map/ppermute | solution.py:203
  20.7 14.4 %copy-start.5 = (bf16[71,16,128]{2,1,0:T(8,128)(2,1)}, bf16[71,16,128]{2,1,0:T(8,128)(2,1)S(1)}, u32[]{:S(2)}) copy-start(bf16[71,16,128]{2,1,0:T(8,128)(2,1)S(1)} %collective-permute-done.2.refs_2_) | copy-start | bytes 872452
  35.1 0.7 copy-start.6
  35.1 0.8 copy-start.7
  38.0 11.0 %collective-permute-start.3 = (bf16[105,16,128]{2,1,0:T(8,128)(2,1)}, bf16[105,16,128]{2,1,0:T(8,128)(2,1)S(1)}, u32[]{:S(2)}, u32[]{:S(2)}) collective-permute-start(bf16[105,16,128]{2,1,0:T(8,128)(2,1)} %get-tuple-element.31.refs_0_), channel_id=1, source_target_pairs={{0,8},{4,12},{8,0},{12,4},{16,24},{20,28},{24,16},{28,20},{1,9},{5... | collective-permute-start | bytes 1290248 | tf_op jit(solution)/shard_map/ppermute | solution.py:215
  39.5 10.7 %collective-permute-start.4 = (bf16[105,16,128]{2,1,0:T(8,128)(2,1)}, bf16[105,16,128]{2,1,0:T(8,128)(2,1)S(1)}, u32[]{:S(2)}, u32[]{:S(2)}) collective-permute-start(bf16[105,16,128]{2,1,0:T(8,128)(2,1)} %get-tuple-element.32.refs_2_), channel_id=1, source_target_pairs={{0,16},{4,20},{8,24},{12,28},{16,0},{20,4},{24,8},{28,12},{1,17},{... | collective-permute-start | bytes 1290248 | tf_op jit(solution)/shard_map/ppermute | solution.py:215
  49.0 1.2 copy-start.3
  50.2 0.8 copy-start.4
  53.6 19.0 %collective-permute-start.5 = (bf16[210,16,128]{2,1,0:T(8,128)(2,1)}, bf16[210,16,128]{2,1,0:T(8,128)(2,1)S(1)}, u32[]{:S(2)}, u32[]{:S(2)}) collective-permute-start(bf16[210,16,128]{2,1,0:T(8,128)(2,1)} %get-tuple-element.34.refs_1_), channel_id=1, source_target_pairs={{0,16},{4,20},{8,24},{12,28},{16,0},{20,4},{24,8},{28,12},{1,17},{... | collective-permute-start | bytes 2580488 | tf_op jit(solution)/shard_map/ppermute | solution.py:215
  55.1 18.7 %collective-permute-start.8 = (bf16[210,16,128]{2,1,0:T(8,128)(2,1)}, bf16[210,16,128]{2,1,0:T(8,128)(2,1)S(1)}, u32[]{:S(2)}, u32[]{:S(2)}) collective-permute-start(bf16[210,16,128]{2,1,0:T(8,128)(2,1)} %get-tuple-element.35.refs_5_), channel_id=1, source_target_pairs={{0,8},{4,12},{8,0},{12,4},{16,24},{20,28},{24,16},{28,20},{1,9},{5... | collective-permute-start | bytes 2580488 | tf_op jit(solution)/shard_map/ppermute | solution.py:215
  55.7 18.2 %collective-permute-start.6 = (bf16[210,16,128]{2,1,0:T(8,128)(2,1)}, bf16[210,16,128]{2,1,0:T(8,128)(2,1)S(1)}, u32[]{:S(2)}, u32[]{:S(2)}) collective-permute-start(bf16[210,16,128]{2,1,0:T(8,128)(2,1)} %get-tuple-element.34.refs_1_), channel_id=1, source_target_pairs={{0,4},{4,0},{8,12},{12,8},{16,20},{20,16},{24,28},{28,24},{1,5},{5... | collective-permute-start | bytes 2580488 | tf_op jit(solution)/shard_map/ppermute | solution.py:215
  55.7 18.2 %collective-permute-start.9 = (bf16[210,16,128]{2,1,0:T(8,128)(2,1)}, bf16[210,16,128]{2,1,0:T(8,128)(2,1)S(1)}, u32[]{:S(2)}, u32[]{:S(2)}) collective-permute-start(bf16[210,16,128]{2,1,0:T(8,128)(2,1)} %get-tuple-element.35.refs_5_), channel_id=1, source_target_pairs={{0,4},{4,0},{8,12},{12,8},{16,20},{20,16},{24,28},{28,24},{1,5},{5... | collective-permute-start | bytes 2580488 | tf_op jit(solution)/shard_map/ppermute | solution.py:215
  72.6 4.6 %copy-start.9 = (bf16[210,16,128]{2,1,0:T(8,128)(2,1)}, bf16[210,16,128]{2,1,0:T(8,128)(2,1)S(1)}, u32[]{:S(2)}) copy-start(bf16[210,16,128]{2,1,0:T(8,128)(2,1)S(1)} %collective-permute-done.5.refs_2_) | copy-start | bytes 2580484
  72.6 2.4 %collective-permute-start.7 = (bf16[210,16,128]{2,1,0:T(8,128)(2,1)S(1)}, bf16[210,16,128]{2,1,0:T(8,128)(2,1)S(1)}, u32[]{:S(2)}, u32[]{:S(2)}) collective-permute-start(bf16[210,16,128]{2,1,0:T(8,128)(2,1)S(1)} %collective-permute-done.5.refs_2_), channel_id=1, source_target_pairs={{0,4},{4,0},{8,12},{12,8},{16,20},{20,16},{24,28},{28,24},{1,5},{5... | collective-permute-start | bytes 2580488 | tf_op jit(solution)/shard_map/ppermute | solution.py:215
  73.9 3.3 %copy-start.10 = (bf16[210,16,128]{2,1,0:T(8,128)(2,1)}, bf16[210,16,128]{2,1,0:T(8,128)(2,1)S(1)}, u32[]{:S(2)}) copy-start(bf16[210,16,128]{2,1,0:T(8,128)(2,1)S(1)} %collective-permute-done.8.refs_6_) | copy-start | bytes 2580484
  73.9 2.4 %collective-permute-start.10 = (bf16[210,16,128]{2,1,0:T(8,128)(2,1)S(1)}, bf16[210,16,128]{2,1,0:T(8,128)(2,1)S(1)}, u32[]{:S(2)}, u32[]{:S(2)}) collective-permute-start(bf16[210,16,128]{2,1,0:T(8,128)(2,1)S(1)} %collective-permute-done.8.refs_6_), channel_id=1, source_target_pairs={{0,4},{4,0},{8,12},{12,8},{16,20},{20,16},{24,28},{28,24},{1,5},{5... | collective-permute-start | bytes 2580488 | tf_op jit(solution)/shard_map/ppermute | solution.py:215
  73.9 3.3 %copy-start.11 = (bf16[210,16,128]{2,1,0:T(8,128)(2,1)}, bf16[210,16,128]{2,1,0:T(8,128)(2,1)S(1)}, u32[]{:S(2)}) copy-start(bf16[210,16,128]{2,1,0:T(8,128)(2,1)S(1)} %collective-permute-done.6.refs_3_) | copy-start | bytes 2580484
  73.9 3.3 %copy-start.12 = (bf16[210,16,128]{2,1,0:T(8,128)(2,1)}, bf16[210,16,128]{2,1,0:T(8,128)(2,1)S(1)}, u32[]{:S(2)}) copy-start(bf16[210,16,128]{2,1,0:T(8,128)(2,1)S(1)} %collective-permute-done.9.refs_7_) | copy-start | bytes 2580484
  75.0 1.2 copy-start.13
  76.2 0.9 copy-start.14
  97.9 46.3 %all-to-all-start = ((bf16[4,1,512,256]{3,2,1,0:T(8,128)(2,1)}), bf16[4,1,512,256]{3,2,1,0:T(8,128)(2,1)S(1)}, u32[]{:S(2)}, u32[]{:S(2)}) async-start(bf16[4,1,512,256]{3,2,1,0:T(8,128)(2,1)} %get-tuple-element.45), calls=%async_computation | async-start | bytes 2097152 | tf_op jit(solution)/shard_map/all_to_all | solution.py:715
  102.4 41.8 %copy-start.2 = (bf16[8,128,128]{2,1,0:T(8,128)(2,1)S(1)}, bf16[8,128,128]{2,1,0:T(8,128)(2,1)}, u32[]{:S(2)}) copy-start(bf16[8,128,128]{2,1,0:T(8,128)(2,1)} %get-tuple-element.44.weight_ref) | copy-start | bytes 786436
  134.9 4.0 %collective-permute-start.11 = (f32[4,8,128]{2,1,0:T(8,128)}, f32[4,8,128]{2,1,0:T(8,128)S(1)}, u32[]{:S(2)}, u32[]{:S(2)}) collective-permute-start(f32[4,8,128]{2,1,0:T(8,128)} %get-tuple-element.43), channel_id=1, source_target_pairs={{0,1},{1,0},{2,3},{3,2},{4,5},{5,4},{6,7},{7,6},{8,9},{9,8},{10,11... | collective-permute-start | bytes 49160 | tf_op jit(solution)/shard_map/ppermute | solution.py:653
  139.6 4.6 %collective-permute-start.12 = (f32[4,8,128]{2,1,0:T(8,128)S(1)}, f32[4,8,128]{2,1,0:T(8,128)S(1)}, u32[]{:S(2)}, u32[]{:S(2)}) collective-permute-start(f32[4,8,128]{2,1,0:T(8,128)S(1)} %add.50), channel_id=1, source_target_pairs={{0,2},{1,3},{2,0},{3,1},{4,6},{5,7},{6,4},{7,5},{8,10},{9,11},{10,... | collective-permute-start | bytes 49160 | tf_op jit(solution)/shard_map/ppermute | solution.py:653
  144.3 1.6 %copy-start.1 = (f32[4,512,256]{2,1,0:T(8,128)S(1)}, f32[4,512,256]{2,1,0:T(8,128)}, u32[]{:S(2)}) copy-start(f32[4,512,256]{2,1,0:T(8,128)} %get-tuple-element.46.image_ref) | copy-start | bytes 6291460

commit v9 on v8

--- a/solution.py
+++ b/solution.py
@@ -102,24 +102,44 @@
     return half, slabs, pack, place
 
 
-def pack_kernel(count, half, modes, where, table, lengths, basis, own, piece):
+def pack_slab(table, basis, line, mode):
     left = lax.broadcasted_iota(jnp.int32, (ROWS, LANES), 1) < 64
-    wave, share = where[0], where[1]
+    first = pl.multiple_of(table[line, 0], LANES)
+    second = pl.multiple_of(table[line, 1], LANES)
+    row = pl.multiple_of(table[line, 2], ROWS)
+    one = basis[mode, pl.ds(row, ROWS), pl.ds(first, LANES)].astype(jnp.float32)
+    two = basis[mode, pl.ds(row, ROWS), pl.ds(second, LANES)].astype(jnp.float32)
+    return jnp.where(left, one, two).astype(basis.dtype)
+
+
+def own_kernel(count, where, table, basis, _, own, token):
+    modes = basis.shape[0]
+    token[...] = jnp.zeros_like(token)
 
     def unit(i, carry):
-        first = pl.multiple_of(table[wave * count + i, 0], LANES)
-        second = pl.multiple_of(table[wave * count + i, 1], LANES)
-        row = pl.multiple_of(table[wave * count + i, 2], ROWS)
         for k in range(modes):
-            one = basis[k, pl.ds(row, ROWS), pl.ds(first, LANES)].astype(jnp.float32)
-            two = basis[k, pl.ds(row, ROWS), pl.ds(second, LANES)].astype(jnp.float32)
-            own[i * modes + k] = jnp.where(left, one, two).astype(own.dtype)
+            own[i * modes + k] = pack_slab(table, basis, where[0] * count + i, k)
         return carry
 
     lax.fori_loop(0, count, unit, 0)
     for n in range(count * modes, own.shape[0]):
         own[n] = jnp.zeros((ROWS, LANES), own.dtype)
-    piece[: 2 * half] = own[pl.ds(share * (2 * half), 2 * half)]
+
+
+def piece_kernel(count, half, where, table, lengths, basis, piece, token):
+    modes = basis.shape[0]
+    token[...] = jnp.zeros_like(token)
+
+    def pair(i, carry):
+        for m in (2 * i, 2 * i + 1):
+            n = where[1] * (2 * half) + m
+            unit = n // modes
+            mode = n - unit * modes
+            unit = jnp.minimum(unit, count - 1)
+            piece[m] = pack_slab(table, basis, where[0] * count + unit, mode)
+        return carry
+
+    lax.fori_loop(0, half, pair, 0)
     line = lax.broadcasted_iota(jnp.int32, (ROWS, LANES), 0)
     slab = jnp.zeros((ROWS, LANES), jnp.float32)
     for i in range(lengths.shape[0]):
@@ -133,21 +153,33 @@
 
 def pack_rows(basis, wave_lengths, plan, where):
     half, slabs, table, _ = plan
-    tile = (ROWS, LANES)
-    return pl.pallas_call(
-        functools.partial(pack_kernel, table.shape[1], half, basis.shape[0]),
+    count, table = table.shape[1], table.reshape(-1, 3)
+    params = pltpu.CompilerParams(vmem_limit_bytes=VMEM_BYTES)
+    piece, token = pl.pallas_call(
+        functools.partial(piece_kernel, count, half),
         out_shape=(
-            jax.ShapeDtypeStruct((slabs,) + tile, basis.dtype),
-            jax.ShapeDtypeStruct((2 * half + 1,) + tile, basis.dtype),
+            jax.ShapeDtypeStruct((2 * half + 1, ROWS, LANES), basis.dtype),
+            jax.ShapeDtypeStruct((8, LANES), jnp.float32),
         ),
         in_specs=[SMEM, SMEM, SMEM, VMEM],
         out_specs=(VMEM, VMEM),
-        compiler_params=pltpu.CompilerParams(vmem_limit_bytes=VMEM_BYTES),
-    )(where, table.reshape(-1, 3), wave_lengths, basis)
+        compiler_params=params,
+    )(where, table, wave_lengths, basis)
+    own, token = pl.pallas_call(
+        functools.partial(own_kernel, count),
+        out_shape=(
+            jax.ShapeDtypeStruct((slabs, ROWS, LANES), basis.dtype),
+            jax.ShapeDtypeStruct((8, LANES), jnp.float32),
+        ),
+        in_specs=[SMEM, SMEM, VMEM, VMEM],
+        out_specs=(VMEM, VMEM),
+        compiler_params=params,
+    )(where, table, basis, token)
+    return own, piece, token
 
 
 def split_kernel(half, sent, parts_count, where, own_lengths, *refs):
-    parts, (low_ref, high_ref, length_ref) = refs[:parts_count], refs[-3:]
+    parts, (low_ref, high_ref, length_ref, inverse_ref) = refs[:parts_count], refs[-4:]
     wave, waves = where[0], parts_count + 1
     kept = own_lengths.shape[0] - sent
     for s in range(waves):
@@ -161,7 +193,9 @@
                     line + 2 : line + 3
                 ]
                 value = jnp.broadcast_to(value, (8, LANES))
-            length_ref[lax.rem(wave + (waves - s), waves) * kept + i] = value
+            place = lax.rem(wave + (waves - s), waves) * kept + i
+            length_ref[place] = value
+            inverse_ref[place] = (1.0 / value)[0, 0]
     for s, part in enumerate(parts):
         low_ref[s * half : (s + 1) * half] = part[:half]
         high_ref[s * half : (s + 1) * half] = part[half : 2 * half]
@@ -172,30 +206,27 @@
     slabs = jax.ShapeDtypeStruct((len(parts) * half, ROWS, LANES), parts[0].dtype)
     return pl.pallas_call(
         functools.partial(split_kernel, half, sent, len(parts)),
-        out_shape=(slabs, slabs, jax.ShapeDtypeStruct((count, 8, LANES), jnp.float32)),
+        out_shape=(
+            slabs,
+            slabs,
+            jax.ShapeDtypeStruct((count, 8, LANES), jnp.float32),
+            jax.ShapeDtypeStruct((count,), jnp.float32),
+        ),
         in_specs=[SMEM, SMEM] + [VMEM] * (len(parts) + len(tokens)),
-        out_specs=(VMEM,) * 3,
+        out_specs=(VMEM,) * 3 + (SMEM,),
         compiler_params=pltpu.CompilerParams(vmem_limit_bytes=VMEM_BYTES),
     )(where, wave_lengths, *parts, *tokens)
 
 
-def join_kernel(pairs, *refs):
-    for i in range(pairs):
-        one, two, out = refs[2 * i], refs[2 * i + 1], refs[i - pairs]
-        out[: one.shape[0]] = one[...]
-        out[one.shape[0] :] = two[...]
-
-
-def join(pairs, token):
+def after(arrays, tokens):
+    any_memory = pl.BlockSpec(memory_space=pl.ANY)
     return pl.pallas_call(
-        functools.partial(join_kernel, len(pairs)),
-        out_shape=tuple(
-            jax.ShapeDtypeStruct((2 * one.shape[0],) + one.shape[1:], one.dtype) for one, _ in pairs
-        ),
-        in_specs=[VMEM] * (2 * len(pairs) + 1),
-        out_specs=(VMEM,) * len(pairs),
-        compiler_params=pltpu.CompilerParams(vmem_limit_bytes=VMEM_BYTES),
-    )(*[one for pair in pairs for one in pair], token)
+        lambda *refs: None,
+        out_shape=tuple(jax.ShapeDtypeStruct(x.shape, x.dtype) for x in arrays),
+        in_specs=[any_memory] * len(arrays) + [VMEM] * len(tokens),
+        out_specs=(any_memory,) * len(arrays),
+        input_output_aliases={i: i for i in range(len(arrays))},
+    )(*arrays, *tokens)
 
 
 def along_wave(piece, waves):
@@ -216,16 +247,15 @@
 
 
 def gather_halves(halves, token):
-    got = []
     routes = ((2, 4), (4, 2))
-    joined = join([(mine, swap(mine, one)) for mine, (one, _) in zip(halves, routes)], token)
-    for h, (both, (one, two)) in enumerate(zip(joined, routes)):
-        far = swap(both, two)
-        got.append((h, both, (0, one)))
-        got.append((h, far, (two, one | two)))
-        got.append((h, swap(both, 1), (1, one | 1)))
-        got.append((h, swap(far, 1), (two | 1, one | two | 1)))
-    return got
+    near = [swap(mine, mask) for mine, route in zip(halves, routes) for mask in route]
+    near = after(near, [token])
+    got = [(h, mine, 0) for h, mine in enumerate(halves)]
+    for h, (one, two) in enumerate(routes):
+        got.append((h, near[2 * h], one))
+        got.append((h, near[2 * h + 1], two))
+        got.append((h, swap(near[2 * h], two), one | two))
+    return got + [(h, swap(array, 1), mask | 1) for h, array, mask in got]
 
 
 def spread_kernel(*refs):
@@ -265,19 +295,16 @@
     wave, share = where[0], where[1]
     copies = [pltpu.make_async_copy(parts[0], basis.at[pl.ds(wave * slabs, slabs)], sems.at[0])]
     n = 1
-    for (h, masks), part in zip(keys, parts[1:]):
-        for m, mask in enumerate(masks):
-            for s in range(1, waves):
-                source = lax.rem(wave + (waves - s), waves)
-                start = source * slabs + (share ^ mask) * (2 * half) + h * half
-                copies.append(
-                    pltpu.make_async_copy(
-                        part.at[pl.ds((m * (waves - 1) + s - 1) * half, half)],
-                        basis.at[pl.ds(start, half)],
-                        sems.at[n],
-                    )
+    for (h, mask), part in zip(keys, parts[1:]):
+        for s in range(1, waves):
+            source = lax.rem(wave + (waves - s), waves)
+            start = source * slabs + (share ^ mask) * (2 * half) + h * half
+            copies.append(
+                pltpu.make_async_copy(
+                    part.at[pl.ds((s - 1) * half, half)], basis.at[pl.ds(start, half)], sems.at[n]
                 )
-                n += 1
+            )
+            n += 1
     for copy in copies:
         copy.start()
     for copy in copies:
@@ -384,7 +411,7 @@
     ]
 
 
-def whole_kernel(sizes, length_ref, place, where, *refs):
+def whole_kernel(sizes, inverse_ref, place, where, *refs):
     positions, modes, waves, half, slabs, keys = sizes
     parts, refs = refs[: 1 + len(keys)], refs[1 + len(keys) :]
     spread, row_ref, column_ref, out_ref, path_out, opening, path, basis, sems, path_sems = refs[:10]
@@ -398,7 +425,8 @@
             copy.start()
 
     rows = PIX
-    transform(positions, rows, 1.0 / length_ref[0, :1], path, opening, row_ref, scratch)
+    inverse = inverse_ref[pl.program_id(0)]
+    transform(positions, rows, inverse, path, opening, row_ref, scratch)
     first = scratch[3]
     share = rows // waves
     for f in range(positions):
@@ -419,7 +447,7 @@
             copy.wait()
 
 
-def rows_kernel(positions, rows, length_ref, path_in, opening, row_ref, column_ref, *refs):
+def rows_kernel(positions, rows, inverse_ref, path_in, opening, row_ref, column_ref, *refs):
     image_ref, sum_ref, path, path_sems = refs[:4]
     scratch = refs[4:]
     copies = chunk_copies(path_in, path, path_sems)
@@ -431,11 +459,17 @@
             copy.start()
 
     def wait(c):
+        if c > 0 and CHUNKS[c - 1][0] == CHUNKS[c][0]:
+            return
+
         @pl.when(begin)
         def _():
-            copies[c].wait()
-
-    transform(positions, rows, 1.0 / length_ref[0, :1], path, opening, row_ref, scratch, wait)
+            for copy, chunk in zip(copies, CHUNKS):
+                if chunk[0] == CHUNKS[c][0]:
+                    copy.wait()
+
+    inverse = inverse_ref[pl.program_id(0)]
+    transform(positions, rows, inverse, path, opening, row_ref, scratch, wait)
     real, imag = columns_of(scratch[3][...], column_ref)
     intensity = real * real + imag * imag
     image_ref[0] = intensity
@@ -468,11 +502,11 @@
     return (len(CHUNKS) * UNITS, positions * ROWS, LANES)
 
 
-def whole_fields(own, got, spread, place, where, length, tables, sizes):
+def whole_fields(own, got, spread, place, where, inverse, tables, sizes):
     positions, modes, waves, half, slabs = sizes
-    keys = tuple((h, masks) for h, _, masks in got)
+    keys = tuple((h, mask) for h, _, mask in got)
     arrays = [array for _, array, _ in got]
-    lengths = length.shape[0]
+    lengths = inverse.shape[0]
     share = positions * PIX // waves
     any_memory = pl.BlockSpec(memory_space=pl.ANY)
     return pl.pallas_call(
@@ -483,7 +517,7 @@
             jax.ShapeDtypeStruct(path_shape(positions), jnp.float32),
             jax.ShapeDtypeStruct((place.shape[0], ROWS, LANES), jnp.float32),
         ),
-        in_specs=[by_length(length), SMEM, SMEM]
+        in_specs=[SMEM, SMEM, SMEM]
         + [any_memory] * (1 + len(keys))
         + [VMEM]
         + [by_length(table) for table in tables],
@@ -495,17 +529,17 @@
         scratch_shapes=[
             pltpu.VMEM(path_shape(positions), jnp.float32),
             pltpu.VMEM((waves * slabs, ROWS, LANES), jnp.bfloat16),
-            pltpu.SemaphoreType.DMA((1 + sum(len(masks) for _, masks in keys) * (waves - 1),)),
+            pltpu.SemaphoreType.DMA((1 + len(keys) * (waves - 1),)),
             pltpu.SemaphoreType.DMA((len(CHUNKS),)),
         ]
         + transform_scratch(positions, PIX),
         cost_estimate=transform_cost(lengths, positions, PIX),
         compiler_params=pltpu.CompilerParams(vmem_limit_bytes=VMEM_BYTES),
-    )(length, place, where, own, *arrays, spread, *tables)
-
-
-def row_fields(path, opening, length, tables, positions):
-    lengths = length.shape[0]
+    )(inverse, place, where, own, *arrays, spread, *tables)
+
+
+def row_fields(path, opening, inverse, tables, positions):
+    lengths = inverse.shape[0]
     rows = tables[0].shape[2] // 2
     out_shape = (
         jax.ShapeDtypeStruct((lengths, positions * rows, PIX), jnp.float32),
@@ -515,7 +549,7 @@
         functools.partial(rows_kernel, positions, rows),
         grid=(lengths,),
         out_shape=out_shape,
-        in_specs=[by_length(length), pl.BlockSpec(memory_space=pl.ANY), VMEM]
+        in_specs=[SMEM, pl.BlockSpec(memory_space=pl.ANY), VMEM]
         + [by_length(table) for table in tables],
         out_specs=tuple(by_length(one) for one in out_shape),
         scratch_shapes=[
@@ -525,7 +559,7 @@
         + transform_scratch(positions, rows),
         cost_estimate=transform_cost(lengths, positions, rows),
         compiler_params=pltpu.CompilerParams(vmem_limit_bytes=VMEM_BYTES),
-    )(length, path, opening, *tables)
+    )(inverse, path, opening, *tables)
 
 
 def mix_kernel(sum_ref, weight_ref, sent_ref, image_ref, out_ref):
@@ -668,7 +702,7 @@
     where = jnp.stack([mine, share]).astype(jnp.int32)
     plan = layout(waves, modes)
     half, slabs, _, place = plan
-    own, piece = pack_rows(mode_basis, wave_lengths, plan, where)
+    own, piece, packed = pack_rows(mode_basis, wave_lengths, plan, where)
     parts = along_wave(piece, waves)
 
     selector = (
@@ -696,8 +730,8 @@
     )
     own_row, own_column, own_token = tables(own_length, 0, PIX)
 
-    low, high, every = split_parts(
-        parts, where, wave_lengths, half, sent_lengths, (spread_token, own_token)
+    low, high, every, inverse = split_parts(
+        parts, where, wave_lengths, half, sent_lengths, (spread_token, own_token, packed)
     )
     all_row, all_column, all_token = tables(every, mine * rows, rows)
     got = gather_halves((low, high), all_token)
@@ -708,13 +742,13 @@
         path_spread,
         place,
         where,
-        own_length,
+        1.0 / wave_lengths[:sent_lengths],
         (own_row, own_column),
         (positions, modes, waves, half, slabs),
     )
     sent = lax.all_to_all(spectra, "wave", split_axis=0, concat_axis=0, tiled=True)
     sent = sent.reshape(waves * sent_lengths, positions * rows, PIX)
-    images, sums = row_fields(path, opening, every, (all_row, all_column), positions)
+    images, sums = row_fields(path, opening, inverse, (all_row, all_column), positions)
     return mix(mix_spread, add_over_wave(sums, waves), sent, images, templates, rows)
 
 

time: 149 us -> 147 us (0.987)
  waiting for transfers between devices: 41.5 us -> 35.8 us
  Pallas kernels: 75.4 us -> 77.7 us
    ppermute x3, waiting for transfers between devices: 14.4 us -> 8.66 us  [along_wave(): lax.ppermute(piece, 'wave', [(i, (i + s) % waves) for i in range(waves)])]
    pallas_call x2 -> x3, Pallas kernels: 6.99 us -> 10.3 us  [the longest x1 5.76 us: pack_rows(): pl.pallas_call(functools.partial(own_kernel, count), out_shape=(jax.Shape...]
    ppermute x8 -> x14, starting transfers between devices: 5.58 us -> 6.99 us  [swap(): return lax.ppermute(x, ('groups', 'field'), pairs)]
    unnamed x38 -> x52, local copies, waits for them, and re-layouts: 4.4 us -> 4.54 us
    ppermute x8 -> x14, waiting for transfers between devices: 23.5 us -> 23.5 us  [swap(): return lax.ppermute(x, ('groups', 'field'), pairs)]
  transfers between devices with their start and end apart: 14 -> 20, of which waited for: 9 -> 10; matrix products, arithmetic and copies ran while one was open for 4% -> 4% of each run, Pallas kernels for 29% -> 33%
where the time goes in v9:
time: 147 us; the launch traced here: 146 us
  Pallas kernels  77.7 us (53%)
  waiting for transfers between devices  35.8 us (24%)
  starting transfers between devices  22.3 us (15%)
  local copies, waits for them, and re-layouts  5.16 us (4%)
  other arithmetic  3.3 us (2%)
  matrix products  1.83 us (1%)
    pallas_call x1, Pallas kernels, row_fields(): pl.pallas_call(functools.partial(rows_kernel, positions, rows), grid=(len...  31.3 us
    ppermute x14, waiting for transfers between devices, swap(): return lax.ppermute(x, ('groups', 'field'), pairs)  23.5 us
    pallas_call x1, Pallas kernels, whole_fields(): pl.pallas_call(functools.partial(whole_kernel, (positions, modes, waves,...  20.9 us
    ppermute x3, waiting for transfers between devices, along_wave(): lax.ppermute(piece, 'wave', [(i, (i + s) % waves) for i in range(waves)])  8.66 us
    pallas_call x2, Pallas kernels, tables(): pl.pallas_call(table_kernel, grid=(lengths,), out_shape=(jax.ShapeDtypeSt...  8.54 us
    ppermute x14, starting transfers between devices, swap(): return lax.ppermute(x, ('groups', 'field'), pairs)  6.99 us
    ppermute x3, starting transfers between devices, along_wave(): lax.ppermute(piece, 'wave', [(i, (i + s) % waves) for i in range(waves)])  6.09 us
    pallas_call x1, Pallas kernels, pack_rows(): pl.pallas_call(functools.partial(own_kernel, count), out_shape=(jax.Shape...  5.76 us
  transfers between devices with their start and end apart: 20, of which 10 were waited for; matrix products, arithmetic and copies ran while one was open for 4% of the time, Pallas kernels for 33%

profile of v9, /device:TPU:0, one launch (start us, length us, event | category | flops | bytes accessed | tf_op | source)
XLA Modules:
  0.0 146.5 jit_solution(15918121205899448756)
XLA Ops:
  0.0 0.6 pad_add_fusion.where
  0.6 3.9 %shard_map.136 = (bf16[71,16,128]{2,1,0:T(8,128)(2,1)}, f32[8,128]{1,0:T(8,128)}) custom-call(s32[2]{0:T(128)} %pad_add_fusion.where, s32[100,3]{1,0:T(8,128)} %constant.57.clone.table, f32[2]{0:T(128)} %own_lengths.1, bf16[22,128,512]{2,1,0:T(8,128)(2,1)} %basis.3), custom_call_target="tpu_custom_call" | custom-call | tf_op jit(solution)/shard_map/pallas_call | solution.py:158
  4.5 5.1 %collective-permute-start.2 = (bf16[71,16,128]{2,1,0:T(8,128)(2,1)}, bf16[71,16,128]{2,1,0:T(8,128)(2,1)S(1)}, u32[]{:S(2)}, u32[]{:S(2)}) collective-permute-start(bf16[71,16,128]{2,1,0:T(8,128)(2,1)} %get-tuple-element.31), channel_id=1, source_target_pairs={{0,3},{1,0},{2,1},{3,2},{4,7},{5,4},{6,5},{7,6},{8,11},{9,8},{10,9... | collective-permute-start | bytes 872456 | tf_op jit(solution)/shard_map/ppermute | solution.py:234
  9.5 0.0 collective-permute-start.1
  9.5 1.0 collective-permute-start
  10.6 1.1 fusion.6
  11.7 0.1 copy.31
  11.8 0.1 copy.32
  11.9 0.7 pad_maximum_fusion.refs_1_
  12.6 5.8 %shard_map.139 = (bf16[560,16,128]{2,1,0:T(8,128)(2,1)}, f32[8,128]{1,0:T(8,128)}) custom-call(s32[2]{0:T(128)} %pad_add_fusion.where, s32[100,3]{1,0:T(8,128)} %constant.57.clone.table, bf16[22,128,512]{2,1,0:T(8,128)(2,1)} %basis.3, f32[8,128]{1,0:T(8,128)} %get-tuple-element.34._), custom_call_target="tpu_custom_call" | custom-call | tf_op jit(solution)/shard_map/pallas_call | solution.py:168
  18.4 0.8 fusion.refs_0_
  19.2 2.0 %shard_map.137 = (bf16[1,128,352]{2,1,0:T(8,128)(2,1)}, bf16[8,128,128]{2,1,0:T(8,128)(2,1)}, f32[8,128]{1,0:T(8,128)}) custom-call(bf16[1,8,22]{2,1,0:T(8,128)(2,1)} %fusion.refs_0_, bf16[8,8,8]{2,1,0:T(8,128)(2,1)} %pad_maximum_fusion.refs_1_), custom_call_target="tpu_custom_call" | custom-call | tf_op jit(solution)/shard_map/pallas_call | solution.py:282
  21.1 0.7 add_convert_fusion.u_ref
  21.8 0.6 broadcast_in_dim.8.length_ref
  22.4 3.4 %shard_map.138 = (bf16[1,4,512,256]{3,2,1,0:T(8,128)(2,1)}, bf16[1,1024,512]{2,1,0:T(8,128)(2,1)}, f32[8,128]{1,0:T(8,128)}) custom-call(f32[1,8,128]{2,1,0:T(8,128)} %broadcast_in_dim.8.length_ref, f32[512,1]{1,0:T(8,128)} %constant.58.clone.y_ref, f32[1,256]{1,0:T(1,128)} %constant.59.clone.v_ref, f32[256,1]{1,0:T(8,128)} %add_convert_fusion.u_ref, ...), custom_call_target="tpu_custom_call" | custom-call | flops 3932160 | bytes 1048576 | tf_op jit(solution)/shard_map/pallas_call | solution.py:651
  25.8 0.0 collective-permute-done.2.refs_2_
  25.9 8.7 %collective-permute-done.1.refs_1_ = bf16[71,16,128]{2,1,0:T(8,128)(2,1)S(1)} collective-permute-done((bf16[71,16,128]{2,1,0:T(8,128)(2,1)}, bf16[71,16,128]{2,1,0:T(8,128)(2,1)S(1)}, u32[]{:S(2)}, u32[]{:S(2)}) %collective-permute-start.1) | collective-permute-done | bytes 290848 | tf_op jit(solution)/shard_map/ppermute | solution.py:234
  34.5 0.0 collective-permute-done.refs_0_
  34.5 0.7 copy-done.8
  35.3 0.1 copy-done.9
  35.3 2.1 %shard_map.140 = (bf16[105,16,128]{2,1,0:T(8,128)(2,1)}, bf16[105,16,128]{2,1,0:T(8,128)(2,1)}, f32[4,8,128]{2,1,0:T(8,128)}, f32[4]{0:T(128)}) custom-call(s32[2]{0:T(128)} %pad_add_fusion.where, f32[2]{0:T(128)} %own_lengths.1, bf16[71,16,128]{2,1,0:T(8,128)(2,1)} %copy-done.9, bf16[71,16,128]{2,1,0:T(8,128)(2,1)} %copy-done.8, ...), custom_call_target="tpu_custom_call" | custom-call | tf_op jit(solution)/shard_map/pallas_call | solution.py:207
  37.4 1.6 %collective-permute-start.4 = (bf16[105,16,128]{2,1,0:T(8,128)(2,1)}, bf16[105,16,128]{2,1,0:T(8,128)(2,1)S(1)}, u32[]{:S(2)}, u32[]{:S(2)}) collective-permute-start(bf16[105,16,128]{2,1,0:T(8,128)(2,1)} %get-tuple-element.38.refs_1_), channel_id=1, source_target_pairs={{0,16},{4,20},{8,24},{12,28},{16,0},{20,4},{24,8},{28,12},{1,17},{... | collective-permute-start | bytes 1290248 | tf_op jit(solution)/shard_map/ppermute | solution.py:246
  39.0 1.5 %collective-permute-start.3 = (bf16[105,16,128]{2,1,0:T(8,128)(2,1)}, bf16[105,16,128]{2,1,0:T(8,128)(2,1)S(1)}, u32[]{:S(2)}, u32[]{:S(2)}) collective-permute-start(bf16[105,16,128]{2,1,0:T(8,128)(2,1)} %get-tuple-element.38.refs_1_), channel_id=1, source_target_pairs={{0,8},{4,12},{8,0},{12,4},{16,24},{20,28},{24,16},{28,20},{1,9},{5... | collective-permute-start | bytes 1290248 | tf_op jit(solution)/shard_map/ppermute | solution.py:246
  40.5 0.5 collective-permute-start.6
  41.1 0.5 collective-permute-start.5
  41.6 0.6 add_convert_fusion.1.u_ref
  42.2 0.0 collective-permute-start.9
  42.2 5.1 %shard_map.141 = (bf16[4,4,128,256]{3,2,1,0:T(8,128)(2,1)}, bf16[4,1024,512]{2,1,0:T(8,128)(2,1)}, f32[8,128]{1,0:T(8,128)}) custom-call(f32[4,8,128]{2,1,0:T(8,128)} %get-tuple-element.40.length_ref, f32[512,1]{1,0:T(8,128)} %constant.58.clone.y_ref, f32[1,256]{1,0:T(1,128)} %constant.59.clone.v_ref, f32[64,1]{1,0:T(8,128)} %add_convert_fusion.1.u_ref, ...), custom_call_target="tpu_custom_call" | custom-call | flops 15728640 | bytes 4194304 | tf_op jit(solution)/shard_map/pallas_call | solution.py:651
  47.3 3.3 %collective-permute-done.4.refs_1_ = bf16[105,16,128]{2,1,0:T(8,128)(2,1)S(1)} collective-permute-done((bf16[105,16,128]{2,1,0:T(8,128)(2,1)}, bf16[105,16,128]{2,1,0:T(8,128)(2,1)S(1)}, u32[]{:S(2)}, u32[]{:S(2)}) %collective-permute-start.4) | collective-permute-done | bytes 430112 | tf_op jit(solution)/shard_map/ppermute | solution.py:246
  50.6 0.0 collective-permute-start.10
  50.6 1.5 %collective-permute-done.3.refs_0_ = bf16[105,16,128]{2,1,0:T(8,128)(2,1)S(1)} collective-permute-done((bf16[105,16,128]{2,1,0:T(8,128)(2,1)}, bf16[105,16,128]{2,1,0:T(8,128)(2,1)S(1)}, u32[]{:S(2)}, u32[]{:S(2)}) %collective-permute-start.3) | collective-permute-done | bytes 430112 | tf_op jit(solution)/shard_map/ppermute | solution.py:246
  52.1 6.9 %collective-permute-done.6.refs_3_ = bf16[105,16,128]{2,1,0:T(8,128)(2,1)S(1)} collective-permute-done((bf16[105,16,128]{2,1,0:T(8,128)(2,1)}, bf16[105,16,128]{2,1,0:T(8,128)(2,1)S(1)}, u32[]{:S(2)}, u32[]{:S(2)}) %collective-permute-start.6) | collective-permute-done | bytes 430112 | tf_op jit(solution)/shard_map/ppermute | solution.py:246
  58.9 0.0 collective-permute-done.5.refs_2_
  59.0 0.7 copy-done.5
  59.7 0.2 copy-done.6
  59.8 0.7 shard_map.142
  60.5 0.0 collective-permute-start.12
  60.5 0.5 collective-permute-start.7
  61.0 1.5 %collective-permute-start.8 = (bf16[105,16,128]{2,1,0:T(8,128)(2,1)}, bf16[105,16,128]{2,1,0:T(8,128)(2,1)S(1)}, u32[]{:S(2)}, u32[]{:S(2)}) collective-permute-start(bf16[105,16,128]{2,1,0:T(8,128)(2,1)} %get-tuple-element.44.refs_6_), channel_id=1, source_target_pairs={{0,8},{4,12},{8,0},{12,4},{16,24},{20,28},{24,16},{28,20},{1,9},{5... | collective-permute-start | bytes 1290248 | tf_op jit(solution)/shard_map/ppermute | solution.py:246
  62.5 0.0 collective-permute-done.9.refs_9_
  62.5 0.0 collective-permute-start.11
  62.6 0.5 collective-permute-start.14
  63.0 0.1 collective-permute-start.15
  63.1 9.9 %collective-permute-done.7.refs_5_ = bf16[105,16,128]{2,1,0:T(8,128)(2,1)S(1)} collective-permute-done((bf16[105,16,128]{2,1,0:T(8,128)(2,1)}, bf16[105,16,128]{2,1,0:T(8,128)(2,1)S(1)}, u32[]{:S(2)}, u32[]{:S(2)}) %collective-permute-start.7) | collective-permute-done | bytes 430112 | tf_op jit(solution)/shard_map/ppermute | solution.py:246
  73.1 0.0 collective-permute-start.13
  73.1 0.2 collective-permute-done.8.refs_8_
  73.3 0.3 collective-permute-start.16
  73.7 0.0 collective-permute-done.15.refs_15_
  73.7 1.1 collective-permute-done.13.refs_13_
  74.8 0.6 collective-permute-done.16.refs_16_
  75.4 0.2 copy-done.20
  75.6 0.8 copy-done.21
  76.4 20.9 %shard_map.143 = (bf16[4,1,512,256]{3,2,1,0:T(8,128)(2,1)}, f32[96,128,128]{2,1,0:T(8,128)}, f32[96,16,128]{2,1,0:T(8,128)}) custom-call(f32[1]{0:T(128)S(6)} %div.13.inverse_ref, s32[96,4]{1,0:T(8,128)} %constant.61.clone.place, s32[2]{0:T(128)} %pad_add_fusion.where, bf16[560,16,128]{2,1,0:T(8,128)(2,1)} %get-tuple-element.37.refs_0_, ...), custom_call_target="tpu_custom_call" | custom-call | flops 7242450944 | bytes 8388608 | tf_op jit(solution)/shard_map/pallas_call | solution.py:512
  97.3 4.3 %all-to-all-start = ((bf16[4,1,512,256]{3,2,1,0:T(8,128)(2,1)}), bf16[4,1,512,256]{3,2,1,0:T(8,128)(2,1)S(1)}, u32[]{:S(2)}, u32[]{:S(2)}) async-start(bf16[4,1,512,256]{3,2,1,0:T(8,128)(2,1)} %get-tuple-element.55), calls=%async_computation | async-start | bytes 2097152 | tf_op jit(solution)/shard_map/all_to_all | solution.py:749
  101.6 31.3 %shard_map.144 = (f32[4,512,256]{2,1,0:T(8,128)}, f32[4,8,128]{2,1,0:T(8,128)}) custom-call(f32[4]{0:T(128)} %get-tuple-element.36.inverse_ref, f32[96,128,128]{2,1,0:T(8,128)} %get-tuple-element.49.path_in, f32[96,16,128]{2,1,0:T(8,128)} %get-tuple-element.50.opening, bf16[4,4,128,256]{3,2,1,0:T(8,128)(2,1)} %get-tuple-element.51.row_ref, ...), custom_call_target="tpu_custom_call" | custom-call | flops 9642450944 | bytes 8388608 | tf_op jit(solution)/shard_map/pallas_call | solution.py:548
  132.9 2.1 %collective-permute-start.17 = (f32[4,8,128]{2,1,0:T(8,128)}, f32[4,8,128]{2,1,0:T(8,128)S(1)}, u32[]{:S(2)}, u32[]{:S(2)}) collective-permute-start(f32[4,8,128]{2,1,0:T(8,128)} %get-tuple-element.53), channel_id=1, source_target_pairs={{0,1},{1,0},{2,3},{3,2},{4,5},{5,4},{6,7},{7,6},{8,9},{9,8},{10,11... | collective-permute-start | bytes 49160 | tf_op jit(solution)/shard_map/ppermute | solution.py:687
  134.9 1.9 %collective-permute-done.17 = f32[4,8,128]{2,1,0:T(8,128)S(1)} collective-permute-done((f32[4,8,128]{2,1,0:T(8,128)}, f32[4,8,128]{2,1,0:T(8,128)S(1)}, u32[]{:S(2)}, u32[]{:S(2)}) %collective-permute-start.17) | collective-permute-done | bytes 16416 | tf_op jit(solution)/shard_map/ppermute | solution.py:687
  136.9 0.7 add.50
  137.6 2.9 %collective-permute-start.18 = (f32[4,8,128]{2,1,0:T(8,128)S(1)}, f32[4,8,128]{2,1,0:T(8,128)S(1)}, u32[]{:S(2)}, u32[]{:S(2)}) collective-permute-start(f32[4,8,128]{2,1,0:T(8,128)S(1)} %add.50), channel_id=1, source_target_pairs={{0,2},{1,3},{2,0},{3,1},{4,6},{5,7},{6,4},{7,5},{8,10},{9,11},{10,... | collective-permute-start | bytes 49160 | tf_op jit(solution)/shard_map/ppermute | solution.py:687
  140.5 1.7 %collective-permute-done.18 = f32[4,8,128]{2,1,0:T(8,128)S(1)} collective-permute-done((f32[4,8,128]{2,1,0:T(8,128)S(1)}, f32[4,8,128]{2,1,0:T(8,128)S(1)}, u32[]{:S(2)}, u32[]{:S(2)}) %collective-permute-start.18) | collective-permute-done | bytes 16416 | tf_op jit(solution)/shard_map/ppermute | solution.py:687
  142.2 0.0 all-to-all-done
  142.3 0.0 copy-start.1
  142.3 1.6 %copy-done.1 = f32[4,512,256]{2,1,0:T(8,128)S(1)} copy-done((f32[4,512,256]{2,1,0:T(8,128)S(1)}, f32[4,512,256]{2,1,0:T(8,128)}, u32[]{:S(2)}) %copy-start.1) | copy-done | bytes 2097176
  143.8 2.6 %shard_map.145 = bf16[8,8,64,256]{3,2,1,0:T(8,128)(2,1)} custom-call(f32[4,8,128]{2,1,0:T(8,128)S(1)} %add.51.sum_ref, bf16[8,128,128]{2,1,0:T(8,128)(2,1)S(1)} %copy-done.2, bf16[4,512,256]{2,1,0:T(8,128)(2,1)S(1)} %bitcast.16, f32[4,512,256]{2,1,0:T(8,128)S(1)} %copy-done.1), custom_call_target="tpu_custom_call" | custom-call | tf_op jit(solution)/shard_map/pallas_call | solution.py:600
  (50 shorter events, 0.1 us)
Async XLA Ops:
  0.0 18.4 %copy-start = (bf16[4096,22]{0,1:T(8,128)(2,1)S(1)}, bf16[4096,22]{0,1:T(8,128)(2,1)}, u32[]{:S(2)}) copy-start(bf16[4096,22]{0,1:T(8,128)(2,1)} %param.15) | copy-start | bytes 540676
  0.0 10.5 %copy-start.23 = (s32[8,8]{1,0:T(8,128)S(1)}, s32[8,8]{1,0:T(8,128)}, u32[]{:S(2)}) copy-start(s32[8,8]{1,0:T(8,128)} %param.19) | copy-start | bytes 772
  0.0 10.5 %copy-start.22 = (f32[1024,8]{0,1:T(8,128)S(1)}, f32[1024,8]{0,1:T(8,128)}, u32[]{:S(2)}) copy-start(f32[1024,8]{0,1:T(8,128)} %param.18) | copy-start | bytes 98308
  0.6 17.8 %copy-start.24 = (s32[8]{0:T(128)S(1)}, s32[8]{0:T(128)}, u32[]{:S(2)}) copy-start(s32[8]{0:T(128)} %param.16) | copy-start | bytes 100
  0.6 21.2 %copy-start.10 = (f32[2]{0:T(128)S(1)}, f32[2]{0:T(128)}, u32[]{:S(2)}) copy-start(f32[2]{0:T(128)} %own_lengths.1) | copy-start | bytes 28
  4.5 21.4 %collective-permute-start.2 = (bf16[71,16,128]{2,1,0:T(8,128)(2,1)}, bf16[71,16,128]{2,1,0:T(8,128)(2,1)S(1)}, u32[]{:S(2)}, u32[]{:S(2)}) collective-permute-start(bf16[71,16,128]{2,1,0:T(8,128)(2,1)} %get-tuple-element.31), channel_id=1, source_target_pairs={{0,3},{1,0},{2,1},{3,2},{4,7},{5,4},{6,5},{7,6},{8,11},{9,8},{10,9... | collective-permute-start | bytes 872456 | tf_op jit(solution)/shard_map/ppermute | solution.py:234
  9.5 25.0 %collective-permute-start.1 = (bf16[71,16,128]{2,1,0:T(8,128)(2,1)}, bf16[71,16,128]{2,1,0:T(8,128)(2,1)S(1)}, u32[]{:S(2)}, u32[]{:S(2)}) collective-permute-start(bf16[71,16,128]{2,1,0:T(8,128)(2,1)} %get-tuple-element.31), channel_id=1, source_target_pairs={{0,2},{1,3},{2,0},{3,1},{4,6},{5,7},{6,4},{7,5},{8,10},{9,11},{10,... | collective-permute-start | bytes 872456 | tf_op jit(solution)/shard_map/ppermute | solution.py:234
  9.5 25.0 %collective-permute-start = (bf16[71,16,128]{2,1,0:T(8,128)(2,1)}, bf16[71,16,128]{2,1,0:T(8,128)(2,1)S(1)}, u32[]{:S(2)}, u32[]{:S(2)}) collective-permute-start(bf16[71,16,128]{2,1,0:T(8,128)(2,1)} %get-tuple-element.31), channel_id=1, source_target_pairs={{0,1},{1,2},{2,3},{3,0},{4,5},{5,6},{6,7},{7,4},{8,9},{9,10},{10,1... | collective-permute-start | bytes 872456 | tf_op jit(solution)/shard_map/ppermute | solution.py:234
  12.6 60.9 %copy-start.11 = (f32[2]{0:T(128)S(1)}, f32[2]{0:T(128)}, u32[]{:S(2)}) copy-start(f32[2]{0:T(128)} %own_lengths.1) | copy-start | bytes 28
  25.8 8.7 %copy-start.7 = (bf16[71,16,128]{2,1,0:T(8,128)(2,1)}, bf16[71,16,128]{2,1,0:T(8,128)(2,1)S(1)}, u32[]{:S(2)}) copy-start(bf16[71,16,128]{2,1,0:T(8,128)(2,1)S(1)} %collective-permute-done.2.refs_2_) | copy-start | bytes 872452
  34.5 0.7 copy-start.8
  34.5 0.8 copy-start.9
  37.4 13.1 %collective-permute-start.4 = (bf16[105,16,128]{2,1,0:T(8,128)(2,1)}, bf16[105,16,128]{2,1,0:T(8,128)(2,1)S(1)}, u32[]{:S(2)}, u32[]{:S(2)}) collective-permute-start(bf16[105,16,128]{2,1,0:T(8,128)(2,1)} %get-tuple-element.38.refs_1_), channel_id=1, source_target_pairs={{0,16},{4,20},{8,24},{12,28},{16,0},{20,4},{24,8},{28,12},{1,17},{... | collective-permute-start | bytes 1290248 | tf_op jit(solution)/shard_map/ppermute | solution.py:246
  39.0 13.1 %collective-permute-start.3 = (bf16[105,16,128]{2,1,0:T(8,128)(2,1)}, bf16[105,16,128]{2,1,0:T(8,128)(2,1)S(1)}, u32[]{:S(2)}, u32[]{:S(2)}) collective-permute-start(bf16[105,16,128]{2,1,0:T(8,128)(2,1)} %get-tuple-element.38.refs_1_), channel_id=1, source_target_pairs={{0,8},{4,12},{8,0},{12,4},{16,24},{20,28},{24,16},{28,20},{1,9},{5... | collective-permute-start | bytes 1290248 | tf_op jit(solution)/shard_map/ppermute | solution.py:246
  40.5 18.4 %collective-permute-start.6 = (bf16[105,16,128]{2,1,0:T(8,128)(2,1)}, bf16[105,16,128]{2,1,0:T(8,128)(2,1)S(1)}, u32[]{:S(2)}, u32[]{:S(2)}) collective-permute-start(bf16[105,16,128]{2,1,0:T(8,128)(2,1)} %get-tuple-element.39.refs_2_), channel_id=1, source_target_pairs={{0,8},{4,12},{8,0},{12,4},{16,24},{20,28},{24,16},{28,20},{1,9},{5... | collective-permute-start | bytes 1290248 | tf_op jit(solution)/shard_map/ppermute | solution.py:246
  41.1 17.9 %collective-permute-start.5 = (bf16[105,16,128]{2,1,0:T(8,128)(2,1)}, bf16[105,16,128]{2,1,0:T(8,128)(2,1)S(1)}, u32[]{:S(2)}, u32[]{:S(2)}) collective-permute-start(bf16[105,16,128]{2,1,0:T(8,128)(2,1)} %get-tuple-element.39.refs_2_), channel_id=1, source_target_pairs={{0,16},{4,20},{8,24},{12,28},{16,0},{20,4},{24,8},{28,12},{1,17},{... | collective-permute-start | bytes 1290248 | tf_op jit(solution)/shard_map/ppermute | solution.py:246
  42.2 20.3 %collective-permute-start.9 = (bf16[105,16,128]{2,1,0:T(8,128)(2,1)}, bf16[105,16,128]{2,1,0:T(8,128)(2,1)S(1)}, u32[]{:S(2)}, u32[]{:S(2)}) collective-permute-start(bf16[105,16,128]{2,1,0:T(8,128)(2,1)} %get-tuple-element.38.refs_1_), channel_id=1, source_target_pairs={{0,4},{4,0},{8,12},{12,8},{16,20},{20,16},{24,28},{28,24},{1,5},{5... | collective-permute-start | bytes 1290248 | tf_op jit(solution)/shard_map/ppermute | solution.py:246
  50.6 8.4 %copy-start.3 = (bf16[105,16,128]{2,1,0:T(8,128)(2,1)}, bf16[105,16,128]{2,1,0:T(8,128)(2,1)S(1)}, u32[]{:S(2)}) copy-start(bf16[105,16,128]{2,1,0:T(8,128)(2,1)S(1)} %collective-permute-done.4.refs_1_) | copy-start | bytes 1290244
  50.6 12.0 %collective-permute-start.10 = (bf16[105,16,128]{2,1,0:T(8,128)(2,1)}, bf16[105,16,128]{2,1,0:T(8,128)(2,1)S(1)}, u32[]{:S(2)}, u32[]{:S(2)}) collective-permute-start(bf16[105,16,128]{2,1,0:T(8,128)(2,1)} %get-tuple-element.39.refs_2_), channel_id=1, source_target_pairs={{0,4},{4,0},{8,12},{12,8},{16,20},{20,16},{24,28},{28,24},{1,5},{5... | collective-permute-start | bytes 1290248 | tf_op jit(solution)/shard_map/ppermute | solution.py:246
  52.1 6.9 %copy-start.4 = (bf16[105,16,128]{2,1,0:T(8,128)(2,1)}, bf16[105,16,128]{2,1,0:T(8,128)(2,1)S(1)}, u32[]{:S(2)}) copy-start(bf16[105,16,128]{2,1,0:T(8,128)(2,1)S(1)} %collective-permute-done.3.refs_0_) | copy-start | bytes 1290244
  58.9 0.7 copy-start.5
  59.0 0.9 copy-start.6
  60.5 2.5 %collective-permute-start.12 = (bf16[105,16,128]{2,1,0:T(8,128)(2,1)}, bf16[105,16,128]{2,1,0:T(8,128)(2,1)S(1)}, u32[]{:S(2)}, u32[]{:S(2)}) collective-permute-start(bf16[105,16,128]{2,1,0:T(8,128)(2,1)} %get-tuple-element.43.refs_4_), channel_id=1, source_target_pairs={{0,4},{4,0},{8,12},{12,8},{16,20},{20,16},{24,28},{28,24},{1,5},{5... | collective-permute-start | bytes 1290248 | tf_op jit(solution)/shard_map/ppermute | solution.py:246
  60.5 12.5 %collective-permute-start.7 = (bf16[105,16,128]{2,1,0:T(8,128)(2,1)}, bf16[105,16,128]{2,1,0:T(8,128)(2,1)S(1)}, u32[]{:S(2)}, u32[]{:S(2)}) collective-permute-start(bf16[105,16,128]{2,1,0:T(8,128)(2,1)} %get-tuple-element.42.refs_3_), channel_id=1, source_target_pairs={{0,16},{4,20},{8,24},{12,28},{16,0},{20,4},{24,8},{28,12},{1,17},{... | collective-permute-start | bytes 1290248 | tf_op jit(solution)/shard_map/ppermute | solution.py:246
  61.0 12.2 %collective-permute-start.8 = (bf16[105,16,128]{2,1,0:T(8,128)(2,1)}, bf16[105,16,128]{2,1,0:T(8,128)(2,1)S(1)}, u32[]{:S(2)}, u32[]{:S(2)}) collective-permute-start(bf16[105,16,128]{2,1,0:T(8,128)(2,1)} %get-tuple-element.44.refs_6_), channel_id=1, source_target_pairs={{0,8},{4,12},{8,0},{12,4},{16,24},{20,28},{24,16},{28,20},{1,9},{5... | collective-permute-start | bytes 1290248 | tf_op jit(solution)/shard_map/ppermute | solution.py:246
  62.5 13.8 %copy-start.12 = (bf16[105,16,128]{2,1,0:T(8,128)(2,1)}, bf16[105,16,128]{2,1,0:T(8,128)(2,1)S(1)}, u32[]{:S(2)}) copy-start(bf16[105,16,128]{2,1,0:T(8,128)(2,1)S(1)} %collective-permute-done.9.refs_9_) | copy-start | bytes 1290244
  62.5 11.2 %collective-permute-start.11 = (bf16[105,16,128]{2,1,0:T(8,128)(2,1)}, bf16[105,16,128]{2,1,0:T(8,128)(2,1)S(1)}, u32[]{:S(2)}, u32[]{:S(2)}) collective-permute-start(bf16[105,16,128]{2,1,0:T(8,128)(2,1)} %get-tuple-element.42.refs_3_), channel_id=1, source_target_pairs={{0,4},{4,0},{8,12},{12,8},{16,20},{20,16},{24,28},{28,24},{1,5},{5... | collective-permute-start | bytes 1290248 | tf_op jit(solution)/shard_map/ppermute | solution.py:246
  62.5 13.8 %copy-start.13 = (bf16[105,16,128]{2,1,0:T(8,128)(2,1)}, bf16[105,16,128]{2,1,0:T(8,128)(2,1)S(1)}, u32[]{:S(2)}) copy-start(bf16[105,16,128]{2,1,0:T(8,128)(2,1)S(1)} %collective-permute-done.10.refs_10_) | copy-start | bytes 1290244
  62.6 11.1 %collective-permute-start.14 = (bf16[105,16,128]{2,1,0:T(8,128)(2,1)}, bf16[105,16,128]{2,1,0:T(8,128)(2,1)S(1)}, u32[]{:S(2)}, u32[]{:S(2)}) collective-permute-start(bf16[105,16,128]{2,1,0:T(8,128)(2,1)} %get-tuple-element.44.refs_6_), channel_id=1, source_target_pairs={{0,4},{4,0},{8,12},{12,8},{16,20},{20,16},{24,28},{28,24},{1,5},{5... | collective-permute-start | bytes 1290248 | tf_op jit(solution)/shard_map/ppermute | solution.py:246
  63.0 13.3 %copy-start.14 = (bf16[105,16,128]{2,1,0:T(8,128)(2,1)}, bf16[105,16,128]{2,1,0:T(8,128)(2,1)S(1)}, u32[]{:S(2)}) copy-start(bf16[105,16,128]{2,1,0:T(8,128)(2,1)S(1)} %collective-permute-done.12.refs_12_) | copy-start | bytes 1290244
  63.0 10.6 %collective-permute-start.15 = (bf16[105,16,128]{2,1,0:T(8,128)(2,1)}, bf16[105,16,128]{2,1,0:T(8,128)(2,1)S(1)}, u32[]{:S(2)}, u32[]{:S(2)}) collective-permute-start(bf16[105,16,128]{2,1,0:T(8,128)(2,1)} %get-tuple-element.45.refs_7_), channel_id=1, source_target_pairs={{0,4},{4,0},{8,12},{12,8},{16,20},{20,16},{24,28},{28,24},{1,5},{5... | collective-permute-start | bytes 1290248 | tf_op jit(solution)/shard_map/ppermute | solution.py:246
  73.1 3.3 %copy-start.15 = (bf16[105,16,128]{2,1,0:T(8,128)(2,1)}, bf16[105,16,128]{2,1,0:T(8,128)(2,1)S(1)}, u32[]{:S(2)}) copy-start(bf16[105,16,128]{2,1,0:T(8,128)(2,1)S(1)} %collective-permute-done.7.refs_5_) | copy-start | bytes 1290244
  73.1 1.8 %collective-permute-start.13 = (bf16[105,16,128]{2,1,0:T(8,128)(2,1)S(1)}, bf16[105,16,128]{2,1,0:T(8,128)(2,1)S(1)}, u32[]{:S(2)}, u32[]{:S(2)}) collective-permute-start(bf16[105,16,128]{2,1,0:T(8,128)(2,1)S(1)} %collective-permute-done.7.refs_5_), channel_id=1, source_target_pairs={{0,4},{4,0},{8,12},{12,8},{16,20},{20,16},{24,28},{28,24},{1,5},{5... | collective-permute-start | bytes 1290248 | tf_op jit(solution)/shard_map/ppermute | solution.py:246
  73.3 3.1 %copy-start.16 = (bf16[105,16,128]{2,1,0:T(8,128)(2,1)}, bf16[105,16,128]{2,1,0:T(8,128)(2,1)S(1)}, u32[]{:S(2)}) copy-start(bf16[105,16,128]{2,1,0:T(8,128)(2,1)S(1)} %collective-permute-done.8.refs_8_) | copy-start | bytes 1290244
  73.3 2.2 %collective-permute-start.16 = (bf16[105,16,128]{2,1,0:T(8,128)(2,1)S(1)}, bf16[105,16,128]{2,1,0:T(8,128)(2,1)S(1)}, u32[]{:S(2)}, u32[]{:S(2)}) collective-permute-start(bf16[105,16,128]{2,1,0:T(8,128)(2,1)S(1)} %collective-permute-done.8.refs_8_), channel_id=1, source_target_pairs={{0,4},{4,0},{8,12},{12,8},{16,20},{20,16},{24,28},{28,24},{1,5},{5... | collective-permute-start | bytes 1290248 | tf_op jit(solution)/shard_map/ppermute | solution.py:246
  73.7 2.7 %copy-start.19 = (bf16[105,16,128]{2,1,0:T(8,128)(2,1)}, bf16[105,16,128]{2,1,0:T(8,128)(2,1)S(1)}, u32[]{:S(2)}) copy-start(bf16[105,16,128]{2,1,0:T(8,128)(2,1)S(1)} %collective-permute-done.15.refs_15_) | copy-start | bytes 1290244
  73.7 2.7 %copy-start.17 = (bf16[105,16,128]{2,1,0:T(8,128)(2,1)}, bf16[105,16,128]{2,1,0:T(8,128)(2,1)S(1)}, u32[]{:S(2)}) copy-start(bf16[105,16,128]{2,1,0:T(8,128)(2,1)S(1)} %collective-permute-done.11.refs_11_) | copy-start | bytes 1290244
  73.7 2.7 %copy-start.18 = (bf16[105,16,128]{2,1,0:T(8,128)(2,1)}, bf16[105,16,128]{2,1,0:T(8,128)(2,1)S(1)}, u32[]{:S(2)}) copy-start(bf16[105,16,128]{2,1,0:T(8,128)(2,1)S(1)} %collective-permute-done.14.refs_14_) | copy-start | bytes 1290244
  74.8 0.8 copy-start.20
  75.6 0.8 copy-start.21
  97.3 44.9 %all-to-all-start = ((bf16[4,1,512,256]{3,2,1,0:T(8,128)(2,1)}), bf16[4,1,512,256]{3,2,1,0:T(8,128)(2,1)S(1)}, u32[]{:S(2)}, u32[]{:S(2)}) async-start(bf16[4,1,512,256]{3,2,1,0:T(8,128)(2,1)} %get-tuple-element.55), calls=%async_computation | async-start | bytes 2097152 | tf_op jit(solution)/shard_map/all_to_all | solution.py:749
  101.6 40.7 %copy-start.2 = (bf16[8,128,128]{2,1,0:T(8,128)(2,1)S(1)}, bf16[8,128,128]{2,1,0:T(8,128)(2,1)}, u32[]{:S(2)}) copy-start(bf16[8,128,128]{2,1,0:T(8,128)(2,1)} %get-tuple-element.54.weight_ref) | copy-start | bytes 786436
  132.9 4.0 %collective-permute-start.17 = (f32[4,8,128]{2,1,0:T(8,128)}, f32[4,8,128]{2,1,0:T(8,128)S(1)}, u32[]{:S(2)}, u32[]{:S(2)}) collective-permute-start(f32[4,8,128]{2,1,0:T(8,128)} %get-tuple-element.53), channel_id=1, source_target_pairs={{0,1},{1,0},{2,3},{3,2},{4,5},{5,4},{6,7},{7,6},{8,9},{9,8},{10,11... | collective-permute-start | bytes 49160 | tf_op jit(solution)/shard_map/ppermute | solution.py:687
  137.6 4.6 %collective-permute-start.18 = (f32[4,8,128]{2,1,0:T(8,128)S(1)}, f32[4,8,128]{2,1,0:T(8,128)S(1)}, u32[]{:S(2)}, u32[]{:S(2)}) collective-permute-start(f32[4,8,128]{2,1,0:T(8,128)S(1)} %add.50), channel_id=1, source_target_pairs={{0,2},{1,3},{2,0},{3,1},{4,6},{5,7},{6,4},{7,5},{8,10},{9,11},{10,... | collective-permute-start | bytes 49160 | tf_op jit(solution)/shard_map/ppermute | solution.py:687
  142.3 1.6 %copy-start.1 = (f32[4,512,256]{2,1,0:T(8,128)S(1)}, f32[4,512,256]{2,1,0:T(8,128)}, u32[]{:S(2)}) copy-start(f32[4,512,256]{2,1,0:T(8,128)} %get-tuple-element.56.image_ref) | copy-start | bytes 6291460

commit v10 on v9

--- a/solution.py
+++ b/solution.py
@@ -178,16 +178,34 @@
     return own, piece, token
 
 
-def split_kernel(half, sent, parts_count, where, own_lengths, *refs):
-    parts, (low_ref, high_ref, length_ref, inverse_ref) = refs[:parts_count], refs[-4:]
-    wave, waves = where[0], parts_count + 1
+def split_kernel(half, count, *refs):
+    parts, (low_ref, high_ref) = refs[:count], refs[-2:]
+    for s, part in enumerate(parts):
+        low_ref[s * half : (s + 1) * half] = part[:half]
+        high_ref[s * half : (s + 1) * half] = part[half : 2 * half]
+
+
+def split_parts(parts, half, tokens):
+    slabs = jax.ShapeDtypeStruct((len(parts) * half, ROWS, LANES), parts[0].dtype)
+    return pl.pallas_call(
+        functools.partial(split_kernel, half, len(parts)),
+        out_shape=(slabs, slabs),
+        in_specs=[VMEM] * (len(parts) + len(tokens)),
+        out_specs=(VMEM,) * 2,
+        compiler_params=pltpu.CompilerParams(vmem_limit_bytes=VMEM_BYTES),
+    )(*parts, *tokens)
+
+
+def lengths_kernel(sent, where, own_lengths, *refs):
+    parts, (length_ref, inverse_ref) = refs[:-2], refs[-2:]
+    wave, waves = where[0], len(parts) + 1
     kept = own_lengths.shape[0] - sent
     for s in range(waves):
         for i in range(kept):
             if s == 0:
                 value = jnp.full((8, LANES), own_lengths[sent + i], jnp.float32)
             else:
-                slab = parts[s - 1][2 * half].astype(jnp.float32)
+                slab = parts[s - 1][0].astype(jnp.float32)
                 line = 3 * (sent + i)
                 value = (slab[line : line + 1] + slab[line + 1 : line + 2]) + slab[
                     line + 2 : line + 3
@@ -196,26 +214,22 @@
             place = lax.rem(wave + (waves - s), waves) * kept + i
             length_ref[place] = value
             inverse_ref[place] = (1.0 / value)[0, 0]
-    for s, part in enumerate(parts):
-        low_ref[s * half : (s + 1) * half] = part[:half]
-        high_ref[s * half : (s + 1) * half] = part[half : 2 * half]
-
-
-def split_parts(parts, where, wave_lengths, half, sent, tokens):
+
+
+def kept_lengths(parts, where, wave_lengths, half, sent):
     count = (len(parts) + 1) * (wave_lengths.shape[0] - sent)
-    slabs = jax.ShapeDtypeStruct((len(parts) * half, ROWS, LANES), parts[0].dtype)
+    last = pl.BlockSpec((1, ROWS, LANES), lambda i: (2 * half, 0, 0))
     return pl.pallas_call(
-        functools.partial(split_kernel, half, sent, len(parts)),
+        functools.partial(lengths_kernel, sent),
+        grid=(1,),
         out_shape=(
-            slabs,
-            slabs,
             jax.ShapeDtypeStruct((count, 8, LANES), jnp.float32),
             jax.ShapeDtypeStruct((count,), jnp.float32),
         ),
-        in_specs=[SMEM, SMEM] + [VMEM] * (len(parts) + len(tokens)),
-        out_specs=(VMEM,) * 3 + (SMEM,),
+        in_specs=[SMEM, SMEM] + [last] * len(parts),
+        out_specs=(VMEM, SMEM),
         compiler_params=pltpu.CompilerParams(vmem_limit_bytes=VMEM_BYTES),
-    )(where, wave_lengths, *parts, *tokens)
+    )(where, wave_lengths, *parts)
 
 
 def after(arrays, tokens):
@@ -246,16 +260,25 @@
     return lax.ppermute(x, ("groups", "field"), pairs)
 
 
-def gather_halves(halves, token):
+def gather_halves(halves, half, shifts, tokens):
     routes = ((2, 4), (4, 2))
     near = [swap(mine, mask) for mine, route in zip(halves, routes) for mask in route]
-    near = after(near, [token])
-    got = [(h, mine, 0) for h, mine in enumerate(halves)]
+    near = after(near + list(halves), tokens)
+    got = [(h, mine, 0) for h, mine in enumerate(near[4:])]
     for h, (one, two) in enumerate(routes):
         got.append((h, near[2 * h], one))
         got.append((h, near[2 * h + 1], two))
         got.append((h, swap(near[2 * h], two), one | two))
-    return got + [(h, swap(array, 1), mask | 1) for h, array, mask in got]
+    got = got + [(h, swap(array, 1), mask | 1) for h, array, mask in got]
+    return [((shifts, h * half, half, half, mask), array) for h, array, mask in got]
+
+
+def gather_direct(pieces, half, shifts, tokens):
+    masks = (6, 2, 4)
+    near = after([swap(pieces, mask) for mask in masks], tokens)
+    got = [(0, pieces)] + list(zip(masks, near))
+    got = got + [(mask | 1, swap(array, 1)) for mask, array in got]
+    return [((shifts, 0, 2 * half, 2 * half + 1, mask), array) for mask, array in got]
 
 
 def spread_kernel(*refs):
@@ -295,13 +318,13 @@
     wave, share = where[0], where[1]
     copies = [pltpu.make_async_copy(parts[0], basis.at[pl.ds(wave * slabs, slabs)], sems.at[0])]
     n = 1
-    for (h, mask), part in zip(keys, parts[1:]):
-        for s in range(1, waves):
+    for (shifts, offset, length, stride, mask), part in zip(keys, parts[1:]):
+        for i, s in enumerate(shifts):
             source = lax.rem(wave + (waves - s), waves)
-            start = source * slabs + (share ^ mask) * (2 * half) + h * half
+            start = source * slabs + (share ^ mask) * (2 * half) + offset
             copies.append(
                 pltpu.make_async_copy(
-                    part.at[pl.ds((s - 1) * half, half)], basis.at[pl.ds(start, half)], sems.at[n]
+                    part.at[pl.ds(i * stride, length)], basis.at[pl.ds(start, length)], sems.at[n]
                 )
             )
             n += 1
@@ -504,8 +527,8 @@
 
 def whole_fields(own, got, spread, place, where, inverse, tables, sizes):
     positions, modes, waves, half, slabs = sizes
-    keys = tuple((h, mask) for h, _, mask in got)
-    arrays = [array for _, array, _ in got]
+    keys = tuple(key for key, _ in got)
+    arrays = [array for _, array in got]
     lengths = inverse.shape[0]
     share = positions * PIX // waves
     any_memory = pl.BlockSpec(memory_space=pl.ANY)
@@ -529,7 +552,7 @@
         scratch_shapes=[
             pltpu.VMEM(path_shape(positions), jnp.float32),
             pltpu.VMEM((waves * slabs, ROWS, LANES), jnp.bfloat16),
-            pltpu.SemaphoreType.DMA((1 + len(keys) * (waves - 1),)),
+            pltpu.SemaphoreType.DMA((1 + sum(len(key[0]) for key in keys),)),
             pltpu.SemaphoreType.DMA((len(CHUNKS),)),
         ]
         + transform_scratch(positions, PIX),
@@ -730,11 +753,15 @@
     )
     own_row, own_column, own_token = tables(own_length, 0, PIX)
 
-    low, high, every, inverse = split_parts(
-        parts, where, wave_lengths, half, sent_lengths, (spread_token, own_token, packed)
-    )
+    far = tuple(s for s in range(1, waves) if min(s, waves - s) > waves // 4)
+    near = tuple(s for s in range(1, waves) if s not in far)
+    halves = split_parts([parts[s - 1] for s in near], half, [packed])
+    got = gather_halves(halves, half, near, [own_token, spread_token])
+    every, inverse = kept_lengths(parts, where, wave_lengths, half, sent_lengths)
     all_row, all_column, all_token = tables(every, mine * rows, rows)
-    got = gather_halves((low, high), all_token)
+    pieces = [parts[s - 1] for s in far]
+    pieces = pieces[0] if len(pieces) == 1 else jnp.concatenate(pieces)
+    got = got + gather_direct(pieces, half, far, [all_token])
 
     spectra, path, opening = whole_fields(
         own,

time: 147 us -> 140 us (0.952)
  waiting for transfers between devices: 35.8 us -> 20.3 us
  starting transfers between devices: 22.3 us -> 29.4 us
  Pallas kernels: 77.7 us -> 79.5 us
    ppermute x14 -> x21, waiting for transfers between devices: 23.5 us -> 5.91 us  [swap(): return lax.ppermute(x, ('groups', 'field'), pairs)]
    ppermute x14 -> x21, starting transfers between devices: 6.99 us -> 13.9 us  [swap(): return lax.ppermute(x, ('groups', 'field'), pairs)]
    ppermute x3, waiting for transfers between devices: 8.66 us -> 10.3 us  [along_wave(): lax.ppermute(piece, 'wave', [(i, (i + s) % waves) for i in range(waves)])]
    pallas_call x1 -> x2, Pallas kernels: 2.1 us -> 3.33 us  [the longest x1 1.9 us: split_parts(): pl.pallas_call(functools.partial(split_kernel, half, len(parts)), out_sha...]
    unnamed x52 -> x62, local copies, waits for them, and re-layouts: 4.54 us -> 4 us
  transfers between devices with their start and end apart: 20 -> 27, of which waited for: 10 -> 11; matrix products, arithmetic and copies ran while one was open for 4% -> 4% of each run, Pallas kernels for 33% -> 37%
where the time goes in v10:
time: 140 us; the launch traced here: 139 us
  Pallas kernels  79.5 us (57%)
  starting transfers between devices  29.4 us (21%)
  waiting for transfers between devices  20.3 us (14%)
  local copies, waits for them, and re-layouts  4.63 us (3%)
  other arithmetic  3.34 us (2%)
  matrix products  1.88 us (1%)
    pallas_call x1, Pallas kernels, row_fields(): pl.pallas_call(functools.partial(rows_kernel, positions, rows), grid=(len...  31.3 us
    pallas_call x1, Pallas kernels, whole_fields(): pl.pallas_call(functools.partial(whole_kernel, (positions, modes, waves,...  20.8 us
    ppermute x21, starting transfers between devices, swap(): return lax.ppermute(x, ('groups', 'field'), pairs)  13.9 us
    ppermute x3, waiting for transfers between devices, along_wave(): lax.ppermute(piece, 'wave', [(i, (i + s) % waves) for i in range(waves)])  10.3 us
    pallas_call x2, Pallas kernels, tables(): pl.pallas_call(table_kernel, grid=(lengths,), out_shape=(jax.ShapeDtypeSt...  8.47 us
    ppermute x3, starting transfers between devices, along_wave(): lax.ppermute(piece, 'wave', [(i, (i + s) % waves) for i in range(waves)])  6.06 us
    ppermute x21, waiting for transfers between devices, swap(): return lax.ppermute(x, ('groups', 'field'), pairs)  5.91 us
    pallas_call x1, Pallas kernels, pack_rows(): pl.pallas_call(functools.partial(own_kernel, count), out_shape=(jax.Shape...  5.77 us
  transfers between devices with their start and end apart: 27, of which 11 were waited for; matrix products, arithmetic and copies ran while one was open for 4% of the time, Pallas kernels for 37%

profile of v10, /device:TPU:0, one launch (start us, length us, event | category | flops | bytes accessed | tf_op | source)
XLA Modules:
  0.0 139.4 jit_solution(10971419948290715527)
XLA Ops:
  0.0 0.6 pad_add_fusion.where
  0.7 3.9 %shard_map.136 = (bf16[71,16,128]{2,1,0:T(8,128)(2,1)}, f32[8,128]{1,0:T(8,128)}) custom-call(s32[2]{0:T(128)} %pad_add_fusion.where, s32[100,3]{1,0:T(8,128)} %constant.57.clone.table, f32[2]{0:T(128)} %own_lengths.1, bf16[22,128,512]{2,1,0:T(8,128)(2,1)} %basis.3), custom_call_target="tpu_custom_call" | custom-call | tf_op jit(solution)/shard_map/pallas_call | solution.py:158
  4.5 5.0 %collective-permute-start.2 = (bf16[71,16,128]{2,1,0:T(8,128)(2,1)}, bf16[71,16,128]{2,1,0:T(8,128)(2,1)S(1)}, u32[]{:S(2)}, u32[]{:S(2)}) collective-permute-start(bf16[71,16,128]{2,1,0:T(8,128)(2,1)} %get-tuple-element.36), channel_id=1, source_target_pairs={{0,3},{1,0},{2,1},{3,2},{4,7},{5,4},{6,5},{7,6},{8,11},{9,8},{10,9... | collective-permute-start | bytes 872456 | tf_op jit(solution)/shard_map/ppermute | solution.py:248
  9.6 1.0 collective-permute-start.1
  10.6 5.8 %shard_map.138 = (bf16[560,16,128]{2,1,0:T(8,128)(2,1)}, f32[8,128]{1,0:T(8,128)}) custom-call(s32[2]{0:T(128)} %pad_add_fusion.where, s32[100,3]{1,0:T(8,128)} %constant.57.clone.table, bf16[22,128,512]{2,1,0:T(8,128)(2,1)} %basis.3, f32[8,128]{1,0:T(8,128)} %get-tuple-element.38._), custom_call_target="tpu_custom_call" | custom-call | tf_op jit(solution)/shard_map/pallas_call | solution.py:168
  16.4 0.0 copy-start.14
  16.4 1.1 fusion.6
  17.4 6.9 %collective-permute-done.refs_0_ = bf16[71,16,128]{2,1,0:T(8,128)(2,1)S(1)} collective-permute-done((bf16[71,16,128]{2,1,0:T(8,128)(2,1)}, bf16[71,16,128]{2,1,0:T(8,128)(2,1)S(1)}, u32[]{:S(2)}, u32[]{:S(2)}) %collective-permute-start) | collective-permute-done | bytes 290848 | tf_op jit(solution)/shard_map/ppermute | solution.py:248
  24.3 0.7 copy-done.4
  25.1 1.9 %shard_map.139 = (bf16[70,16,128]{2,1,0:T(8,128)(2,1)}, bf16[70,16,128]{2,1,0:T(8,128)(2,1)}) custom-call(bf16[71,16,128]{2,1,0:T(8,128)(2,1)} %copy-done.4, bf16[71,16,128]{2,1,0:T(8,128)(2,1)} %copy-done.3, f32[8,128]{1,0:T(8,128)} %get-tuple-element.40.refs_2_), custom_call_target="tpu_custom_call" | custom-call | tf_op jit(solution)/shard_map/pallas_call | solution.py:190
  27.0 1.5 %collective-permute-start.4 = (bf16[70,16,128]{2,1,0:T(8,128)(2,1)}, bf16[70,16,128]{2,1,0:T(8,128)(2,1)S(1)}, u32[]{:S(2)}, u32[]{:S(2)}) collective-permute-start(bf16[70,16,128]{2,1,0:T(8,128)(2,1)} %get-tuple-element.41.refs_4_), channel_id=1, source_target_pairs={{0,16},{4,20},{8,24},{12,28},{16,0},{20,4},{24,8},{28,12},{1,17},{... | collective-permute-start | bytes 860168 | tf_op jit(solution)/shard_map/ppermute | solution.py:260
  28.5 1.6 %collective-permute-start.3 = (bf16[70,16,128]{2,1,0:T(8,128)(2,1)}, bf16[70,16,128]{2,1,0:T(8,128)(2,1)S(1)}, u32[]{:S(2)}, u32[]{:S(2)}) collective-permute-start(bf16[70,16,128]{2,1,0:T(8,128)(2,1)} %get-tuple-element.41.refs_4_), channel_id=1, source_target_pairs={{0,8},{4,12},{8,0},{12,4},{16,24},{20,28},{24,16},{28,20},{1,9},{5... | collective-permute-start | bytes 860168 | tf_op jit(solution)/shard_map/ppermute | solution.py:260
  30.1 0.5 collective-permute-start.6
  30.6 0.5 collective-permute-start.5
  31.1 3.4 %collective-permute-done.1.refs_1_.refs_17_ = bf16[71,16,128]{2,1,0:T(8,128)(2,1)S(1)} collective-permute-done((bf16[71,16,128]{2,1,0:T(8,128)(2,1)}, bf16[71,16,128]{2,1,0:T(8,128)(2,1)S(1)}, u32[]{:S(2)}, u32[]{:S(2)}) %collective-permute-start.1) | collective-permute-done | bytes 290848 | tf_op jit(solution)/shard_map/ppermute | solution.py:248
  34.5 2.2 %collective-permute-done.4.refs_1_ = bf16[70,16,128]{2,1,0:T(8,128)(2,1)S(1)} collective-permute-done((bf16[70,16,128]{2,1,0:T(8,128)(2,1)}, bf16[70,16,128]{2,1,0:T(8,128)(2,1)S(1)}, u32[]{:S(2)}, u32[]{:S(2)}) %collective-permute-start.4) | collective-permute-done | bytes 286752 | tf_op jit(solution)/shard_map/ppermute | solution.py:260
  36.8 1.5 %collective-permute-start.19 = (bf16[71,16,128]{2,1,0:T(8,128)(2,1)S(1)}, bf16[71,16,128]{2,1,0:T(8,128)(2,1)S(1)}, u32[]{:S(2)}, u32[]{:S(2)}) collective-permute-start(bf16[71,16,128]{2,1,0:T(8,128)(2,1)S(1)} %collective-permute-done.1.refs_1_.refs_17_), channel_id=1, source_target_pairs={{0,16},{4,20},{8,24},{12,28},{16,0},{20,4},{24,8},{28,12},{1,17},{... | collective-permute-start | bytes 872456 | tf_op jit(solution)/shard_map/ppermute | solution.py:260
  38.3 0.7 add_convert_fusion.u_ref
  38.9 0.1 copy.36
  39.1 0.1 copy.37
  39.2 0.8 fusion.refs_0_
  40.0 1.5 %collective-permute-start.18 = (bf16[71,16,128]{2,1,0:T(8,128)(2,1)S(1)}, bf16[71,16,128]{2,1,0:T(8,128)(2,1)S(1)}, u32[]{:S(2)}, u32[]{:S(2)}) collective-permute-start(bf16[71,16,128]{2,1,0:T(8,128)(2,1)S(1)} %collective-permute-done.1.refs_1_.refs_17_), channel_id=1, source_target_pairs={{0,8},{4,12},{8,0},{12,4},{16,24},{20,28},{24,16},{28,20},{1,9},{5... | collective-permute-start | bytes 872456 | tf_op jit(solution)/shard_map/ppermute | solution.py:260
  41.5 0.1 collective-permute-done.6.refs_3_
  41.6 1.4 %collective-permute-start.17 = (bf16[71,16,128]{2,1,0:T(8,128)(2,1)S(1)}, bf16[71,16,128]{2,1,0:T(8,128)(2,1)S(1)}, u32[]{:S(2)}, u32[]{:S(2)}) collective-permute-start(bf16[71,16,128]{2,1,0:T(8,128)(2,1)S(1)} %collective-permute-done.1.refs_1_.refs_17_), channel_id=1, source_target_pairs={{0,24},{4,28},{8,16},{12,20},{16,8},{20,12},{24,0},{28,4},{1,25},{... | collective-permute-start | bytes 872456 | tf_op jit(solution)/shard_map/ppermute | solution.py:260
  43.0 0.7 pad_maximum_fusion.refs_1_
  43.7 2.0 %shard_map.141 = (bf16[1,128,352]{2,1,0:T(8,128)(2,1)}, bf16[8,128,128]{2,1,0:T(8,128)(2,1)}, f32[8,128]{1,0:T(8,128)}) custom-call(bf16[1,8,22]{2,1,0:T(8,128)(2,1)} %fusion.refs_0_, bf16[8,8,8]{2,1,0:T(8,128)(2,1)} %pad_maximum_fusion.refs_1_), custom_call_target="tpu_custom_call" | custom-call | tf_op jit(solution)/shard_map/pallas_call | solution.py:305
  45.7 0.6 broadcast_in_dim.7.length_ref
  46.3 3.4 %shard_map.140 = (bf16[1,4,512,256]{3,2,1,0:T(8,128)(2,1)}, bf16[1,1024,512]{2,1,0:T(8,128)(2,1)}, f32[8,128]{1,0:T(8,128)}) custom-call(f32[1,8,128]{2,1,0:T(8,128)} %broadcast_in_dim.7.length_ref, f32[512,1]{1,0:T(8,128)} %constant.58.clone.y_ref, f32[1,256]{1,0:T(1,128)} %constant.59.clone.v_ref, f32[256,1]{1,0:T(8,128)} %add_convert_fusion.u_ref, ...), custom_call_target="tpu_custom_call" | custom-call | flops 3932160 | bytes 1048576 | tf_op jit(solution)/shard_map/pallas_call | solution.py:674
  49.8 0.7 copy-done.12
  50.5 0.7 shard_map.142
  51.1 0.5 collective-permute-start.10
  51.7 0.1 collective-permute-start.12
  51.7 0.4 collective-permute-start.15
  52.2 1.4 collective-permute-done.17.refs_0_
  53.6 1.6 %collective-permute-start.7 = (bf16[70,16,128]{2,1,0:T(8,128)(2,1)}, bf16[70,16,128]{2,1,0:T(8,128)(2,1)S(1)}, u32[]{:S(2)}, u32[]{:S(2)}) collective-permute-start(bf16[70,16,128]{2,1,0:T(8,128)(2,1)} %get-tuple-element.47.refs_3_), channel_id=1, source_target_pairs={{0,16},{4,20},{8,24},{12,28},{16,0},{20,4},{24,8},{28,12},{1,17},{... | collective-permute-start | bytes 860168 | tf_op jit(solution)/shard_map/ppermute | solution.py:260
  55.2 0.2 collective-permute-start.14
  55.3 1.5 %collective-permute-start.8 = (bf16[70,16,128]{2,1,0:T(8,128)(2,1)}, bf16[70,16,128]{2,1,0:T(8,128)(2,1)}, u32[]{:S(2)}, u32[]{:S(2)}) collective-permute-start(bf16[70,16,128]{2,1,0:T(8,128)(2,1)} %get-tuple-element.49.refs_6_), channel_id=1, source_target_pairs={{0,8},{4,12},{8,0},{12,4},{16,24},{20,28},{24,16},{28,20},{1,9},{5... | collective-permute-start | bytes 860168 | tf_op jit(solution)/shard_map/ppermute | solution.py:260
  56.8 0.6 add_convert_fusion.1.u_ref
  57.5 1.4 %shard_map.137 = (f32[4,8,128]{2,1,0:T(8,128)}, f32[4]{0:T(128)}) custom-call(s32[2]{0:T(128)} %pad_add_fusion.where, f32[2]{0:T(128)} %own_lengths.1, bf16[71,16,128]{2,1,0:T(8,128)(2,1)} %copy-done.4, bf16[71,16,128]{2,1,0:T(8,128)(2,1)} %copy-done.5, bf16[71,16,128]{2,1,0:T(8,128)(2,1)} %copy-done.3), custom_call_target="tpu_custom_call" | custom-call | tf_op jit(solution)/shard_map/pallas_call | solution.py:222
  58.9 5.0 %shard_map.143 = (bf16[4,4,128,256]{3,2,1,0:T(8,128)(2,1)}, bf16[4,1024,512]{2,1,0:T(8,128)(2,1)}, f32[8,128]{1,0:T(8,128)}) custom-call(f32[4,8,128]{2,1,0:T(8,128)} %get-tuple-element.51.length_ref, f32[512,1]{1,0:T(8,128)} %constant.58.clone.y_ref, f32[1,256]{1,0:T(1,128)} %constant.59.clone.v_ref, f32[64,1]{1,0:T(8,128)} %add_convert_fusion.1.u_ref, ...), custom_call_target="tpu_custom_call" | custom-call | flops 15728640 | bytes 4194304 | tf_op jit(solution)/shard_map/pallas_call | solution.py:674
  64.0 0.7 shard_map.144
  64.7 0.1 collective-permute-start.21
  64.7 0.4 collective-permute-start.22
  65.2 0.1 collective-permute-start.23
  65.3 0.4 collective-permute-start.13
  65.7 0.1 collective-permute-start.16
  65.9 0.6 collective-permute-done.21.refs_22_
  66.4 0.4 collective-permute-done.22.refs_23_
  66.9 0.8 collective-permute-done.23.refs_24_
  67.7 0.4 collective-permute-done.16.refs_16_
  68.2 0.2 copy-done.18
  68.4 0.1 copy-done.25
  68.5 0.3 copy-done.26
  68.8 20.8 %shard_map.145 = (bf16[4,1,512,256]{3,2,1,0:T(8,128)(2,1)}, f32[96,128,128]{2,1,0:T(8,128)}, f32[96,16,128]{2,1,0:T(8,128)}) custom-call(f32[1]{0:T(128)S(6)} %div.11.inverse_ref, s32[96,4]{1,0:T(8,128)} %constant.61.clone.place, s32[2]{0:T(128)} %pad_add_fusion.where, bf16[560,16,128]{2,1,0:T(8,128)(2,1)} %get-tuple-element.39.refs_0_, ...), custom_call_target="tpu_custom_call" | custom-call | flops 7242450944 | bytes 8388608 | tf_op jit(solution)/shard_map/pallas_call | solution.py:535
  89.6 4.4 %all-to-all-start = ((bf16[4,1,512,256]{3,2,1,0:T(8,128)(2,1)}), bf16[4,1,512,256]{3,2,1,0:T(8,128)(2,1)S(1)}, u32[]{:S(2)}, u32[]{:S(2)}) async-start(bf16[4,1,512,256]{3,2,1,0:T(8,128)(2,1)} %get-tuple-element.65), calls=%async_computation | async-start | bytes 2097152 | tf_op jit(solution)/shard_map/all_to_all | solution.py:776
  94.0 31.3 %shard_map.146 = (f32[4,512,256]{2,1,0:T(8,128)}, f32[4,8,128]{2,1,0:T(8,128)}) custom-call(f32[4]{0:T(128)} %get-tuple-element.37.inverse_ref, f32[96,128,128]{2,1,0:T(8,128)} %get-tuple-element.59.path_in, f32[96,16,128]{2,1,0:T(8,128)} %get-tuple-element.60.opening, bf16[4,4,128,256]{3,2,1,0:T(8,128)(2,1)} %get-tuple-element.61.row_ref, ...), custom_call_target="tpu_custom_call" | custom-call | flops 9642450944 | bytes 8388608 | tf_op jit(solution)/shard_map/pallas_call | solution.py:571
  125.3 2.5 %collective-permute-start.24 = (f32[4,8,128]{2,1,0:T(8,128)}, f32[4,8,128]{2,1,0:T(8,128)S(1)}, u32[]{:S(2)}, u32[]{:S(2)}) collective-permute-start(f32[4,8,128]{2,1,0:T(8,128)} %get-tuple-element.63), channel_id=1, source_target_pairs={{0,1},{1,0},{2,3},{3,2},{4,5},{5,4},{6,7},{7,6},{8,9},{9,8},{10,11... | collective-permute-start | bytes 49160 | tf_op jit(solution)/shard_map/ppermute | solution.py:710
  127.8 1.9 %collective-permute-done.24 = f32[4,8,128]{2,1,0:T(8,128)S(1)} collective-permute-done((f32[4,8,128]{2,1,0:T(8,128)}, f32[4,8,128]{2,1,0:T(8,128)S(1)}, u32[]{:S(2)}, u32[]{:S(2)}) %collective-permute-start.24) | collective-permute-done | bytes 16416 | tf_op jit(solution)/shard_map/ppermute | solution.py:710
  129.8 0.7 add.50
  130.5 2.5 %collective-permute-start.25 = (f32[4,8,128]{2,1,0:T(8,128)S(1)}, f32[4,8,128]{2,1,0:T(8,128)S(1)}, u32[]{:S(2)}, u32[]{:S(2)}) collective-permute-start(f32[4,8,128]{2,1,0:T(8,128)S(1)} %add.50), channel_id=1, source_target_pairs={{0,2},{1,3},{2,0},{3,1},{4,6},{5,7},{6,4},{7,5},{8,10},{9,11},{10,... | collective-permute-start | bytes 49160 | tf_op jit(solution)/shard_map/ppermute | solution.py:710
  133.0 2.2 %collective-permute-done.25 = f32[4,8,128]{2,1,0:T(8,128)S(1)} collective-permute-done((f32[4,8,128]{2,1,0:T(8,128)S(1)}, f32[4,8,128]{2,1,0:T(8,128)S(1)}, u32[]{:S(2)}, u32[]{:S(2)}) %collective-permute-start.25) | collective-permute-done | bytes 16416 | tf_op jit(solution)/shard_map/ppermute | solution.py:710
  135.2 0.0 copy-start.1
  135.2 1.6 %copy-done.1 = f32[4,512,256]{2,1,0:T(8,128)S(1)} copy-done((f32[4,512,256]{2,1,0:T(8,128)S(1)}, f32[4,512,256]{2,1,0:T(8,128)}, u32[]{:S(2)}) %copy-start.1) | copy-done | bytes 2097176
  136.7 2.6 %shard_map.147 = bf16[8,8,64,256]{3,2,1,0:T(8,128)(2,1)} custom-call(f32[4,8,128]{2,1,0:T(8,128)S(1)} %add.51.sum_ref, bf16[8,128,128]{2,1,0:T(8,128)(2,1)S(1)} %copy-done.2, bf16[4,512,256]{2,1,0:T(8,128)(2,1)S(1)} %bitcast.16, f32[4,512,256]{2,1,0:T(8,128)S(1)} %copy-done.1), custom_call_target="tpu_custom_call" | custom-call | tf_op jit(solution)/shard_map/pallas_call | solution.py:623
  (76 shorter events, 0.2 us)
Async XLA Ops:
  0.0 39.2 %copy-start = (bf16[4096,22]{0,1:T(8,128)(2,1)S(1)}, bf16[4096,22]{0,1:T(8,128)(2,1)}, u32[]{:S(2)}) copy-start(bf16[4096,22]{0,1:T(8,128)(2,1)} %param.15) | copy-start | bytes 540676
  0.6 15.7 %copy-start.27 = (f32[1024,8]{0,1:T(8,128)S(1)}, f32[1024,8]{0,1:T(8,128)}, u32[]{:S(2)}) copy-start(f32[1024,8]{0,1:T(8,128)} %param.18) | copy-start | bytes 98308
  0.6 15.7 %copy-start.28 = (s32[8,8]{1,0:T(8,128)S(1)}, s32[8,8]{1,0:T(8,128)}, u32[]{:S(2)}) copy-start(s32[8,8]{1,0:T(8,128)} %param.19) | copy-start | bytes 772
  0.6 38.6 %copy-start.29 = (s32[8]{0:T(128)S(1)}, s32[8]{0:T(128)}, u32[]{:S(2)}) copy-start(s32[8]{0:T(128)} %param.16) | copy-start | bytes 100
  0.6 45.0 %copy-start.13 = (f32[2]{0:T(128)S(1)}, f32[2]{0:T(128)}, u32[]{:S(2)}) copy-start(f32[2]{0:T(128)} %own_lengths.1) | copy-start | bytes 28
  4.5 12.9 %collective-permute-start.2 = (bf16[71,16,128]{2,1,0:T(8,128)(2,1)}, bf16[71,16,128]{2,1,0:T(8,128)(2,1)S(1)}, u32[]{:S(2)}, u32[]{:S(2)}) collective-permute-start(bf16[71,16,128]{2,1,0:T(8,128)(2,1)} %get-tuple-element.36), channel_id=1, source_target_pairs={{0,3},{1,0},{2,1},{3,2},{4,7},{5,4},{6,5},{7,6},{8,11},{9,8},{10,9... | collective-permute-start | bytes 872456 | tf_op jit(solution)/shard_map/ppermute | solution.py:248
  9.6 14.8 %collective-permute-start = (bf16[71,16,128]{2,1,0:T(8,128)(2,1)}, bf16[71,16,128]{2,1,0:T(8,128)(2,1)S(1)}, u32[]{:S(2)}, u32[]{:S(2)}) collective-permute-start(bf16[71,16,128]{2,1,0:T(8,128)(2,1)} %get-tuple-element.36), channel_id=1, source_target_pairs={{0,1},{1,2},{2,3},{3,0},{4,5},{5,6},{6,7},{7,4},{8,9},{9,10},{10,1... | collective-permute-start | bytes 872456 | tf_op jit(solution)/shard_map/ppermute | solution.py:248
  9.6 25.0 %collective-permute-start.1 = (bf16[71,16,128]{2,1,0:T(8,128)(2,1)}, bf16[71,16,128]{2,1,0:T(8,128)(2,1)S(1)}, u32[]{:S(2)}, u32[]{:S(2)}) collective-permute-start(bf16[71,16,128]{2,1,0:T(8,128)(2,1)} %get-tuple-element.36), channel_id=1, source_target_pairs={{0,2},{1,3},{2,0},{3,1},{4,6},{5,7},{6,4},{7,5},{8,10},{9,11},{10,... | collective-permute-start | bytes 872456 | tf_op jit(solution)/shard_map/ppermute | solution.py:248
  16.4 49.4 %copy-start.14 = (f32[2]{0:T(128)S(1)}, f32[2]{0:T(128)}, u32[]{:S(2)}) copy-start(f32[2]{0:T(128)} %own_lengths.1) | copy-start | bytes 28
  17.4 6.9 %copy-start.3 = (bf16[71,16,128]{2,1,0:T(8,128)(2,1)}, bf16[71,16,128]{2,1,0:T(8,128)(2,1)S(1)}, u32[]{:S(2)}) copy-start(bf16[71,16,128]{2,1,0:T(8,128)(2,1)S(1)} %collective-permute-done.2.refs_2_.refs_1_) | copy-start | bytes 872452
  24.3 0.7 copy-start.4
  27.0 9.8 %collective-permute-start.4 = (bf16[70,16,128]{2,1,0:T(8,128)(2,1)}, bf16[70,16,128]{2,1,0:T(8,128)(2,1)S(1)}, u32[]{:S(2)}, u32[]{:S(2)}) collective-permute-start(bf16[70,16,128]{2,1,0:T(8,128)(2,1)} %get-tuple-element.41.refs_4_), channel_id=1, source_target_pairs={{0,16},{4,20},{8,24},{12,28},{16,0},{20,4},{24,8},{28,12},{1,17},{... | collective-permute-start | bytes 860168 | tf_op jit(solution)/shard_map/ppermute | solution.py:260
  28.5 11.5 %collective-permute-start.3 = (bf16[70,16,128]{2,1,0:T(8,128)(2,1)}, bf16[70,16,128]{2,1,0:T(8,128)(2,1)S(1)}, u32[]{:S(2)}, u32[]{:S(2)}) collective-permute-start(bf16[70,16,128]{2,1,0:T(8,128)(2,1)} %get-tuple-element.41.refs_4_), channel_id=1, source_target_pairs={{0,8},{4,12},{8,0},{12,4},{16,24},{20,28},{24,16},{28,20},{1,9},{5... | collective-permute-start | bytes 860168 | tf_op jit(solution)/shard_map/ppermute | solution.py:260
  30.1 11.5 %collective-permute-start.6 = (bf16[70,16,128]{2,1,0:T(8,128)(2,1)}, bf16[70,16,128]{2,1,0:T(8,128)(2,1)S(1)}, u32[]{:S(2)}, u32[]{:S(2)}) collective-permute-start(bf16[70,16,128]{2,1,0:T(8,128)(2,1)} %get-tuple-element.42.refs_5_), channel_id=1, source_target_pairs={{0,8},{4,12},{8,0},{12,4},{16,24},{20,28},{24,16},{28,20},{1,9},{5... | collective-permute-start | bytes 860168 | tf_op jit(solution)/shard_map/ppermute | solution.py:260
  30.6 19.1 %collective-permute-start.5 = (bf16[70,16,128]{2,1,0:T(8,128)(2,1)}, bf16[70,16,128]{2,1,0:T(8,128)(2,1)S(1)}, u32[]{:S(2)}, u32[]{:S(2)}) collective-permute-start(bf16[70,16,128]{2,1,0:T(8,128)(2,1)} %get-tuple-element.42.refs_5_), channel_id=1, source_target_pairs={{0,16},{4,20},{8,24},{12,28},{16,0},{20,4},{24,8},{28,12},{1,17},{... | collective-permute-start | bytes 860168 | tf_op jit(solution)/shard_map/ppermute | solution.py:260
  34.5 22.9 %copy-start.5 = (bf16[71,16,128]{2,1,0:T(8,128)(2,1)}, bf16[71,16,128]{2,1,0:T(8,128)(2,1)S(1)}, u32[]{:S(2)}) copy-start(bf16[71,16,128]{2,1,0:T(8,128)(2,1)S(1)} %collective-permute-done.1.refs_1_.refs_17_) | copy-start | bytes 872452
  34.5 16.6 %collective-permute-start.20 = (bf16[71,16,128]{2,1,0:T(8,128)(2,1)S(1)}, bf16[71,16,128]{2,1,0:T(8,128)(2,1)S(1)}, u32[]{:S(2)}, u32[]{:S(2)}) collective-permute-start(bf16[71,16,128]{2,1,0:T(8,128)(2,1)S(1)} %collective-permute-done.1.refs_1_.refs_17_), channel_id=1, source_target_pairs={{0,4},{4,0},{8,12},{12,8},{16,20},{20,16},{24,28},{28,24},{1,5},{5... | collective-permute-start | bytes 872456 | tf_op jit(solution)/shard_map/ppermute | solution.py:260
  36.7 13.0 %copy-start.9 = (bf16[70,16,128]{2,1,0:T(8,128)(2,1)}, bf16[70,16,128]{2,1,0:T(8,128)(2,1)S(1)}, u32[]{:S(2)}) copy-start(bf16[70,16,128]{2,1,0:T(8,128)(2,1)S(1)} %collective-permute-done.4.refs_1_) | copy-start | bytes 860164
  36.8 14.9 %collective-permute-start.19 = (bf16[71,16,128]{2,1,0:T(8,128)(2,1)S(1)}, bf16[71,16,128]{2,1,0:T(8,128)(2,1)S(1)}, u32[]{:S(2)}, u32[]{:S(2)}) collective-permute-start(bf16[71,16,128]{2,1,0:T(8,128)(2,1)S(1)} %collective-permute-done.1.refs_1_.refs_17_), channel_id=1, source_target_pairs={{0,16},{4,20},{8,24},{12,28},{16,0},{20,4},{24,8},{28,12},{1,17},{... | collective-permute-start | bytes 872456 | tf_op jit(solution)/shard_map/ppermute | solution.py:260
  40.0 9.7 %copy-start.10 = (bf16[70,16,128]{2,1,0:T(8,128)(2,1)}, bf16[70,16,128]{2,1,0:T(8,128)(2,1)S(1)}, u32[]{:S(2)}) copy-start(bf16[70,16,128]{2,1,0:T(8,128)(2,1)S(1)} %collective-permute-done.3.refs_0_) | copy-start | bytes 860164
  40.0 11.7 %collective-permute-start.18 = (bf16[71,16,128]{2,1,0:T(8,128)(2,1)S(1)}, bf16[71,16,128]{2,1,0:T(8,128)(2,1)S(1)}, u32[]{:S(2)}, u32[]{:S(2)}) collective-permute-start(bf16[71,16,128]{2,1,0:T(8,128)(2,1)S(1)} %collective-permute-done.1.refs_1_.refs_17_), channel_id=1, source_target_pairs={{0,8},{4,12},{8,0},{12,4},{16,24},{20,28},{24,16},{28,20},{1,9},{5... | collective-permute-start | bytes 872456 | tf_op jit(solution)/shard_map/ppermute | solution.py:260
  41.6 8.2 %copy-start.11 = (bf16[70,16,128]{2,1,0:T(8,128)(2,1)}, bf16[70,16,128]{2,1,0:T(8,128)(2,1)S(1)}, u32[]{:S(2)}) copy-start(bf16[70,16,128]{2,1,0:T(8,128)(2,1)S(1)} %collective-permute-done.6.refs_3_) | copy-start | bytes 860164
  41.6 12.0 %collective-permute-start.17 = (bf16[71,16,128]{2,1,0:T(8,128)(2,1)S(1)}, bf16[71,16,128]{2,1,0:T(8,128)(2,1)S(1)}, u32[]{:S(2)}, u32[]{:S(2)}) collective-permute-start(bf16[71,16,128]{2,1,0:T(8,128)(2,1)S(1)} %collective-permute-done.1.refs_1_.refs_17_), channel_id=1, source_target_pairs={{0,24},{4,28},{8,16},{12,20},{16,8},{20,12},{24,0},{28,4},{1,25},{... | collective-permute-start | bytes 872456 | tf_op jit(solution)/shard_map/ppermute | solution.py:260
  49.7 0.7 copy-start.12
  51.1 2.4 %collective-permute-start.9 = (bf16[70,16,128]{2,1,0:T(8,128)(2,1)}, bf16[70,16,128]{2,1,0:T(8,128)(2,1)S(1)}, u32[]{:S(2)}, u32[]{:S(2)}) collective-permute-start(bf16[70,16,128]{2,1,0:T(8,128)(2,1)} %get-tuple-element.45.refs_1_), channel_id=1, source_target_pairs={{0,4},{4,0},{8,12},{12,8},{16,20},{20,16},{24,28},{28,24},{1,5},{5... | collective-permute-start | bytes 860168 | tf_op jit(solution)/shard_map/ppermute | solution.py:260
  51.1 17.0 %copy-start.15 = (bf16[71,16,128]{2,1,0:T(8,128)(2,1)}, bf16[71,16,128]{2,1,0:T(8,128)(2,1)S(1)}, u32[]{:S(2)}) copy-start(bf16[71,16,128]{2,1,0:T(8,128)(2,1)S(1)} %collective-permute-done.20.refs_21_) | copy-start | bytes 872452
  51.1 4.0 %collective-permute-start.10 = (bf16[70,16,128]{2,1,0:T(8,128)(2,1)}, bf16[70,16,128]{2,1,0:T(8,128)(2,1)S(1)}, u32[]{:S(2)}, u32[]{:S(2)}) collective-permute-start(bf16[70,16,128]{2,1,0:T(8,128)(2,1)} %get-tuple-element.46.refs_2_), channel_id=1, source_target_pairs={{0,4},{4,0},{8,12},{12,8},{16,20},{20,16},{24,28},{28,24},{1,5},{5... | collective-permute-start | bytes 860168 | tf_op jit(solution)/shard_map/ppermute | solution.py:260
  51.7 12.3 %copy-start.6 = (bf16[71,16,128]{2,1,0:T(8,128)(2,1)}, bf16[71,16,128]{2,1,0:T(8,128)(2,1)S(1)}, u32[]{:S(2)}) copy-start(bf16[71,16,128]{2,1,0:T(8,128)(2,1)S(1)} %collective-permute-done.19.refs_2_) | copy-start | bytes 872452
  51.7 3.7 %collective-permute-start.12 = (bf16[70,16,128]{2,1,0:T(8,128)(2,1)}, bf16[70,16,128]{2,1,0:T(8,128)(2,1)S(1)}, u32[]{:S(2)}, u32[]{:S(2)}) collective-permute-start(bf16[70,16,128]{2,1,0:T(8,128)(2,1)} %get-tuple-element.48.refs_4_), channel_id=1, source_target_pairs={{0,4},{4,0},{8,12},{12,8},{16,20},{20,16},{24,28},{28,24},{1,5},{5... | collective-permute-start | bytes 860168 | tf_op jit(solution)/shard_map/ppermute | solution.py:260
  51.7 12.2 %copy-start.7 = (bf16[71,16,128]{2,1,0:T(8,128)(2,1)}, bf16[71,16,128]{2,1,0:T(8,128)(2,1)S(1)}, u32[]{:S(2)}) copy-start(bf16[71,16,128]{2,1,0:T(8,128)(2,1)S(1)} %collective-permute-done.18.refs_1_) | copy-start | bytes 872452
  51.7 12.9 %collective-permute-start.15 = (bf16[70,16,128]{2,1,0:T(8,128)(2,1)}, bf16[70,16,128]{2,1,0:T(8,128)(2,1)S(1)}, u32[]{:S(2)}, u32[]{:S(2)}) collective-permute-start(bf16[70,16,128]{2,1,0:T(8,128)(2,1)} %get-tuple-element.50.refs_7_), channel_id=1, source_target_pairs={{0,4},{4,0},{8,12},{12,8},{16,20},{20,16},{24,28},{28,24},{1,5},{5... | collective-permute-start | bytes 860168 | tf_op jit(solution)/shard_map/ppermute | solution.py:260
  53.6 10.4 %copy-start.8 = (bf16[71,16,128]{2,1,0:T(8,128)(2,1)}, bf16[71,16,128]{2,1,0:T(8,128)(2,1)S(1)}, u32[]{:S(2)}) copy-start(bf16[71,16,128]{2,1,0:T(8,128)(2,1)S(1)} %collective-permute-done.17.refs_0_) | copy-start | bytes 872452
  53.6 11.2 %collective-permute-start.11 = (bf16[70,16,128]{2,1,0:T(8,128)(2,1)}, bf16[70,16,128]{2,1,0:T(8,128)(2,1)S(1)}, u32[]{:S(2)}, u32[]{:S(2)}) collective-permute-start(bf16[70,16,128]{2,1,0:T(8,128)(2,1)} %get-tuple-element.47.refs_3_), channel_id=1, source_target_pairs={{0,4},{4,0},{8,12},{12,8},{16,20},{20,16},{24,28},{28,24},{1,5},{5... | collective-permute-start | bytes 860168 | tf_op jit(solution)/shard_map/ppermute | solution.py:260
  53.6 14.5 %copy-start.19 = (bf16[70,16,128]{2,1,0:T(8,128)(2,1)}, bf16[70,16,128]{2,1,0:T(8,128)(2,1)S(1)}, u32[]{:S(2)}) copy-start(bf16[70,16,128]{2,1,0:T(8,128)(2,1)S(1)} %collective-permute-done.9.refs_9_) | copy-start | bytes 860164
  53.6 11.6 %collective-permute-start.7 = (bf16[70,16,128]{2,1,0:T(8,128)(2,1)}, bf16[70,16,128]{2,1,0:T(8,128)(2,1)S(1)}, u32[]{:S(2)}, u32[]{:S(2)}) collective-permute-start(bf16[70,16,128]{2,1,0:T(8,128)(2,1)} %get-tuple-element.47.refs_3_), channel_id=1, source_target_pairs={{0,16},{4,20},{8,24},{12,28},{16,0},{20,4},{24,8},{28,12},{1,17},{... | collective-permute-start | bytes 860168 | tf_op jit(solution)/shard_map/ppermute | solution.py:260
  55.2 12.9 %copy-start.20 = (bf16[70,16,128]{2,1,0:T(8,128)(2,1)}, bf16[70,16,128]{2,1,0:T(8,128)(2,1)S(1)}, u32[]{:S(2)}) copy-start(bf16[70,16,128]{2,1,0:T(8,128)(2,1)S(1)} %collective-permute-done.10.refs_10_) | copy-start | bytes 860164
  55.2 10.1 %collective-permute-start.14 = (bf16[70,16,128]{2,1,0:T(8,128)(2,1)}, bf16[70,16,128]{2,1,0:T(8,128)(2,1)}, u32[]{:S(2)}, u32[]{:S(2)}) collective-permute-start(bf16[70,16,128]{2,1,0:T(8,128)(2,1)} %get-tuple-element.49.refs_6_), channel_id=1, source_target_pairs={{0,4},{4,0},{8,12},{12,8},{16,20},{20,16},{24,28},{28,24},{1,5},{5... | collective-permute-start | bytes 860168 | tf_op jit(solution)/shard_map/ppermute | solution.py:260
  55.3 12.8 %copy-start.21 = (bf16[70,16,128]{2,1,0:T(8,128)(2,1)}, bf16[70,16,128]{2,1,0:T(8,128)(2,1)S(1)}, u32[]{:S(2)}) copy-start(bf16[70,16,128]{2,1,0:T(8,128)(2,1)S(1)} %collective-permute-done.12.refs_12_) | copy-start | bytes 860164
  55.3 10.3 %collective-permute-start.8 = (bf16[70,16,128]{2,1,0:T(8,128)(2,1)}, bf16[70,16,128]{2,1,0:T(8,128)(2,1)}, u32[]{:S(2)}, u32[]{:S(2)}) collective-permute-start(bf16[70,16,128]{2,1,0:T(8,128)(2,1)} %get-tuple-element.49.refs_6_), channel_id=1, source_target_pairs={{0,8},{4,12},{8,0},{12,4},{16,24},{20,28},{24,16},{28,20},{1,9},{5... | collective-permute-start | bytes 860168 | tf_op jit(solution)/shard_map/ppermute | solution.py:260
  64.7 3.5 %copy-start.22 = (bf16[70,16,128]{2,1,0:T(8,128)(2,1)}, bf16[70,16,128]{2,1,0:T(8,128)(2,1)S(1)}, u32[]{:S(2)}) copy-start(bf16[70,16,128]{2,1,0:T(8,128)(2,1)S(1)} %collective-permute-done.15.refs_15_) | copy-start | bytes 860164
  64.7 1.8 %collective-permute-start.21 = (bf16[71,16,128]{2,1,0:T(8,128)(2,1)}, bf16[71,16,128]{2,1,0:T(8,128)(2,1)S(1)}, u32[]{:S(2)}, u32[]{:S(2)}) collective-permute-start(bf16[71,16,128]{2,1,0:T(8,128)(2,1)} %get-tuple-element.53.refs_18_), channel_id=1, source_target_pairs={{0,4},{4,0},{8,12},{12,8},{16,20},{20,16},{24,28},{28,24},{1,5},{5... | collective-permute-start | bytes 872456 | tf_op jit(solution)/shard_map/ppermute | solution.py:260
  64.7 3.4 %copy-start.23 = (bf16[70,16,128]{2,1,0:T(8,128)(2,1)}, bf16[70,16,128]{2,1,0:T(8,128)(2,1)S(1)}, u32[]{:S(2)}) copy-start(bf16[70,16,128]{2,1,0:T(8,128)(2,1)S(1)} %collective-permute-done.11.refs_11_) | copy-start | bytes 860164
  64.7 2.1 %collective-permute-start.22 = (bf16[71,16,128]{2,1,0:T(8,128)(2,1)}, bf16[71,16,128]{2,1,0:T(8,128)(2,1)S(1)}, u32[]{:S(2)}, u32[]{:S(2)}) collective-permute-start(bf16[71,16,128]{2,1,0:T(8,128)(2,1)} %get-tuple-element.54.refs_19_), channel_id=1, source_target_pairs={{0,4},{4,0},{8,12},{12,8},{16,20},{20,16},{24,28},{28,24},{1,5},{5... | collective-permute-start | bytes 872456 | tf_op jit(solution)/shard_map/ppermute | solution.py:260
  65.2 3.0 %copy-start.24 = (bf16[70,16,128]{2,1,0:T(8,128)(2,1)}, bf16[70,16,128]{2,1,0:T(8,128)(2,1)S(1)}, u32[]{:S(2)}) copy-start(bf16[70,16,128]{2,1,0:T(8,128)(2,1)S(1)} %collective-permute-done.7.refs_5_) | copy-start | bytes 860164
  65.2 2.5 %collective-permute-start.23 = (bf16[71,16,128]{2,1,0:T(8,128)(2,1)}, bf16[71,16,128]{2,1,0:T(8,128)(2,1)S(1)}, u32[]{:S(2)}, u32[]{:S(2)}) collective-permute-start(bf16[71,16,128]{2,1,0:T(8,128)(2,1)} %get-tuple-element.55.refs_20_), channel_id=1, source_target_pairs={{0,4},{4,0},{8,12},{12,8},{16,20},{20,16},{24,28},{28,24},{1,5},{5... | collective-permute-start | bytes 872456 | tf_op jit(solution)/shard_map/ppermute | solution.py:260
  65.3 2.4 %collective-permute-start.13 = (bf16[70,16,128]{2,1,0:T(8,128)(2,1)S(1)}, bf16[70,16,128]{2,1,0:T(8,128)(2,1)S(1)}, u32[]{:S(2)}, u32[]{:S(2)}) collective-permute-start(bf16[70,16,128]{2,1,0:T(8,128)(2,1)S(1)} %collective-permute-done.7.refs_5_), channel_id=1, source_target_pairs={{0,4},{4,0},{8,12},{12,8},{16,20},{20,16},{24,28},{28,24},{1,5},{5... | collective-permute-start | bytes 860168 | tf_op jit(solution)/shard_map/ppermute | solution.py:260
  65.7 2.4 %collective-permute-start.16 = (bf16[70,16,128]{2,1,0:T(8,128)(2,1)}, bf16[70,16,128]{2,1,0:T(8,128)(2,1)S(1)}, u32[]{:S(2)}, u32[]{:S(2)}) collective-permute-start(bf16[70,16,128]{2,1,0:T(8,128)(2,1)} %collective-permute-done.8.refs_8_), channel_id=1, source_target_pairs={{0,4},{4,0},{8,12},{12,8},{16,20},{20,16},{24,28},{28,24},{1,5},{5... | collective-permute-start | bytes 860168 | tf_op jit(solution)/shard_map/ppermute | solution.py:260
  66.4 1.7 %copy-start.16 = (bf16[71,16,128]{2,1,0:T(8,128)(2,1)}, bf16[71,16,128]{2,1,0:T(8,128)(2,1)S(1)}, u32[]{:S(2)}) copy-start(bf16[71,16,128]{2,1,0:T(8,128)(2,1)S(1)} %collective-permute-done.21.refs_22_) | copy-start | bytes 872452
  66.9 1.3 copy-start.17
  67.7 0.7 copy-start.18
  67.7 0.8 copy-start.25
  68.1 0.7 copy-start.26
  89.6 45.5 %all-to-all-start = ((bf16[4,1,512,256]{3,2,1,0:T(8,128)(2,1)}), bf16[4,1,512,256]{3,2,1,0:T(8,128)(2,1)S(1)}, u32[]{:S(2)}, u32[]{:S(2)}) async-start(bf16[4,1,512,256]{3,2,1,0:T(8,128)(2,1)} %get-tuple-element.65), calls=%async_computation | async-start | bytes 2097152 | tf_op jit(solution)/shard_map/all_to_all | solution.py:776
  94.0 41.1 %copy-start.2 = (bf16[8,128,128]{2,1,0:T(8,128)(2,1)S(1)}, bf16[8,128,128]{2,1,0:T(8,128)(2,1)}, u32[]{:S(2)}) copy-start(bf16[8,128,128]{2,1,0:T(8,128)(2,1)} %get-tuple-element.64.weight_ref) | copy-start | bytes 786436
  125.3 4.5 %collective-permute-start.24 = (f32[4,8,128]{2,1,0:T(8,128)}, f32[4,8,128]{2,1,0:T(8,128)S(1)}, u32[]{:S(2)}, u32[]{:S(2)}) collective-permute-start(f32[4,8,128]{2,1,0:T(8,128)} %get-tuple-element.63), channel_id=1, source_target_pairs={{0,1},{1,0},{2,3},{3,2},{4,5},{5,4},{6,7},{7,6},{8,9},{9,8},{10,11... | collective-permute-start | bytes 49160 | tf_op jit(solution)/shard_map/ppermute | solution.py:710
  130.5 4.6 %collective-permute-start.25 = (f32[4,8,128]{2,1,0:T(8,128)S(1)}, f32[4,8,128]{2,1,0:T(8,128)S(1)}, u32[]{:S(2)}, u32[]{:S(2)}) collective-permute-start(f32[4,8,128]{2,1,0:T(8,128)S(1)} %add.50), channel_id=1, source_target_pairs={{0,2},{1,3},{2,0},{3,1},{4,6},{5,7},{6,4},{7,5},{8,10},{9,11},{10,... | collective-permute-start | bytes 49160 | tf_op jit(solution)/shard_map/ppermute | solution.py:710
  135.2 1.6 %copy-start.1 = (f32[4,512,256]{2,1,0:T(8,128)S(1)}, f32[4,512,256]{2,1,0:T(8,128)}, u32[]{:S(2)}) copy-start(f32[4,512,256]{2,1,0:T(8,128)} %get-tuple-element.66.image_ref) | copy-start | bytes 6291460

commit v11 on v10

--- a/solution.py
+++ b/solution.py
@@ -755,10 +755,12 @@
 
     far = tuple(s for s in range(1, waves) if min(s, waves - s) > waves // 4)
     near = tuple(s for s in range(1, waves) if s not in far)
-    halves = split_parts([parts[s - 1] for s in near], half, [packed])
-    got = gather_halves(halves, half, near, [own_token, spread_token])
+    halves = split_parts(
+        [parts[s - 1] for s in near], half, [packed, own_token, spread_token]
+    )
     every, inverse = kept_lengths(parts, where, wave_lengths, half, sent_lengths)
     all_row, all_column, all_token = tables(every, mine * rows, rows)
+    got = gather_halves(halves, half, near, [all_token])
     pieces = [parts[s - 1] for s in far]
     pieces = pieces[0] if len(pieces) == 1 else jnp.concatenate(pieces)
     got = got + gather_direct(pieces, half, far, [all_token])

time: 140 us -> 150 us (1.071)
  waiting for transfers between devices: 20.3 us -> 27.4 us
  starting transfers between devices: 29.4 us -> 33 us
    ppermute x21, waiting for transfers between devices: 5.91 us -> 20.2 us  [swap(): return lax.ppermute(x, ('groups', 'field'), pairs)]
    ppermute x3, waiting for transfers between devices: 10.3 us -> 3.49 us  [along_wave(): lax.ppermute(piece, 'wave', [(i, (i + s) % waves) for i in range(waves)])]
    all_to_all x1, starting transfers between devices: 4.39 us -> 9.2 us  [local(): lax.all_to_all(spectra, 'wave', split_axis=0, concat_axis=0, tiled=True)]
  transfers between devices with their start and end apart: 27 -> 27, of which waited for: 11 -> 9; matrix products, arithmetic and copies ran while one was open for 4% -> 4% of each run, Pallas kernels for 37% -> 35%
where the time goes in v11:
time: 150 us
  Pallas kernels  79.6 us (53%)
  starting transfers between devices  33 us (22%)
  waiting for transfers between devices  27.4 us (18%)
  local copies, waits for them, and re-layouts  3.98 us (3%)
  other arithmetic  3.37 us (2%)
  matrix products  1.83 us (1%)
    pallas_call x1, Pallas kernels, row_fields(): pl.pallas_call(functools.partial(rows_kernel, positions, rows), grid=(len...  31.3 us
    pallas_call x1, Pallas kernels, whole_fields(): pl.pallas_call(functools.partial(whole_kernel, (positions, modes, waves,...  20.9 us
    ppermute x21, waiting for transfers between devices, swap(): return lax.ppermute(x, ('groups', 'field'), pairs)  20.2 us
    ppermute x21, starting transfers between devices, swap(): return lax.ppermute(x, ('groups', 'field'), pairs)  12.7 us
    all_to_all x1, starting transfers between devices, local(): lax.all_to_all(spectra, 'wave', split_axis=0, concat_axis=0, tiled=True)  9.2 us
    pallas_call x2, Pallas kernels, tables(): pl.pallas_call(table_kernel, grid=(lengths,), out_shape=(jax.ShapeDtypeSt...  8.51 us
    ppermute x3, starting transfers between devices, along_wave(): lax.ppermute(piece, 'wave', [(i, (i + s) % waves) for i in range(waves)])  6.07 us
    pallas_call x1, Pallas kernels, pack_rows(): pl.pallas_call(functools.partial(own_kernel, count), out_shape=(jax.Shape...  5.77 us
  transfers between devices with their start and end apart: 27, of which 9 were waited for; matrix products, arithmetic and copies ran while one was open for 4% of the time, Pallas kernels for 35%

profile of v11, /device:TPU:0, one launch (start us, length us, event | category | flops | bytes accessed | tf_op | source)
XLA Modules:
  0.0 149.6 jit_solution(6467457401888237889)
XLA Ops:
  0.0 0.6 pad_add_fusion.where
  0.7 3.8 %shard_map.136 = (bf16[71,16,128]{2,1,0:T(8,128)(2,1)}, f32[8,128]{1,0:T(8,128)}) custom-call(s32[2]{0:T(128)} %pad_add_fusion.where, s32[100,3]{1,0:T(8,128)} %constant.57.clone.table, f32[2]{0:T(128)} %own_lengths.1, bf16[22,128,512]{2,1,0:T(8,128)(2,1)} %basis.3), custom_call_target="tpu_custom_call" | custom-call | tf_op jit(solution)/shard_map/pallas_call | solution.py:158
  4.5 5.1 %collective-permute-start.2 = (bf16[71,16,128]{2,1,0:T(8,128)(2,1)}, bf16[71,16,128]{2,1,0:T(8,128)(2,1)S(1)}, u32[]{:S(2)}, u32[]{:S(2)}) collective-permute-start(bf16[71,16,128]{2,1,0:T(8,128)(2,1)} %get-tuple-element.36), channel_id=1, source_target_pairs={{0,3},{1,0},{2,1},{3,2},{4,7},{5,4},{6,5},{7,6},{8,11},{9,8},{10,9... | collective-permute-start | bytes 872456 | tf_op jit(solution)/shard_map/ppermute | solution.py:248
  9.6 0.0 collective-permute-start.1
  9.6 1.0 collective-permute-start
  10.6 1.1 fusion.6
  11.7 0.7 add_convert_fusion.u_ref
  12.4 0.1 copy.36
  12.5 0.1 copy.37
  12.7 0.8 fusion.refs_0_
  13.4 0.7 pad_maximum_fusion.refs_1_
  14.1 5.8 %shard_map.138 = (bf16[560,16,128]{2,1,0:T(8,128)(2,1)}, f32[8,128]{1,0:T(8,128)}) custom-call(s32[2]{0:T(128)} %pad_add_fusion.where, s32[100,3]{1,0:T(8,128)} %constant.57.clone.table, bf16[22,128,512]{2,1,0:T(8,128)(2,1)} %basis.3, f32[8,128]{1,0:T(8,128)} %get-tuple-element.38._), custom_call_target="tpu_custom_call" | custom-call | tf_op jit(solution)/shard_map/pallas_call | solution.py:168
  19.9 2.0 %shard_map.140 = (bf16[1,128,352]{2,1,0:T(8,128)(2,1)}, bf16[8,128,128]{2,1,0:T(8,128)(2,1)}, f32[8,128]{1,0:T(8,128)}) custom-call(bf16[1,8,22]{2,1,0:T(8,128)(2,1)} %fusion.refs_0_, bf16[8,8,8]{2,1,0:T(8,128)(2,1)} %pad_maximum_fusion.refs_1_), custom_call_target="tpu_custom_call" | custom-call | tf_op jit(solution)/shard_map/pallas_call | solution.py:305
  21.9 0.6 broadcast_in_dim.7.length_ref
  22.5 3.4 %shard_map.139 = (bf16[1,4,512,256]{3,2,1,0:T(8,128)(2,1)}, bf16[1,1024,512]{2,1,0:T(8,128)(2,1)}, f32[8,128]{1,0:T(8,128)}) custom-call(f32[1,8,128]{2,1,0:T(8,128)} %broadcast_in_dim.7.length_ref, f32[512,1]{1,0:T(8,128)} %constant.58.clone.y_ref, f32[1,256]{1,0:T(1,128)} %constant.59.clone.v_ref, f32[256,1]{1,0:T(8,128)} %add_convert_fusion.u_ref, ...), custom_call_target="tpu_custom_call" | custom-call | flops 3932160 | bytes 1048576 | tf_op jit(solution)/shard_map/pallas_call | solution.py:674
  26.0 3.5 %collective-permute-done.refs_0_ = bf16[71,16,128]{2,1,0:T(8,128)(2,1)S(1)} collective-permute-done((bf16[71,16,128]{2,1,0:T(8,128)(2,1)}, bf16[71,16,128]{2,1,0:T(8,128)(2,1)S(1)}, u32[]{:S(2)}, u32[]{:S(2)}) %collective-permute-start) | collective-permute-done | bytes 290848 | tf_op jit(solution)/shard_map/ppermute | solution.py:248
  29.4 0.7 copy-done.4
  30.1 1.9 %shard_map.141 = (bf16[70,16,128]{2,1,0:T(8,128)(2,1)}, bf16[70,16,128]{2,1,0:T(8,128)(2,1)}) custom-call(bf16[71,16,128]{2,1,0:T(8,128)(2,1)} %copy-done.4, bf16[71,16,128]{2,1,0:T(8,128)(2,1)} %copy-done.3, f32[8,128]{1,0:T(8,128)} %get-tuple-element.40.refs_2_, f32[8,128]{1,0:T(8,128)} %get-tuple-element.41.refs_3_, f32[8,128]{1,0:T(8,128)} %get-tuple-element.42.refs_4_), custom_call_target="tpu_custom_call" | custom-call | tf_op jit(solution)/shard_map/pallas_call | solution.py:190
  32.1 1.5 %collective-permute-start.4 = (bf16[70,16,128]{2,1,0:T(8,128)(2,1)}, bf16[70,16,128]{2,1,0:T(8,128)(2,1)S(1)}, u32[]{:S(2)}, u32[]{:S(2)}) collective-permute-start(bf16[70,16,128]{2,1,0:T(8,128)(2,1)} %get-tuple-element.43.refs_4_), channel_id=1, source_target_pairs={{0,16},{4,20},{8,24},{12,28},{16,0},{20,4},{24,8},{28,12},{1,17},{... | collective-permute-start | bytes 860168 | tf_op jit(solution)/shard_map/ppermute | solution.py:260
  33.6 1.5 collective-permute-start.3
  35.1 0.5 collective-permute-start.6
  35.6 0.5 collective-permute-start.5
  36.1 0.0 collective-permute-done.1.refs_1_.refs_17_
  36.1 0.0 collective-permute-start.20
  36.1 5.9 %collective-permute-done.4.refs_1_ = bf16[70,16,128]{2,1,0:T(8,128)(2,1)S(1)} collective-permute-done((bf16[70,16,128]{2,1,0:T(8,128)(2,1)}, bf16[70,16,128]{2,1,0:T(8,128)(2,1)S(1)}, u32[]{:S(2)}, u32[]{:S(2)}) %collective-permute-start.4) | collective-permute-done | bytes 286752 | tf_op jit(solution)/shard_map/ppermute | solution.py:260
  42.0 1.5 %collective-permute-start.19 = (bf16[71,16,128]{2,1,0:T(8,128)(2,1)S(1)}, bf16[71,16,128]{2,1,0:T(8,128)(2,1)S(1)}, u32[]{:S(2)}, u32[]{:S(2)}) collective-permute-start(bf16[71,16,128]{2,1,0:T(8,128)(2,1)S(1)} %collective-permute-done.1.refs_1_.refs_17_), channel_id=1, source_target_pairs={{0,16},{4,20},{8,24},{12,28},{16,0},{20,4},{24,8},{28,12},{1,17},{... | collective-permute-start | bytes 872456 | tf_op jit(solution)/shard_map/ppermute | solution.py:260
  43.6 1.5 collective-permute-start.18
  45.1 4.6 %collective-permute-done.6.refs_3_ = bf16[70,16,128]{2,1,0:T(8,128)(2,1)S(1)} collective-permute-done((bf16[70,16,128]{2,1,0:T(8,128)(2,1)}, bf16[70,16,128]{2,1,0:T(8,128)(2,1)S(1)}, u32[]{:S(2)}, u32[]{:S(2)}) %collective-permute-start.6) | collective-permute-done | bytes 286752 | tf_op jit(solution)/shard_map/ppermute | solution.py:260
  49.7 1.4 collective-permute-start.17
  51.1 0.6 add_convert_fusion.1.u_ref
  51.8 1.4 shard_map.137
  53.2 5.1 %shard_map.142 = (bf16[4,4,128,256]{3,2,1,0:T(8,128)(2,1)}, bf16[4,1024,512]{2,1,0:T(8,128)(2,1)}, f32[8,128]{1,0:T(8,128)}) custom-call(f32[4,8,128]{2,1,0:T(8,128)} %get-tuple-element.45.length_ref, f32[512,1]{1,0:T(8,128)} %constant.58.clone.y_ref, f32[1,256]{1,0:T(1,128)} %constant.59.clone.v_ref, f32[64,1]{1,0:T(8,128)} %add_convert_fusion.1.u_ref, ...), custom_call_target="tpu_custom_call" | custom-call | flops 15728640 | bytes 4194304 | tf_op jit(solution)/shard_map/pallas_call | solution.py:674
  58.3 0.7 copy-done.12
  59.0 0.7 shard_map.143
  59.7 0.0 collective-permute-done.20.refs_21_
  59.7 0.5 collective-permute-start.10
  60.2 0.1 collective-permute-start.12
  60.3 0.0 collective-permute-done.18.refs_1_
  60.3 0.4 collective-permute-start.15
  60.7 0.0 collective-permute-done.17.refs_0_
  60.7 0.1 collective-permute-start.11
  60.8 0.7 collective-permute-done.9.refs_9_
  61.5 1.5 %collective-permute-start.7 = (bf16[70,16,128]{2,1,0:T(8,128)(2,1)}, bf16[70,16,128]{2,1,0:T(8,128)(2,1)S(1)}, u32[]{:S(2)}, u32[]{:S(2)}) collective-permute-start(bf16[70,16,128]{2,1,0:T(8,128)(2,1)} %get-tuple-element.49.refs_3_), channel_id=1, source_target_pairs={{0,16},{4,20},{8,24},{12,28},{16,0},{20,4},{24,8},{28,12},{1,17},{... | collective-permute-start | bytes 860168 | tf_op jit(solution)/shard_map/ppermute | solution.py:260
  63.0 0.0 collective-permute-done.10.refs_10_
  63.0 0.0 collective-permute-start.14
  63.0 0.6 collective-permute-start.8
  63.6 0.7 shard_map.144
  64.3 0.2 collective-permute-start.21
  64.5 0.4 collective-permute-start.22
  64.8 5.7 %collective-permute-done.7.refs_5_ = bf16[70,16,128]{2,1,0:T(8,128)(2,1)S(1)} collective-permute-done((bf16[70,16,128]{2,1,0:T(8,128)(2,1)}, bf16[70,16,128]{2,1,0:T(8,128)(2,1)S(1)}, u32[]{:S(2)}, u32[]{:S(2)}) %collective-permute-start.7) | collective-permute-done | bytes 286752 | tf_op jit(solution)/shard_map/ppermute | solution.py:260
  70.6 0.5 collective-permute-start.13
  71.1 1.5 %collective-permute-done.8.refs_8_ = bf16[70,16,128]{2,1,0:T(8,128)(2,1)} collective-permute-done((bf16[70,16,128]{2,1,0:T(8,128)(2,1)}, bf16[70,16,128]{2,1,0:T(8,128)(2,1)}, u32[]{:S(2)}, u32[]{:S(2)}) %collective-permute-start.8) | collective-permute-done | bytes 286752 | tf_op jit(solution)/shard_map/ppermute | solution.py:260
  72.7 1.7 %collective-permute-done.16.refs_16_ = bf16[70,16,128]{2,1,0:T(8,128)(2,1)} collective-permute-done((bf16[70,16,128]{2,1,0:T(8,128)(2,1)}, bf16[70,16,128]{2,1,0:T(8,128)(2,1)}, u32[]{:S(2)}, u32[]{:S(2)}) %collective-permute-start.16) | collective-permute-done | bytes 286752 | tf_op jit(solution)/shard_map/ppermute | solution.py:260
  74.6 20.9 %shard_map.145 = (bf16[4,1,512,256]{3,2,1,0:T(8,128)(2,1)}, f32[96,128,128]{2,1,0:T(8,128)}, f32[96,16,128]{2,1,0:T(8,128)}) custom-call(f32[1]{0:T(128)S(6)} %div.11.inverse_ref, s32[96,4]{1,0:T(8,128)} %constant.61.clone.place, s32[2]{0:T(128)} %pad_add_fusion.where, bf16[560,16,128]{2,1,0:T(8,128)(2,1)} %get-tuple-element.39.refs_0_, ...), custom_call_target="tpu_custom_call" | custom-call | flops 7242450944 | bytes 8388608 | tf_op jit(solution)/shard_map/pallas_call | solution.py:535
  95.5 9.2 %all-to-all-start = ((bf16[4,1,512,256]{3,2,1,0:T(8,128)(2,1)}), bf16[4,1,512,256]{3,2,1,0:T(8,128)(2,1)S(1)}, u32[]{:S(2)}, u32[]{:S(2)}) async-start(bf16[4,1,512,256]{3,2,1,0:T(8,128)(2,1)} %get-tuple-element.65), calls=%async_computation | async-start | bytes 2097152 | tf_op jit(solution)/shard_map/all_to_all | solution.py:778
  104.7 31.3 %shard_map.146 = (f32[4,512,256]{2,1,0:T(8,128)}, f32[4,8,128]{2,1,0:T(8,128)}) custom-call(f32[4]{0:T(128)} %get-tuple-element.37.inverse_ref, f32[96,128,128]{2,1,0:T(8,128)} %get-tuple-element.59.path_in, f32[96,16,128]{2,1,0:T(8,128)} %get-tuple-element.60.opening, bf16[4,4,128,256]{3,2,1,0:T(8,128)(2,1)} %get-tuple-element.61.row_ref, ...), custom_call_target="tpu_custom_call" | custom-call | flops 9642450944 | bytes 8388608 | tf_op jit(solution)/shard_map/pallas_call | solution.py:571
  135.9 2.1 %collective-permute-start.24 = (f32[4,8,128]{2,1,0:T(8,128)}, f32[4,8,128]{2,1,0:T(8,128)S(1)}, u32[]{:S(2)}, u32[]{:S(2)}) collective-permute-start(f32[4,8,128]{2,1,0:T(8,128)} %get-tuple-element.63), channel_id=1, source_target_pairs={{0,1},{1,0},{2,3},{3,2},{4,5},{5,4},{6,7},{7,6},{8,9},{9,8},{10,11... | collective-permute-start | bytes 49160 | tf_op jit(solution)/shard_map/ppermute | solution.py:710
  138.0 1.9 %collective-permute-done.24 = f32[4,8,128]{2,1,0:T(8,128)S(1)} collective-permute-done((f32[4,8,128]{2,1,0:T(8,128)}, f32[4,8,128]{2,1,0:T(8,128)S(1)}, u32[]{:S(2)}, u32[]{:S(2)}) %collective-permute-start.24) | collective-permute-done | bytes 16416 | tf_op jit(solution)/shard_map/ppermute | solution.py:710
  140.0 0.7 add.50
  140.7 2.9 %collective-permute-start.25 = (f32[4,8,128]{2,1,0:T(8,128)S(1)}, f32[4,8,128]{2,1,0:T(8,128)S(1)}, u32[]{:S(2)}, u32[]{:S(2)}) collective-permute-start(f32[4,8,128]{2,1,0:T(8,128)S(1)} %add.50), channel_id=1, source_target_pairs={{0,2},{1,3},{2,0},{3,1},{4,6},{5,7},{6,4},{7,5},{8,10},{9,11},{10,... | collective-permute-start | bytes 49160 | tf_op jit(solution)/shard_map/ppermute | solution.py:710
  143.6 1.7 %collective-permute-done.25 = f32[4,8,128]{2,1,0:T(8,128)S(1)} collective-permute-done((f32[4,8,128]{2,1,0:T(8,128)S(1)}, f32[4,8,128]{2,1,0:T(8,128)S(1)}, u32[]{:S(2)}, u32[]{:S(2)}) %collective-permute-start.25) | collective-permute-done | bytes 16416 | tf_op jit(solution)/shard_map/ppermute | solution.py:710
  145.3 0.0 copy-start.1
  145.4 1.6 %copy-done.1 = f32[4,512,256]{2,1,0:T(8,128)S(1)} copy-done((f32[4,512,256]{2,1,0:T(8,128)S(1)}, f32[4,512,256]{2,1,0:T(8,128)}, u32[]{:S(2)}) %copy-start.1) | copy-done | bytes 2097176
  146.9 2.7 %shard_map.147 = bf16[8,8,64,256]{3,2,1,0:T(8,128)(2,1)} custom-call(f32[4,8,128]{2,1,0:T(8,128)S(1)} %add.51.sum_ref, bf16[8,128,128]{2,1,0:T(8,128)(2,1)S(1)} %copy-done.2, bf16[4,512,256]{2,1,0:T(8,128)(2,1)S(1)} %bitcast.16, f32[4,512,256]{2,1,0:T(8,128)S(1)} %copy-done.1), custom_call_target="tpu_custom_call" | custom-call | tf_op jit(solution)/shard_map/pallas_call | solution.py:623
  (76 shorter events, 0.2 us)
Async XLA Ops:
  0.0 12.7 %copy-start = (bf16[4096,22]{0,1:T(8,128)(2,1)S(1)}, bf16[4096,22]{0,1:T(8,128)(2,1)}, u32[]{:S(2)}) copy-start(bf16[4096,22]{0,1:T(8,128)(2,1)} %param.15) | copy-start | bytes 540676
  0.0 10.6 %copy-start.28 = (s32[8,8]{1,0:T(8,128)S(1)}, s32[8,8]{1,0:T(8,128)}, u32[]{:S(2)}) copy-start(s32[8,8]{1,0:T(8,128)} %param.19) | copy-start | bytes 772
  0.0 10.6 %copy-start.27 = (f32[1024,8]{0,1:T(8,128)S(1)}, f32[1024,8]{0,1:T(8,128)}, u32[]{:S(2)}) copy-start(f32[1024,8]{0,1:T(8,128)} %param.18) | copy-start | bytes 98308
  0.0 12.7 %copy-start.29 = (s32[8]{0:T(128)S(1)}, s32[8]{0:T(128)}, u32[]{:S(2)}) copy-start(s32[8]{0:T(128)} %param.16) | copy-start | bytes 100
  0.7 21.2 %copy-start.13 = (f32[2]{0:T(128)S(1)}, f32[2]{0:T(128)}, u32[]{:S(2)}) copy-start(f32[2]{0:T(128)} %own_lengths.1) | copy-start | bytes 28
  4.5 21.4 %collective-permute-start.2 = (bf16[71,16,128]{2,1,0:T(8,128)(2,1)}, bf16[71,16,128]{2,1,0:T(8,128)(2,1)S(1)}, u32[]{:S(2)}, u32[]{:S(2)}) collective-permute-start(bf16[71,16,128]{2,1,0:T(8,128)(2,1)} %get-tuple-element.36), channel_id=1, source_target_pairs={{0,3},{1,0},{2,1},{3,2},{4,7},{5,4},{6,5},{7,6},{8,11},{9,8},{10,9... | collective-permute-start | bytes 872456 | tf_op jit(solution)/shard_map/ppermute | solution.py:248
  9.6 26.5 %collective-permute-start.1 = (bf16[71,16,128]{2,1,0:T(8,128)(2,1)}, bf16[71,16,128]{2,1,0:T(8,128)(2,1)S(1)}, u32[]{:S(2)}, u32[]{:S(2)}) collective-permute-start(bf16[71,16,128]{2,1,0:T(8,128)(2,1)} %get-tuple-element.36), channel_id=1, source_target_pairs={{0,2},{1,3},{2,0},{3,1},{4,6},{5,7},{6,4},{7,5},{8,10},{9,11},{10,... | collective-permute-start | bytes 872456 | tf_op jit(solution)/shard_map/ppermute | solution.py:248
  9.6 19.9 %collective-permute-start = (bf16[71,16,128]{2,1,0:T(8,128)(2,1)}, bf16[71,16,128]{2,1,0:T(8,128)(2,1)S(1)}, u32[]{:S(2)}, u32[]{:S(2)}) collective-permute-start(bf16[71,16,128]{2,1,0:T(8,128)(2,1)} %get-tuple-element.36), channel_id=1, source_target_pairs={{0,1},{1,2},{2,3},{3,0},{4,5},{5,6},{6,7},{7,4},{8,9},{9,10},{10,1... | collective-permute-start | bytes 872456 | tf_op jit(solution)/shard_map/ppermute | solution.py:248
  19.9 52.7 %copy-start.14 = (f32[2]{0:T(128)S(1)}, f32[2]{0:T(128)}, u32[]{:S(2)}) copy-start(f32[2]{0:T(128)} %own_lengths.1) | copy-start | bytes 28
  25.9 3.5 %copy-start.3 = (bf16[71,16,128]{2,1,0:T(8,128)(2,1)}, bf16[71,16,128]{2,1,0:T(8,128)(2,1)S(1)}, u32[]{:S(2)}) copy-start(bf16[71,16,128]{2,1,0:T(8,128)(2,1)S(1)} %collective-permute-done.2.refs_2_.refs_1_) | copy-start | bytes 872452
  29.4 0.7 copy-start.4
  32.1 10.0 %collective-permute-start.4 = (bf16[70,16,128]{2,1,0:T(8,128)(2,1)}, bf16[70,16,128]{2,1,0:T(8,128)(2,1)S(1)}, u32[]{:S(2)}, u32[]{:S(2)}) collective-permute-start(bf16[70,16,128]{2,1,0:T(8,128)(2,1)} %get-tuple-element.43.refs_4_), channel_id=1, source_target_pairs={{0,16},{4,20},{8,24},{12,28},{16,0},{20,4},{24,8},{28,12},{1,17},{... | collective-permute-start | bytes 860168 | tf_op jit(solution)/shard_map/ppermute | solution.py:260
  33.6 10.0 %collective-permute-start.3 = (bf16[70,16,128]{2,1,0:T(8,128)(2,1)}, bf16[70,16,128]{2,1,0:T(8,128)(2,1)S(1)}, u32[]{:S(2)}, u32[]{:S(2)}) collective-permute-start(bf16[70,16,128]{2,1,0:T(8,128)(2,1)} %get-tuple-element.43.refs_4_), channel_id=1, source_target_pairs={{0,8},{4,12},{8,0},{12,4},{16,24},{20,28},{24,16},{28,20},{1,9},{5... | collective-permute-start | bytes 860168 | tf_op jit(solution)/shard_map/ppermute | solution.py:260
  35.1 14.6 %collective-permute-start.6 = (bf16[70,16,128]{2,1,0:T(8,128)(2,1)}, bf16[70,16,128]{2,1,0:T(8,128)(2,1)S(1)}, u32[]{:S(2)}, u32[]{:S(2)}) collective-permute-start(bf16[70,16,128]{2,1,0:T(8,128)(2,1)} %get-tuple-element.44.refs_5_), channel_id=1, source_target_pairs={{0,8},{4,12},{8,0},{12,4},{16,24},{20,28},{24,16},{28,20},{1,9},{5... | collective-permute-start | bytes 860168 | tf_op jit(solution)/shard_map/ppermute | solution.py:260
  35.6 22.7 %collective-permute-start.5 = (bf16[70,16,128]{2,1,0:T(8,128)(2,1)}, bf16[70,16,128]{2,1,0:T(8,128)(2,1)S(1)}, u32[]{:S(2)}, u32[]{:S(2)}) collective-permute-start(bf16[70,16,128]{2,1,0:T(8,128)(2,1)} %get-tuple-element.44.refs_5_), channel_id=1, source_target_pairs={{0,16},{4,20},{8,24},{12,28},{16,0},{20,4},{24,8},{28,12},{1,17},{... | collective-permute-start | bytes 860168 | tf_op jit(solution)/shard_map/ppermute | solution.py:260
  36.1 15.6 %copy-start.5 = (bf16[71,16,128]{2,1,0:T(8,128)(2,1)}, bf16[71,16,128]{2,1,0:T(8,128)(2,1)S(1)}, u32[]{:S(2)}) copy-start(bf16[71,16,128]{2,1,0:T(8,128)(2,1)S(1)} %collective-permute-done.1.refs_1_.refs_17_) | copy-start | bytes 872452
  36.1 23.6 %collective-permute-start.20 = (bf16[71,16,128]{2,1,0:T(8,128)(2,1)S(1)}, bf16[71,16,128]{2,1,0:T(8,128)(2,1)S(1)}, u32[]{:S(2)}, u32[]{:S(2)}) collective-permute-start(bf16[71,16,128]{2,1,0:T(8,128)(2,1)S(1)} %collective-permute-done.1.refs_1_.refs_17_), channel_id=1, source_target_pairs={{0,4},{4,0},{8,12},{12,8},{16,20},{20,16},{24,28},{28,24},{1,5},{5... | collective-permute-start | bytes 872456 | tf_op jit(solution)/shard_map/ppermute | solution.py:260
  42.0 16.3 %copy-start.9 = (bf16[70,16,128]{2,1,0:T(8,128)(2,1)}, bf16[70,16,128]{2,1,0:T(8,128)(2,1)S(1)}, u32[]{:S(2)}) copy-start(bf16[70,16,128]{2,1,0:T(8,128)(2,1)S(1)} %collective-permute-done.4.refs_1_) | copy-start | bytes 860164
  42.0 18.2 %collective-permute-start.19 = (bf16[71,16,128]{2,1,0:T(8,128)(2,1)S(1)}, bf16[71,16,128]{2,1,0:T(8,128)(2,1)S(1)}, u32[]{:S(2)}, u32[]{:S(2)}) collective-permute-start(bf16[71,16,128]{2,1,0:T(8,128)(2,1)S(1)} %collective-permute-done.1.refs_1_.refs_17_), channel_id=1, source_target_pairs={{0,16},{4,20},{8,24},{12,28},{16,0},{20,4},{24,8},{28,12},{1,17},{... | collective-permute-start | bytes 872456 | tf_op jit(solution)/shard_map/ppermute | solution.py:260
  43.6 14.7 %copy-start.10 = (bf16[70,16,128]{2,1,0:T(8,128)(2,1)}, bf16[70,16,128]{2,1,0:T(8,128)(2,1)S(1)}, u32[]{:S(2)}) copy-start(bf16[70,16,128]{2,1,0:T(8,128)(2,1)S(1)} %collective-permute-done.3.refs_0_) | copy-start | bytes 860164
  43.6 16.7 %collective-permute-start.18 = (bf16[71,16,128]{2,1,0:T(8,128)(2,1)S(1)}, bf16[71,16,128]{2,1,0:T(8,128)(2,1)S(1)}, u32[]{:S(2)}, u32[]{:S(2)}) collective-permute-start(bf16[71,16,128]{2,1,0:T(8,128)(2,1)S(1)} %collective-permute-done.1.refs_1_.refs_17_), channel_id=1, source_target_pairs={{0,8},{4,12},{8,0},{12,4},{16,24},{20,28},{24,16},{28,20},{1,9},{5... | collective-permute-start | bytes 872456 | tf_op jit(solution)/shard_map/ppermute | solution.py:260
  49.7 8.6 %copy-start.11 = (bf16[70,16,128]{2,1,0:T(8,128)(2,1)}, bf16[70,16,128]{2,1,0:T(8,128)(2,1)S(1)}, u32[]{:S(2)}) copy-start(bf16[70,16,128]{2,1,0:T(8,128)(2,1)S(1)} %collective-permute-done.6.refs_3_) | copy-start | bytes 860164
  49.7 11.0 %collective-permute-start.17 = (bf16[71,16,128]{2,1,0:T(8,128)(2,1)S(1)}, bf16[71,16,128]{2,1,0:T(8,128)(2,1)S(1)}, u32[]{:S(2)}, u32[]{:S(2)}) collective-permute-start(bf16[71,16,128]{2,1,0:T(8,128)(2,1)S(1)} %collective-permute-done.1.refs_1_.refs_17_), channel_id=1, source_target_pairs={{0,24},{4,28},{8,16},{12,20},{16,8},{20,12},{24,0},{28,4},{1,25},{... | collective-permute-start | bytes 872456 | tf_op jit(solution)/shard_map/ppermute | solution.py:260
  58.3 0.7 copy-start.12
  59.7 1.8 %collective-permute-start.9 = (bf16[70,16,128]{2,1,0:T(8,128)(2,1)}, bf16[70,16,128]{2,1,0:T(8,128)(2,1)S(1)}, u32[]{:S(2)}, u32[]{:S(2)}) collective-permute-start(bf16[70,16,128]{2,1,0:T(8,128)(2,1)} %get-tuple-element.47.refs_1_), channel_id=1, source_target_pairs={{0,4},{4,0},{8,12},{12,8},{16,20},{20,16},{24,28},{28,24},{1,5},{5... | collective-permute-start | bytes 860168 | tf_op jit(solution)/shard_map/ppermute | solution.py:260
  59.7 14.8 %copy-start.15 = (bf16[71,16,128]{2,1,0:T(8,128)(2,1)}, bf16[71,16,128]{2,1,0:T(8,128)(2,1)S(1)}, u32[]{:S(2)}) copy-start(bf16[71,16,128]{2,1,0:T(8,128)(2,1)S(1)} %collective-permute-done.20.refs_21_) | copy-start | bytes 872452
  59.7 3.3 %collective-permute-start.10 = (bf16[70,16,128]{2,1,0:T(8,128)(2,1)}, bf16[70,16,128]{2,1,0:T(8,128)(2,1)S(1)}, u32[]{:S(2)}, u32[]{:S(2)}) collective-permute-start(bf16[70,16,128]{2,1,0:T(8,128)(2,1)} %get-tuple-element.48.refs_2_), channel_id=1, source_target_pairs={{0,4},{4,0},{8,12},{12,8},{16,20},{20,16},{24,28},{28,24},{1,5},{5... | collective-permute-start | bytes 860168 | tf_op jit(solution)/shard_map/ppermute | solution.py:260
  60.2 3.4 %copy-start.6 = (bf16[71,16,128]{2,1,0:T(8,128)(2,1)}, bf16[71,16,128]{2,1,0:T(8,128)(2,1)S(1)}, u32[]{:S(2)}) copy-start(bf16[71,16,128]{2,1,0:T(8,128)(2,1)S(1)} %collective-permute-done.19.refs_2_) | copy-start | bytes 872452
  60.2 2.8 %collective-permute-start.12 = (bf16[70,16,128]{2,1,0:T(8,128)(2,1)}, bf16[70,16,128]{2,1,0:T(8,128)(2,1)S(1)}, u32[]{:S(2)}, u32[]{:S(2)}) collective-permute-start(bf16[70,16,128]{2,1,0:T(8,128)(2,1)} %get-tuple-element.50.refs_4_), channel_id=1, source_target_pairs={{0,4},{4,0},{8,12},{12,8},{16,20},{20,16},{24,28},{28,24},{1,5},{5... | collective-permute-start | bytes 860168 | tf_op jit(solution)/shard_map/ppermute | solution.py:260
  60.3 3.3 %copy-start.7 = (bf16[71,16,128]{2,1,0:T(8,128)(2,1)}, bf16[71,16,128]{2,1,0:T(8,128)(2,1)S(1)}, u32[]{:S(2)}) copy-start(bf16[71,16,128]{2,1,0:T(8,128)(2,1)S(1)} %collective-permute-done.18.refs_1_) | copy-start | bytes 872452
  60.3 4.0 %collective-permute-start.15 = (bf16[70,16,128]{2,1,0:T(8,128)(2,1)}, bf16[70,16,128]{2,1,0:T(8,128)(2,1)S(1)}, u32[]{:S(2)}, u32[]{:S(2)}) collective-permute-start(bf16[70,16,128]{2,1,0:T(8,128)(2,1)} %get-tuple-element.52.refs_7_), channel_id=1, source_target_pairs={{0,4},{4,0},{8,12},{12,8},{16,20},{20,16},{24,28},{28,24},{1,5},{5... | collective-permute-start | bytes 860168 | tf_op jit(solution)/shard_map/ppermute | solution.py:260
  60.7 2.9 %copy-start.8 = (bf16[71,16,128]{2,1,0:T(8,128)(2,1)}, bf16[71,16,128]{2,1,0:T(8,128)(2,1)S(1)}, u32[]{:S(2)}) copy-start(bf16[71,16,128]{2,1,0:T(8,128)(2,1)S(1)} %collective-permute-done.17.refs_0_) | copy-start | bytes 872452
  60.7 3.7 %collective-permute-start.11 = (bf16[70,16,128]{2,1,0:T(8,128)(2,1)}, bf16[70,16,128]{2,1,0:T(8,128)(2,1)S(1)}, u32[]{:S(2)}, u32[]{:S(2)}) collective-permute-start(bf16[70,16,128]{2,1,0:T(8,128)(2,1)} %get-tuple-element.49.refs_3_), channel_id=1, source_target_pairs={{0,4},{4,0},{8,12},{12,8},{16,20},{20,16},{24,28},{28,24},{1,5},{5... | collective-permute-start | bytes 860168 | tf_op jit(solution)/shard_map/ppermute | solution.py:260
  61.5 13.0 %copy-start.19 = (bf16[70,16,128]{2,1,0:T(8,128)(2,1)}, bf16[70,16,128]{2,1,0:T(8,128)(2,1)S(1)}, u32[]{:S(2)}) copy-start(bf16[70,16,128]{2,1,0:T(8,128)(2,1)S(1)} %collective-permute-done.9.refs_9_) | copy-start | bytes 860164
  61.5 9.1 %collective-permute-start.7 = (bf16[70,16,128]{2,1,0:T(8,128)(2,1)}, bf16[70,16,128]{2,1,0:T(8,128)(2,1)S(1)}, u32[]{:S(2)}, u32[]{:S(2)}) collective-permute-start(bf16[70,16,128]{2,1,0:T(8,128)(2,1)} %get-tuple-element.49.refs_3_), channel_id=1, source_target_pairs={{0,16},{4,20},{8,24},{12,28},{16,0},{20,4},{24,8},{28,12},{1,17},{... | collective-permute-start | bytes 860168 | tf_op jit(solution)/shard_map/ppermute | solution.py:260
  63.0 11.5 %copy-start.20 = (bf16[70,16,128]{2,1,0:T(8,128)(2,1)}, bf16[70,16,128]{2,1,0:T(8,128)(2,1)S(1)}, u32[]{:S(2)}) copy-start(bf16[70,16,128]{2,1,0:T(8,128)(2,1)S(1)} %collective-permute-done.10.refs_10_) | copy-start | bytes 860164
  63.0 7.6 %collective-permute-start.14 = (bf16[70,16,128]{2,1,0:T(8,128)(2,1)}, bf16[70,16,128]{2,1,0:T(8,128)(2,1)S(1)}, u32[]{:S(2)}, u32[]{:S(2)}) collective-permute-start(bf16[70,16,128]{2,1,0:T(8,128)(2,1)} %get-tuple-element.51.refs_6_), channel_id=1, source_target_pairs={{0,4},{4,0},{8,12},{12,8},{16,20},{20,16},{24,28},{28,24},{1,5},{5... | collective-permute-start | bytes 860168 | tf_op jit(solution)/shard_map/ppermute | solution.py:260
  63.0 11.5 %copy-start.21 = (bf16[70,16,128]{2,1,0:T(8,128)(2,1)}, bf16[70,16,128]{2,1,0:T(8,128)(2,1)S(1)}, u32[]{:S(2)}) copy-start(bf16[70,16,128]{2,1,0:T(8,128)(2,1)S(1)} %collective-permute-done.12.refs_12_) | copy-start | bytes 860164
  63.0 9.6 %collective-permute-start.8 = (bf16[70,16,128]{2,1,0:T(8,128)(2,1)}, bf16[70,16,128]{2,1,0:T(8,128)(2,1)}, u32[]{:S(2)}, u32[]{:S(2)}) collective-permute-start(bf16[70,16,128]{2,1,0:T(8,128)(2,1)} %get-tuple-element.51.refs_6_), channel_id=1, source_target_pairs={{0,8},{4,12},{8,0},{12,4},{16,24},{20,28},{24,16},{28,20},{1,9},{5... | collective-permute-start | bytes 860168 | tf_op jit(solution)/shard_map/ppermute | solution.py:260
  64.3 10.2 %copy-start.22 = (bf16[70,16,128]{2,1,0:T(8,128)(2,1)}, bf16[70,16,128]{2,1,0:T(8,128)(2,1)S(1)}, u32[]{:S(2)}) copy-start(bf16[70,16,128]{2,1,0:T(8,128)(2,1)S(1)} %collective-permute-done.15.refs_15_) | copy-start | bytes 860164
  64.3 8.4 %collective-permute-start.21 = (bf16[71,16,128]{2,1,0:T(8,128)(2,1)}, bf16[71,16,128]{2,1,0:T(8,128)(2,1)S(1)}, u32[]{:S(2)}, u32[]{:S(2)}) collective-permute-start(bf16[71,16,128]{2,1,0:T(8,128)(2,1)} %get-tuple-element.53.refs_18_), channel_id=1, source_target_pairs={{0,4},{4,0},{8,12},{12,8},{16,20},{20,16},{24,28},{28,24},{1,5},{5... | collective-permute-start | bytes 872456 | tf_op jit(solution)/shard_map/ppermute | solution.py:260
  64.5 10.1 %copy-start.23 = (bf16[70,16,128]{2,1,0:T(8,128)(2,1)}, bf16[70,16,128]{2,1,0:T(8,128)(2,1)S(1)}, u32[]{:S(2)}) copy-start(bf16[70,16,128]{2,1,0:T(8,128)(2,1)S(1)} %collective-permute-done.11.refs_11_) | copy-start | bytes 860164
  64.5 8.2 %collective-permute-start.22 = (bf16[71,16,128]{2,1,0:T(8,128)(2,1)}, bf16[71,16,128]{2,1,0:T(8,128)(2,1)S(1)}, u32[]{:S(2)}, u32[]{:S(2)}) collective-permute-start(bf16[71,16,128]{2,1,0:T(8,128)(2,1)} %get-tuple-element.54.refs_19_), channel_id=1, source_target_pairs={{0,4},{4,0},{8,12},{12,8},{16,20},{20,16},{24,28},{28,24},{1,5},{5... | collective-permute-start | bytes 872456 | tf_op jit(solution)/shard_map/ppermute | solution.py:260
  70.5 4.0 %copy-start.24 = (bf16[70,16,128]{2,1,0:T(8,128)(2,1)}, bf16[70,16,128]{2,1,0:T(8,128)(2,1)S(1)}, u32[]{:S(2)}) copy-start(bf16[70,16,128]{2,1,0:T(8,128)(2,1)S(1)} %collective-permute-done.7.refs_5_) | copy-start | bytes 860164
  70.5 2.2 %collective-permute-start.23 = (bf16[71,16,128]{2,1,0:T(8,128)(2,1)}, bf16[71,16,128]{2,1,0:T(8,128)(2,1)S(1)}, u32[]{:S(2)}, u32[]{:S(2)}) collective-permute-start(bf16[71,16,128]{2,1,0:T(8,128)(2,1)} %get-tuple-element.55.refs_20_), channel_id=1, source_target_pairs={{0,4},{4,0},{8,12},{12,8},{16,20},{20,16},{24,28},{28,24},{1,5},{5... | collective-permute-start | bytes 872456 | tf_op jit(solution)/shard_map/ppermute | solution.py:260
  70.6 4.0 %copy-start.25 = (bf16[70,16,128]{2,1,0:T(8,128)(2,1)}, bf16[70,16,128]{2,1,0:T(8,128)(2,1)S(1)}, u32[]{:S(2)}) copy-start(bf16[70,16,128]{2,1,0:T(8,128)(2,1)S(1)} %collective-permute-done.14.refs_14_) | copy-start | bytes 860164
  70.6 2.2 %collective-permute-start.13 = (bf16[70,16,128]{2,1,0:T(8,128)(2,1)S(1)}, bf16[70,16,128]{2,1,0:T(8,128)(2,1)S(1)}, u32[]{:S(2)}, u32[]{:S(2)}) collective-permute-start(bf16[70,16,128]{2,1,0:T(8,128)(2,1)S(1)} %collective-permute-done.7.refs_5_), channel_id=1, source_target_pairs={{0,4},{4,0},{8,12},{12,8},{16,20},{20,16},{24,28},{28,24},{1,5},{5... | collective-permute-start | bytes 860168 | tf_op jit(solution)/shard_map/ppermute | solution.py:260
  72.6 1.9 %collective-permute-start.16 = (bf16[70,16,128]{2,1,0:T(8,128)(2,1)}, bf16[70,16,128]{2,1,0:T(8,128)(2,1)}, u32[]{:S(2)}, u32[]{:S(2)}) collective-permute-start(bf16[70,16,128]{2,1,0:T(8,128)(2,1)} %collective-permute-done.8.refs_8_), channel_id=1, source_target_pairs={{0,4},{4,0},{8,12},{12,8},{16,20},{20,16},{24,28},{28,24},{1,5},{5... | collective-permute-start | bytes 860168 | tf_op jit(solution)/shard_map/ppermute | solution.py:260
  72.7 1.9 %copy-start.16 = (bf16[71,16,128]{2,1,0:T(8,128)(2,1)}, bf16[71,16,128]{2,1,0:T(8,128)(2,1)S(1)}, u32[]{:S(2)}) copy-start(bf16[71,16,128]{2,1,0:T(8,128)(2,1)S(1)} %collective-permute-done.21.refs_22_) | copy-start | bytes 872452
  72.7 1.9 %copy-start.17 = (bf16[71,16,128]{2,1,0:T(8,128)(2,1)}, bf16[71,16,128]{2,1,0:T(8,128)(2,1)S(1)}, u32[]{:S(2)}) copy-start(bf16[71,16,128]{2,1,0:T(8,128)(2,1)S(1)} %collective-permute-done.22.refs_23_) | copy-start | bytes 872452
  72.7 1.9 %copy-start.18 = (bf16[71,16,128]{2,1,0:T(8,128)(2,1)}, bf16[71,16,128]{2,1,0:T(8,128)(2,1)S(1)}, u32[]{:S(2)}) copy-start(bf16[71,16,128]{2,1,0:T(8,128)(2,1)S(1)} %collective-permute-done.23.refs_24_) | copy-start | bytes 872452
  72.7 1.8 %copy-start.26 = (bf16[70,16,128]{2,1,0:T(8,128)(2,1)}, bf16[70,16,128]{2,1,0:T(8,128)(2,1)S(1)}, u32[]{:S(2)}) copy-start(bf16[70,16,128]{2,1,0:T(8,128)(2,1)S(1)} %collective-permute-done.13.refs_13_) | copy-start | bytes 860164
  95.5 49.9 %all-to-all-start = ((bf16[4,1,512,256]{3,2,1,0:T(8,128)(2,1)}), bf16[4,1,512,256]{3,2,1,0:T(8,128)(2,1)S(1)}, u32[]{:S(2)}, u32[]{:S(2)}) async-start(bf16[4,1,512,256]{3,2,1,0:T(8,128)(2,1)} %get-tuple-element.65), calls=%async_computation | async-start | bytes 2097152 | tf_op jit(solution)/shard_map/all_to_all | solution.py:778
  104.7 40.7 %copy-start.2 = (bf16[8,128,128]{2,1,0:T(8,128)(2,1)S(1)}, bf16[8,128,128]{2,1,0:T(8,128)(2,1)}, u32[]{:S(2)}) copy-start(bf16[8,128,128]{2,1,0:T(8,128)(2,1)} %get-tuple-element.64.weight_ref) | copy-start | bytes 786436
  135.9 4.0 %collective-permute-start.24 = (f32[4,8,128]{2,1,0:T(8,128)}, f32[4,8,128]{2,1,0:T(8,128)S(1)}, u32[]{:S(2)}, u32[]{:S(2)}) collective-permute-start(f32[4,8,128]{2,1,0:T(8,128)} %get-tuple-element.63), channel_id=1, source_target_pairs={{0,1},{1,0},{2,3},{3,2},{4,5},{5,4},{6,7},{7,6},{8,9},{9,8},{10,11... | collective-permute-start | bytes 49160 | tf_op jit(solution)/shard_map/ppermute | solution.py:710
  140.7 4.6 %collective-permute-start.25 = (f32[4,8,128]{2,1,0:T(8,128)S(1)}, f32[4,8,128]{2,1,0:T(8,128)S(1)}, u32[]{:S(2)}, u32[]{:S(2)}) collective-permute-start(f32[4,8,128]{2,1,0:T(8,128)S(1)} %add.50), channel_id=1, source_target_pairs={{0,2},{1,3},{2,0},{3,1},{4,6},{5,7},{6,4},{7,5},{8,10},{9,11},{10,... | collective-permute-start | bytes 49160 | tf_op jit(solution)/shard_map/ppermute | solution.py:710
  145.3 1.6 %copy-start.1 = (f32[4,512,256]{2,1,0:T(8,128)S(1)}, f32[4,512,256]{2,1,0:T(8,128)}, u32[]{:S(2)}) copy-start(f32[4,512,256]{2,1,0:T(8,128)} %get-tuple-element.66.image_ref) | copy-start | bytes 6291460
